TPU v7x, 32 devices: a whole 2x2x4 slice. The times are simulated.
32 devices in a mesh: dev: 32 (over z, y, x, core).
Axes of the slice: x: 2, y: 2, z: 4, core: 2. Of those that a mesh axis runs over, the one named last changes fastest.
Arguments:
- tokens: bfloat16 [8192, 2048], P('dev'), may hold values from -6 to 6
- cotangent: bfloat16 [8192, 2048], P('dev'), may hold values from -6 to 6
- segment_ids: int32 [8192], replicated, may hold values from 0 to 14, as said below
- piece_ids: int32 [8192], replicated, may hold values from 0 to 15, as said below
- w_query: float32 [2048, 2048], P('dev'), may hold values from -0.125 to 0.125
- w_key: float32 [2048, 2048], P('dev'), may hold values from -0.125 to 0.125
- w_value: float32 [2048, 2048], P('dev'), may hold values from -0.125 to 0.125
- w_out: float32 [2048, 2048], P('dev'), may hold values from -0.125 to 0.125
- query_gain: float32 [2048], P('dev'), may hold values from 0.1 to 1.9
- key_gain: float32 [2048], P('dev'), may hold values from 0.1 to 1.9
- mixer_gain: float32 [2048], P('dev'), may hold values from 0.1 to 1.9
- w_gate: float32 [2048, 8192], P('dev'), may hold values from -0.125 to 0.125
- w_up: float32 [2048, 8192], P('dev'), may hold values from -0.125 to 0.125
- w_down: float32 [8192, 2048], P('dev'), may hold values from -0.0625 to 0.0625
- feed_gain: float32 [2048], P('dev'), may hold values from 0.1 to 1.9
Outputs:
- out_tokens: bfloat16 [8192, 2048], P('dev')
- g_tokens: float32 [8192, 2048], P('dev')
- g_w_query: float32 [2048, 2048], P('dev')
- g_w_key: float32 [2048, 2048], P('dev')
- g_w_value: float32 [2048, 2048], P('dev')
- g_w_out: float32 [2048, 2048], P('dev')
- g_query_gain: float32 [2048], P('dev')
- g_key_gain: float32 [2048], P('dev')
- g_mixer_gain: float32 [2048], P('dev')
- g_w_gate: float32 [2048, 8192], P('dev')
- g_w_up: float32 [2048, 8192], P('dev')
- g_w_down: float32 [8192, 2048], P('dev')
- g_feed_gain: float32 [2048], P('dev')
Inputs may be any that keep to these rules, and one draw needn't show every extreme that they name: `segment_ids`: starts at 0, never falls, rises by one at each new sequence; no sequence crosses a multiple of 1024 tokens; the first sequence holds exactly 1024 tokens, and each following aligned run of 1024 tokens holds exactly two sequences of 256 tokens or more. `piece_ids`: 0 marks text; value s + 1 marks the picture piece of sequence s, one run of exactly 256 tokens inside that sequence; a sequence has at most one piece, and the first and the last sequence have one.
All inputs are finite; a program needn't handle non-finite values.
Results may differ from a plain program's by a relative error of at most 0.015.
The roundings to bfloat16 on the way count: a program that leaves them out, or rounds other values in their place, can miss the bound.
Values may be sent and summed in bfloat16 or wider, within the bound.
No kernel may reach another device: no remote copies, remote signals or barrier semaphores. Data moves between devices by JAX's collectives and lax.ppermute only.
A program may use at most 512 MiB of HBM per device.

v0:
```python
import math

import jax
import jax.numpy as jnp
from jax import lax
from jax.sharding import PartitionSpec as P

HEAD = 128
SEQ_MAX = 1024
PIECE = 256


NORM_EPS = 1e-06
ROPE_BASE = 500000.0
MASKED = -1e30


def from_behind(block, axis, distance):
    devices = range(lax.axis_size(axis))
    route = [(i - distance, i) for i in devices if i - distance in devices]
    return lax.ppermute(block, axis, route)


def rms_norm(values, norm_gain):
    return (
        values * lax.rsqrt(jnp.mean(values * values, axis=-1, keepdims=True) + NORM_EPS) * norm_gain
    )


def segment_positions(segment_ids):
    places = jnp.arange(segment_ids.shape[0], dtype=jnp.int32)
    opens = jnp.concatenate([jnp.ones((1,), bool), segment_ids[1:] != segment_ids[:-1]])
    starts = lax.cummax(jnp.where(opens, places, 0), axis=0)
    return places - starts


def rope_tables(positions):
    freqs = jnp.exp(jnp.arange(HEAD // 2, dtype=jnp.float32) * (-2.0 * math.log(ROPE_BASE) / HEAD))
    angles = positions.astype(jnp.float32)[:, None] * freqs[None, :]
    return (jnp.cos(angles), jnp.sin(angles))


def rotate(values, cosine, sine_table):
    row_count = values.shape[0]
    head_count = values.shape[1] // HEAD
    shaped = values.reshape(row_count, head_count, HEAD)
    first_half = shaped[:, :, : HEAD // 2]
    second_half = shaped[:, :, HEAD // 2 :]
    cos_rows = cosine[:, None, :]
    sin_rows = sine_table[:, None, :]
    turned = jnp.concatenate(
        [
            first_half * cos_rows - second_half * sin_rows,
            second_half * cos_rows + first_half * sin_rows,
        ],
        axis=-1,
    )
    return turned.reshape(row_count, head_count * HEAD)


def gated(gate_proj, up_proj):
    return jax.nn.silu(gate_proj) * up_proj


def matmul(left, right):
    return jnp.dot(left, right, preferred_element_type=jnp.float32)


def matmul_t(left, right):
    return lax.dot_general(
        left, right, (((1,), (1,)), ((), ())), preferred_element_type=jnp.float32
    )


def inner_t(left, right):
    return lax.dot_general(
        left, right, (((0,), (0,)), ((), ())), preferred_element_type=jnp.float32
    )


def move_keys(stacked, offset):
    return from_behind(stacked, "dev", offset)


def move_grads(stacked, offset):
    return from_behind(stacked.astype(jnp.bfloat16), "dev", offset).astype(stacked.dtype)


def gather_near(own_pair, behind):
    earlier = []
    for offset in range(1, behind + 1):
        earlier.append(move_keys(own_pair, offset))
    offset = 1
    later = [move_keys(own_pair, -offset)]
    return earlier[::-1] + [own_pair] + later


def return_near(pieces, behind):
    earlier = pieces[:behind][::-1]
    later = pieces[behind + 1 :]
    total = pieces[behind]
    for offset in range(1, behind + 1):
        total = total + move_grads(earlier[offset - 1], -offset)
    offset = 1
    total = total + move_grads(later[offset - 1], offset)
    return total


def gather_mixer(w_query, w_key, w_value, w_out, query_gain, key_gain, mixer_gain):
    return (
        lax.all_gather(w_query.astype(jnp.bfloat16), "dev", axis=0, tiled=True),
        lax.all_gather(w_key.astype(jnp.bfloat16), "dev", axis=0, tiled=True),
        lax.all_gather(w_value.astype(jnp.bfloat16), "dev", axis=0, tiled=True),
        lax.all_gather(w_out.astype(jnp.bfloat16), "dev", axis=0, tiled=True),
        lax.all_gather(query_gain.astype(jnp.bfloat16), "dev", axis=0, tiled=True),
        lax.all_gather(key_gain.astype(jnp.bfloat16), "dev", axis=0, tiled=True),
        lax.all_gather(mixer_gain.astype(jnp.bfloat16), "dev", axis=0, tiled=True),
    )


def gather_mixer_again(w_query, w_key, w_value, w_out, query_gain, key_gain, mixer_gain):
    return (
        lax.all_gather(w_query.astype(jnp.bfloat16), "dev", axis=0, tiled=True),
        lax.all_gather(w_key.astype(jnp.bfloat16), "dev", axis=0, tiled=True),
        lax.all_gather(w_value.astype(jnp.bfloat16), "dev", axis=0, tiled=True),
        lax.all_gather(w_out.astype(jnp.bfloat16), "dev", axis=0, tiled=True),
        lax.all_gather(query_gain.astype(jnp.bfloat16), "dev", axis=0, tiled=True),
        lax.all_gather(key_gain.astype(jnp.bfloat16), "dev", axis=0, tiled=True),
        lax.all_gather(mixer_gain.astype(jnp.bfloat16), "dev", axis=0, tiled=True),
    )


def gather_feed(w_gate, w_up, w_down, feed_gain):
    return (
        lax.all_gather(w_gate.astype(jnp.bfloat16), "dev", axis=0, tiled=True),
        lax.all_gather(w_up.astype(jnp.bfloat16), "dev", axis=0, tiled=True),
        lax.all_gather(w_down.astype(jnp.bfloat16), "dev", axis=0, tiled=True),
        lax.all_gather(feed_gain.astype(jnp.bfloat16), "dev", axis=0, tiled=True),
    )


def gather_feed_again(w_gate, w_up, w_down, feed_gain):
    return (
        lax.all_gather(w_gate.astype(jnp.bfloat16), "dev", axis=0, tiled=True),
        lax.all_gather(w_up.astype(jnp.bfloat16), "dev", axis=0, tiled=True),
        lax.all_gather(w_down.astype(jnp.bfloat16), "dev", axis=0, tiled=True),
        lax.all_gather(feed_gain.astype(jnp.bfloat16), "dev", axis=0, tiled=True),
    )


def body(
    tokens,
    cotangent,
    segment_ids,
    piece_ids,
    w_query,
    w_key,
    w_value,
    w_out,
    query_gain,
    key_gain,
    mixer_gain,
    w_gate,
    w_up,
    w_down,
    feed_gain,
):
    row_count = tokens.shape[0]
    width = tokens.shape[1]
    head_count = width // HEAD
    device = lax.axis_index("dev")
    first_row = device * row_count
    behind = (SEQ_MAX + row_count - 2) // row_count
    ahead = (PIECE + row_count - 2) // row_count
    window = row_count * (behind + 1 + ahead)
    score_scale = HEAD ** (-0.5)
    positions = lax.dynamic_slice_in_dim(segment_positions(segment_ids), first_row, row_count, 0)
    cosine, sine_table = rope_tables(positions)
    segment_pad = jnp.pad(segment_ids, (behind * row_count, ahead * row_count), constant_values=-1)
    piece_pad = jnp.pad(piece_ids, (behind * row_count, ahead * row_count))
    segment_query = lax.dynamic_slice_in_dim(segment_ids, first_row, row_count, 0)
    piece_query = lax.dynamic_slice_in_dim(piece_ids, first_row, row_count, 0)
    segment_key = lax.dynamic_slice_in_dim(segment_pad, first_row, window, 0)
    piece_key = lax.dynamic_slice_in_dim(piece_pad, first_row, window, 0)
    query_place = first_row + jnp.arange(row_count, dtype=jnp.int32)
    key_place = first_row - behind * row_count + jnp.arange(window, dtype=jnp.int32)
    visible = (segment_query[:, None] == segment_key[None, :]) & (
        (key_place[None, :] <= query_place[:, None])
        | (piece_query[:, None] == piece_key[None, :]) & (piece_query[:, None] > 0)
    )

    def embed(values, norm_gain):
        return rotate(rms_norm(values, norm_gain), cosine, sine_table)

    mixer = gather_mixer(w_query, w_key, w_value, w_out, query_gain, key_gain, mixer_gain)
    query_gain_full = mixer[4].astype(jnp.float32)
    key_gain_full = mixer[5].astype(jnp.float32)
    mixer_gain_full = mixer[6].astype(jnp.float32)
    query = matmul(tokens, mixer[0])
    key_proj = matmul(tokens, mixer[1])
    value_proj = matmul(tokens, mixer[2])
    query_rot = embed(query, query_gain_full).astype(jnp.bfloat16)
    key_rot = embed(key_proj, key_gain_full).astype(jnp.bfloat16)
    value_low = value_proj.astype(jnp.bfloat16)
    near_pairs = gather_near(jnp.stack([key_rot, value_low]), behind)
    window_pair = jnp.concatenate(near_pairs, axis=1)
    key_block = window_pair[0].reshape(window, head_count, HEAD)
    value_block = window_pair[1].reshape(window, head_count, HEAD)
    query_block = query_rot.reshape(row_count, head_count, HEAD)
    scores = (
        jnp.einsum("qhd,khd->hqk", query_block, key_block, preferred_element_type=jnp.float32)
        * score_scale
    )
    masked = jnp.where(visible[None], scores, MASKED)
    row_max = jnp.max(masked, axis=-1, keepdims=True)
    weights = jnp.exp(masked - row_max)
    totals = jnp.sum(weights, axis=-1, keepdims=True)
    softmax_low = (weights / totals).astype(jnp.bfloat16)
    mixed = jnp.einsum("hqk,khd->qhd", softmax_low, value_block, preferred_element_type=jnp.float32)
    mixed_low = mixed.reshape(row_count, width).astype(jnp.bfloat16)
    branch = matmul(mixed_low, mixer[3])
    hidden_in = tokens.astype(jnp.float32) + rms_norm(branch, mixer_gain_full)
    hidden_low = hidden_in.astype(jnp.bfloat16)
    feed = gather_feed(w_gate, w_up, w_down, feed_gain)
    feed_gain_full = feed[3].astype(jnp.float32)
    gate_proj = matmul(hidden_low, feed[0])
    up_proj = matmul(hidden_low, feed[1])
    hidden = gated(gate_proj, up_proj).astype(jnp.bfloat16)
    result = matmul(hidden, feed[2])
    out_tokens = (hidden_in + rms_norm(result, feed_gain_full)).astype(jnp.bfloat16)
    grad_out = cotangent.astype(jnp.float32)
    feed_norm_pull = jax.vjp(rms_norm, result, feed_gain_full)[1]
    result_grad, feed_gain_term = feed_norm_pull(grad_out)
    result_grad_low = result_grad.astype(jnp.bfloat16)
    feed_back = gather_feed_again(w_gate, w_up, w_down, feed_gain)
    hidden_grad = matmul_t(result_grad_low, feed_back[2])
    gated_pull = jax.vjp(gated, gate_proj, up_proj)[1]
    gate_grad, up_grad = gated_pull(hidden_grad)
    gate_grad_low = gate_grad.astype(jnp.bfloat16)
    up_grad_low = up_grad.astype(jnp.bfloat16)
    hidden_in_grad = (
        grad_out + matmul_t(gate_grad_low, feed_back[0]) + matmul_t(up_grad_low, feed_back[1])
    )
    gate_term = inner_t(hidden_low, gate_grad_low)
    up_term = inner_t(hidden_low, up_grad_low)
    g_w_down = lax.psum_scatter(
        inner_t(hidden, result_grad_low), "dev", scatter_dimension=0, tiled=True
    )
    g_w_gate, g_w_up, g_feed_gain = (
        lax.psum_scatter(gate_term, "dev", scatter_dimension=0, tiled=True),
        lax.psum_scatter(up_term, "dev", scatter_dimension=0, tiled=True),
        lax.psum_scatter(feed_gain_term, "dev", scatter_dimension=0, tiled=True),
    )
    mixer_norm_pull = jax.vjp(rms_norm, branch, mixer_gain_full)[1]
    branch_grad, mixer_gain_term = mixer_norm_pull(hidden_in_grad)
    branch_grad_low = branch_grad.astype(jnp.bfloat16)
    back_weights = gather_mixer_again(
        w_query, w_key, w_value, w_out, query_gain, key_gain, mixer_gain
    )
    out_term = inner_t(mixed_low, branch_grad_low)
    mixed_grad = matmul_t(branch_grad_low, back_weights[3]).astype(jnp.bfloat16)
    mixed_grad_block = mixed_grad.reshape(row_count, head_count, HEAD)
    scores_again = (
        jnp.einsum("qhd,khd->hqk", query_block, key_block, preferred_element_type=jnp.float32)
        * score_scale
    )
    masked_again = jnp.where(visible[None], scores_again, MASKED)
    softmax_again = jnp.exp(masked_again - row_max) / totals
    softmax_again_low = softmax_again.astype(jnp.bfloat16)
    value_grad = jnp.einsum(
        "hqk,qhd->khd", softmax_again_low, mixed_grad_block, preferred_element_type=jnp.float32
    )
    softmax_grad = jnp.einsum(
        "qhd,khd->hqk", mixed_grad_block, value_block, preferred_element_type=jnp.float32
    )
    score_grad = (
        softmax_again
        * (softmax_grad - jnp.sum(softmax_again * softmax_grad, axis=-1, keepdims=True))
    ).astype(jnp.bfloat16)
    query_rot_grad = (
        jnp.einsum("hqk,khd->qhd", score_grad, key_block, preferred_element_type=jnp.float32)
        * score_scale
    ).reshape(row_count, width)
    key_rot_grad = (
        jnp.einsum("hqk,qhd->khd", score_grad, query_block, preferred_element_type=jnp.float32)
        * score_scale
    ).reshape(window, width)
    pair_grad = jnp.stack([key_rot_grad, value_grad.reshape(window, width)])
    pieces = [
        pair_grad[:, offset * row_count : (offset + 1) * row_count]
        for offset in range(behind + 1 + ahead)
    ]
    own_grad = return_near(pieces, behind)
    query_pull = jax.vjp(embed, query, query_gain_full)[1]
    query_grad, query_gain_term = query_pull(query_rot_grad)
    key_pull = jax.vjp(embed, key_proj, key_gain_full)[1]
    key_grad, key_gain_term = key_pull(own_grad[0])
    query_grad_low = query_grad.astype(jnp.bfloat16)
    key_grad_low = key_grad.astype(jnp.bfloat16)
    value_grad_low = own_grad[1].astype(jnp.bfloat16)
    query_term = inner_t(tokens, query_grad_low)
    key_term = inner_t(tokens, key_grad_low)
    value_term = inner_t(tokens, value_grad_low)
    g_tokens = (
        hidden_in_grad
        + matmul_t(query_grad_low, back_weights[0])
        + matmul_t(key_grad_low, back_weights[1])
        + matmul_t(value_grad_low, back_weights[2])
    )
    g_w_query, g_w_key, g_w_value, g_w_out, g_query_gain, g_key_gain, g_mixer_gain = (
        lax.psum_scatter(query_term, "dev", scatter_dimension=0, tiled=True),
        lax.psum_scatter(key_term, "dev", scatter_dimension=0, tiled=True),
        lax.psum_scatter(value_term, "dev", scatter_dimension=0, tiled=True),
        lax.psum_scatter(out_term, "dev", scatter_dimension=0, tiled=True),
        lax.psum_scatter(query_gain_term, "dev", scatter_dimension=0, tiled=True),
        lax.psum_scatter(key_gain_term, "dev", scatter_dimension=0, tiled=True),
        lax.psum_scatter(mixer_gain_term, "dev", scatter_dimension=0, tiled=True),
    )
    return (
        out_tokens,
        g_tokens,
        g_w_query,
        g_w_key,
        g_w_value,
        g_w_out,
        g_query_gain,
        g_key_gain,
        g_mixer_gain,
        g_w_gate,
        g_w_up,
        g_w_down,
        g_feed_gain,
    )


def solution(mesh):
    in_specs = (
        P("dev", None),
        P("dev", None),
        P(),
        P(),
        P("dev", None),
        P("dev", None),
        P("dev", None),
        P("dev", None),
        P("dev"),
        P("dev"),
        P("dev"),
        P("dev", None),
        P("dev", None),
        P("dev", None),
        P("dev"),
    )
    out_specs = (
        P("dev", None),
        P("dev", None),
        P("dev", None),
        P("dev", None),
        P("dev", None),
        P("dev", None),
        P("dev"),
        P("dev"),
        P("dev"),
        P("dev", None),
        P("dev", None),
        P("dev", None),
        P("dev"),
    )
    return jax.shard_map(body, mesh=mesh, in_specs=in_specs, out_specs=out_specs, check_vma=False)
```

profile of v0, /device:TPU:0, one launch (start us, length us, event | category | flops | bytes accessed | tf_op | source)
XLA Modules:
  0.0 4191.8 jit_solution(10779116398440897246)
XLA Ops:
  19.1 42.6 %all-reduce.15 = (bf16[2048]{0:T(1024)(128)(2,1)S(1)}, bf16[2048]{0:T(1024)(128)(2,1)S(1)}, bf16[2048]{0:T(1024)(128)(2,1)S(1)}, bf16[2048]{0:T(1024)(128)(2,1)S(1)}) all-reduce(bf16[2048]{0:T(1024)(128)(2,1)S(1)} %dynamic-update-slice, bf16[2048]{0:T(1024)(128)(2,1)S(1)} %dynamic-update-slice.1, ...), channel_id=1, replica_groups=mesh['dev'=32] {'dev'}, use_global_device_ids=true, to_apply=%add.6 | all-reduce | flops 8192 | bytes 32768
  63.3 28.4 all-gather.12.cloned.1.call-done
  99.2 72.0 %all-gather.8.cloned.1.call-done = bf16[2048,2048]{1,0:T(8,128)(2,1)} async-done(((bf16[64,2048]{1,0:T(8,128)(2,1)}), bf16[2048,2048]{1,0:T(8,128)(2,1)}) %all-gather.8.cloned.1.call-update) | async-done | bytes 8388624 | tf_op jit(solution)/shard_map/all_gather | solution.py:112
  187.9 62.9 %all-gather.10.cloned.1.call-done = bf16[2048,2048]{1,0:T(8,128)(2,1)} async-done(((bf16[64,2048]{1,0:T(8,128)(2,1)}), bf16[2048,2048]{1,0:T(8,128)(2,1)}) %all-gather.10.cloned.1.call-update) | async-done | bytes 8388624 | tf_op jit(solution)/shard_map/all_gather | solution.py:113
  277.8 129.1 %collective-permute-done = bf16[2,256,2048]{2,1,0:T(8,128)(2,1)} collective-permute-done((bf16[2,256,2048]{2,1,0:T(8,128)(2,1)}, bf16[2,256,2048]{2,1,0:T(8,128)(2,1)}, u32[]{:S(2)}, u32[]{:S(2)}) %collective-permute-start) | collective-permute-done | bytes 2097184 | tf_op jit(solution)/shard_map/ppermute | solution.py:21
  425.0 8.7 copy.100
  433.7 16.5 fusion.57
  450.2 17.0 fusion.36
  467.3 6.2 multiply_reduce_fusion.6
  475.2 167.5 %all-gather.16.cloned.1.call-done = bf16[2048,8192]{1,0:T(8,128)(2,1)} async-done(((bf16[64,8192]{1,0:T(8,128)(2,1)}), bf16[2048,8192]{1,0:T(8,128)(2,1)}) %all-gather.16.cloned.1.call-update) | async-done | bytes 33554448 | tf_op jit(solution)/shard_map/all_gather | solution.py:135
  642.8 18.0 fusion.61
  660.8 178.3 %all-gather.18.cloned.1.call-done = bf16[2048,8192]{1,0:T(8,128)(2,1)} async-done(((bf16[64,8192]{1,0:T(8,128)(2,1)}), bf16[2048,8192]{1,0:T(8,128)(2,1)}) %all-gather.18.cloned.1.call-update) | async-done | bytes 33554448 | tf_op jit(solution)/shard_map/all_gather | solution.py:136
  839.0 23.8 multiply_convert_fusion.2
  862.8 172.0 %all-gather.20.cloned.1.call-done = bf16[8192,2048]{1,0:T(8,128)(2,1)} async-done(((bf16[256,2048]{1,0:T(8,128)(2,1)}), bf16[8192,2048]{1,0:T(8,128)(2,1)}) %all-gather.20.cloned.1.call-update) | async-done | bytes 33554448 | tf_op jit(solution)/shard_map/all_gather | solution.py:137
  1034.9 16.8 multiply_reduce_fusion.5
  1053.2 22.9 multiply_convert_fusion.1
  1076.1 17.4 convert_add_fusion
  1093.4 17.5 multiply_reduce_fusion.1
  1113.9 8.2 fusion.62
  1123.3 7.0 convolution_convert_fusion
  1132.2 16.4 fusion.10
  1148.5 20.6 multiply_reduce_fusion
  1169.1 22.1 multiply_convert_fusion
  1191.2 7.4 convolution_multiply_fusion
  1198.7 15.7 fusion.1
  1214.4 8.3 fusion.52
  1231.4 6.8 multiply_bitcast_fusion
  1238.2 45.3 %collective-permute-done.8 = bf16[2,256,2048]{1,2,0:T(8,128)(2,1)} collective-permute-done((bf16[2,256,2048]{1,2,0:T(8,128)(2,1)}, bf16[2,256,2048]{1,2,0:T(8,128)(2,1)}, u32[]{:S(2)}, u32[]{:S(2)}) %collective-permute-start.8) | collective-permute-done | bytes 2097184 | tf_op jit(solution)/shard_map/ppermute | solution.py:21
  1283.4 107.4 %collective-permute-done.7 = bf16[2,256,2048]{1,2,0:T(8,128)(2,1)} collective-permute-done((bf16[2,256,2048]{1,2,0:T(8,128)(2,1)}, bf16[2,256,2048]{1,2,0:T(8,128)(2,1)}, u32[]{:S(2)}, u32[]{:S(2)}) %collective-permute-start.7) | collective-permute-done | bytes 2097184 | tf_op jit(solution)/shard_map/ppermute | solution.py:21
  1390.9 6.1 fusion.22
  1405.1 6.0 multiply_add_fusion.1
  1414.6 8.2 convolution_bitcast_fusion.2
  1422.8 17.6 copy.88
  1447.8 8.2 convolution_bitcast_fusion.1
  1456.0 17.6 copy.90
  1473.7 9.7 convolution_bitcast_fusion
  1483.4 17.9 copy.92
  1502.6 26.2 fusion.63
  1528.8 26.2 fusion.64
  1556.9 26.3 fusion.58
  1583.9 94.5 %all-reduce.14 = (f32[2048]{0:T(1024)S(1)}, f32[2048]{0:T(1024)S(1)}, f32[2048]{0:T(1024)S(1)}, f32[2048]{0:T(1024)S(1)}) all-reduce(f32[2048]{0:T(1024)S(1)} %copy-done.53, f32[2048]{0:T(1024)S(1)} %copy-done.54, f32[2048]{0:T(1024)S(1)} %copy-done.62, f32[2048]{0:T(1024)S(1)} %copy-done.52), channel_id=6, replica_groups=mesh['dev'=32] {'dev'}, use_global_device_ids=true, to_apply=%region_18.19.clone | all-reduce | flops 8192 | bytes 65536
  1680.8 5.9 convolution_add_fusion.3
  1686.7 6.2 convolution_add_fusion.2
  1696.8 167.8 %reduce-scatter.24.cloned.1.call-done = f32[64,2048]{1,0:T(8,128)} async-done(((f32[2048,2048]{1,0:T(8,128)}), f32[64,2048]{1,0:T(8,128)}) %reduce-scatter.24.cloned.1.call-update) | async-done | bytes 524304
  1864.6 187.4 %reduce-scatter.26.cloned.1.call-done = f32[64,2048]{1,0:T(8,128)} async-done(((f32[2048,2048]{1,0:T(8,128)}), f32[64,2048]{1,0:T(8,128)}) %reduce-scatter.26.cloned.1.call-update) | async-done | bytes 524304
  2052.0 706.9 %reduce-scatter.16.cloned.1.call-done = f32[64,8192]{1,0:T(8,128)} async-done(((f32[2048,8192]{1,0:T(8,128)}), f32[64,8192]{1,0:T(8,128)}) %reduce-scatter.16.cloned.1.call-update) | async-done | bytes 2097168 | tf_op jit(solution)/shard_map/reduce_scatter | solution.py:250
  2758.9 713.2 %reduce-scatter.18.cloned.1.call-done = f32[64,8192]{1,0:T(8,128)} async-done(((f32[2048,8192]{1,0:T(8,128)}), f32[64,8192]{1,0:T(8,128)}) %reduce-scatter.18.cloned.1.call-update) | async-done | bytes 2097168 | tf_op jit(solution)/shard_map/reduce_scatter | solution.py:251
  3472.1 713.0 %reduce-scatter.20.cloned.1.call-done = f32[256,2048]{1,0:T(8,128)} async-done(((f32[8192,2048]{1,0:T(8,128)}), f32[256,2048]{1,0:T(8,128)}) %reduce-scatter.20.cloned.1.call-update) | async-done | bytes 2097168 | tf_op jit(solution)/shard_map/reduce_scatter | solution.py:246
  (289 shorter events, 128.8 us)
Async XLA Ops:
  7.2 84.5 %all-gather.12.cloned.1.call-start = ((), (), s32[]{:S(2)}) async-start(), calls=%async_computation.9 | async-start | bytes 8650752 | tf_op jit(solution)/shard_map/all_gather | solution.py:111
  9.2 162.1 %all-gather.8.cloned.1.call-start = ((), (), s32[]{:S(2)}) async-start(), calls=%async_computation.7 | async-start | bytes 8650752 | tf_op jit(solution)/shard_map/all_gather | solution.py:112
  11.1 239.8 %all-gather.10.cloned.1.call-start = ((), (), s32[]{:S(2)}) async-start(), calls=%async_computation.8 | async-start | bytes 8650752 | tf_op jit(solution)/shard_map/all_gather | solution.py:113
  11.9 455.4 %all-gather.14.cloned.1.call-start = ((), (), s32[]{:S(2)}) async-start(), calls=%async_computation.10 | async-start | bytes 8650752 | tf_op jit(solution)/shard_map/all_gather | solution.py:114
  12.7 630.1 %all-gather.16.cloned.1.call-start = ((), (), s32[]{:S(2)}) async-start(), calls=%async_computation.11 | async-start | bytes 34603008 | tf_op jit(solution)/shard_map/all_gather | solution.py:135
  13.9 825.2 %all-gather.18.cloned.1.call-start = ((), (), s32[]{:S(2)}) async-start(), calls=%async_computation.12 | async-start | bytes 34603008 | tf_op jit(solution)/shard_map/all_gather | solution.py:136
  16.8 45.0 %copy-start.44 = (s32[8192]{0:T(1024)S(1)}, s32[8192]{0:T(1024)}, u32[]{:S(2)}) copy-start(s32[8192]{0:T(1024)} %param.17) | copy-start | bytes 98308
  16.8 74.9 %copy-start.1 = (bf16[256,2048]{1,0:T(8,128)(2,1)S(1)}, bf16[256,2048]{1,0:T(8,128)(2,1)}, u32[]{:S(2)}) copy-start(bf16[256,2048]{1,0:T(8,128)(2,1)} %param.15) | copy-start | bytes 3145732
  16.8 1018.1 %all-gather.20.cloned.1.call-start = ((), (), s32[]{:S(2)}) async-start(), calls=%async_computation.13 | async-start | bytes 34603008 | tf_op jit(solution)/shard_map/all_gather | solution.py:137
  18.0 1678.7 %reduce-scatter.14.cloned.1.call-start = ((), (), s32[]{:S(2)}) async-start(), calls=%async_computation.14 | async-start | bytes 17301504 | tf_op jit(solution)/shard_map/reduce_scatter | solution.py:314
  61.7 35.8 copy-start.47
  61.8 115.3 %copy-start.45 = (f32[2048]{0:T(1024)}, f32[2048]{0:T(1024)S(1)}, u32[]{:S(2)}) copy-start(f32[2048]{0:T(1024)S(1)} %convert_element_type.150) | copy-start | bytes 24580
  63.3 116.9 %copy-start.37 = (f32[256,64]{1,0:T(8,128)}, f32[256,64]{1,0:T(8,128)S(1)}, u32[]{:S(2)}) copy-start(f32[256,64]{1,0:T(8,128)S(1)} %get-tuple-element.99) | copy-start | bytes 196612
  63.3 116.9 %copy-start.39 = (f32[256,64]{1,0:T(8,128)}, f32[256,64]{1,0:T(8,128)S(1)}, u32[]{:S(2)}) copy-start(f32[256,64]{1,0:T(8,128)S(1)} %get-tuple-element.100) | copy-start | bytes 196612
  183.9 266.3 %copy-start.21 = (bf16[256,16,64]{2,0,1:T(8,128)(2,1)}, bf16[256,16,64]{2,0,1:T(8,128)(2,1)S(1)}, u32[]{:S(2)}) copy-start(bf16[256,16,64]{2,0,1:T(8,128)(2,1)S(1)} %get-tuple-element.81) | copy-start | bytes 1572868
  256.5 16.6 copy-start.51
  258.2 148.7 %collective-permute-start = (bf16[2,256,2048]{2,1,0:T(8,128)(2,1)}, bf16[2,256,2048]{2,1,0:T(8,128)(2,1)}, u32[]{:S(2)}, u32[]{:S(2)}) collective-permute-start(bf16[2,256,2048]{2,1,0:T(8,128)(2,1)} %pad_maximum_fusion.1), channel_id=1, source_target_pairs={{0,4},{1,5},{2,6},{3,7},{4,8},{5,9},{6,10},{7,11},{8,12},{9,13},{1... | collective-permute-start | bytes 6291464 | tf_op jit(solution)/shard_map/ppermute | solution.py:21
  262.9 145.9 %collective-permute-start.1 = (bf16[2,256,2048]{2,1,0:T(8,128)(2,1)}, bf16[2,256,2048]{2,1,0:T(8,128)(2,1)}, u32[]{:S(2)}, u32[]{:S(2)}) collective-permute-start(bf16[2,256,2048]{2,1,0:T(8,128)(2,1)} %pad_maximum_fusion.1), channel_id=1, source_target_pairs={{0,3},{1,4},{2,5},{3,6},{4,7},{5,8},{6,9},{7,10},{8,11},{9,12},{10... | collective-permute-start | bytes 6291464 | tf_op jit(solution)/shard_map/ppermute | solution.py:21
  266.2 144.3 %collective-permute-start.2 = (bf16[2,256,2048]{2,1,0:T(8,128)(2,1)}, bf16[2,256,2048]{2,1,0:T(8,128)(2,1)}, u32[]{:S(2)}, u32[]{:S(2)}) collective-permute-start(bf16[2,256,2048]{2,1,0:T(8,128)(2,1)} %pad_maximum_fusion.1), channel_id=1, source_target_pairs={{0,2},{1,3},{2,4},{3,5},{4,6},{5,7},{6,8},{7,9},{8,10},{9,11},{10,... | collective-permute-start | bytes 6291464 | tf_op jit(solution)/shard_map/ppermute | solution.py:21
  270.6 141.9 %collective-permute-start.3 = (bf16[2,256,2048]{2,1,0:T(8,128)(2,1)}, bf16[2,256,2048]{2,1,0:T(8,128)(2,1)}, u32[]{:S(2)}, u32[]{:S(2)}) collective-permute-start(bf16[2,256,2048]{2,1,0:T(8,128)(2,1)} %pad_maximum_fusion.1), channel_id=1, source_target_pairs={{0,1},{1,2},{2,3},{3,4},{4,5},{5,6},{6,7},{7,8},{8,9},{9,10},{10,1... | collective-permute-start | bytes 6291464 | tf_op jit(solution)/shard_map/ppermute | solution.py:21
  273.8 140.7 %collective-permute-start.4 = (bf16[2,256,2048]{2,1,0:T(8,128)(2,1)}, bf16[2,256,2048]{2,1,0:T(8,128)(2,1)}, u32[]{:S(2)}, u32[]{:S(2)}) collective-permute-start(bf16[2,256,2048]{2,1,0:T(8,128)(2,1)} %pad_maximum_fusion.1), channel_id=1, source_target_pairs={{1,0},{2,1},{3,2},{4,3},{5,4},{6,5},{7,6},{8,7},{9,8},{10,9},{11,1... | collective-permute-start | bytes 6291464 | tf_op jit(solution)/shard_map/ppermute | solution.py:21
  276.3 834.6 %copy-start.49 = (f32[2048]{0:T(1024)}, f32[2048]{0:T(1024)S(1)}, u32[]{:S(2)}) copy-start(f32[2048]{0:T(1024)S(1)} %convert_element_type.171) | copy-start | bytes 24580
  277.8 172.4 %copy-start.43 = (pred[256,1536]{1,0:T(8,128)(4,1)}, pred[256,1536]{1,0:T(8,128)(4,1)S(1)}, u32[]{:S(2)}) copy-start(pred[256,1536]{1,0:T(8,128)(4,1)S(1)} %or_and_fusion) | copy-start | bytes 1179652
  424.9 8.7 copy-start.23
  475.2 363.8 %copy-start.15 = (bf16[256,2048]{1,0:T(8,128)(2,1)}, bf16[256,2048]{1,0:T(8,128)(2,1)S(1)}, u32[]{:S(2)}) copy-start(bf16[256,2048]{1,0:T(8,128)(2,1)S(1)} %fusion.41) | copy-start | bytes 3145732
  1034.9 16.9 copy-start.19
  1051.7 59.2 %copy-start.7 = (f32[256,2048]{1,0:T(8,128)}, f32[256,2048]{1,0:T(8,128)S(1)}, u32[]{:S(2)}) copy-start(f32[256,2048]{1,0:T(8,128)S(1)} %get-tuple-element.112) | copy-start | bytes 6291460
  1051.7 59.2 %copy-start.60 = (f32[256]{0:T(256)}, f32[256]{0:T(256)S(1)}, u32[]{:S(2)}) copy-start(f32[256]{0:T(256)S(1)} %fusion.49) | copy-start | bytes 3076
  1053.2 22.9 copy-start.63
  1093.4 17.5 copy-start.12
  1122.1 574.7 %reduce-scatter.22.cloned.1.call-start = ((), (), s32[]{:S(2)}) async-start(), calls=%async_computation.18 | async-start | bytes 17301504
  1123.3 8.7 copy-start.55
  1191.2 40.1 slice-start
  1198.6 15.7 copy-start
  1198.7 32.7 slice-start.1
  1222.7 15.5 collective-permute-start.9
  1226.1 57.3 %collective-permute-start.8 = (bf16[2,256,2048]{1,2,0:T(8,128)(2,1)}, bf16[2,256,2048]{1,2,0:T(8,128)(2,1)}, u32[]{:S(2)}, u32[]{:S(2)}) collective-permute-start(bf16[2,256,2048]{1,2,0:T(8,128)(2,1)} %get-tuple-element.74), channel_id=1, source_target_pairs={{4,0},{5,1},{6,2},{7,3},{8,4},{9,5},{10,6},{11,7},{12,8},{13,9},{1... | collective-permute-start | bytes 6291464 | tf_op jit(solution)/shard_map/ppermute | solution.py:21
  1227.4 163.4 %collective-permute-start.7 = (bf16[2,256,2048]{1,2,0:T(8,128)(2,1)}, bf16[2,256,2048]{1,2,0:T(8,128)(2,1)}, u32[]{:S(2)}, u32[]{:S(2)}) collective-permute-start(bf16[2,256,2048]{1,2,0:T(8,128)(2,1)} %get-tuple-element.75), channel_id=1, source_target_pairs={{3,0},{4,1},{5,2},{6,3},{7,4},{8,5},{9,6},{10,7},{11,8},{12,9},{13... | collective-permute-start | bytes 6291464 | tf_op jit(solution)/shard_map/ppermute | solution.py:21
  1228.7 162.1 %collective-permute-start.6 = (bf16[2,256,2048]{1,2,0:T(8,128)(2,1)}, bf16[2,256,2048]{1,2,0:T(8,128)(2,1)}, u32[]{:S(2)}, u32[]{:S(2)}) collective-permute-start(bf16[2,256,2048]{1,2,0:T(8,128)(2,1)} %get-tuple-element.76), channel_id=1, source_target_pairs={{2,0},{3,1},{4,2},{5,3},{6,4},{7,5},{8,6},{9,7},{10,8},{11,9},{12,... | collective-permute-start | bytes 6291464 | tf_op jit(solution)/shard_map/ppermute | solution.py:21
  1230.0 160.8 %collective-permute-start.5 = (bf16[2,256,2048]{1,2,0:T(8,128)(2,1)}, bf16[2,256,2048]{1,2,0:T(8,128)(2,1)}, u32[]{:S(2)}, u32[]{:S(2)}) collective-permute-start(bf16[2,256,2048]{1,2,0:T(8,128)(2,1)} %get-tuple-element.72), channel_id=1, source_target_pairs={{1,0},{2,1},{3,2},{4,3},{5,4},{6,5},{7,6},{8,7},{9,8},{10,9},{11,1... | collective-permute-start | bytes 6291464 | tf_op jit(solution)/shard_map/ppermute | solution.py:21
  1440.5 424.1 %reduce-scatter.24.cloned.1.call-start = ((), (), s32[]{:S(2)}) async-start(), calls=%async_computation.19 | async-start | bytes 17301504
  1473.6 578.3 %reduce-scatter.26.cloned.1.call-start = ((), (), s32[]{:S(2)}) async-start(), calls=%async_computation.20 | async-start | bytes 17301504
  1501.4 1257.5 %reduce-scatter.16.cloned.1.call-start = ((), (), s32[]{:S(2)}) async-start(), calls=%async_computation.15 | async-start | bytes 69206016 | tf_op jit(solution)/shard_map/reduce_scatter | solution.py:250
  1528.8 1943.3 %reduce-scatter.18.cloned.1.call-start = ((), (), s32[]{:S(2)}) async-start(), calls=%async_computation.16 | async-start | bytes 69206016 | tf_op jit(solution)/shard_map/reduce_scatter | solution.py:251
  1555.1 2630.0 %reduce-scatter.20.cloned.1.call-start = ((), (), s32[]{:S(2)}) async-start(), calls=%async_computation.17 | async-start | bytes 69206016 | tf_op jit(solution)/shard_map/reduce_scatter | solution.py:246
  1583.2 97.6 %copy-start.26 = (bf16[256,2048]{1,0:T(8,128)(2,1)S(1)}, bf16[256,2048]{1,0:T(8,128)(2,1)}, u32[]{:S(2)}) copy-start(bf16[256,2048]{1,0:T(8,128)(2,1)} %copy-done.25) | copy-start | bytes 3145732
  1583.2 97.6 %copy-start.36 = (f32[256,2048]{1,0:T(8,128)S(1)}, f32[256,2048]{1,0:T(8,128)}, u32[]{:S(2)}) copy-start(f32[256,2048]{1,0:T(8,128)} %copy-done.35) | copy-start | bytes 6291460
  1680.8 12.2 slice-start.2
  (53 other events, 129.8 us)
Sparse Core Ops, SparseCore 0:
  11.5 80.1 all-gather.11
  95.1 76.0 all-gather.7
  174.7 76.0 all-gather.9
  254.1 186.9 all-gather.13
  444.4 198.3 all-gather.15
  646.1 192.9 all-gather.17
  841.9 192.9 all-gather.19
  1122.2 273.3 reduce-scatter.13
  1440.6 236.6 reduce-scatter.21
  1680.1 184.4 reduce-scatter.23
  1867.4 184.4 reduce-scatter.25
  2054.7 704.1 reduce-scatter.15
  2761.8 710.2 reduce-scatter.17
  3474.9 710.1 reduce-scatter.19
where the time goes:
time: 4200 us; the launch traced here: 4190 us
  waiting for transfers between devices  3450 us (82%)
  matrix products  360 us (9%)
  blocking collectives  137 us (3%)
  local copies, waits for them, and re-layouts  120 us (3%)
  other arithmetic  81.5 us (2%)
    reduce_scatter x1, waiting for transfers between devices, body(): lax.psum_scatter(up_term, 'dev', scatter_dimension=0, tiled=True)  713 us
    reduce_scatter x1, waiting for transfers between devices, body(): lax.psum_scatter(inner_t(hidden, result_grad_low), 'dev', scatter_dimensi...  713 us
    reduce_scatter x1, waiting for transfers between devices, body(): lax.psum_scatter(gate_term, 'dev', scatter_dimension=0, tiled=True)  707 us
    unnamed x17, waiting for transfers between devices  355 us
    ppermute x10, waiting for transfers between devices, from_behind(): return lax.ppermute(block, axis, route)  282 us
    all_gather x1, waiting for transfers between devices, gather_feed(): lax.all_gather(w_up.astype(jnp.bfloat16), 'dev', axis=0, tiled=True)  178 us
    all_gather x1, waiting for transfers between devices, gather_feed(): lax.all_gather(w_down.astype(jnp.bfloat16), 'dev', axis=0, tiled=True)  172 us
    all_gather x1, waiting for transfers between devices, gather_feed(): lax.all_gather(w_gate.astype(jnp.bfloat16), 'dev', axis=0, tiled=True)  168 us
  transfers between devices with their start and end apart: 24, of which 14 were waited for; matrix products, arithmetic and copies ran while one was open for 11% of the time, Pallas kernels for 0%

commit v1 on v0

v1 whole, which is shorter than its diff:
```python
import math

import jax
import jax.numpy as jnp
from jax import lax
from jax.sharding import Mesh, PartitionSpec as P

HEAD = 128
SEQ_MAX = 1024
NORM_EPS = 1e-06
ROPE_BASE = 500000.0
MASKED = -1e30
BF16 = jnp.bfloat16
F32 = jnp.float32
GROUP = ("y", "x", "c")
ALL = ("r", "y", "x", "c")


def matmul(left, right):
    return jnp.dot(left, right, preferred_element_type=F32)


def matmul_t(left, right):
    return lax.dot_general(left, right, (((1,), (1,)), ((), ())), preferred_element_type=F32)


def inner_t(left, right):
    return lax.dot_general(left, right, (((0,), (0,)), ((), ())), preferred_element_type=F32)


def inverse_rms(values):
    return lax.rsqrt(jnp.mean(values * values, axis=-1, keepdims=True) + NORM_EPS)


def swap(block, axis):
    return lax.ppermute(block, axis, [(0, 1), (1, 0)])


def group_gather(own):
    half = own.shape[0] // 2
    top, low = own[:half], own[half:]
    top_x = swap(top, "x")
    low_y = swap(low, "y")
    top_y = swap(top, "y")
    low_x = swap(low, "x")
    top_xy = swap(top_x, "y")
    low_xy = swap(low_y, "x")
    chip = jnp.concatenate([own, top_x, low_x, top_y, low_y, top_xy, low_xy], 0)
    parts = [own, jnp.concatenate([top_x, low_y]), jnp.concatenate([top_y, low_x]), jnp.concatenate([top_xy, low_xy])]
    first, second, third, fourth = [swap(part, "c") for part in parts]
    other = jnp.concatenate(
        [
            first,
            second[:half],
            third[half:],
            third[:half],
            second[half:],
            fourth,
        ],
        0,
    )
    return jnp.concatenate([chip, other], 0)


def group_sum(terms):
    total = terms.reshape(terms.shape[0], 2, 2, 2, -1)
    for dim, axis in enumerate(("c", "y", "x")):
        total = total + jnp.flip(swap(total, axis), dim + 1)
    return total.reshape(terms.shape)


def group_scatter(parts, rows):
    width = parts.shape[1]
    half = rows // 2
    low = parts.astype(BF16)
    arrived = swap(low[4 * rows :], "c")
    mine = low[: 4 * rows].astype(F32) + arrived.astype(F32)
    mine = mine.astype(BF16).reshape(2, 2, 2, half, width)
    got_x = swap(mine[:, 1, 0], "x")
    got_y = swap(mine[1, :, 1], "y")
    top = mine[:, 0, 0].astype(F32) + got_x.astype(F32)
    bottom = mine[0, :, 1].astype(F32) + got_y.astype(F32)
    top_last = swap(top[1].astype(BF16), "y")
    bottom_last = swap(bottom[1].astype(BF16), "x")
    return jnp.concatenate([top[0] + top_last.astype(F32), bottom[0] + bottom_last.astype(F32)], 0)


def make_body(inner):
    replicas, per_head = inner
    head_axes = GROUP[3 - int(math.log2(per_head)) :]
    head_groups = 8 // per_head
    own_heads = replicas // per_head

    def body(
        tokens,
        cotangent,
        segment_ids,
        piece_ids,
        w_query,
        w_key,
        w_value,
        w_out,
        query_gain,
        key_gain,
        mixer_gain,
        w_gate,
        w_up,
        w_down,
        feed_gain,
    ):
        rows, width = tokens.shape
        weight_rows = w_query.shape[0]
        unit_rows = w_down.shape[0]
        units = replicas * unit_rows
        columns = own_heads * HEAD
        group_rows = 8 * rows
        blocks = group_rows // SEQ_MAX
        member = lax.axis_index(GROUP)
        replica = lax.axis_index("r")

        def by_head(weight):
            shaped = weight.astype(BF16).reshape(weight_rows, per_head, own_heads, head_groups, HEAD)
            return shaped.transpose(3, 1, 0, 2, 4).reshape(8, weight_rows, columns)

        def by_unit(weight):
            shaped = weight.astype(BF16).reshape(weight_rows, replicas, 8, unit_rows)
            return shaped.transpose(2, 0, 1, 3).reshape(8, weight_rows, units)

        def exchange(parts):
            return lax.all_to_all(parts, GROUP, 0, 0, tiled=True)

        def gather(part):
            return lax.all_gather(part, "r", axis=0, tiled=True)

        qkv_parts = jnp.concatenate([by_head(w_query), by_head(w_key), by_head(w_value)], 2)
        weight_qkv = gather(exchange(qkv_parts).reshape(8 * weight_rows, 3 * columns))
        gate_up_parts = jnp.concatenate([by_unit(w_gate), by_unit(w_up)], 2)
        out_halves = gather(w_out.astype(BF16)).reshape(per_head, own_heads, weight_rows, width)
        out_heads = lax.all_to_all(out_halves, head_axes, 0, 0, tiled=True)
        weight_out = out_heads.transpose(1, 0, 2, 3).reshape(columns, width)
        weight_gate_up = gather(exchange(gate_up_parts).reshape(8 * weight_rows, 2 * units))
        weight_gate, weight_up = weight_gate_up[:, :units], weight_gate_up[:, units:]
        weight_down = gather(w_down.astype(BF16))

        gains = lax.all_gather(
            jnp.stack([query_gain, key_gain, mixer_gain, feed_gain]).astype(BF16), ALL, axis=1, tiled=True
        ).astype(F32)
        head_gains = gains[:2].reshape(2, per_head, own_heads, head_groups, HEAD)
        place = lax.axis_index(head_axes)
        head_group = member // per_head
        head_gains = lax.dynamic_index_in_dim(head_gains, place, 1, keepdims=False)
        head_gains = lax.dynamic_index_in_dim(head_gains, head_group, 2, keepdims=False)
        gain_q, gain_k = head_gains.reshape(2, 1, columns)
        gain_a, gain_f = gains[2:3], gains[3:4]

        orders = [c + 4 * y + 2 * x for c in (0, 1) for y in (0, 1) for x in (0, 1)]
        starts = [(replica * 8 + (member ^ k)) * rows for k in orders]

        def of_group(ids):
            return jnp.concatenate([lax.dynamic_slice_in_dim(ids, s, rows, 0) for s in starts])

        places = jnp.concatenate([s + jnp.arange(rows, dtype=jnp.int32) for s in starts])

        def by_block(array):
            shaped = array.reshape((2, blocks, group_rows // (2 * blocks)) + array.shape[1:])
            return jnp.moveaxis(shaped, 1, 0).reshape((blocks, SEQ_MAX) + array.shape[1:])

        def from_block(array):
            shaped = array.reshape((blocks, 2, SEQ_MAX // 2) + array.shape[2:])
            return jnp.moveaxis(shaped, 0, 1).reshape((group_rows,) + array.shape[2:])

        segment = by_block(of_group(segment_ids))
        piece = by_block(of_group(piece_ids))
        place_block = by_block(places)
        same = segment[:, :, None] == segment[:, None, :]
        visible = same & (
            (place_block[:, None, :] <= place_block[:, :, None])
            | (piece[:, :, None] == piece[:, None, :]) & (piece[:, :, None] > 0)
        )
        before = jnp.sum((segment[:, None, :] < segment[:, :, None]).astype(jnp.int32), -1)
        positions = from_block(place_block % SEQ_MAX - before)
        freqs = jnp.exp(jnp.arange(HEAD // 2, dtype=F32) * (-2.0 * math.log(ROPE_BASE) / HEAD))
        angles = positions.astype(F32)[:, None] * freqs[None, :]
        cosine = jnp.concatenate([jnp.cos(angles), jnp.cos(angles)], 1)[:, None, :]
        sine = jnp.concatenate([-jnp.sin(angles), jnp.sin(angles)], 1)[:, None, :]

        def turned(values, sine_table):
            shaped = values.reshape(group_rows, own_heads, HEAD)
            crossed = jnp.concatenate([shaped[:, :, HEAD // 2 :], shaped[:, :, : HEAD // 2]], -1)
            return (shaped * cosine + crossed * sine_table).reshape(group_rows, columns)

        scale = HEAD ** (-0.5)

        def heads_of(array):
            return by_block(array.reshape(group_rows, own_heads, HEAD))

        group_tokens = group_gather(tokens)
        projected = matmul(group_tokens, weight_qkv)
        query, key, value = jnp.split(projected, 3, axis=1)
        squares = jnp.stack([jnp.sum(query * query, -1), jnp.sum(key * key, -1)])
        squares = group_sum(squares)
        r_q, r_k = lax.rsqrt(squares / width + NORM_EPS)[:, :, None]
        query_rot = turned(query * r_q * gain_q, sine).astype(BF16)
        key_rot = turned(key * r_k * gain_k, sine).astype(BF16)
        q, k, v = heads_of(query_rot), heads_of(key_rot), heads_of(value.astype(BF16))
        scores = jnp.einsum("bqhd,bkhd->bhqk", q, k, preferred_element_type=F32) * scale
        masked = jnp.where(visible[:, None], scores, MASKED)
        row_max = jnp.max(masked, axis=-1, keepdims=True)
        weights = jnp.exp(masked - row_max)
        totals = jnp.sum(weights, axis=-1, keepdims=True)
        softmax = weights / totals
        softmax_low = softmax.astype(BF16)
        mixed = jnp.einsum("bhqk,bkhd->bqhd", softmax_low, v, preferred_element_type=F32)
        mixed_low = from_block(mixed.astype(BF16)).reshape(group_rows, columns)
        branch = group_scatter(matmul(mixed_low, weight_out), rows)
        r_a = inverse_rms(branch)
        hidden_in = tokens.astype(F32) + branch * r_a * gain_a
        group_hidden_in = group_gather(hidden_in.astype(BF16))
        gate = matmul(group_hidden_in, weight_gate)
        up = matmul(group_hidden_in, weight_up)
        sig = 1.0 / (1.0 + jnp.exp(-gate))
        hidden = (gate * sig * up).astype(BF16)
        result = group_scatter(matmul(hidden, weight_down), rows)
        r_m = inverse_rms(result)
        out_tokens = (hidden_in + result * r_m * gain_f).astype(BF16)

        def norm_back(values, r, gain, grad):
            scaled = gain * grad
            mean = jnp.mean(scaled * values, -1, keepdims=True)
            return r * (scaled - values * (r * r) * mean), jnp.sum(grad * values * r, 0)

        grad_out = cotangent.astype(F32)
        result_grad, feed_gain_term = norm_back(result, r_m, gain_f, grad_out)
        group_result_grad = group_gather(result_grad.astype(BF16))

        def scatter(term):
            return lax.psum_scatter(term.astype(BF16), "r", scatter_dimension=0, tiled=True)

        g_w_down = scatter(inner_t(hidden, group_result_grad)).astype(F32)
        hidden_grad = matmul_t(group_result_grad, weight_down)
        gate_grad = (hidden_grad * up * sig * (1.0 + gate * (1.0 - sig))).astype(BF16)
        up_grad = (hidden_grad * gate * sig).astype(BF16)
        hidden_in_grad = cotangent.astype(F32) + group_scatter(
            matmul_t(gate_grad, weight_gate) + matmul_t(up_grad, weight_up), rows
        )
        gate_share = scatter(inner_t(group_hidden_in, gate_grad))
        up_share = scatter(inner_t(group_hidden_in, up_grad))
        branch_grad, mixer_gain_term = norm_back(branch, r_a, gain_a, hidden_in_grad)
        group_branch_grad = group_gather(branch_grad.astype(BF16))
        out_term = inner_t(mixed_low, group_branch_grad)
        mixed_grad = heads_of(matmul_t(group_branch_grad, weight_out).astype(BF16))
        softmax_grad = jnp.einsum("bqhd,bkhd->bhqk", mixed_grad, v, preferred_element_type=F32)
        inner = jnp.sum(softmax * softmax_grad, axis=-1, keepdims=True)
        score_grad = (softmax * (softmax_grad - inner)).astype(BF16)
        v_grad = jnp.einsum("bhqk,bqhd->bkhd", softmax_low, mixed_grad, preferred_element_type=F32)
        q_grad = jnp.einsum("bhqk,bkhd->bqhd", score_grad, k, preferred_element_type=F32) * scale
        k_grad = jnp.einsum("bhqk,bqhd->bkhd", score_grad, q, preferred_element_type=F32) * scale

        def flat(array):
            return from_block(array).reshape(group_rows, columns)

        q_back = turned(flat(q_grad), -sine)
        k_back = turned(flat(k_grad), -sine)
        means = jnp.stack([jnp.sum(q_back * gain_q * query, -1), jnp.sum(k_back * gain_k * key, -1)])
        mean_q, mean_k = (group_sum(means) / width)[:, :, None]
        query_grad = (r_q * (gain_q * q_back - query * (r_q * r_q) * mean_q)).astype(BF16)
        key_grad = (r_k * (gain_k * k_back - key * (r_k * r_k) * mean_k)).astype(BF16)
        query_gain_term = jnp.sum(q_back * query * r_q, 0)
        key_gain_term = jnp.sum(k_back * key * r_k, 0)
        grads = jnp.concatenate([query_grad, key_grad, flat(v_grad).astype(BF16)], 1)
        g_tokens = hidden_in_grad + group_scatter(matmul_t(grads, weight_qkv), rows)

        def from_units(share):
            parts = exchange(share.reshape(8, weight_rows, units))
            shaped = parts.reshape(8, weight_rows, replicas, unit_rows).transpose(1, 2, 0, 3)
            return shaped.reshape(weight_rows, 8 * units).astype(F32)

        qkv_share = scatter(inner_t(group_tokens, grads))
        qkv_parts = exchange(qkv_share.reshape(8, weight_rows, 3 * columns))
        qkv_parts = qkv_parts.reshape(head_groups, per_head, weight_rows, 3, own_heads, HEAD)
        g_qkv = qkv_parts.transpose(3, 2, 1, 4, 0, 5).reshape(3, weight_rows, width).astype(F32)
        out_parts = out_term.astype(BF16).reshape(own_heads, per_head, weight_rows, width).transpose(1, 0, 2, 3)
        out_parts = lax.all_to_all(out_parts, head_axes, 0, 0, tiled=True)
        g_w_out = scatter(out_parts.reshape(replicas * weight_rows, width)).astype(F32)
        g_w_gate = from_units(gate_share)
        g_w_up = from_units(up_share)

        head_terms = jnp.stack([query_gain_term, key_gain_term]).reshape(2, 1, own_heads, 1, HEAD)
        spread = jnp.zeros((2, per_head, own_heads, head_groups, HEAD), F32)
        spread = lax.dynamic_update_slice(spread, head_terms, (0, place, 0, head_group, 0))
        gain_terms = jnp.concatenate(
            [spread.reshape(2, width), jnp.stack([mixer_gain_term, feed_gain_term])], 0
        )
        g_gains = lax.psum_scatter(gain_terms, ALL, scatter_dimension=1, tiled=True)
        return (
            out_tokens,
            g_tokens,
            g_qkv[0],
            g_qkv[1],
            g_qkv[2],
            g_w_out,
            g_gains[0],
            g_gains[1],
            g_gains[2],
            g_w_gate,
            g_w_up,
            g_w_down,
            g_gains[3],
        )

    return body


def solution(mesh):
    count = mesh.shape["dev"]
    grid = Mesh(mesh.devices.reshape(count // 8, 2, 2, 2), ALL)

    def run(tokens, cotangent, segment_ids, piece_ids, w_query, *rest):
        per_head = count * HEAD // w_query.shape[0]
        rows, whole, gain = P(ALL, None), P(), P(ALL)
        in_specs = (rows, rows, whole, whole) + (rows,) * 4 + (gain,) * 3 + (rows,) * 3 + (gain,)
        out_specs = (rows,) * 6 + (gain,) * 3 + (rows,) * 3 + (gain,)
        return jax.shard_map(
            make_body((count // 8, per_head)), mesh=grid, in_specs=in_specs, out_specs=out_specs, check_vma=False
        )(tokens, cotangent, segment_ids, piece_ids, w_query, *rest)

    return run
```

time: 4200 us -> 1100 us (0.26)
  waiting for transfers between devices: 3450 us -> 477 us
  matrix products: 360 us -> 218 us
  blocking collectives: 137 us -> 44.7 us
  local copies, waits for them, and re-layouts: 120 us -> 173 us
  starting transfers between devices: 26 us -> 75.6 us
    reduce_scatter x4 -> x5, waiting for transfers between devices: 2130 us -> 149 us  [scatter(): lax.psum_scatter(term.astype(BF16), 'r', scatter_dimension=0, tiled=True)]
    all_gather x7 -> x4, waiting for transfers between devices: 681 us -> 72.6 us  [gather(): return lax.all_gather(part, 'r', axis=0, tiled=True)]
    unnamed x17 -> x11, waiting for transfers between devices: 355 us -> 0.62 us
    unnamed x2 -> x0, blocking collectives: 137 us -> none
    dot_general x7 -> x5, matrix products: 113 us -> 50.6 us  [inner_t(): lax.dot_general(left, right, (((0,), (0,)), ((), ())), preferred_element_...]
    dot_general x12 -> x10, matrix products: 150 us -> 89.4 us  [the longest x5 56.7 us: matmul(): return jnp.dot(left, right, preferred_element_type=F32)]
    ppermute x10 -> x66, waiting for transfers between devices: 282 us -> 239 us  [swap(): return lax.ppermute(block, axis, [(0, 1), (1, 0)])]
    unnamed x178 -> x218, local copies, waits for them, and re-layouts: 88.8 us -> 71 us
  transfers between devices with their start and end apart: 24 -> 82, of which waited for: 14 -> 44; matrix products, arithmetic and copies ran while one was open for 11% -> 35% of each run, Pallas kernels for 0% -> 0%
where the time goes in v1:
time: 1100 us; the launch traced here: 1090 us
  waiting for transfers between devices  477 us (43%)
  matrix products  218 us (20%)
  local copies, waits for them, and re-layouts  173 us (16%)
  other arithmetic  86.9 us (8%)
  starting transfers between devices  75.6 us (7%)
  blocking collectives  44.7 us (4%)
  between operations  16.7 us (2%)
    ppermute x66, waiting for transfers between devices, swap(): return lax.ppermute(block, axis, [(0, 1), (1, 0)])  239 us
    reduce_scatter x5, waiting for transfers between devices, scatter(): lax.psum_scatter(term.astype(BF16), 'r', scatter_dimension=0, tiled=True)  149 us
    all_gather x4, waiting for transfers between devices, gather(): return lax.all_gather(part, 'r', axis=0, tiled=True)  72.6 us
    unnamed x218, local copies, waits for them, and re-layouts  71 us
    dot_general x5, matrix products, matmul_t(): lax.dot_general(left, right, (((1,), (1,)), ((), ())), preferred_element_...  66.2 us
    dot_general x5, matrix products, matmul(): return jnp.dot(left, right, preferred_element_type=F32)  56.7 us
    dot_general x5, matrix products, inner_t(): lax.dot_general(left, right, (((0,), (0,)), ((), ())), preferred_element_...  50.6 us
    ppermute x66, starting transfers between devices, swap(): return lax.ppermute(block, axis, [(0, 1), (1, 0)])  48.9 us
  transfers between devices with their start and end apart: 82, of which 44 were waited for; matrix products, arithmetic and copies ran while one was open for 35% of the time, Pallas kernels for 0%

profile of v1, /device:TPU:0, one launch (start us, length us, event | category | flops | bytes accessed | tf_op | source)
XLA Modules:
  0.0 1092.7 jit_solution(3292206529355101098)
XLA Ops:
  94.0 25.7 %all-gather.6.cloned.1.call-done = bf16[2048,768]{1,0:T(8,128)(2,1)} async-done(((bf16[512,768]{1,0:T(8,128)(2,1)}), bf16[2048,768]{1,0:T(8,128)(2,1)}) %all-gather.6.cloned.1.call-update) | async-done | bytes 3145744 | tf_op jit(solution)/shard_map/all_gather | solution.py:133
  119.7 10.4 fusion.92
  133.4 39.1 %all-gather = bf16[32,64,4]{1,2,0:T(4,128)(2,1)S(1)} all-gather(bf16[1,64,4]{1,2,0:T(4,128)(2,1)S(1)} %maximum_bitcast_fusion), channel_id=1, replica_groups=mesh['r'=4,'y'=2,'x'=2,'c'=2] {'r','y','x','c'}, dimensions={0}, use_global_device_ids=true | all-gather | bytes 16896 | tf_op jit(solution)/shard_map/all_gather | solution.py:145
  202.6 11.9 %fusion.91 = (f32[2,2,1024]{2,1,0:T(2,128)S(1)}, f32[2,2,1024,1024]{2,3,1,0:T(8,128)}) fusion(pred[2,1024,1024]{1,2,0:T(8,128)(4,1)} %or_and_fusion, bf16[2,1024,2,128]{1,3,2,0:T(8,128)(2,1)} %reshape.393, bf16[2,1024,2,128]{1,3,2,0:T(8,128)(2,1)S(1)} %reshape.395), kind=kOutput, calls=%fused_computation.312 | convolution fusion | flops 1090520064 | bytes 20987904 | tf_op jit(solution)/shard_map/sub | solution.py:209
  214.5 7.2 fusion.40
  229.2 7.1 collective-permute-done.13
  241.2 23.2 %collective-permute-done.14 = bf16[2,128,2048]{2,1,0:T(8,128)(2,1)S(1)} collective-permute-done((bf16[2,128,2048]{2,1,0:T(8,128)(2,1)S(1)}, bf16[2,128,2048]{2,1,0:T(8,128)(2,1)S(1)}, u32[]{:S(2)}, u32[]{:S(2)}) %collective-permute-start.14) | collective-permute-done | bytes 1048608 | tf_op jit(solution)/shard_map/ppermute | solution.py:36
  267.6 12.1 %collective-permute-done.17 = bf16[128,2048]{1,0:T(8,128)(2,1)S(1)} collective-permute-done((bf16[128,2048]{1,0:T(8,128)(2,1)S(1)}, bf16[128,2048]{1,0:T(8,128)(2,1)S(1)}, u32[]{:S(2)}, u32[]{:S(2)}) %collective-permute-start.17) | collective-permute-done | bytes 524320 | tf_op jit(solution)/shard_map/ppermute | solution.py:36
  288.9 9.8 collective-permute-done.18
  300.1 7.0 collective-permute-done.19
  312.7 9.6 collective-permute-done.22
  330.0 15.3 %fusion.14 = f32[2048,1024]{1,0:T(8,128)} fusion(bf16[2048,2048]{1,0:T(8,128)(2,1)} %constant_dynamic-update-slice_fusion.14, bf16[2048,2048]{1,0:T(8,128)(2,1)} %all-gather.10.cloned.1.call-done), kind=kOutput, calls=%fused_computation.40 | convolution fusion | flops 8589934592 | bytes 20971520 | tf_op jit(solution)/shard_map/dot_general | solution.py:20
  345.3 14.7 %multiply_convert_fusion.3 = (bf16[2048,1024]{1,0:T(8,128)(2,1)}, f32[2048,1024]{1,0:T(8,128)}) fusion(f32[2048,1024]{1,0:T(8,128)} %fusion.14, bf16[2048,2048]{1,0:T(8,128)(2,1)S(1)} %copy-done.45, bf16[2048,2048]{1,0:T(8,128)(2,1)S(1)} %copy-done.61), kind=kOutput, calls=%fused_computation.12 | convolution fusion | flops 8602517504 | bytes 33554432 | tf_op jit(solution)/shard_map/dot_general | solution.py:20
  360.0 46.8 %all-gather.12.cloned.1.call-done = bf16[1024,2048]{1,0:T(8,128)(2,1)} async-done(((bf16[256,2048]{1,0:T(8,128)(2,1)}), bf16[1024,2048]{1,0:T(8,128)(2,1)}) %all-gather.12.cloned.1.call-update) | async-done | bytes 4194320 | tf_op jit(solution)/shard_map/all_gather | solution.py:133
  406.8 12.3 %convolution_convert_fusion.1 = bf16[2048,2048]{1,0:T(8,128)(2,1)S(1)} fusion(bf16[2048,1024]{1,0:T(8,128)(2,1)} %get-tuple-element.96, bf16[1024,2048]{1,0:T(8,128)(2,1)} %all-gather.12.cloned.1.call-done), kind=kOutput, calls=%fused_computation.22 | convolution fusion | flops 8594128896 | bytes 16777216 | tf_op jit(solution)/shard_map/dot_general | solution.py:20
  419.5 7.1 collective-permute-done.28
  432.2 22.2 %collective-permute-done.29 = bf16[2,128,2048]{2,1,0:T(8,128)(2,1)S(1)} collective-permute-done((bf16[2,128,2048]{2,1,0:T(8,128)(2,1)S(1)}, bf16[2,128,2048]{2,1,0:T(8,128)(2,1)S(1)}, u32[]{:S(2)}, u32[]{:S(2)}) %collective-permute-start.29) | collective-permute-done | bytes 1048608 | tf_op jit(solution)/shard_map/ppermute | solution.py:36
  458.7 10.6 collective-permute-done.32
  476.2 10.8 collective-permute-done.33
  488.6 6.5 collective-permute-done.34
  498.7 12.0 %collective-permute-done.37 = bf16[128,2048]{1,0:T(8,128)(2,1)S(1)} collective-permute-done((bf16[128,2048]{1,0:T(8,128)(2,1)S(1)}, bf16[128,2048]{1,0:T(8,128)(2,1)S(1)}, u32[]{:S(2)}, u32[]{:S(2)}) %collective-permute-start.37) | collective-permute-done | bytes 524320 | tf_op jit(solution)/shard_map/ppermute | solution.py:36
  518.0 20.4 %multiply_convert_fusion.1 = (bf16[2048,1024]{1,0:T(8,128)(2,1)}, bf16[2048,1024]{1,0:T(8,128)(2,1)}) fusion(f32[2048,1024]{1,0:T(8,128)} %fusion.14, f32[2048,1024]{1,0:T(8,128)} %get-tuple-element.97, bf16[2048,2048]{1,0:T(8,128)(2,1)} %copy-done.46, bf16[1024,2048]{1,0:T(8,128)(2,1)S(1)} %copy-done.62), kind=kOutput, calls=%fused_computation.9 | convolution fusion | flops 8617197568 | bytes 37748736 | tf_op jit(solution)/shard_map/dot_general | solution.py:24
  538.4 15.3 %fusion.12 = f32[2048,2048]{1,0:T(8,128)} fusion(bf16[2048,1024]{1,0:T(8,128)(2,1)} %get-tuple-element.34, bf16[2048,2048]{1,0:T(8,128)(2,1)} %all-gather.10.cloned.1.call-done), kind=kOutput, calls=%fused_computation.38 | convolution fusion | flops 8589934592 | bytes 25165824 | tf_op jit(solution)/shard_map/dot_general | solution.py:24
  553.7 15.5 %add_convert_fusion = bf16[2048,2048]{1,0:T(8,128)(2,1)} fusion(f32[2048,2048]{1,0:T(8,128)} %fusion.12, bf16[2048,1024]{1,0:T(8,128)(2,1)S(1)} %copy-done.63, bf16[2048,2048]{1,0:T(8,128)(2,1)} %all-gather.10.cloned.1.call-done), kind=kOutput, calls=%fused_computation.3 | convolution fusion | flops 8598323200 | bytes 33554432 | tf_op jit(solution)/shard_map/dot_general | solution.py:24
  569.2 4.9 slice.403
  574.3 12.9 %convolution_convert_fusion.5 = bf16[2048,1024]{1,0:T(8,128)(2,1)} fusion(bf16[2048,2048]{1,0:T(8,128)(2,1)} %constant_dynamic-update-slice_fusion.14, bf16[2048,1024]{1,0:T(8,128)(2,1)S(1)} %copy-done.65), kind=kOutput, calls=%fused_computation.34 | convolution fusion | flops 8592031744 | bytes 16777216 | tf_op jit(solution)/shard_map/dot_general | solution.py:28
  587.2 5.9 add_convert_fusion.2
  594.1 24.8 %collective-permute-done.44 = bf16[2,128,2048]{2,1,0:T(8,128)(2,1)S(1)} collective-permute-done((bf16[2,128,2048]{2,1,0:T(8,128)(2,1)S(1)}, bf16[2,128,2048]{2,1,0:T(8,128)(2,1)S(1)}, u32[]{:S(2)}, u32[]{:S(2)}) %collective-permute-start.44) | collective-permute-done | bytes 1048608 | tf_op jit(solution)/shard_map/ppermute | solution.py:36
  622.0 11.4 %collective-permute-done.47 = bf16[128,2048]{1,0:T(8,128)(2,1)S(1)} collective-permute-done((bf16[128,2048]{1,0:T(8,128)(2,1)S(1)}, bf16[128,2048]{1,0:T(8,128)(2,1)S(1)}, u32[]{:S(2)}, u32[]{:S(2)}) %collective-permute-start.47) | collective-permute-done | bytes 524320 | tf_op jit(solution)/shard_map/ppermute | solution.py:36
  644.2 10.9 %convolution_convert_fusion.4 = bf16[2048,1024]{1,0:T(8,128)(2,1)} fusion(bf16[2048,2048]{1,0:T(8,128)(2,1)S(1)} %bitcast.456, bf16[2048,1024]{1,0:T(8,128)(2,1)S(1)} %copy-done.64), kind=kOutput, calls=%fused_computation.33 | convolution fusion | flops 8592031744 | bytes 16777216 | tf_op jit(solution)/shard_map/dot_general | solution.py:28
  655.4 9.0 collective-permute-done.51
  670.5 8.6 collective-permute-done.52
  686.9 5.8 convolution_convert_fusion.8
  696.7 8.2 multiply_reduce_fusion
  704.9 7.6 multiply_convert_fusion
  728.6 6.4 multiply_bitcast_fusion
  758.5 14.1 %convolution_convert_fusion.3 = bf16[1024,2048]{1,0:T(8,128)(2,1)} fusion(bf16[2048,1024]{1,0:T(8,128)(2,1)} %get-tuple-element.96, bf16[2048,2048]{1,0:T(8,128)(2,1)} %copy-done.46), kind=kOutput, calls=%fused_computation.32 | convolution fusion | flops 8592031744 | bytes 16777216 | tf_op jit(solution)/shard_map/dot_general | solution.py:28
  779.8 9.6 fusion.37
  800.9 9.3 convolution_convert_fusion
  817.4 5.5 all_to_all.35
  823.2 10.4 convolution_convert_fusion.6
  833.6 5.4 add_convert_fusion.1
  846.8 22.3 %collective-permute-done.62 = bf16[2,128,2048]{2,1,0:T(8,128)(2,1)} collective-permute-done((bf16[2,128,2048]{2,1,0:T(8,128)(2,1)S(1)}, bf16[2,128,2048]{2,1,0:T(8,128)(2,1)}, u32[]{:S(2)}, u32[]{:S(2)}) %collective-permute-start.62) | collective-permute-done | bytes 1048608 | tf_op jit(solution)/shard_map/ppermute | solution.py:36
  873.4 7.8 all-to-all-done.5
  895.9 75.4 %reduce-scatter.17.cloned.1.call-done = bf16[256,2048]{1,0:T(8,128)(2,1)} async-done(((bf16[1024,2048]{1,0:T(8,128)(2,1)}), bf16[256,2048]{1,0:T(8,128)(2,1)}) %reduce-scatter.17.cloned.1.call-update) | async-done | bytes 1048592 | tf_op jit(solution)/shard_map/reduce_scatter | solution.py:237
  984.5 16.7 %reduce-scatter.11.cloned.1.call-done = bf16[64,2048]{1,0:T(8,128)(2,1)} async-done(((bf16[256,2048]{1,0:T(8,128)(2,1)}), bf16[64,2048]{1,0:T(8,128)(2,1)}) %reduce-scatter.11.cloned.1.call-update) | async-done | bytes 262160 | tf_op jit(solution)/shard_map/reduce_scatter | solution.py:237
  1005.5 57.0 %reduce-scatter.9.cloned.1.call-done = bf16[512,768]{1,0:T(8,128)(2,1)} async-done(((bf16[2048,768]{1,0:T(8,128)(2,1)}), bf16[512,768]{1,0:T(8,128)(2,1)}) %reduce-scatter.9.cloned.1.call-update) | async-done | bytes 786448 | tf_op jit(solution)/shard_map/reduce_scatter | solution.py:237
  1071.2 8.1 all-to-all-done.3
  (569 shorter events, 345.2 us)
Async XLA Ops:
  7.2 75.2 %all-gather.8.cloned.1.call-start = ((), (), s32[]{:S(2)}) async-start(), calls=%async_computation.14 | async-start | bytes 1310720 | tf_op jit(solution)/shard_map/all_gather | solution.py:133
  9.6 44.6 %collective-permute-start = (bf16[128,2048]{1,0:T(8,128)(2,1)}, bf16[128,2048]{1,0:T(8,128)(2,1)}, u32[]{:S(2)}, u32[]{:S(2)}) collective-permute-start(bf16[128,2048]{1,0:T(8,128)(2,1)} %get-tuple-element.74), channel_id=1, source_target_pairs={{0,2},{2,0},{1,3},{3,1},{4,6},{6,4},{5,7},{7,5},{8,10},{10,8},{9,1... | collective-permute-start | bytes 1572872 | tf_op jit(solution)/shard_map/ppermute | solution.py:36
  12.5 43.8 %collective-permute-start.2 = (bf16[128,2048]{1,0:T(8,128)(2,1)}, bf16[128,2048]{1,0:T(8,128)(2,1)}, u32[]{:S(2)}, u32[]{:S(2)}) collective-permute-start(bf16[128,2048]{1,0:T(8,128)(2,1)} %get-tuple-element.74), channel_id=1, source_target_pairs={{0,4},{4,0},{1,5},{5,1},{2,6},{6,2},{3,7},{7,3},{8,12},{12,8},{9,1... | collective-permute-start | bytes 1572872 | tf_op jit(solution)/shard_map/ppermute | solution.py:36
  14.0 42.3 %collective-permute-start.1 = (bf16[128,2048]{1,0:T(8,128)(2,1)}, bf16[128,2048]{1,0:T(8,128)(2,1)}, u32[]{:S(2)}, u32[]{:S(2)}) collective-permute-start(bf16[128,2048]{1,0:T(8,128)(2,1)} %get-tuple-element.73), channel_id=1, source_target_pairs={{0,2},{2,0},{1,3},{3,1},{4,6},{6,4},{5,7},{7,5},{8,10},{10,8},{9,1... | collective-permute-start | bytes 1572872 | tf_op jit(solution)/shard_map/ppermute | solution.py:36
  14.6 39.7 %collective-permute-start.3 = (bf16[128,2048]{1,0:T(8,128)(2,1)}, bf16[128,2048]{1,0:T(8,128)(2,1)}, u32[]{:S(2)}, u32[]{:S(2)}) collective-permute-start(bf16[128,2048]{1,0:T(8,128)(2,1)} %get-tuple-element.73), channel_id=1, source_target_pairs={{0,4},{4,0},{1,5},{5,1},{2,6},{6,2},{3,7},{7,3},{8,12},{12,8},{9,1... | collective-permute-start | bytes 1572872 | tf_op jit(solution)/shard_map/ppermute | solution.py:36
  14.6 62.1 %collective-permute-start.6 = (bf16[256,2048]{1,0:T(8,128)(2,1)}, bf16[256,2048]{1,0:T(8,128)(2,1)}, u32[]{:S(2)}, u32[]{:S(2)}) collective-permute-start(bf16[256,2048]{1,0:T(8,128)(2,1)} %param.15), channel_id=1, source_target_pairs={{0,1},{1,0},{2,3},{3,2},{4,5},{5,4},{6,7},{7,6},{8,9},{9,8},{10,11... | collective-permute-start | bytes 3145736 | tf_op jit(solution)/shard_map/ppermute | solution.py:36
  21.2 32.9 %all-to-all-start = ((bf16[8,64,768]{2,1,0:T(8,128)(2,1)}), bf16[8,64,768]{2,1,0:T(8,128)(2,1)}, u32[]{:S(2)}, u32[]{:S(2)}) async-start(bf16[8,64,768]{2,1,0:T(8,128)(2,1)} %pad_maximum_fusion.20), calls=%async_computation | async-start | bytes 1572864 | tf_op jit(solution)/shard_map/all_to_all | solution.py:130
  25.6 94.1 %all-gather.6.cloned.1.call-start = ((), (), s32[]{:S(2)}) async-start(), calls=%async_computation.13 | async-start | bytes 3932160 | tf_op jit(solution)/shard_map/all_gather | solution.py:133
  55.8 23.2 %collective-permute-start.7 = (bf16[256,2048]{1,0:T(8,128)(2,1)S(1)}, bf16[256,2048]{1,0:T(8,128)(2,1)S(1)}, u32[]{:S(2)}, u32[]{:S(2)}) collective-permute-start(bf16[256,2048]{1,0:T(8,128)(2,1)S(1)} %pad_maximum_fusion.6), channel_id=1, source_target_pairs={{0,1},{1,0},{2,3},{3,2},{4,5},{5,4},{6,7},{7,6},{8,9},{9,8},{10,11... | collective-permute-start | bytes 3145736 | tf_op jit(solution)/shard_map/ppermute | solution.py:36
  57.6 22.3 %collective-permute-start.8 = (bf16[256,2048]{1,0:T(8,128)(2,1)S(1)}, bf16[256,2048]{1,0:T(8,128)(2,1)S(1)}, u32[]{:S(2)}, u32[]{:S(2)}) collective-permute-start(bf16[256,2048]{1,0:T(8,128)(2,1)S(1)} %pad_maximum_fusion.7), channel_id=1, source_target_pairs={{0,1},{1,0},{2,3},{3,2},{4,5},{5,4},{6,7},{7,6},{8,9},{9,8},{10,11... | collective-permute-start | bytes 3145736 | tf_op jit(solution)/shard_map/ppermute | solution.py:36
  89.2 89.6 %all-to-all-start.2 = ((bf16[8,64,2048]{2,1,0:T(8,128)(2,1)}), bf16[8,64,2048]{2,1,0:T(8,128)(2,1)}, u32[]{:S(2)}, u32[]{:S(2)}) async-start(bf16[8,64,2048]{2,1,0:T(8,128)(2,1)} %pad_maximum_fusion.2), calls=%async_computation.2 | async-start | bytes 4194304 | tf_op jit(solution)/shard_map/all_to_all | solution.py:130
  93.6 236.4 %all-gather.10.cloned.1.call-start = ((), (), s32[]{:S(2)}) async-start(), calls=%async_computation.15 | async-start | bytes 10485760 | tf_op jit(solution)/shard_map/all_gather | solution.py:133
  133.3 39.2 %collective-permute-start.10 = (f32[2,2,2,2,256]{4,3,2,1,0:T(2,128)S(1)}, f32[2,2,2,2,256]{4,3,2,1,0:T(2,128)S(1)}, u32[]{:S(2)}, u32[]{:S(2)}) collective-permute-start(f32[2,2,2,2,256]{4,3,2,1,0:T(2,128)S(1)} %constant_dynamic-update-slice_fusion.12), channel_id=1, source_target_pairs={{0,1},{1,0},{2,3},{3,2},{4,5},{5,4},{6,7},{7,6},{8,9},{9,8},{10,11... | collective-permute-start | bytes 49160 | tf_op jit(solution)/shard_map/ppermute | solution.py:36
  178.8 228.0 %all-gather.12.cloned.1.call-start = ((), (), s32[]{:S(2)}) async-start(), calls=%async_computation.16 | async-start | bytes 5242880 | tf_op jit(solution)/shard_map/all_gather | solution.py:133
  238.9 25.5 %collective-permute-start.14 = (bf16[2,128,2048]{2,1,0:T(8,128)(2,1)S(1)}, bf16[2,128,2048]{2,1,0:T(8,128)(2,1)S(1)}, u32[]{:S(2)}, u32[]{:S(2)}) collective-permute-start(bf16[2,128,2048]{2,1,0:T(8,128)(2,1)S(1)} %slice_bitcast_fusion.22), channel_id=1, source_target_pairs={{0,2},{2,0},{1,3},{3,1},{4,6},{6,4},{5,7},{7,5},{8,10},{10,8},{9,1... | collective-permute-start | bytes 3145736 | tf_op jit(solution)/shard_map/ppermute | solution.py:36
  241.0 24.9 %collective-permute-start.16 = (bf16[2,128,2048]{2,1,0:T(8,128)(2,1)S(1)}, bf16[2,128,2048]{2,1,0:T(8,128)(2,1)S(1)}, u32[]{:S(2)}, u32[]{:S(2)}) collective-permute-start(bf16[2,128,2048]{2,1,0:T(8,128)(2,1)S(1)} %slice_bitcast_fusion.19), channel_id=1, source_target_pairs={{0,4},{4,0},{1,5},{5,1},{2,6},{6,2},{3,7},{7,3},{8,12},{12,8},{9,1... | collective-permute-start | bytes 3145736 | tf_op jit(solution)/shard_map/ppermute | solution.py:36
  285.3 21.9 %collective-permute-start.19 = (bf16[128,2048]{1,0:T(8,128)(2,1)}, bf16[128,2048]{1,0:T(8,128)(2,1)S(1)}, u32[]{:S(2)}, u32[]{:S(2)}) collective-permute-start(bf16[128,2048]{1,0:T(8,128)(2,1)} %get-tuple-element.67), channel_id=1, source_target_pairs={{0,2},{2,0},{1,3},{3,1},{4,6},{6,4},{5,7},{7,5},{8,10},{10,8},{9,1... | collective-permute-start | bytes 1572872 | tf_op jit(solution)/shard_map/ppermute | solution.py:36
  285.9 22.0 %collective-permute-start.20 = (bf16[128,2048]{1,0:T(8,128)(2,1)}, bf16[128,2048]{1,0:T(8,128)(2,1)S(1)}, u32[]{:S(2)}, u32[]{:S(2)}) collective-permute-start(bf16[128,2048]{1,0:T(8,128)(2,1)} %get-tuple-element.68), channel_id=1, source_target_pairs={{0,4},{4,0},{1,5},{5,1},{2,6},{6,2},{3,7},{7,3},{8,12},{12,8},{9,1... | collective-permute-start | bytes 1572872 | tf_op jit(solution)/shard_map/ppermute | solution.py:36
  288.8 554.5 %reduce-scatter.13.cloned.1.call-start = ((), (), s32[]{:S(2)}) async-start(), calls=%async_computation.19 | async-start | bytes 5242880 | tf_op jit(solution)/shard_map/reduce_scatter | solution.py:237
  288.8 35.6 %collective-permute-start.24 = (bf16[256,2048]{1,0:T(8,128)(2,1)S(1)}, bf16[256,2048]{1,0:T(8,128)(2,1)S(1)}, u32[]{:S(2)}, u32[]{:S(2)}) collective-permute-start(bf16[256,2048]{1,0:T(8,128)(2,1)S(1)} %get-tuple-element.32), channel_id=1, source_target_pairs={{0,1},{1,0},{2,3},{3,2},{4,5},{5,4},{6,7},{7,6},{8,9},{9,8},{10,11... | collective-permute-start | bytes 3145736 | tf_op jit(solution)/shard_map/ppermute | solution.py:36
  300.1 25.4 %collective-permute-start.25 = (bf16[256,2048]{1,0:T(8,128)(2,1)S(1)}, bf16[256,2048]{1,0:T(8,128)(2,1)S(1)}, u32[]{:S(2)}, u32[]{:S(2)}) collective-permute-start(bf16[256,2048]{1,0:T(8,128)(2,1)S(1)} %pad_maximum_fusion.11), channel_id=1, source_target_pairs={{0,1},{1,0},{2,3},{3,2},{4,5},{5,4},{6,7},{7,6},{8,9},{9,8},{10,11... | collective-permute-start | bytes 3145736 | tf_op jit(solution)/shard_map/ppermute | solution.py:36
  308.0 18.4 %collective-permute-start.26 = (bf16[256,2048]{1,0:T(8,128)(2,1)S(1)}, bf16[256,2048]{1,0:T(8,128)(2,1)S(1)}, u32[]{:S(2)}, u32[]{:S(2)}) collective-permute-start(bf16[256,2048]{1,0:T(8,128)(2,1)S(1)} %pad_maximum_fusion.12), channel_id=1, source_target_pairs={{0,1},{1,0},{2,3},{3,2},{4,5},{5,4},{6,7},{7,6},{8,9},{9,8},{10,11... | collective-permute-start | bytes 3145736 | tf_op jit(solution)/shard_map/ppermute | solution.py:36
  429.2 25.3 %collective-permute-start.29 = (bf16[2,128,2048]{2,1,0:T(8,128)(2,1)S(1)}, bf16[2,128,2048]{2,1,0:T(8,128)(2,1)S(1)}, u32[]{:S(2)}, u32[]{:S(2)}) collective-permute-start(bf16[2,128,2048]{2,1,0:T(8,128)(2,1)S(1)} %slice_bitcast_fusion.16), channel_id=1, source_target_pairs={{0,2},{2,0},{1,3},{3,1},{4,6},{6,4},{5,7},{7,5},{8,10},{10,8},{9,1... | collective-permute-start | bytes 3145736 | tf_op jit(solution)/shard_map/ppermute | solution.py:36
  430.8 24.9 %collective-permute-start.31 = (bf16[2,128,2048]{2,1,0:T(8,128)(2,1)S(1)}, bf16[2,128,2048]{2,1,0:T(8,128)(2,1)S(1)}, u32[]{:S(2)}, u32[]{:S(2)}) collective-permute-start(bf16[2,128,2048]{2,1,0:T(8,128)(2,1)S(1)} %slice_bitcast_fusion.13), channel_id=1, source_target_pairs={{0,4},{4,0},{1,5},{5,1},{2,6},{6,2},{3,7},{7,3},{8,12},{12,8},{9,1... | collective-permute-start | bytes 3145736 | tf_op jit(solution)/shard_map/ppermute | solution.py:36
  475.1 20.0 %collective-permute-start.34 = (bf16[128,2048]{1,0:T(8,128)(2,1)S(1)}, bf16[128,2048]{1,0:T(8,128)(2,1)S(1)}, u32[]{:S(2)}, u32[]{:S(2)}) collective-permute-start(bf16[128,2048]{1,0:T(8,128)(2,1)S(1)} %get-tuple-element.65), channel_id=1, source_target_pairs={{0,2},{2,0},{1,3},{3,1},{4,6},{6,4},{5,7},{7,5},{8,10},{10,8},{9,1... | collective-permute-start | bytes 1572872 | tf_op jit(solution)/shard_map/ppermute | solution.py:36
  475.7 20.5 %collective-permute-start.35 = (bf16[128,2048]{1,0:T(8,128)(2,1)S(1)}, bf16[128,2048]{1,0:T(8,128)(2,1)S(1)}, u32[]{:S(2)}, u32[]{:S(2)}) collective-permute-start(bf16[128,2048]{1,0:T(8,128)(2,1)S(1)} %get-tuple-element.66), channel_id=1, source_target_pairs={{0,4},{4,0},{1,5},{5,1},{2,6},{6,2},{3,7},{7,3},{8,12},{12,8},{9,1... | collective-permute-start | bytes 1572872 | tf_op jit(solution)/shard_map/ppermute | solution.py:36
  476.2 35.9 %collective-permute-start.39 = (bf16[256,2048]{1,0:T(8,128)(2,1)S(1)}, bf16[256,2048]{1,0:T(8,128)(2,1)S(1)}, u32[]{:S(2)}, u32[]{:S(2)}) collective-permute-start(bf16[256,2048]{1,0:T(8,128)(2,1)S(1)} %get-tuple-element.30), channel_id=1, source_target_pairs={{0,1},{1,0},{2,3},{3,2},{4,5},{5,4},{6,7},{7,6},{8,9},{9,8},{10,11... | collective-permute-start | bytes 3145736 | tf_op jit(solution)/shard_map/ppermute | solution.py:36
  488.5 23.7 %collective-permute-start.40 = (bf16[256,2048]{1,0:T(8,128)(2,1)S(1)}, bf16[256,2048]{1,0:T(8,128)(2,1)S(1)}, u32[]{:S(2)}, u32[]{:S(2)}) collective-permute-start(bf16[256,2048]{1,0:T(8,128)(2,1)S(1)} %pad_maximum_fusion.14), channel_id=1, source_target_pairs={{0,1},{1,0},{2,3},{3,2},{4,5},{5,4},{6,7},{7,6},{8,9},{9,8},{10,11... | collective-permute-start | bytes 3145736 | tf_op jit(solution)/shard_map/ppermute | solution.py:36
  587.1 286.3 %reduce-scatter.15.cloned.1.call-start = ((), (), s32[]{:S(2)}) async-start(), calls=%async_computation.20 | async-start | bytes 5242880 | tf_op jit(solution)/shard_map/reduce_scatter | solution.py:237
  593.3 25.6 %collective-permute-start.44 = (bf16[2,128,2048]{2,1,0:T(8,128)(2,1)S(1)}, bf16[2,128,2048]{2,1,0:T(8,128)(2,1)S(1)}, u32[]{:S(2)}, u32[]{:S(2)}) collective-permute-start(bf16[2,128,2048]{2,1,0:T(8,128)(2,1)S(1)} %slice_bitcast_fusion.10), channel_id=1, source_target_pairs={{0,2},{2,0},{1,3},{3,1},{4,6},{6,4},{5,7},{7,5},{8,10},{10,8},{9,1... | collective-permute-start | bytes 3145736 | tf_op jit(solution)/shard_map/ppermute | solution.py:36
  593.5 25.4 %collective-permute-start.46 = (bf16[2,128,2048]{2,1,0:T(8,128)(2,1)S(1)}, bf16[2,128,2048]{2,1,0:T(8,128)(2,1)S(1)}, u32[]{:S(2)}, u32[]{:S(2)}) collective-permute-start(bf16[2,128,2048]{2,1,0:T(8,128)(2,1)S(1)} %slice_bitcast_fusion.7), channel_id=1, source_target_pairs={{0,4},{4,0},{1,5},{5,1},{2,6},{6,2},{3,7},{7,3},{8,12},{12,8},{9,1... | collective-permute-start | bytes 3145736 | tf_op jit(solution)/shard_map/ppermute | solution.py:36
  640.8 23.7 %collective-permute-start.50 = (bf16[128,2048]{1,0:T(8,128)(2,1)}, bf16[128,2048]{1,0:T(8,128)(2,1)S(1)}, u32[]{:S(2)}, u32[]{:S(2)}) collective-permute-start(bf16[128,2048]{1,0:T(8,128)(2,1)} %get-tuple-element.64), channel_id=1, source_target_pairs={{0,4},{4,0},{1,5},{5,1},{2,6},{6,2},{3,7},{7,3},{8,12},{12,8},{9,1... | collective-permute-start | bytes 1572872 | tf_op jit(solution)/shard_map/ppermute | solution.py:36
  641.1 23.5 %collective-permute-start.49 = (bf16[128,2048]{1,0:T(8,128)(2,1)}, bf16[128,2048]{1,0:T(8,128)(2,1)S(1)}, u32[]{:S(2)}, u32[]{:S(2)}) collective-permute-start(bf16[128,2048]{1,0:T(8,128)(2,1)} %get-tuple-element.63), channel_id=1, source_target_pairs={{0,2},{2,0},{1,3},{3,1},{4,6},{6,4},{5,7},{7,5},{8,10},{10,8},{9,1... | collective-permute-start | bytes 1572872 | tf_op jit(solution)/shard_map/ppermute | solution.py:36
  642.8 21.6 %collective-permute-start.51 = (bf16[128,2048]{1,0:T(8,128)(2,1)}, bf16[128,2048]{1,0:T(8,128)(2,1)S(1)}, u32[]{:S(2)}, u32[]{:S(2)}) collective-permute-start(bf16[128,2048]{1,0:T(8,128)(2,1)} %get-tuple-element.63), channel_id=1, source_target_pairs={{0,4},{4,0},{1,5},{5,1},{2,6},{6,2},{3,7},{7,3},{8,12},{12,8},{9,1... | collective-permute-start | bytes 1572872 | tf_op jit(solution)/shard_map/ppermute | solution.py:36
  655.2 237.3 %reduce-scatter.19.cloned.1.call-start = ((), (), s32[]{:S(2)}) async-start(), calls=%async_computation.22 | async-start | bytes 1081344
  655.3 26.0 %collective-permute-start.54 = (bf16[256,2048]{1,0:T(8,128)(2,1)S(1)}, bf16[256,2048]{1,0:T(8,128)(2,1)S(1)}, u32[]{:S(2)}, u32[]{:S(2)}) collective-permute-start(bf16[256,2048]{1,0:T(8,128)(2,1)S(1)} %get-tuple-element.28), channel_id=1, source_target_pairs={{0,1},{1,0},{2,3},{3,2},{4,5},{5,4},{6,7},{7,6},{8,9},{9,8},{10,11... | collective-permute-start | bytes 3145736 | tf_op jit(solution)/shard_map/ppermute | solution.py:36
  664.6 18.6 %collective-permute-start.56 = (bf16[256,2048]{1,0:T(8,128)(2,1)S(1)}, bf16[256,2048]{1,0:T(8,128)(2,1)S(1)}, u32[]{:S(2)}, u32[]{:S(2)}) collective-permute-start(bf16[256,2048]{1,0:T(8,128)(2,1)S(1)} %pad_maximum_fusion.18), channel_id=1, source_target_pairs={{0,1},{1,0},{2,3},{3,2},{4,5},{5,4},{6,7},{7,6},{8,9},{9,8},{10,11... | collective-permute-start | bytes 3145736 | tf_op jit(solution)/shard_map/ppermute | solution.py:36
  758.4 212.9 %reduce-scatter.17.cloned.1.call-start = ((), (), s32[]{:S(2)}) async-start(), calls=%async_computation.21 | async-start | bytes 5242880 | tf_op jit(solution)/shard_map/reduce_scatter | solution.py:237
  772.6 228.7 %reduce-scatter.11.cloned.1.call-start = ((), (), s32[]{:S(2)}) async-start(), calls=%async_computation.18 | async-start | bytes 1310720 | tf_op jit(solution)/shard_map/reduce_scatter | solution.py:237
  778.3 18.2 %collective-permute-start.60 = (f32[2,2,2,2,256]{4,3,2,1,0:T(2,128)S(1)}, f32[2,2,2,2,256]{4,3,2,1,0:T(2,128)S(1)}, u32[]{:S(2)}, u32[]{:S(2)}) collective-permute-start(f32[2,2,2,2,256]{4,3,2,1,0:T(2,128)S(1)} %reverse_add_fusion), channel_id=1, source_target_pairs={{0,2},{2,0},{1,3},{3,1},{4,6},{6,4},{5,7},{7,5},{8,10},{10,8},{9,1... | collective-permute-start | bytes 49160 | tf_op jit(solution)/shard_map/ppermute | solution.py:36
  814.9 18.7 %collective-permute-start.61 = (bf16[1024,2048]{1,0:T(8,128)(2,1)}, bf16[1024,2048]{1,0:T(8,128)(2,1)}, u32[]{:S(2)}, u32[]{:S(2)}) collective-permute-start(bf16[1024,2048]{1,0:T(8,128)(2,1)} %slice.423), channel_id=1, source_target_pairs={{0,1},{1,0},{2,3},{3,2},{4,5},{5,4},{6,7},{7,6},{8,9},{9,8},{10,11... | collective-permute-start | bytes 12582920 | tf_op jit(solution)/shard_map/ppermute | solution.py:36
  822.9 239.5 %reduce-scatter.9.cloned.1.call-start = ((), (), s32[]{:S(2)}) async-start(), calls=%async_computation.17 | async-start | bytes 3932160 | tf_op jit(solution)/shard_map/reduce_scatter | solution.py:237
  841.0 28.1 %collective-permute-start.62 = (bf16[2,128,2048]{2,1,0:T(8,128)(2,1)S(1)}, bf16[2,128,2048]{2,1,0:T(8,128)(2,1)}, u32[]{:S(2)}, u32[]{:S(2)}) collective-permute-start(bf16[2,128,2048]{2,1,0:T(8,128)(2,1)S(1)} %slice_bitcast_fusion.4), channel_id=1, source_target_pairs={{0,2},{2,0},{1,3},{3,1},{4,6},{6,4},{5,7},{7,5},{8,10},{10,8},{9,1... | collective-permute-start | bytes 3145736 | tf_op jit(solution)/shard_map/ppermute | solution.py:36
  841.8 27.3 %collective-permute-start.64 = (bf16[2,128,2048]{2,1,0:T(8,128)(2,1)S(1)}, bf16[2,128,2048]{2,1,0:T(8,128)(2,1)}, u32[]{:S(2)}, u32[]{:S(2)}) collective-permute-start(bf16[2,128,2048]{2,1,0:T(8,128)(2,1)S(1)} %slice_bitcast_fusion.1), channel_id=1, source_target_pairs={{0,4},{4,0},{1,5},{5,1},{2,6},{6,2},{3,7},{7,3},{8,12},{12,8},{9,1... | collective-permute-start | bytes 3145736 | tf_op jit(solution)/shard_map/ppermute | solution.py:36
  843.2 38.0 %all-to-all-start.5 = ((bf16[8,64,1024]{2,1,0:T(8,128)(2,1)}), bf16[8,64,1024]{2,1,0:T(8,128)(2,1)S(1)}, u32[]{:S(2)}, u32[]{:S(2)}) async-start(bf16[8,64,1024]{2,1,0:T(8,128)(2,1)} %bitcast.424), calls=%async_computation.8 | async-start | bytes 2097152 | tf_op jit(solution)/shard_map/all_to_all | solution.py:130
  881.2 97.5 %all-to-all-start.6 = ((bf16[8,64,1024]{2,1,0:T(8,128)(2,1)}), bf16[8,64,1024]{2,1,0:T(8,128)(2,1)}, u32[]{:S(2)}, u32[]{:S(2)}) async-start(bf16[8,64,1024]{2,1,0:T(8,128)(2,1)} %bitcast.425), calls=%async_computation.10 | async-start | bytes 2097152 | tf_op jit(solution)/shard_map/all_to_all | solution.py:130
  887.8 115.3 %collective-permute-start.65 = (bf16[128,2048]{1,0:T(8,128)(2,1)}, bf16[128,2048]{1,0:T(8,128)(2,1)}, u32[]{:S(2)}, u32[]{:S(2)}) collective-permute-start(bf16[128,2048]{1,0:T(8,128)(2,1)} %fusion.63), channel_id=1, source_target_pairs={{0,2},{2,0},{1,3},{3,1},{4,6},{6,4},{5,7},{7,5},{8,10},{10,8},{9,1... | collective-permute-start | bytes 1572872 | tf_op jit(solution)/shard_map/ppermute | solution.py:36
  890.6 176.1 %collective-permute-start.63 = (bf16[128,2048]{1,0:T(8,128)(2,1)}, bf16[128,2048]{1,0:T(8,128)(2,1)}, u32[]{:S(2)}, u32[]{:S(2)}) collective-permute-start(bf16[128,2048]{1,0:T(8,128)(2,1)} %fusion.62), channel_id=1, source_target_pairs={{0,4},{4,0},{1,5},{5,1},{2,6},{6,2},{3,7},{7,3},{8,12},{12,8},{9,1... | collective-permute-start | bytes 1572872 | tf_op jit(solution)/shard_map/ppermute | solution.py:36
  (106 other events, 1389.4 us)
Sparse Core Ops, SparseCore 0:
  16.5 29.8 all-gather.7
  54.3 65.3 all-gather.5
  178.9 147.3 all-gather.9
  327.8 78.9 all-gather.11
  587.3 73.6 reduce-scatter.12
  663.2 77.2 reduce-scatter.14
  758.5 133.9 reduce-scatter.18
  895.0 76.2 reduce-scatter.16
  973.6 27.6 reduce-scatter.10
  1003.5 58.8 reduce-scatter.8

commit v2 on v1

v2 whole, which is shorter than its diff:
```python
import math

import jax
import jax.numpy as jnp
from jax import lax
from jax.experimental import pallas as pl
from jax.experimental.pallas import tpu as pltpu
from jax.sharding import Mesh, PartitionSpec as P

HEAD = 128
SEQ_MAX = 1024
NORM_EPS = 1e-06
ROPE_BASE = 500000.0
MASKED = -1e30
BF16 = jnp.bfloat16
F32 = jnp.float32
GROUP = ("y", "x", "c")
ALL = ("zh", "zl", "y", "x", "c")
PLANES = ("zh", "zl")


def matmul(left, right):
    return jnp.dot(left, right, preferred_element_type=F32)


def matmul_t(left, right):
    return lax.dot_general(left, right, (((1,), (1,)), ((), ())), preferred_element_type=F32)


def inner_t(left, right):
    return lax.dot_general(left, right, (((0,), (0,)), ((), ())), preferred_element_type=F32)


def inverse_rms(values):
    return lax.rsqrt(jnp.mean(values * values, axis=-1, keepdims=True) + NORM_EPS)


def after(value, *others):
    return lax.optimization_barrier((value,) + others)[0]


def swap(block, axis):
    return lax.ppermute(block, axis, [(0, 1), (1, 0)])


def group_gather(own):
    half = own.shape[0] // 2
    near_x = swap(own, "x")
    near_y = swap(own, "y")
    top = swap(near_x[:half], "y")
    low = swap(near_y[half:], "x")
    first = jnp.concatenate([own, near_x, near_y], 0)
    last = jnp.concatenate([top, low], 0)
    return jnp.concatenate([first, last, swap(first, "c"), swap(last, "c")], 0)


def group_sum(terms):
    total = terms.reshape(terms.shape[0], 2, 2, 2, -1)
    for dim, axis in enumerate(("c", "y", "x")):
        total = total + jnp.flip(swap(total, axis), dim + 1)
    return total.reshape(terms.shape)


def group_scatter(parts, rows):
    width = parts.shape[1]
    half = rows // 2
    arrived = swap(parts[4 * rows :], "c")
    mine = parts[: 4 * rows].astype(F32) + arrived.astype(F32)
    mine = mine.astype(BF16).reshape(2, 2, 2, half, width)
    got_x = swap(mine[:, 1, 0], "x")
    got_y = swap(mine[1, :, 1], "y")
    top = mine[:, 0, 0].astype(F32) + got_x.astype(F32)
    bottom = mine[0, :, 1].astype(F32) + got_y.astype(F32)
    top_last = swap(top[1].astype(BF16), "y")
    bottom_last = swap(bottom[1].astype(BF16), "x")
    return jnp.concatenate([top[0] + top_last.astype(F32), bottom[0] + bottom_last.astype(F32)], 0)


def doubled(own, axes):
    for axis in reversed(axes):
        size = lax.axis_size(axis)
        step = 1
        while step < size:
            got = lax.ppermute(own, axis, [(i, i ^ step) for i in range(size)])
            low_side = lax.axis_index(axis) & step == 0
            own = jnp.concatenate([jnp.where(low_side, own, got), jnp.where(low_side, got, own)], 0)
            step *= 2
    return own


def halved(terms, axes):
    for axis in axes:
        size = lax.axis_size(axis)
        step = size // 2
        while step:
            low_side = lax.axis_index(axis) & step == 0
            first, second = jnp.split(terms, 2)
            got = lax.ppermute(
                jnp.where(low_side, second, first), axis, [(i, i ^ step) for i in range(size)]
            )
            terms = jnp.where(low_side, first, second) + got
            step //= 2
    return terms


def gather_planes(part):
    return lax.all_gather(part, PLANES, axis=0, tiled=True)


def scatter_planes(term):
    return lax.psum_scatter(term, PLANES, scatter_dimension=0, tiled=True)


SCALE = HEAD ** (-0.5)
ROWS = 256
PARAMS = pltpu.CompilerParams(vmem_limit_bytes=48 * 2**20)


def flat_rows(ref):
    return ref[...].reshape(-1, ref.shape[-1])


def turn(values, cosine, sine):
    return values * cosine + pltpu.roll(values, HEAD // 2, 1) * sine


def softmax_rows(query, key, place, info):
    scores = matmul_t(query, key) * SCALE
    visible = (place >= info[:, 0:1]) & (place < info[:, 1:2])
    masked = jnp.where(visible, scores, MASKED)
    weights = jnp.exp(masked - jnp.max(masked, -1, keepdims=True))
    return weights * (1.0 / jnp.sum(weights, -1, keepdims=True))


def attend_kernel(q_ref, k_ref, v_ref, info_ref, cos_ref, sin_ref, gq_ref, gk_ref, place_ref, o_ref):
    info, cosine, sine = flat_rows(info_ref), flat_rows(cos_ref), flat_rows(sin_ref)
    query = turn(flat_rows(q_ref) * info[:, 2:3] * gq_ref[...], cosine, sine).astype(BF16)
    key = turn(flat_rows(k_ref) * info[:, 3:4] * gk_ref[...], cosine, sine).astype(BF16)
    value = flat_rows(v_ref).astype(BF16)
    place = place_ref[...]
    for start in range(0, SEQ_MAX, ROWS):
        softmax = softmax_rows(query[start : start + ROWS], key, place, info[start : start + ROWS])
        mixed = matmul(softmax.astype(BF16), value).astype(BF16)
        half, at = divmod(start, SEQ_MAX // 2)
        o_ref[half, 0, at : at + ROWS] = mixed


def attend_back_kernel(
    q_ref, k_ref, v_ref, info_ref, cos_ref, sin_ref, gq_ref, gk_ref, place_ref, do_ref,
    dq_ref, dk_ref, dv_ref, mean_ref, dk_sum, dv_sum, dq_all,
):
    info, cosine, sine = flat_rows(info_ref), flat_rows(cos_ref), flat_rows(sin_ref)
    query_in, key_in = flat_rows(q_ref), flat_rows(k_ref)
    query = turn(query_in * info[:, 2:3] * gq_ref[...], cosine, sine).astype(BF16)
    key = turn(key_in * info[:, 3:4] * gk_ref[...], cosine, sine).astype(BF16)
    value = flat_rows(v_ref).astype(BF16)
    grad = flat_rows(do_ref)
    place = place_ref[...]
    for start in range(0, SEQ_MAX, ROWS):
        part = slice(start, start + ROWS)
        softmax = softmax_rows(query[part], key, place, info[part])
        softmax_grad = matmul_t(grad[part], value)
        inner = jnp.sum(softmax * softmax_grad, -1, keepdims=True)
        score_grad = (softmax * (softmax_grad - inner)).astype(BF16)
        dq_all[part] = matmul(score_grad, key) * SCALE
        dk_term = inner_t(score_grad, query[part])
        dv_term = inner_t(softmax.astype(BF16), grad[part])
        if start:
            dk_sum[...] += dk_term
            dv_sum[...] += dv_term
        else:
            dk_sum[...] = dk_term
            dv_sum[...] = dv_term
    dq = turn(dq_all[...], cosine, -sine)
    dk = turn(dk_sum[...] * SCALE, cosine, -sine)
    dq_ref[...] = dq.reshape(dq_ref.shape)
    dk_ref[...] = dk.reshape(dk_ref.shape)
    dv_ref[...] = dv_sum[...].astype(BF16).reshape(dv_ref.shape)
    mean_q = jnp.sum(dq * gq_ref[...] * query_in, -1, keepdims=True)
    mean_k = jnp.sum(dk * gk_ref[...] * key_in, -1, keepdims=True)
    mean_ref[...] = jnp.concatenate([mean_q, mean_k], 1).reshape(mean_ref.shape)


def qkv_grad_kernel(p_ref, dq_ref, dk_ref, dv_ref, info_ref, mean_ref, gq_ref, gk_ref, grads_ref, gains_ref):
    columns = dq_ref.shape[1]
    info, mean = info_ref[...], mean_ref[...]
    terms = []
    for i, (d_ref, gain_ref) in enumerate(((dq_ref, gq_ref), (dk_ref, gk_ref))):
        values, r, d = p_ref[:, i * columns : (i + 1) * columns], info[:, 2 + i : 3 + i], d_ref[...]
        grad = r * (gain_ref[...] * d - values * (r * r) * mean[:, i : i + 1])
        grads_ref[:, i * columns : (i + 1) * columns] = grad.astype(BF16)
        terms.append(jnp.sum(d * values * r, 0, keepdims=True))
    grads_ref[:, 2 * columns :] = dv_ref[...]
    term = jnp.concatenate(terms, 0)

    @pl.when(pl.program_id(0) == 0)
    def _():
        gains_ref[...] = term

    @pl.when(pl.program_id(0) > 0)
    def _():
        gains_ref[...] += term


def to_units(gate, up, unit_rows):
    rows, width = gate.shape
    units = width // 8

    def kernel(gate_ref, up_ref, out_ref):
        for i, w_ref in enumerate((gate_ref, up_ref)):
            for m in range(8):
                for r in range(units // unit_rows):
                    source, target = (r * 8 + m) * unit_rows, i * units + r * unit_rows
                    out_ref[m, :, target : target + unit_rows] = w_ref[:, source : source + unit_rows].astype(BF16)

    step = min(rows, 16)
    return pl.pallas_call(
        kernel,
        grid=(rows // step,),
        in_specs=[pl.BlockSpec((step, width), lambda i: (i, 0))] * 2,
        out_specs=pl.BlockSpec((8, step, 2 * units), lambda i: (0, i, 0)),
        out_shape=jax.ShapeDtypeStruct((8, rows, 2 * units), BF16),
        compiler_params=PARAMS,
    )(gate, up)


def from_units(parts, unit_rows):
    _, rows, units = parts.shape

    def kernel(p_ref, out_ref):
        for m in range(8):
            for r in range(units // unit_rows):
                target, source = (r * 8 + m) * unit_rows, r * unit_rows
                out_ref[:, target : target + unit_rows] = p_ref[m, :, source : source + unit_rows].astype(F32)

    step = min(rows, 16)
    return pl.pallas_call(
        kernel,
        grid=(rows // step,),
        in_specs=[pl.BlockSpec((8, step, units), lambda i: (0, i, 0))],
        out_specs=pl.BlockSpec((step, 8 * units), lambda i: (i, 0)),
        out_shape=jax.ShapeDtypeStruct((rows, 8 * units), F32),
        compiler_params=PARAMS,
    )(parts)


def head_specs(heads):
    def of(width, column):
        return pl.BlockSpec((2, 1, SEQ_MAX // 2, width), lambda b, h: (0, b, 0, column(h)))

    gain = pl.BlockSpec((1, HEAD), lambda b, h: (0, h))
    return of, [
        of(HEAD, lambda h: h),
        of(HEAD, lambda h: heads + h),
        of(HEAD, lambda h: 2 * heads + h),
        of(4, lambda h: 0),
        of(HEAD, lambda h: 0),
        of(HEAD, lambda h: 0),
        gain,
        gain,
        pl.BlockSpec((1, SEQ_MAX), lambda b, h: (0, 0)),
    ]


def in_blocks(array):
    return array.reshape(2, -1, SEQ_MAX // 2, array.shape[-1])


def attend(projected, info, cosine, sine, gain_q, gain_k, place):
    rows, columns = projected.shape[0], projected.shape[1] // 3
    heads, blocks = columns // HEAD, rows // SEQ_MAX
    of, specs = head_specs(heads)
    p = in_blocks(projected)
    mixed = pl.pallas_call(
        attend_kernel,
        grid=(blocks, heads),
        in_specs=specs,
        out_specs=of(HEAD, lambda h: h),
        out_shape=jax.ShapeDtypeStruct((2, blocks, SEQ_MAX // 2, columns), BF16),
        compiler_params=PARAMS,
        cost_estimate=pl.CostEstimate(
            flops=4 * rows * SEQ_MAX * columns, bytes_accessed=8 * rows * columns * 2, transcendentals=rows * SEQ_MAX * heads
        ),
    )(p, p, p, in_blocks(info), in_blocks(cosine), in_blocks(sine), gain_q, gain_k, place)
    return mixed.reshape(rows, columns)


def attend_back(projected, info, cosine, sine, gain_q, gain_k, place, mixed_grad):
    rows, columns = projected.shape[0], projected.shape[1] // 3
    heads, blocks = columns // HEAD, rows // SEQ_MAX
    of, specs = head_specs(heads)
    p = in_blocks(projected)
    shape = (2, blocks, SEQ_MAX // 2, columns)
    dq, dk, dv, means = pl.pallas_call(
        attend_back_kernel,
        grid=(blocks, heads),
        in_specs=specs + [of(HEAD, lambda h: h)],
        out_specs=[of(HEAD, lambda h: h)] * 3
        + [pl.BlockSpec((1, 2, 1, SEQ_MAX // 2, 2), lambda b, h: (h, 0, b, 0, 0))],
        out_shape=[
            jax.ShapeDtypeStruct(shape, F32),
            jax.ShapeDtypeStruct(shape, F32),
            jax.ShapeDtypeStruct(shape, BF16),
            jax.ShapeDtypeStruct((heads,) + shape[:3] + (2,), F32),
        ],
        scratch_shapes=[pltpu.VMEM((SEQ_MAX, HEAD), F32)] * 3,
        compiler_params=PARAMS,
        cost_estimate=pl.CostEstimate(
            flops=10 * rows * SEQ_MAX * columns, bytes_accessed=12 * rows * columns * 2, transcendentals=rows * SEQ_MAX * heads
        ),
    )(p, p, p, in_blocks(info), in_blocks(cosine), in_blocks(sine), gain_q, gain_k, place, in_blocks(mixed_grad))
    flat = [array.reshape(rows, columns) for array in (dq, dk, dv)]
    return *flat, jnp.sum(means, 0).reshape(rows, 2)


def qkv_grads(projected, dq, dk, dv, info, mean, gain_q, gain_k):
    rows, columns = dq.shape
    step = 512

    def by_row(width):
        return pl.BlockSpec((step, width), lambda i: (i, 0))

    def fixed(height):
        return pl.BlockSpec((height, columns), lambda i: (0, 0))

    return pl.pallas_call(
        qkv_grad_kernel,
        grid=(rows // step,),
        in_specs=[by_row(3 * columns)] + [by_row(columns)] * 3 + [by_row(4), by_row(2), fixed(1), fixed(1)],
        out_specs=[by_row(3 * columns), fixed(2)],
        out_shape=[
            jax.ShapeDtypeStruct((rows, 3 * columns), BF16),
            jax.ShapeDtypeStruct((2, columns), F32),
        ],
        compiler_params=PARAMS,
    )(projected, dq, dk, dv, info, mean, gain_q, gain_k)


def make_body(count, per_head):
    replicas = count // 8
    own_heads = replicas // per_head
    head_axes = GROUP[3 - int(math.log2(per_head)) :]
    head_shape = (per_head, own_heads, 8 // per_head)
    head_shape_put = (8 // per_head, per_head, own_heads)

    def body(
        tokens,
        cotangent,
        segment_ids,
        piece_ids,
        w_query,
        w_key,
        w_value,
        w_out,
        query_gain,
        key_gain,
        mixer_gain,
        w_gate,
        w_up,
        w_down,
        feed_gain,
    ):
        rows, width = tokens.shape
        weight_rows = w_query.shape[0]
        unit_rows = w_down.shape[0]
        units = replicas * unit_rows
        columns = own_heads * HEAD
        group_rows = 8 * rows
        blocks = group_rows // SEQ_MAX
        member = lax.axis_index(GROUP)
        device = lax.axis_index(ALL)

        def by_head(weight):
            shaped = weight.astype(BF16).reshape((weight_rows,) + head_shape + (HEAD,))
            return shaped.transpose(3, 1, 0, 2, 4).reshape(8, weight_rows, columns)

        def exchange(parts, group):
            return lax.all_to_all(parts, group, 0, 0, tiled=True)

        own_gains = jnp.stack([query_gain, key_gain, mixer_gain, feed_gain]).astype(BF16)
        plane_gains = doubled(own_gains.reshape(1, 4, weight_rows), PLANES)
        gains = doubled(plane_gains, GROUP).reshape(8, replicas, 4, weight_rows)
        gains = gains.transpose(2, 1, 0, 3).reshape(4, width).astype(F32)

        qkv_parts = jnp.concatenate([by_head(w_query), by_head(w_key), by_head(w_value)], 2)
        qkv_piece = exchange(qkv_parts, GROUP).reshape(8 * weight_rows, 3 * columns)
        out_halves = gather_planes(after(w_out.astype(BF16), plane_gains))
        feed_parts = after(to_units(w_gate, w_up, unit_rows), qkv_piece)
        feed_piece = exchange(feed_parts, GROUP).reshape(8 * weight_rows, 2 * units)
        group_tokens = group_gather(after(tokens, qkv_piece))
        weight_qkv = gather_planes(after(qkv_piece, plane_gains))
        weight_feed = gather_planes(feed_piece)
        weight_down = gather_planes(after(w_down.astype(BF16), weight_qkv))
        out_halves = out_halves.reshape(per_head, own_heads, weight_rows, width)
        out_heads = lax.all_to_all(out_halves, head_axes, 0, 0, tiled=True)
        weight_out = out_heads.transpose(1, 0, 2, 3).reshape(columns, width)

        head_gains = gains[:2].reshape((2,) + head_shape + (HEAD,)).transpose(0, 3, 1, 2, 4)
        head_gains = lax.dynamic_index_in_dim(head_gains.reshape(2, 8, columns), member, 1, keepdims=False)
        gain_q, gain_k = head_gains.reshape(2, 1, columns)
        gain_a, gain_f = gains[2:3], gains[3:4]

        orders = [c + 4 * y + 2 * x for c in (0, 1) for y in (0, 1) for x in (0, 1)]
        starts = [(device ^ k) * rows for k in orders]

        def of_group(ids):
            return jnp.concatenate([lax.dynamic_slice_in_dim(ids, s, rows, 0) for s in starts])

        places = jnp.concatenate([s + jnp.arange(rows, dtype=jnp.int32) for s in starts])

        def by_block(array):
            shaped = array.reshape((2, blocks, group_rows // (2 * blocks)) + array.shape[1:])
            return jnp.moveaxis(shaped, 1, 0).reshape((blocks, SEQ_MAX) + array.shape[1:])

        def from_block(array):
            shaped = array.reshape((blocks, 2, SEQ_MAX // 2) + array.shape[2:])
            return jnp.moveaxis(shaped, 0, 1).reshape((group_rows,) + array.shape[2:])

        segment = by_block(of_group(segment_ids))
        piece = by_block(of_group(piece_ids))
        place_block = by_block(places) % SEQ_MAX
        before = jnp.sum((segment[:, None, :] < segment[:, :, None]).astype(jnp.int32), -1)
        positions = from_block(place_block - before)
        in_piece = (piece[:, None, :] == piece[:, :, None]) & (piece[:, :, None] > 0)
        piece_end = jnp.max(jnp.where(in_piece, place_block[:, None, :] + 1, 0), -1)
        first_seen = from_block(before).astype(F32)
        end_seen = from_block(jnp.maximum(place_block + 1, piece_end)).astype(F32)
        place = place_block[:1].astype(F32)
        freqs = jnp.exp(jnp.arange(HEAD // 2, dtype=F32) * (-2.0 * math.log(ROPE_BASE) / HEAD))
        angles = positions.astype(F32)[:, None] * freqs[None, :]
        cosine = jnp.concatenate([jnp.cos(angles), jnp.cos(angles)], 1)
        sine = jnp.concatenate([-jnp.sin(angles), jnp.sin(angles)], 1)

        projected = matmul(after(group_tokens, feed_piece), weight_qkv)
        squares = jnp.sum(jnp.square(projected[:, : 2 * columns]).reshape(group_rows, 2, columns), -1)
        inverse = lax.rsqrt(group_sum(squares.T) / width + NORM_EPS)
        inverse = after(inverse, weight_out)
        info = jnp.stack([first_seen, end_seen, inverse[0], inverse[1]], 1)
        attention = (projected, info, cosine, sine, gain_q, gain_k, place)
        mixed_low = attend(*attention)
        branch = group_scatter(matmul(mixed_low, weight_out).astype(BF16), rows)
        r_a = inverse_rms(branch)
        hidden_in = tokens.astype(F32) + branch * r_a * gain_a
        group_hidden_in = group_gather(hidden_in.astype(BF16))
        gate = matmul(group_hidden_in, weight_feed[:, :units])
        up = matmul(group_hidden_in, weight_feed[:, units:])
        sig = 1.0 / (1.0 + jnp.exp(-gate))
        hidden = (gate * sig * up).astype(BF16)
        result = group_scatter(matmul(hidden, weight_down).astype(BF16), rows)
        r_m = inverse_rms(result)
        out_tokens = (hidden_in + result * r_m * gain_f).astype(BF16)

        def norm_back(values, r, gain, grad):
            scaled = gain * grad
            mean = jnp.mean(scaled * values, -1, keepdims=True)
            return r * (scaled - values * (r * r) * mean), jnp.sum(grad * values * r, 0)

        grad_out = cotangent.astype(F32)
        result_grad, feed_gain_term = norm_back(result, r_m, gain_f, grad_out)
        group_result_grad = group_gather(result_grad.astype(BF16))

        down_term = inner_t(hidden, group_result_grad).astype(BF16)
        hidden_grad = matmul_t(after(group_result_grad, down_term), weight_down)
        gate_grad = (hidden_grad * up * sig * (1.0 + gate * (1.0 - sig))).astype(BF16)
        up_grad = (hidden_grad * gate * sig).astype(BF16)
        hidden_in_parts = (
            matmul_t(gate_grad, weight_feed[:, :units]) + matmul_t(up_grad, weight_feed[:, units:])
        ).astype(BF16)
        gate_term = inner_t(after(group_hidden_in, hidden_in_parts), gate_grad).astype(BF16)
        up_term = inner_t(after(group_hidden_in, gate_term), up_grad).astype(BF16)
        down_share = scatter_planes(down_term)
        gate_share = scatter_planes(gate_term)
        up_share = scatter_planes(up_term)
        hidden_in_grad = grad_out + group_scatter(hidden_in_parts, rows)
        hidden_in_grad = after(hidden_in_grad, up_term)
        branch_grad, mixer_gain_term = norm_back(branch, r_a, gain_a, hidden_in_grad)
        group_branch_grad = group_gather(branch_grad.astype(BF16))
        group_branch_grad = after(group_branch_grad, down_share)
        mixed_grad = matmul_t(group_branch_grad, weight_out).astype(BF16)
        q_back, k_back, v_grad, means = attend_back(*attention, mixed_grad)
        out_term = inner_t(mixed_low, after(group_branch_grad, mixed_grad))
        means = after(means, gate_share, out_term)
        means = group_sum(means.T).T / width
        grads, head_terms = qkv_grads(projected, q_back, k_back, v_grad, info, means, gain_q, gain_k)
        qkv_term = inner_t(group_tokens, grads).astype(BF16)
        grads = after(grads, qkv_term)
        g_tokens = hidden_in_grad + group_scatter(matmul_t(grads, weight_qkv).astype(BF16), rows)

        qkv_share = scatter_planes(qkv_term)
        qkv_back = exchange(qkv_share.reshape(8, weight_rows, 3 * columns), GROUP)
        qkv_back = qkv_back.reshape(head_shape_put[:2] + (weight_rows, 3, own_heads, HEAD))
        g_qkv = qkv_back.transpose(3, 2, 1, 4, 0, 5).reshape(3, weight_rows, width).astype(F32)
        out_parts = out_term.astype(BF16).reshape(own_heads, per_head, weight_rows, width)
        out_parts = lax.all_to_all(out_parts.transpose(1, 0, 2, 3), head_axes, 0, 0, tiled=True)
        g_w_out = scatter_planes(out_parts.reshape(replicas * weight_rows, width)).astype(F32)
        g_w_down = down_share.astype(F32)
        g_w_gate = from_units(exchange(gate_share.reshape(8, weight_rows, units), GROUP), unit_rows)
        g_w_up = from_units(exchange(up_share.reshape(8, weight_rows, units), GROUP), unit_rows)

        head_terms = head_terms.reshape(2, 1, columns)
        spread = jnp.zeros((2, 8, columns), F32)
        spread = lax.dynamic_update_slice(spread, head_terms, (0, member, 0))
        spread = spread.reshape((2,) + head_shape_put + (HEAD,)).transpose(0, 2, 3, 1, 4)
        gain_terms = jnp.concatenate([spread.reshape(2, width), jnp.stack([mixer_gain_term, feed_gain_term])], 0)
        gain_terms = gain_terms.reshape(4, replicas, 8, weight_rows).transpose(2, 1, 0, 3)
        g_gains = halved(gain_terms.reshape(count, 4, weight_rows), GROUP + PLANES)[0]
        return (
            out_tokens,
            g_tokens,
            g_qkv[0],
            g_qkv[1],
            g_qkv[2],
            g_w_out,
            g_gains[0],
            g_gains[1],
            g_gains[2],
            g_w_gate,
            g_w_up,
            g_w_down,
            g_gains[3],
        )

    return body


def solution(mesh):
    count = mesh.shape["dev"]
    grid = Mesh(mesh.devices.reshape(count // 16, 2, 2, 2, 2), ALL)

    def run(tokens, cotangent, segment_ids, piece_ids, w_query, *rest):
        per_head = count * HEAD // w_query.shape[0]
        rows, whole, gain = P(ALL, None), P(), P(ALL)
        in_specs = (rows, rows, whole, whole) + (rows,) * 4 + (gain,) * 3 + (rows,) * 3 + (gain,)
        out_specs = (rows,) * 6 + (gain,) * 3 + (rows,) * 3 + (gain,)
        return jax.shard_map(
            make_body(count, per_head), mesh=grid, in_specs=in_specs, out_specs=out_specs, check_vma=False
        )(tokens, cotangent, segment_ids, piece_ids, w_query, *rest)

    return run
```

time: 1100 us -> 966 us (0.88)
  waiting for transfers between devices: 477 us -> 396 us
  Pallas kernels: 0 us -> 64.5 us
  local copies, waits for them, and re-layouts: 173 us -> 118 us
  matrix products: 218 us -> 179 us
  blocking collectives: 44.7 us -> 13.9 us
    reduce_scatter x5, waiting for transfers between devices: 149 us -> 1.78 us  [scatter_planes(): return lax.psum_scatter(term, PLANES, scatter_dimension=0, tiled=True)]
    pallas_call x0 -> x6, Pallas kernels: none -> 64.5 us  [the longest x1 35 us: attend_back(): pl.pallas_call(attend_back_kernel, grid=(blocks, heads), in_specs=specs +...]
    all_gather x1 -> x0, blocking collectives: 39.1 us -> none  [body(): lax.all_gather(jnp.stack([query_gain, key_gain, mixer_gain, feed_gain]).a...]
    dot_general x5 -> x0, matrix products: 32.7 us -> none  [the longest x1 9.63 us: body(): jnp.einsum('bhqk,bqhd->bkhd', softmax_low, mixed_grad, preferred_element_...]
    ppermute x66 -> x50, waiting for transfers between devices: 239 us -> 271 us  [swap(): return lax.ppermute(block, axis, [(0, 1), (1, 0)])]
    reshape x22 -> x13, local copies, waits for them, and re-layouts: 25.8 us -> 9 us  [the longest x1 5.88 us: body(): jnp.square(projected[:, :2 * columns]).reshape(group_rows, 2, columns)]
    convert_element_type x13 -> x10, other arithmetic: 25.4 us -> 9.62 us  [the longest x3 2.17 us: by_head(): shaped = weight.astype(BF16).reshape((weight_rows,) + head_shape + (HEAD,))]
    all_to_all x6 -> x5, waiting for transfers between devices: 15.9 us -> 28.3 us  [exchange(): return lax.all_to_all(parts, group, 0, 0, tiled=True)]
  transfers between devices with their start and end apart: 82 -> 74, of which waited for: 44 -> 48; matrix products, arithmetic and copies ran while one was open for 35% -> 34% of each run, Pallas kernels for 0% -> 5%
where the time goes in v2:
time: 966 us; the launch traced here: 957 us
  waiting for transfers between devices  396 us (41%)
  matrix products  179 us (19%)
  local copies, waits for them, and re-layouts  118 us (12%)
  other arithmetic  97.4 us (10%)
  starting transfers between devices  73 us (8%)
  Pallas kernels  64.5 us (7%)
  between operations  15.8 us (2%)
  blocking collectives  13.9 us (1%)
    ppermute x50, waiting for transfers between devices, swap(): return lax.ppermute(block, axis, [(0, 1), (1, 0)])  271 us
    all_gather x4, waiting for transfers between devices, gather_planes(): return lax.all_gather(part, PLANES, axis=0, tiled=True)  84.7 us
    dot_general x5, matrix products, matmul_t(): lax.dot_general(left, right, (((1,), (1,)), ((), ())), preferred_element_...  69.8 us
    unnamed x168, local copies, waits for them, and re-layouts  59.9 us
    dot_general x5, matrix products, inner_t(): lax.dot_general(left, right, (((0,), (0,)), ((), ())), preferred_element_...  55.6 us
    dot_general x5, matrix products, matmul(): return jnp.dot(left, right, preferred_element_type=F32)  53.7 us
    ppermute x50, starting transfers between devices, swap(): return lax.ppermute(block, axis, [(0, 1), (1, 0)])  41.5 us
    pallas_call x1, Pallas kernels, attend_back(): pl.pallas_call(attend_back_kernel, grid=(blocks, heads), in_specs=specs +...  35 us
  transfers between devices with their start and end apart: 74, of which 48 were waited for; matrix products, arithmetic and copies ran while one was open for 34% of the time, Pallas kernels for 5%

profile of v2, /device:TPU:0, one launch (start us, length us, event | category | flops | bytes accessed | tf_op | source)
XLA Modules:
  0.0 957.4 jit_solution(7522953192269153663)
XLA Ops:
  43.5 19.8 %collective-permute-done = bf16[256,2048]{1,0:T(8,128)(2,1)S(1)} collective-permute-done((bf16[256,2048]{1,0:T(8,128)(2,1)S(1)}, bf16[256,2048]{1,0:T(8,128)(2,1)S(1)}, u32[]{:S(2)}, u32[]{:S(2)}) %collective-permute-start) | collective-permute-done | bytes 1048608 | tf_op jit(solution)/shard_map/ppermute | solution.py:43
  68.6 5.5 fusion.31
  95.3 4.4 all-to-all-start.1
  119.4 10.0 %all-to-all-done.1 = bf16[8,64,2048]{2,1,0:T(8,128)(2,1)} async-done(((bf16[8,64,2048]{2,1,0:T(8,128)(2,1)}), bf16[8,64,2048]{2,1,0:T(8,128)(2,1)}, u32[]{:S(2)}, u32[]{:S(2)}) %all-to-all-start.1) | async-done | bytes 2097184 | tf_op jit(solution)/shard_map/all_to_all | solution.py:378
  129.4 10.0 %fusion.40.p_ref = f32[2048,768]{1,0:T(8,128)S(1)} fusion(bf16[2048,2048]{1,0:T(8,128)(2,1)} %constant_dynamic-update-slice_fusion, bf16[2048,768]{1,0:T(8,128)(2,1)} %all-gather.5.cloned.1.call-done), kind=kOutput, calls=%fused_computation.252 | convolution fusion | flops 6442450944 | bytes 17825792 | tf_op jit(solution)/shard_map/dot_general | solution.py:23
  144.6 5.9 reshape.462
  150.5 6.2 reduce_sum.82
  164.0 5.9 all_to_all.35
  178.5 16.8 %shard_map.247 = bf16[2,2,512,256]{3,2,1,0:T(8,128)(2,1)S(1)} custom-call(f32[2,2,512,768]{3,2,1,0:T(8,128)} %bitcast.283, f32[2,2,512,768]{3,2,1,0:T(8,128)} %bitcast.284, f32[2,2,512,768]{3,2,1,0:T(8,128)} %bitcast.285, f32[2,2,512,4]{3,2,1,0:T(8,128)S(1)} %pad_maximum_fusion.7.info_ref, f32[2,2,512,128]{3,2,1,0:T(8,128)S(1)} %pad_maximum_fusion.8.cos_ref, ...), custom_call_target="tpu_custom_call" | custom-call | flops 2147483648 | bytes 8388608 | tf_op jit(solution)/shard_map/pallas_call | solution.py:274
  202.9 6.9 collective-permute-done.14
  209.8 6.3 add_convert_fusion.4
  218.3 23.2 %collective-permute-done.15 = bf16[2,128,2048]{2,1,0:T(8,128)(2,1)S(1)} collective-permute-done((bf16[2,128,2048]{2,1,0:T(8,128)(2,1)S(1)}, bf16[2,128,2048]{2,1,0:T(8,128)(2,1)S(1)}, u32[]{:S(2)}, u32[]{:S(2)}) %collective-permute-start.15) | collective-permute-done | bytes 1048608 | tf_op jit(solution)/shard_map/ppermute | solution.py:43
  247.7 10.0 %collective-permute-done.18 = bf16[128,2048]{1,0:T(8,128)(2,1)S(1)} collective-permute-done((bf16[128,2048]{1,0:T(8,128)(2,1)}, bf16[128,2048]{1,0:T(8,128)(2,1)S(1)}, u32[]{:S(2)}, u32[]{:S(2)}) %collective-permute-start.18) | collective-permute-done | bytes 524320 | tf_op jit(solution)/shard_map/ppermute | solution.py:43
  265.4 21.1 %collective-permute-done.19 = bf16[256,2048]{1,0:T(8,128)(2,1)S(1)} collective-permute-done((bf16[256,2048]{1,0:T(8,128)(2,1)S(1)}, bf16[256,2048]{1,0:T(8,128)(2,1)S(1)}, u32[]{:S(2)}, u32[]{:S(2)}) %collective-permute-start.19) | collective-permute-done | bytes 1048608 | tf_op jit(solution)/shard_map/ppermute | solution.py:43
  294.0 10.2 %collective-permute-done.21 = bf16[128,2048]{1,0:T(8,128)(2,1)} collective-permute-done((bf16[128,2048]{1,0:T(8,128)(2,1)}, bf16[128,2048]{1,0:T(8,128)(2,1)}, u32[]{:S(2)}, u32[]{:S(2)}) %collective-permute-start.21) | collective-permute-done | bytes 524320 | tf_op jit(solution)/shard_map/ppermute | solution.py:43
  318.8 32.9 %all-gather.9.cloned.1.call-done = bf16[2048,2048]{1,0:T(8,128)(2,1)} async-done(((bf16[512,2048]{1,0:T(8,128)(2,1)}), bf16[2048,2048]{1,0:T(8,128)(2,1)}) %all-gather.9.cloned.1.call-update) | async-done | bytes 8388624 | tf_op jit(solution)/shard_map/all_gather | solution.py:107
  351.7 14.6 %fusion.5 = f32[2048,1024]{1,0:T(8,128)} fusion(bf16[2048,2048]{1,0:T(8,128)(2,1)} %constant_dynamic-update-slice_fusion.10, bf16[2048,2048]{1,0:T(8,128)(2,1)} %all-gather.9.cloned.1.call-done), kind=kOutput, calls=%fused_computation.23 | convolution fusion | flops 8589934592 | bytes 20971520 | tf_op jit(solution)/shard_map/dot_general | solution.py:23
  366.3 14.6 %multiply_convert_fusion.2 = (bf16[2048,1024]{1,0:T(8,128)(2,1)}, f32[2048,1024]{1,0:T(8,128)}) fusion(f32[2048,1024]{1,0:T(8,128)} %fusion.5, bf16[2048,2048]{1,0:T(8,128)(2,1)S(1)} %copy-done.50, bf16[2048,2048]{1,0:T(8,128)(2,1)} %all-gather.9.cloned.1.call-done), kind=kOutput, calls=%fused_computation.6 | convolution fusion | flops 8602517504 | bytes 33554432 | tf_op jit(solution)/shard_map/dot_general | solution.py:23
  380.9 51.8 %all-gather.11.cloned.1.call-done = bf16[1024,2048]{1,0:T(8,128)(2,1)} async-done(((bf16[256,2048]{1,0:T(8,128)(2,1)}), bf16[1024,2048]{1,0:T(8,128)(2,1)}) %all-gather.11.cloned.1.call-update) | async-done | bytes 4194320 | tf_op jit(solution)/shard_map/all_gather | solution.py:107
  432.7 12.1 %convolution_convert_fusion.1 = bf16[2048,2048]{1,0:T(8,128)(2,1)S(1)} fusion(bf16[2048,1024]{1,0:T(8,128)(2,1)} %get-tuple-element.120, bf16[1024,2048]{1,0:T(8,128)(2,1)} %all-gather.11.cloned.1.call-done), kind=kOutput, calls=%fused_computation.12 | convolution fusion | flops 8594128896 | bytes 16777216 | tf_op jit(solution)/shard_map/dot_general | solution.py:23
  445.2 7.1 collective-permute-done.25
  457.9 22.2 %collective-permute-done.26 = bf16[2,128,2048]{2,1,0:T(8,128)(2,1)S(1)} collective-permute-done((bf16[2,128,2048]{2,1,0:T(8,128)(2,1)S(1)}, bf16[2,128,2048]{2,1,0:T(8,128)(2,1)S(1)}, u32[]{:S(2)}, u32[]{:S(2)}) %collective-permute-start.26) | collective-permute-done | bytes 1048608 | tf_op jit(solution)/shard_map/ppermute | solution.py:43
  485.7 9.4 collective-permute-done.29
  504.0 21.0 %collective-permute-done.30 = bf16[256,2048]{1,0:T(8,128)(2,1)S(1)} collective-permute-done((bf16[256,2048]{1,0:T(8,128)(2,1)S(1)}, bf16[256,2048]{1,0:T(8,128)(2,1)S(1)}, u32[]{:S(2)}, u32[]{:S(2)}) %collective-permute-start.30) | collective-permute-done | bytes 1048608 | tf_op jit(solution)/shard_map/ppermute | solution.py:43
  529.1 11.4 %collective-permute-done.32 = bf16[128,2048]{1,0:T(8,128)(2,1)S(1)} collective-permute-done((bf16[128,2048]{1,0:T(8,128)(2,1)S(1)}, bf16[128,2048]{1,0:T(8,128)(2,1)S(1)}, u32[]{:S(2)}, u32[]{:S(2)}) %collective-permute-start.32) | collective-permute-done | bytes 524320 | tf_op jit(solution)/shard_map/ppermute | solution.py:43
  547.9 11.0 %convolution_convert_fusion.3 = bf16[1024,2048]{1,0:T(8,128)(2,1)} fusion(bf16[2048,1024]{1,0:T(8,128)(2,1)S(1)} %copy-done.63, bf16[2048,2048]{1,0:T(8,128)(2,1)S(1)} %constant_dynamic-update-slice_fusion.17), kind=kOutput, calls=%fused_computation.15 | convolution fusion | flops 8592031744 | bytes 16777216 | tf_op jit(solution)/shard_map/dot_general | solution.py:31
  559.0 22.3 %multiply_convert_fusion = (bf16[2048,1024]{1,0:T(8,128)(2,1)S(1)}, bf16[2048,1024]{1,0:T(8,128)(2,1)}) fusion(f32[2048,1024]{1,0:T(8,128)} %fusion.5, f32[2048,1024]{1,0:T(8,128)} %get-tuple-element.121, bf16[2048,2048]{1,0:T(8,128)(2,1)} %copy-done.51, bf16[1024,2048]{1,0:T(8,128)(2,1)} %all-gather.11.cloned.1.call-done), kind=kOutput, calls=%fused_computation.3 | convolution fusion | flops 8617197568 | bytes 37748736 | tf_op jit(solution)/shard_map/dot_general | solution.py:27
  581.3 16.8 %fusion.3 = f32[2048,2048]{1,0:T(8,128)} fusion(bf16[2048,1024]{1,0:T(8,128)(2,1)} %get-tuple-element.72, bf16[2048,2048]{1,0:T(8,128)(2,1)} %all-gather.9.cloned.1.call-done), kind=kOutput, calls=%fused_computation.21 | convolution fusion | flops 8589934592 | bytes 25165824 | tf_op jit(solution)/shard_map/dot_general | solution.py:27
  598.1 15.6 %add_convert_fusion = bf16[2048,2048]{1,0:T(8,128)(2,1)} fusion(f32[2048,2048]{1,0:T(8,128)} %fusion.3, bf16[2048,1024]{1,0:T(8,128)(2,1)S(1)} %get-tuple-element.71, bf16[2048,2048]{1,0:T(8,128)(2,1)} %all-gather.9.cloned.1.call-done), kind=kOutput, calls=%fused_computation | convolution fusion | flops 8598323200 | bytes 33554432 | tf_op jit(solution)/shard_map/dot_general | solution.py:27
  616.7 7.0 collective-permute-done.36
  630.4 12.8 %convolution_convert_fusion.5 = bf16[2048,1024]{1,0:T(8,128)(2,1)} fusion(bf16[2048,2048]{1,0:T(8,128)(2,1)} %constant_dynamic-update-slice_fusion.10, bf16[2048,1024]{1,0:T(8,128)(2,1)S(1)} %copy-done.66), kind=kOutput, calls=%fused_computation.17 | convolution fusion | flops 8592031744 | bytes 16777216 | tf_op jit(solution)/shard_map/dot_general | solution.py:31
  643.4 9.2 collective-permute-done.37
  662.0 13.0 %convolution_convert_fusion.4 = bf16[2048,1024]{1,0:T(8,128)(2,1)} fusion(bf16[2048,2048]{1,0:T(8,128)(2,1)} %constant_dynamic-update-slice_fusion.10, bf16[2048,1024]{1,0:T(8,128)(2,1)S(1)} %copy-done.65), kind=kOutput, calls=%fused_computation.16 | convolution fusion | flops 8592031744 | bytes 16777216 | tf_op jit(solution)/shard_map/dot_general | solution.py:31
  685.1 21.7 %collective-permute-done.41 = bf16[256,2048]{1,0:T(8,128)(2,1)S(1)} collective-permute-done((bf16[256,2048]{1,0:T(8,128)(2,1)S(1)}, bf16[256,2048]{1,0:T(8,128)(2,1)S(1)}, u32[]{:S(2)}, u32[]{:S(2)}) %collective-permute-start.41) | collective-permute-done | bytes 1048608 | tf_op jit(solution)/shard_map/ppermute | solution.py:43
  713.5 10.8 %collective-permute-done.43 = bf16[128,2048]{1,0:T(8,128)(2,1)} collective-permute-done((bf16[128,2048]{1,0:T(8,128)(2,1)}, bf16[128,2048]{1,0:T(8,128)(2,1)}, u32[]{:S(2)}, u32[]{:S(2)}) %collective-permute-start.43) | collective-permute-done | bytes 524320 | tf_op jit(solution)/shard_map/ppermute | solution.py:43
  739.2 6.2 convolution_convert_fusion.7
  745.5 35.0 %shard_map.248 = (f32[2,2,512,256]{3,2,1,0:T(8,128)}, f32[2,2,512,256]{3,2,1,0:T(8,128)}, bf16[2,2,512,256]{3,2,1,0:T(8,128)(2,1)S(1)}, f32[2,2,2,512,2]{4,3,2,1,0:T(8,128)}) custom-call(f32[2,2,512,768]{3,2,1,0:T(8,128)} %bitcast.286, f32[2,2,512,768]{3,2,1,0:T(8,128)} %bitcast.287, f32[2,2,512,768]{3,2,1,0:T(8,128)} %bitcast.288, ...), custom_call_target="tpu_custom_call" | custom-call | flops 5368709120 | bytes 12582912 | tf_op jit(solution)/shard_map/pallas_call | solution.py:294
  783.5 6.7 fusion.41
  801.8 6.5 shard_map.249
  808.3 11.9 %convolution_convert_fusion.6 = bf16[2048,768]{1,0:T(8,128)(2,1)} fusion(bf16[2048,2048]{1,0:T(8,128)(2,1)} %constant_dynamic-update-slice_fusion, bf16[2048,768]{1,0:T(8,128)(2,1)} %get-tuple-element.53), kind=kOutput, calls=%fused_computation.25 | convolution fusion | flops 6444023808 | bytes 14680064 | tf_op jit(solution)/shard_map/dot_general | solution.py:31
  820.2 8.8 convolution_convert_fusion
  833.8 8.0 all_to_all.36
  852.0 7.8 add_convert_fusion.1
  862.2 4.6 all-to-all-done.5.p_ref
  888.2 19.3 %collective-permute-done.51 = bf16[2,128,2048]{2,1,0:T(8,128)(2,1)} collective-permute-done((bf16[2,128,2048]{2,1,0:T(8,128)(2,1)}, bf16[2,128,2048]{2,1,0:T(8,128)(2,1)}, u32[]{:S(2)}, u32[]{:S(2)}) %collective-permute-start.51) | collective-permute-done | bytes 1048608 | tf_op jit(solution)/shard_map/ppermute | solution.py:43
  916.5 7.8 collective-permute-done.54
  927.5 4.4 all-to-all-start.3
  935.0 9.3 all-to-all-done.3
  (491 shorter events, 305.6 us)
Async XLA Ops:
  8.6 17.2 %collective-permute-start.6 = (bf16[1,4,64]{2,1,0:T(4,128)(2,1)S(1)}, bf16[1,4,64]{2,1,0:T(4,128)(2,1)S(1)}, u32[]{:S(2)}, u32[]{:S(2)}) collective-permute-start(bf16[1,4,64]{2,1,0:T(4,128)(2,1)S(1)} %pad_maximum_fusion.20), channel_id=1, source_target_pairs={{0,8},{8,0},{1,9},{9,1},{2,10},{10,2},{3,11},{11,3},{4,12},{12,4},... | collective-permute-start | bytes 1544 | tf_op jit(solution)/shard_map/ppermute | solution.py:84
  16.5 16.3 %all-to-all-start = ((bf16[8,64,768]{2,1,0:T(8,128)(2,1)}), bf16[8,64,768]{2,1,0:T(8,128)(2,1)S(1)}, u32[]{:S(2)}, u32[]{:S(2)}) async-start(bf16[8,64,768]{2,1,0:T(8,128)(2,1)} %pad_maximum_fusion.13), calls=%async_computation | async-start | bytes 1572864 | tf_op jit(solution)/shard_map/all_to_all | solution.py:378
  20.3 109.2 %all-gather.5.cloned.1.call-start = ((), (), s32[]{:S(2)}) async-start(), calls=%async_computation.12 | async-start | bytes 3932160 | tf_op jit(solution)/shard_map/all_gather | solution.py:107
  33.8 130.2 %all-gather.7.cloned.1.call-start = ((), (), s32[]{:S(2)}) async-start(), calls=%async_computation.13 | async-start | bytes 1310720 | tf_op jit(solution)/shard_map/all_gather | solution.py:107
  39.3 24.0 %collective-permute-start = (bf16[256,2048]{1,0:T(8,128)(2,1)S(1)}, bf16[256,2048]{1,0:T(8,128)(2,1)S(1)}, u32[]{:S(2)}, u32[]{:S(2)}) collective-permute-start(bf16[256,2048]{1,0:T(8,128)(2,1)S(1)} %copy-done.26), channel_id=1, source_target_pairs={{0,2},{2,0},{1,3},{3,1},{4,6},{6,4},{5,7},{7,5},{8,10},{10,8},{9,1... | collective-permute-start | bytes 3145736 | tf_op jit(solution)/shard_map/ppermute | solution.py:43
  39.9 24.9 %collective-permute-start.1 = (bf16[256,2048]{1,0:T(8,128)(2,1)S(1)}, bf16[256,2048]{1,0:T(8,128)(2,1)S(1)}, u32[]{:S(2)}, u32[]{:S(2)}) collective-permute-start(bf16[256,2048]{1,0:T(8,128)(2,1)S(1)} %copy-done.26), channel_id=1, source_target_pairs={{0,4},{4,0},{1,5},{5,1},{2,6},{6,2},{3,7},{7,3},{8,12},{12,8},{9,1... | collective-permute-start | bytes 3145736 | tf_op jit(solution)/shard_map/ppermute | solution.py:43
  66.8 47.5 %collective-permute-start.4 = (bf16[768,2048]{1,0:T(8,128)(2,1)}, bf16[768,2048]{1,0:T(8,128)(2,1)}, u32[]{:S(2)}, u32[]{:S(2)}) collective-permute-start(bf16[768,2048]{1,0:T(8,128)(2,1)} %pad_maximum_fusion), channel_id=1, source_target_pairs={{0,1},{1,0},{2,3},{3,2},{4,5},{5,4},{6,7},{7,6},{8,9},{9,8},{10,11... | collective-permute-start | bytes 9437192 | tf_op jit(solution)/shard_map/ppermute | solution.py:43
  75.5 18.0 %collective-permute-start.12 = (bf16[8,4,64]{2,1,0:T(4,128)(2,1)S(1)}, bf16[8,4,64]{2,1,0:T(4,128)(2,1)S(1)}, u32[]{:S(2)}, u32[]{:S(2)}) collective-permute-start(bf16[8,4,64]{2,1,0:T(4,128)(2,1)S(1)} %pad_maximum_fusion.17), channel_id=1, source_target_pairs={{0,2},{2,0},{1,3},{3,1},{4,6},{6,4},{5,7},{7,5},{8,10},{10,8},{9,1... | collective-permute-start | bytes 12296 | tf_op jit(solution)/shard_map/ppermute | solution.py:84
  89.6 15.1 %collective-permute-start.2 = (bf16[128,2048]{1,0:T(8,128)(2,1)}, bf16[128,2048]{1,0:T(8,128)(2,1)}, u32[]{:S(2)}, u32[]{:S(2)}) collective-permute-start(bf16[128,2048]{1,0:T(8,128)(2,1)} %slice.278), channel_id=1, source_target_pairs={{0,4},{4,0},{1,5},{5,1},{2,6},{6,2},{3,7},{7,3},{8,12},{12,8},{9,1... | collective-permute-start | bytes 1572872 | tf_op jit(solution)/shard_map/ppermute | solution.py:43
  91.9 15.1 %collective-permute-start.3 = (bf16[128,2048]{1,0:T(8,128)(2,1)}, bf16[128,2048]{1,0:T(8,128)(2,1)}, u32[]{:S(2)}, u32[]{:S(2)}) collective-permute-start(bf16[128,2048]{1,0:T(8,128)(2,1)} %slice.279), channel_id=1, source_target_pairs={{0,2},{2,0},{1,3},{3,1},{4,6},{6,4},{5,7},{7,5},{8,10},{10,8},{9,1... | collective-permute-start | bytes 1572872 | tf_op jit(solution)/shard_map/ppermute | solution.py:43
  93.6 64.7 %collective-permute-start.13 = (bf16[16,4,64]{2,1,0:T(4,128)(2,1)S(1)}, bf16[16,4,64]{2,1,0:T(4,128)(2,1)S(1)}, u32[]{:S(2)}, u32[]{:S(2)}) collective-permute-start(bf16[16,4,64]{2,1,0:T(4,128)(2,1)S(1)} %pad_maximum_fusion.16), channel_id=1, source_target_pairs={{0,4},{4,0},{1,5},{5,1},{2,6},{6,2},{3,7},{7,3},{8,12},{12,8},{9,1... | collective-permute-start | bytes 24584 | tf_op jit(solution)/shard_map/ppermute | solution.py:84
  95.3 34.1 %all-to-all-start.1 = ((bf16[8,64,2048]{2,1,0:T(8,128)(2,1)}), bf16[8,64,2048]{2,1,0:T(8,128)(2,1)}, u32[]{:S(2)}, u32[]{:S(2)}) async-start(bf16[8,64,2048]{2,1,0:T(8,128)(2,1)} %copy-done.6), calls=%async_computation.1 | async-start | bytes 4194304 | tf_op jit(solution)/shard_map/all_to_all | solution.py:378
  99.7 252.0 %all-gather.9.cloned.1.call-start = ((), (), s32[]{:S(2)}) async-start(), calls=%async_computation.14 | async-start | bytes 10485760 | tf_op jit(solution)/shard_map/all_gather | solution.py:107
  202.4 230.3 %all-gather.11.cloned.1.call-start = ((), (), s32[]{:S(2)}) async-start(), calls=%async_computation.15 | async-start | bytes 5242880 | tf_op jit(solution)/shard_map/all_gather | solution.py:107
  216.3 25.3 %collective-permute-start.15 = (bf16[2,128,2048]{2,1,0:T(8,128)(2,1)S(1)}, bf16[2,128,2048]{2,1,0:T(8,128)(2,1)S(1)}, u32[]{:S(2)}, u32[]{:S(2)}) collective-permute-start(bf16[2,128,2048]{2,1,0:T(8,128)(2,1)S(1)} %slice_bitcast_fusion.22), channel_id=1, source_target_pairs={{0,2},{2,0},{1,3},{3,1},{4,6},{6,4},{5,7},{7,5},{8,10},{10,8},{9,1... | collective-permute-start | bytes 3145736 | tf_op jit(solution)/shard_map/ppermute | solution.py:43
  217.8 24.9 %collective-permute-start.17 = (bf16[2,128,2048]{2,1,0:T(8,128)(2,1)S(1)}, bf16[2,128,2048]{2,1,0:T(8,128)(2,1)S(1)}, u32[]{:S(2)}, u32[]{:S(2)}) collective-permute-start(bf16[2,128,2048]{2,1,0:T(8,128)(2,1)S(1)} %slice_bitcast_fusion.19), channel_id=1, source_target_pairs={{0,4},{4,0},{1,5},{5,1},{2,6},{6,2},{3,7},{7,3},{8,12},{12,8},{9,1... | collective-permute-start | bytes 3145736 | tf_op jit(solution)/shard_map/ppermute | solution.py:43
  263.1 23.4 %collective-permute-start.19 = (bf16[256,2048]{1,0:T(8,128)(2,1)S(1)}, bf16[256,2048]{1,0:T(8,128)(2,1)S(1)}, u32[]{:S(2)}, u32[]{:S(2)}) collective-permute-start(bf16[256,2048]{1,0:T(8,128)(2,1)S(1)} %get-tuple-element.68), channel_id=1, source_target_pairs={{0,2},{2,0},{1,3},{3,1},{4,6},{6,4},{5,7},{7,5},{8,10},{10,8},{9,1... | collective-permute-start | bytes 3145736 | tf_op jit(solution)/shard_map/ppermute | solution.py:43
  264.0 22.8 %collective-permute-start.20 = (bf16[256,2048]{1,0:T(8,128)(2,1)S(1)}, bf16[256,2048]{1,0:T(8,128)(2,1)S(1)}, u32[]{:S(2)}, u32[]{:S(2)}) collective-permute-start(bf16[256,2048]{1,0:T(8,128)(2,1)S(1)} %get-tuple-element.68), channel_id=1, source_target_pairs={{0,4},{4,0},{1,5},{5,1},{2,6},{6,2},{3,7},{7,3},{8,12},{12,8},{9,1... | collective-permute-start | bytes 3145736 | tf_op jit(solution)/shard_map/ppermute | solution.py:43
  288.7 25.0 %collective-permute-start.23 = (bf16[768,2048]{1,0:T(8,128)(2,1)}, bf16[768,2048]{1,0:T(8,128)(2,1)}, u32[]{:S(2)}, u32[]{:S(2)}) collective-permute-start(bf16[768,2048]{1,0:T(8,128)(2,1)} %pad_maximum_fusion.1), channel_id=1, source_target_pairs={{0,1},{1,0},{2,3},{3,2},{4,5},{5,4},{6,7},{7,6},{8,9},{9,8},{10,11... | collective-permute-start | bytes 9437192 | tf_op jit(solution)/shard_map/ppermute | solution.py:43
  289.5 14.7 %collective-permute-start.21 = (bf16[128,2048]{1,0:T(8,128)(2,1)}, bf16[128,2048]{1,0:T(8,128)(2,1)}, u32[]{:S(2)}, u32[]{:S(2)}) collective-permute-start(bf16[128,2048]{1,0:T(8,128)(2,1)} %slice.294), channel_id=1, source_target_pairs={{0,4},{4,0},{1,5},{5,1},{2,6},{6,2},{3,7},{7,3},{8,12},{12,8},{9,1... | collective-permute-start | bytes 1572872 | tf_op jit(solution)/shard_map/ppermute | solution.py:43
  294.0 445.2 %reduce-scatter.6.cloned.1.call-start = ((), (), s32[]{:S(2)}) async-start(), calls=%async_computation.16 | async-start | bytes 5242880 | tf_op jit(solution)/shard_map/reduce_scatter | solution.py:111
  454.9 25.3 %collective-permute-start.26 = (bf16[2,128,2048]{2,1,0:T(8,128)(2,1)S(1)}, bf16[2,128,2048]{2,1,0:T(8,128)(2,1)S(1)}, u32[]{:S(2)}, u32[]{:S(2)}) collective-permute-start(bf16[2,128,2048]{2,1,0:T(8,128)(2,1)S(1)} %slice_bitcast_fusion.16), channel_id=1, source_target_pairs={{0,2},{2,0},{1,3},{3,1},{4,6},{6,4},{5,7},{7,5},{8,10},{10,8},{9,1... | collective-permute-start | bytes 3145736 | tf_op jit(solution)/shard_map/ppermute | solution.py:43
  456.4 24.9 %collective-permute-start.28 = (bf16[2,128,2048]{2,1,0:T(8,128)(2,1)S(1)}, bf16[2,128,2048]{2,1,0:T(8,128)(2,1)S(1)}, u32[]{:S(2)}, u32[]{:S(2)}) collective-permute-start(bf16[2,128,2048]{2,1,0:T(8,128)(2,1)S(1)} %slice_bitcast_fusion.13), channel_id=1, source_target_pairs={{0,4},{4,0},{1,5},{5,1},{2,6},{6,2},{3,7},{7,3},{8,12},{12,8},{9,1... | collective-permute-start | bytes 3145736 | tf_op jit(solution)/shard_map/ppermute | solution.py:43
  501.8 23.2 %collective-permute-start.30 = (bf16[256,2048]{1,0:T(8,128)(2,1)S(1)}, bf16[256,2048]{1,0:T(8,128)(2,1)S(1)}, u32[]{:S(2)}, u32[]{:S(2)}) collective-permute-start(bf16[256,2048]{1,0:T(8,128)(2,1)S(1)} %get-tuple-element.66), channel_id=1, source_target_pairs={{0,2},{2,0},{1,3},{3,1},{4,6},{6,4},{5,7},{7,5},{8,10},{10,8},{9,1... | collective-permute-start | bytes 3145736 | tf_op jit(solution)/shard_map/ppermute | solution.py:43
  502.5 22.9 %collective-permute-start.31 = (bf16[256,2048]{1,0:T(8,128)(2,1)S(1)}, bf16[256,2048]{1,0:T(8,128)(2,1)S(1)}, u32[]{:S(2)}, u32[]{:S(2)}) collective-permute-start(bf16[256,2048]{1,0:T(8,128)(2,1)S(1)} %get-tuple-element.66), channel_id=1, source_target_pairs={{0,4},{4,0},{1,5},{5,1},{2,6},{6,2},{3,7},{7,3},{8,12},{12,8},{9,1... | collective-permute-start | bytes 3145736 | tf_op jit(solution)/shard_map/ppermute | solution.py:43
  525.9 16.3 %collective-permute-start.34 = (bf16[768,2048]{1,0:T(8,128)(2,1)S(1)}, bf16[768,2048]{1,0:T(8,128)(2,1)S(1)}, u32[]{:S(2)}, u32[]{:S(2)}) collective-permute-start(bf16[768,2048]{1,0:T(8,128)(2,1)S(1)} %pad_maximum_fusion.2), channel_id=1, source_target_pairs={{0,1},{1,0},{2,3},{3,2},{4,5},{5,4},{6,7},{7,6},{8,9},{9,8},{10,11... | collective-permute-start | bytes 9437192 | tf_op jit(solution)/shard_map/ppermute | solution.py:43
  526.1 14.4 %collective-permute-start.32 = (bf16[128,2048]{1,0:T(8,128)(2,1)S(1)}, bf16[128,2048]{1,0:T(8,128)(2,1)S(1)}, u32[]{:S(2)}, u32[]{:S(2)}) collective-permute-start(bf16[128,2048]{1,0:T(8,128)(2,1)S(1)} %slice.309), channel_id=1, source_target_pairs={{0,4},{4,0},{1,5},{5,1},{2,6},{6,2},{3,7},{7,3},{8,12},{12,8},{9,1... | collective-permute-start | bytes 1572872 | tf_op jit(solution)/shard_map/ppermute | solution.py:43
  559.0 231.2 %reduce-scatter.8.cloned.1.call-start = ((), (), s32[]{:S(2)}) async-start(), calls=%async_computation.17 | async-start | bytes 5242880 | tf_op jit(solution)/shard_map/reduce_scatter | solution.py:111
  627.0 25.5 %collective-permute-start.37 = (bf16[2,128,2048]{2,1,0:T(8,128)(2,1)}, bf16[2,128,2048]{2,1,0:T(8,128)(2,1)}, u32[]{:S(2)}, u32[]{:S(2)}) collective-permute-start(bf16[2,128,2048]{2,1,0:T(8,128)(2,1)} %slice_bitcast_fusion.10), channel_id=1, source_target_pairs={{0,2},{2,0},{1,3},{3,1},{4,6},{6,4},{5,7},{7,5},{8,10},{10,8},{9,1... | collective-permute-start | bytes 3145736 | tf_op jit(solution)/shard_map/ppermute | solution.py:43
  629.7 25.5 %collective-permute-start.39 = (bf16[2,128,2048]{2,1,0:T(8,128)(2,1)}, bf16[2,128,2048]{2,1,0:T(8,128)(2,1)}, u32[]{:S(2)}, u32[]{:S(2)}) collective-permute-start(bf16[2,128,2048]{2,1,0:T(8,128)(2,1)} %slice_bitcast_fusion.7), channel_id=1, source_target_pairs={{0,4},{4,0},{1,5},{5,1},{2,6},{6,2},{3,7},{7,3},{8,12},{12,8},{9,1... | collective-permute-start | bytes 3145736 | tf_op jit(solution)/shard_map/ppermute | solution.py:43
  643.3 218.9 %reduce-scatter.14.cloned.1.call-start = ((), (), s32[]{:S(2)}) async-start(), calls=%async_computation.20 | async-start | bytes 5242880 | tf_op jit(solution)/shard_map/reduce_scatter | solution.py:111
  659.2 15.8 %collective-permute-start.40 = (bf16[128,2048]{1,0:T(8,128)(2,1)}, bf16[128,2048]{1,0:T(8,128)(2,1)}, u32[]{:S(2)}, u32[]{:S(2)}) collective-permute-start(bf16[128,2048]{1,0:T(8,128)(2,1)} %fusion.28), channel_id=1, source_target_pairs={{0,2},{2,0},{1,3},{3,1},{4,6},{6,4},{5,7},{7,5},{8,10},{10,8},{9,1... | collective-permute-start | bytes 1572872 | tf_op jit(solution)/shard_map/ppermute | solution.py:43
  661.4 15.2 %collective-permute-start.38 = (bf16[128,2048]{1,0:T(8,128)(2,1)}, bf16[128,2048]{1,0:T(8,128)(2,1)}, u32[]{:S(2)}, u32[]{:S(2)}) collective-permute-start(bf16[128,2048]{1,0:T(8,128)(2,1)} %fusion.27), channel_id=1, source_target_pairs={{0,4},{4,0},{1,5},{5,1},{2,6},{6,2},{3,7},{7,3},{8,12},{12,8},{9,1... | collective-permute-start | bytes 1572872 | tf_op jit(solution)/shard_map/ppermute | solution.py:43
  682.8 23.9 %collective-permute-start.41 = (bf16[256,2048]{1,0:T(8,128)(2,1)S(1)}, bf16[256,2048]{1,0:T(8,128)(2,1)S(1)}, u32[]{:S(2)}, u32[]{:S(2)}) collective-permute-start(bf16[256,2048]{1,0:T(8,128)(2,1)S(1)} %get-tuple-element.64), channel_id=1, source_target_pairs={{0,2},{2,0},{1,3},{3,1},{4,6},{6,4},{5,7},{7,5},{8,10},{10,8},{9,1... | collective-permute-start | bytes 3145736 | tf_op jit(solution)/shard_map/ppermute | solution.py:43
  683.6 23.5 %collective-permute-start.42 = (bf16[256,2048]{1,0:T(8,128)(2,1)S(1)}, bf16[256,2048]{1,0:T(8,128)(2,1)S(1)}, u32[]{:S(2)}, u32[]{:S(2)}) collective-permute-start(bf16[256,2048]{1,0:T(8,128)(2,1)S(1)} %get-tuple-element.64), channel_id=1, source_target_pairs={{0,4},{4,0},{1,5},{5,1},{2,6},{6,2},{3,7},{7,3},{8,12},{12,8},{9,1... | collective-permute-start | bytes 3145736 | tf_op jit(solution)/shard_map/ppermute | solution.py:43
  708.9 25.1 %collective-permute-start.45 = (bf16[768,2048]{1,0:T(8,128)(2,1)}, bf16[768,2048]{1,0:T(8,128)(2,1)}, u32[]{:S(2)}, u32[]{:S(2)}) collective-permute-start(bf16[768,2048]{1,0:T(8,128)(2,1)} %pad_maximum_fusion.3), channel_id=1, source_target_pairs={{0,1},{1,0},{2,3},{3,2},{4,5},{5,4},{6,7},{7,6},{8,9},{9,8},{10,11... | collective-permute-start | bytes 9437192 | tf_op jit(solution)/shard_map/ppermute | solution.py:43
  709.7 14.7 %collective-permute-start.43 = (bf16[128,2048]{1,0:T(8,128)(2,1)}, bf16[128,2048]{1,0:T(8,128)(2,1)}, u32[]{:S(2)}, u32[]{:S(2)}) collective-permute-start(bf16[128,2048]{1,0:T(8,128)(2,1)} %slice.321), channel_id=1, source_target_pairs={{0,4},{4,0},{1,5},{5,1},{2,6},{6,2},{3,7},{7,3},{8,12},{12,8},{9,1... | collective-permute-start | bytes 1572872 | tf_op jit(solution)/shard_map/ppermute | solution.py:43
  712.0 14.4 %collective-permute-start.44 = (bf16[128,2048]{1,0:T(8,128)(2,1)}, bf16[128,2048]{1,0:T(8,128)(2,1)}, u32[]{:S(2)}, u32[]{:S(2)}) collective-permute-start(bf16[128,2048]{1,0:T(8,128)(2,1)} %slice.322), channel_id=1, source_target_pairs={{0,2},{2,0},{1,3},{3,1},{4,6},{6,4},{5,7},{7,5},{8,10},{10,8},{9,1... | collective-permute-start | bytes 1572872 | tf_op jit(solution)/shard_map/ppermute | solution.py:43
  713.5 201.2 %reduce-scatter.12.cloned.1.call-start = ((), (), s32[]{:S(2)}) async-start(), calls=%async_computation.19 | async-start | bytes 1310720 | tf_op jit(solution)/shard_map/reduce_scatter | solution.py:111
  833.7 18.3 %collective-permute-start.50 = (bf16[1024,2048]{1,0:T(8,128)(2,1)}, bf16[1024,2048]{1,0:T(8,128)(2,1)}, u32[]{:S(2)}, u32[]{:S(2)}) collective-permute-start(bf16[1024,2048]{1,0:T(8,128)(2,1)} %slice.324), channel_id=1, source_target_pairs={{0,1},{1,0},{2,3},{3,2},{4,5},{5,4},{6,7},{7,6},{8,9},{9,8},{10,11... | collective-permute-start | bytes 12582920 | tf_op jit(solution)/shard_map/ppermute | solution.py:43
  841.8 85.7 %reduce-scatter.10.cloned.1.call-start = ((), (), s32[]{:S(2)}) async-start(), calls=%async_computation.18 | async-start | bytes 3932160 | tf_op jit(solution)/shard_map/reduce_scatter | solution.py:111
  847.9 18.9 %all-to-all-start.5 = ((bf16[8,64,1024]{2,1,0:T(8,128)(2,1)}), bf16[8,64,1024]{2,1,0:T(8,128)(2,1)S(1)}, u32[]{:S(2)}, u32[]{:S(2)}) async-start(bf16[8,64,1024]{2,1,0:T(8,128)(2,1)} %bitcast.100), calls=%async_computation.9 | async-start | bytes 2097152 | tf_op jit(solution)/shard_map/all_to_all | solution.py:378
  851.5 24.6 %collective-permute-start.57 = (f32[4,4,64]{2,1,0:T(4,128)S(1)}, f32[4,4,64]{2,1,0:T(4,128)S(1)}, u32[]{:S(2)}, u32[]{:S(2)}) collective-permute-start(f32[4,4,64]{2,1,0:T(4,128)S(1)} %slice_select_fusion.3), channel_id=1, source_target_pairs={{0,1},{1,0},{2,3},{3,2},{4,5},{5,4},{6,7},{7,6},{8,9},{9,8},{10,11... | collective-permute-start | bytes 12296 | tf_op jit(solution)/shard_map/ppermute | solution.py:98
  866.8 19.4 %all-to-all-start.6 = ((bf16[8,64,1024]{2,1,0:T(8,128)(2,1)}), bf16[8,64,1024]{2,1,0:T(8,128)(2,1)S(1)}, u32[]{:S(2)}, u32[]{:S(2)}) async-start(bf16[8,64,1024]{2,1,0:T(8,128)(2,1)} %bitcast.309), calls=%async_computation.11 | async-start | bytes 2097152 | tf_op jit(solution)/shard_map/all_to_all | solution.py:378
  872.8 34.7 %collective-permute-start.51 = (bf16[2,128,2048]{2,1,0:T(8,128)(2,1)}, bf16[2,128,2048]{2,1,0:T(8,128)(2,1)}, u32[]{:S(2)}, u32[]{:S(2)}) collective-permute-start(bf16[2,128,2048]{2,1,0:T(8,128)(2,1)} %slice_bitcast_fusion.4), channel_id=1, source_target_pairs={{0,2},{2,0},{1,3},{3,1},{4,6},{6,4},{5,7},{7,5},{8,10},{10,8},{9,1... | collective-permute-start | bytes 3145736 | tf_op jit(solution)/shard_map/ppermute | solution.py:43
  874.7 32.7 %collective-permute-start.53 = (bf16[2,128,2048]{2,1,0:T(8,128)(2,1)}, bf16[2,128,2048]{2,1,0:T(8,128)(2,1)}, u32[]{:S(2)}, u32[]{:S(2)}) collective-permute-start(bf16[2,128,2048]{2,1,0:T(8,128)(2,1)} %slice_bitcast_fusion.1), channel_id=1, source_target_pairs={{0,4},{4,0},{1,5},{5,1},{2,6},{6,2},{3,7},{7,3},{8,12},{12,8},{9,1... | collective-permute-start | bytes 3145736 | tf_op jit(solution)/shard_map/ppermute | solution.py:43
  912.9 19.0 %collective-permute-start.52 = (bf16[128,2048]{1,0:T(8,128)(2,1)}, bf16[128,2048]{1,0:T(8,128)(2,1)}, u32[]{:S(2)}, u32[]{:S(2)}) collective-permute-start(bf16[128,2048]{1,0:T(8,128)(2,1)} %fusion.29), channel_id=1, source_target_pairs={{0,4},{4,0},{1,5},{5,1},{2,6},{6,2},{3,7},{7,3},{8,12},{12,8},{9,1... | collective-permute-start | bytes 1572872 | tf_op jit(solution)/shard_map/ppermute | solution.py:43
  927.5 16.8 %all-to-all-start.3 = ((bf16[8,64,768]{2,1,0:T(8,128)(2,1)}), bf16[8,64,768]{2,1,0:T(8,128)(2,1)}, u32[]{:S(2)}, u32[]{:S(2)}) async-start(bf16[8,64,768]{2,1,0:T(8,128)(2,1)} %bitcast.314), calls=%async_computation.6 | async-start | bytes 1572864 | tf_op jit(solution)/shard_map/all_to_all | solution.py:378
  (93 other events, 943.6 us)
Sparse Core Ops, SparseCore 0:
  33.9 61.8 all-gather.4
  98.0 26.5 all-gather.6
  202.6 149.0 all-gather.8
  353.7 78.9 all-gather.10
  559.1 74.2 reduce-scatter.5
  643.4 74.9 reduce-scatter.7
  720.7 77.2 reduce-scatter.13
  841.9 24.1 reduce-scatter.11
  868.4 59.0 reduce-scatter.9

commit v3 on v2

--- a/solution.py
+++ b/solution.py
@@ -39,6 +39,13 @@
     return lax.optimization_barrier((value,) + others)[0]
 
 
+def region(function, ids, *operands):
+    def nothing(*operands):
+        return jax.tree.map(lambda leaf: jnp.zeros(leaf.shape, leaf.dtype), jax.eval_shape(function, *operands))
+
+    return lax.cond(ids[0] == 0, function, nothing, *operands)
+
+
 def swap(block, axis):
     return lax.ppermute(block, axis, [(0, 1), (1, 0)])
 
@@ -61,19 +68,25 @@
     return total.reshape(terms.shape)
 
 
-def group_scatter(parts, rows):
+def scatter_start(parts, rows, *others):
     width = parts.shape[1]
     half = rows // 2
     arrived = swap(parts[4 * rows :], "c")
     mine = parts[: 4 * rows].astype(F32) + arrived.astype(F32)
     mine = mine.astype(BF16).reshape(2, 2, 2, half, width)
-    got_x = swap(mine[:, 1, 0], "x")
-    got_y = swap(mine[1, :, 1], "y")
-    top = mine[:, 0, 0].astype(F32) + got_x.astype(F32)
-    bottom = mine[0, :, 1].astype(F32) + got_y.astype(F32)
+    got_x = after(swap(mine[:, 1, 0], "x"), *others)
+    got_y = after(swap(mine[1, :, 1], "y"), *others)
+    return mine[:, 0, 0].astype(F32) + got_x.astype(F32), mine[0, :, 1].astype(F32) + got_y.astype(F32)
+
+
+def scatter_end(top, bottom):
     top_last = swap(top[1].astype(BF16), "y")
     bottom_last = swap(bottom[1].astype(BF16), "x")
     return jnp.concatenate([top[0] + top_last.astype(F32), bottom[0] + bottom_last.astype(F32)], 0)
+
+
+def group_scatter(parts, rows):
+    return scatter_end(*scatter_start(parts, rows))
 
 
 def doubled(own, axes):
@@ -113,7 +126,7 @@
 
 SCALE = HEAD ** (-0.5)
 ROWS = 256
-PARAMS = pltpu.CompilerParams(vmem_limit_bytes=48 * 2**20)
+PARAMS = pltpu.CompilerParams(vmem_limit_bytes=56 * 2**20)
 
 
 def flat_rows(ref):
@@ -163,8 +176,8 @@
         inner = jnp.sum(softmax * softmax_grad, -1, keepdims=True)
         score_grad = (softmax * (softmax_grad - inner)).astype(BF16)
         dq_all[part] = matmul(score_grad, key) * SCALE
-        dk_term = inner_t(score_grad, query[part])
-        dv_term = inner_t(softmax.astype(BF16), grad[part])
+        dk_term = inner_t(query[part], score_grad)
+        dv_term = inner_t(grad[part], softmax.astype(BF16))
         if start:
             dk_sum[...] += dk_term
             dv_sum[...] += dv_term
@@ -172,10 +185,10 @@
             dk_sum[...] = dk_term
             dv_sum[...] = dv_term
     dq = turn(dq_all[...], cosine, -sine)
-    dk = turn(dk_sum[...] * SCALE, cosine, -sine)
+    dk = turn(dk_sum[...].T * SCALE, cosine, -sine)
     dq_ref[...] = dq.reshape(dq_ref.shape)
     dk_ref[...] = dk.reshape(dk_ref.shape)
-    dv_ref[...] = dv_sum[...].astype(BF16).reshape(dv_ref.shape)
+    dv_ref[...] = dv_sum[...].T.astype(BF16).reshape(dv_ref.shape)
     mean_q = jnp.sum(dq * gq_ref[...] * query_in, -1, keepdims=True)
     mean_k = jnp.sum(dk * gk_ref[...] * key_in, -1, keepdims=True)
     mean_ref[...] = jnp.concatenate([mean_q, mean_k], 1).reshape(mean_ref.shape)
@@ -226,22 +239,125 @@
 
 def from_units(parts, unit_rows):
     _, rows, units = parts.shape
-
-    def kernel(p_ref, out_ref):
-        for m in range(8):
-            for r in range(units // unit_rows):
-                target, source = (r * 8 + m) * unit_rows, r * unit_rows
-                out_ref[:, target : target + unit_rows] = p_ref[m, :, source : source + unit_rows].astype(F32)
+    units //= 2
+
+    def kernel(p_ref, *out_refs):
+        for i, out_ref in enumerate(out_refs):
+            for m in range(8):
+                for r in range(units // unit_rows):
+                    target, source = (r * 8 + m) * unit_rows, i * units + r * unit_rows
+                    out_ref[:, target : target + unit_rows] = p_ref[m, :, source : source + unit_rows].astype(F32)
 
     step = min(rows, 16)
     return pl.pallas_call(
         kernel,
         grid=(rows // step,),
-        in_specs=[pl.BlockSpec((8, step, units), lambda i: (0, i, 0))],
-        out_specs=pl.BlockSpec((step, 8 * units), lambda i: (i, 0)),
-        out_shape=jax.ShapeDtypeStruct((rows, 8 * units), F32),
+        in_specs=[pl.BlockSpec((8, step, 2 * units), lambda i: (0, i, 0))],
+        out_specs=[pl.BlockSpec((step, 8 * units), lambda i: (i, 0))] * 2,
+        out_shape=[jax.ShapeDtypeStruct((rows, 8 * units), F32)] * 2,
         compiler_params=PARAMS,
     )(parts)
+
+
+def from_heads(parts, members):
+    _, rows, columns = parts.shape
+    columns //= 3
+
+    def kernel(p_ref, *out_refs):
+        for i, out_ref in enumerate(out_refs):
+            for m, targets in enumerate(members):
+                for j, head in enumerate(targets):
+                    source = i * columns + j * HEAD
+                    out_ref[:, head * HEAD : (head + 1) * HEAD] = p_ref[m, :, source : source + HEAD].astype(F32)
+
+    step = min(rows, 16)
+    return pl.pallas_call(
+        kernel,
+        grid=(rows // step,),
+        in_specs=[pl.BlockSpec((8, step, 3 * columns), lambda i: (0, i, 0))],
+        out_specs=[pl.BlockSpec((step, 8 * columns), lambda i: (i, 0))] * 3,
+        out_shape=[jax.ShapeDtypeStruct((rows, 8 * columns), F32)] * 3,
+        compiler_params=PARAMS,
+    )(parts)
+
+
+def whole(array):
+    return pl.BlockSpec(array.shape, lambda i: (0, 0), pipeline_mode=pl.Buffered(1))
+
+
+def by_rows(step, width):
+    return pl.BlockSpec((step, width), lambda i: (i, 0))
+
+
+def gate_up(values, weight):
+    rows, depth = values.shape
+    units = weight.shape[1] // 2
+
+    def kernel(v_ref, w_ref, both_ref, hidden_ref):
+        for c in range(0, units, 512):
+            gate = matmul(v_ref[...], w_ref[:, c : c + 512])
+            up = matmul(v_ref[...], w_ref[:, units + c : units + c + 512])
+            both_ref[:, c : c + 512] = gate
+            both_ref[:, units + c : units + c + 512] = up
+            hidden_ref[:, c : c + 512] = (gate / (1.0 + jnp.exp(-gate)) * up).astype(BF16)
+
+    return pl.pallas_call(
+        kernel,
+        grid=(rows // ROWS,),
+        in_specs=[by_rows(ROWS, depth), whole(weight)],
+        out_specs=[by_rows(ROWS, 2 * units), by_rows(ROWS, units)],
+        out_shape=[jax.ShapeDtypeStruct((rows, 2 * units), F32), jax.ShapeDtypeStruct((rows, units), BF16)],
+        compiler_params=PARAMS,
+        cost_estimate=pl.CostEstimate(
+            flops=4 * rows * depth * units, bytes_accessed=14 * rows * units, transcendentals=rows * units
+        ),
+    )(values, weight)
+
+
+def gate_up_back(grad, weight, both):
+    rows, depth = grad.shape
+    units = weight.shape[0]
+
+    def kernel(g_ref, w_ref, both_ref, out_ref):
+        for c in range(0, units, 512):
+            hidden_grad = matmul_t(g_ref[...], w_ref[c : c + 512, :])
+            gate, up = both_ref[:, c : c + 512], both_ref[:, units + c : units + c + 512]
+            sig = 1.0 / (1.0 + jnp.exp(-gate))
+            out_ref[:, c : c + 512] = (hidden_grad * up * sig * (1.0 + gate * (1.0 - sig))).astype(BF16)
+            out_ref[:, units + c : units + c + 512] = (hidden_grad * (gate * sig)).astype(BF16)
+
+    return pl.pallas_call(
+        kernel,
+        grid=(rows // ROWS,),
+        in_specs=[by_rows(ROWS, depth), whole(weight), by_rows(ROWS, 2 * units)],
+        out_specs=by_rows(ROWS, 2 * units),
+        out_shape=jax.ShapeDtypeStruct((rows, 2 * units), BF16),
+        compiler_params=PARAMS,
+        cost_estimate=pl.CostEstimate(
+            flops=2 * rows * depth * units, bytes_accessed=16 * rows * units, transcendentals=rows * units
+        ),
+    )(grad, weight, both)
+
+
+def times_transposed(values, weight):
+    rows, depth = values.shape
+    width = weight.shape[0]
+
+    def kernel(v_ref, w_ref, out_ref):
+        for c in range(0, width, 512):
+            out_ref[:, c : c + 512] = matmul_t(v_ref[...], w_ref[c : c + 512, :]).astype(BF16)
+
+    return pl.pallas_call(
+        kernel,
+        grid=(rows // ROWS,),
+        in_specs=[by_rows(ROWS, depth), whole(weight)],
+        out_specs=by_rows(ROWS, width),
+        out_shape=jax.ShapeDtypeStruct((rows, width), BF16),
+        compiler_params=PARAMS,
+        cost_estimate=pl.CostEstimate(
+            flops=2 * rows * depth * width, bytes_accessed=2 * rows * (depth + width), transcendentals=0
+        ),
+    )(values, weight)
 
 
 def head_specs(heads):
@@ -303,7 +419,7 @@
             jax.ShapeDtypeStruct(shape, BF16),
             jax.ShapeDtypeStruct((heads,) + shape[:3] + (2,), F32),
         ],
-        scratch_shapes=[pltpu.VMEM((SEQ_MAX, HEAD), F32)] * 3,
+        scratch_shapes=[pltpu.VMEM((HEAD, SEQ_MAX), F32)] * 2 + [pltpu.VMEM((SEQ_MAX, HEAD), F32)],
         compiler_params=PARAMS,
         cost_estimate=pl.CostEstimate(
             flops=10 * rows * SEQ_MAX * columns, bytes_accessed=12 * rows * columns * 2, transcendentals=rows * SEQ_MAX * heads
@@ -385,12 +501,12 @@
         qkv_parts = jnp.concatenate([by_head(w_query), by_head(w_key), by_head(w_value)], 2)
         qkv_piece = exchange(qkv_parts, GROUP).reshape(8 * weight_rows, 3 * columns)
         out_halves = gather_planes(after(w_out.astype(BF16), plane_gains))
-        feed_parts = after(to_units(w_gate, w_up, unit_rows), qkv_piece)
+        feed_parts = after(to_units(w_gate, w_up, unit_rows), qkv_piece, out_halves)
         feed_piece = exchange(feed_parts, GROUP).reshape(8 * weight_rows, 2 * units)
-        group_tokens = group_gather(after(tokens, qkv_piece))
+        group_tokens = group_gather(after(tokens, feed_piece))
         weight_qkv = gather_planes(after(qkv_piece, plane_gains))
         weight_feed = gather_planes(feed_piece)
-        weight_down = gather_planes(after(w_down.astype(BF16), weight_qkv))
+        weight_down = gather_planes(after(w_down.astype(BF16), feed_piece))
         out_halves = out_halves.reshape(per_head, own_heads, weight_rows, width)
         out_heads = lax.all_to_all(out_halves, head_axes, 0, 0, tiled=True)
         weight_out = out_heads.transpose(1, 0, 2, 3).reshape(columns, width)
@@ -431,21 +547,22 @@
         cosine = jnp.concatenate([jnp.cos(angles), jnp.cos(angles)], 1)
         sine = jnp.concatenate([-jnp.sin(angles), jnp.sin(angles)], 1)
 
-        projected = matmul(after(group_tokens, feed_piece), weight_qkv)
-        squares = jnp.sum(jnp.square(projected[:, : 2 * columns]).reshape(group_rows, 2, columns), -1)
-        inverse = lax.rsqrt(group_sum(squares.T) / width + NORM_EPS)
+        projected = matmul(group_tokens, weight_qkv)
+        squares = [jnp.sum(jnp.square(projected[:, i * columns : (i + 1) * columns]), -1) for i in (0, 1)]
+        inverse = lax.rsqrt(group_sum(jnp.stack(squares)) / width + NORM_EPS)
         inverse = after(inverse, weight_out)
         info = jnp.stack([first_seen, end_seen, inverse[0], inverse[1]], 1)
         attention = (projected, info, cosine, sine, gain_q, gain_k, place)
-        mixed_low = attend(*attention)
-        branch = group_scatter(matmul(mixed_low, weight_out).astype(BF16), rows)
+
+        def mix(attention, weight_out):
+            mixed_low = attend(*attention)
+            branch = group_scatter(matmul(mixed_low, weight_out).astype(BF16), rows)
+            hidden_in = tokens.astype(F32) + branch * inverse_rms(branch) * gain_a
+            return mixed_low, branch, hidden_in, group_gather(hidden_in.astype(BF16))
+
+        mixed_low, branch, hidden_in, group_hidden_in = region(mix, segment_ids, attention, weight_out)
         r_a = inverse_rms(branch)
-        hidden_in = tokens.astype(F32) + branch * r_a * gain_a
-        group_hidden_in = group_gather(hidden_in.astype(BF16))
-        gate = matmul(group_hidden_in, weight_feed[:, :units])
-        up = matmul(group_hidden_in, weight_feed[:, units:])
-        sig = 1.0 / (1.0 + jnp.exp(-gate))
-        hidden = (gate * sig * up).astype(BF16)
+        both, hidden = gate_up(group_hidden_in, weight_feed)
         result = group_scatter(matmul(hidden, weight_down).astype(BF16), rows)
         r_m = inverse_rms(result)
         out_tokens = (hidden_in + result * r_m * gain_f).astype(BF16)
@@ -460,42 +577,48 @@
         group_result_grad = group_gather(result_grad.astype(BF16))
 
         down_term = inner_t(hidden, group_result_grad).astype(BF16)
-        hidden_grad = matmul_t(after(group_result_grad, down_term), weight_down)
-        gate_grad = (hidden_grad * up * sig * (1.0 + gate * (1.0 - sig))).astype(BF16)
-        up_grad = (hidden_grad * gate * sig).astype(BF16)
-        hidden_in_parts = (
-            matmul_t(gate_grad, weight_feed[:, :units]) + matmul_t(up_grad, weight_feed[:, units:])
-        ).astype(BF16)
-        gate_term = inner_t(after(group_hidden_in, hidden_in_parts), gate_grad).astype(BF16)
-        up_term = inner_t(after(group_hidden_in, gate_term), up_grad).astype(BF16)
+        feed_grad = gate_up_back(after(group_result_grad, down_term), weight_down, both)
+        hidden_in_parts = times_transposed(feed_grad, weight_feed)
+        feed_term = inner_t(group_hidden_in, after(feed_grad, hidden_in_parts)).astype(BF16)
         down_share = scatter_planes(down_term)
-        gate_share = scatter_planes(gate_term)
-        up_share = scatter_planes(up_term)
-        hidden_in_grad = grad_out + group_scatter(hidden_in_parts, rows)
-        hidden_in_grad = after(hidden_in_grad, up_term)
-        branch_grad, mixer_gain_term = norm_back(branch, r_a, gain_a, hidden_in_grad)
-        group_branch_grad = group_gather(branch_grad.astype(BF16))
+        top, bottom = scatter_start(hidden_in_parts, rows, feed_term)
+        feed_share = scatter_planes(feed_term)
+
+        def to_mixer(top, bottom, branch, r_a):
+            hidden_in_grad = grad_out + scatter_end(top, bottom)
+            branch_grad, mixer_gain_term = norm_back(branch, r_a, gain_a, hidden_in_grad)
+            return hidden_in_grad, mixer_gain_term, group_gather(branch_grad.astype(BF16))
+
+        hidden_in_grad, mixer_gain_term, group_branch_grad = region(to_mixer, segment_ids, top, bottom, branch, r_a)
         group_branch_grad = after(group_branch_grad, down_share)
         mixed_grad = matmul_t(group_branch_grad, weight_out).astype(BF16)
         q_back, k_back, v_grad, means = attend_back(*attention, mixed_grad)
-        out_term = inner_t(mixed_low, after(group_branch_grad, mixed_grad))
-        means = after(means, gate_share, out_term)
         means = group_sum(means.T).T / width
         grads, head_terms = qkv_grads(projected, q_back, k_back, v_grad, info, means, gain_q, gain_k)
+        feed_back = exchange(after(feed_share, means).reshape(8, weight_rows, 2 * units), GROUP)
+        grads = after(grads, feed_back)
         qkv_term = inner_t(group_tokens, grads).astype(BF16)
-        grads = after(grads, qkv_term)
-        g_tokens = hidden_in_grad + group_scatter(matmul_t(grads, weight_qkv).astype(BF16), rows)
-
         qkv_share = scatter_planes(qkv_term)
-        qkv_back = exchange(qkv_share.reshape(8, weight_rows, 3 * columns), GROUP)
-        qkv_back = qkv_back.reshape(head_shape_put[:2] + (weight_rows, 3, own_heads, HEAD))
-        g_qkv = qkv_back.transpose(3, 2, 1, 4, 0, 5).reshape(3, weight_rows, width).astype(F32)
+        out_term = inner_t(mixed_low, after(group_branch_grad, qkv_term))
         out_parts = out_term.astype(BF16).reshape(own_heads, per_head, weight_rows, width)
         out_parts = lax.all_to_all(out_parts.transpose(1, 0, 2, 3), head_axes, 0, 0, tiled=True)
-        g_w_out = scatter_planes(out_parts.reshape(replicas * weight_rows, width)).astype(F32)
+        out_share = scatter_planes(out_parts.reshape(replicas * weight_rows, width))
+
+        def to_tokens(grads, weight_qkv, hidden_in_grad):
+            return hidden_in_grad + group_scatter(matmul_t(grads, weight_qkv).astype(BF16), rows)
+
+        g_tokens = region(to_tokens, segment_ids, after(grads, out_parts), weight_qkv, hidden_in_grad)
+
+        qkv_back = exchange(after(qkv_share, g_tokens).reshape(8, weight_rows, 3 * columns), GROUP)
+        heads_of = [
+            [(e * own_heads + j) * (8 // per_head) + t for j in range(own_heads)]
+            for t in range(8 // per_head)
+            for e in range(per_head)
+        ]
+        g_qkv = from_heads(qkv_back, heads_of)
+        g_w_out = out_share.astype(F32)
         g_w_down = down_share.astype(F32)
-        g_w_gate = from_units(exchange(gate_share.reshape(8, weight_rows, units), GROUP), unit_rows)
-        g_w_up = from_units(exchange(up_share.reshape(8, weight_rows, units), GROUP), unit_rows)
+        g_w_gate, g_w_up = from_units(feed_back, unit_rows)
 
         head_terms = head_terms.reshape(2, 1, columns)
         spread = jnp.zeros((2, 8, columns), F32)

time: 966 us -> 867 us (0.90)
  matrix products: 179 us -> 93.8 us
  Pallas kernels: 64.5 us -> 132 us
  waiting for transfers between devices: 396 us -> 341 us
  blocking collectives: 13.9 us -> 57.2 us
  local copies, waits for them, and re-layouts: 118 us -> 78 us
  starting transfers between devices: 73 us -> 56.4 us
  other arithmetic: 97.4 us -> 83.5 us
    pallas_call x0 -> x4, Pallas kernels: none -> 71.3 us  [the longest x1 24.5 us: gate_up(): pl.pallas_call(kernel, grid=(rows // ROWS,), in_specs=[by_rows(ROWS, dept...]
    all_gather x4, waiting for transfers between devices: 84.7 us -> 17 us  [gather_planes(): return lax.all_gather(part, PLANES, axis=0, tiled=True)]
    dot_general x5 -> x2, matrix products: 69.8 us -> 16.1 us  [matmul_t(): lax.dot_general(left, right, (((1,), (1,)), ((), ())), preferred_element_...]
    all_to_all x0 -> x2, blocking collectives: none -> 47.2 us  [exchange(): return lax.all_to_all(parts, group, 0, 0, tiled=True)]
    unnamed x168 -> x92, local copies, waits for them, and re-layouts: 59.9 us -> 29.7 us
    dot_general x5 -> x3, matrix products: 53.7 us -> 24.3 us  [matmul(): return jnp.dot(left, right, preferred_element_type=F32)]
    ppermute x50, waiting for transfers between devices: 271 us -> 297 us  [swap(): return lax.ppermute(block, axis, [(0, 1), (1, 0)])]
    cond x0 -> x30, local copies, waits for them, and re-layouts: none -> 15.7 us
  transfers between devices with their start and end apart: 74 -> 70, of which waited for: 48 -> 50; matrix products, arithmetic and copies ran while one was open for 34% -> 23% of each run, Pallas kernels for 5% -> 15%
where the time goes in v3:
time: 867 us; the launch traced here: 859 us
  waiting for transfers between devices  341 us (39%)
  Pallas kernels  132 us (15%)
  matrix products  93.8 us (11%)
  other arithmetic  83.5 us (10%)
  local copies, waits for them, and re-layouts  78 us (9%)
  blocking collectives  57.2 us (7%)
  starting transfers between devices  56.4 us (7%)
  between operations  16.1 us (2%)
    ppermute x50, waiting for transfers between devices, swap(): return lax.ppermute(block, axis, [(0, 1), (1, 0)])  297 us
    dot_general x4, matrix products, inner_t(): lax.dot_general(left, right, (((0,), (0,)), ((), ())), preferred_element_...  53.3 us
    all_to_all x2, blocking collectives, exchange(): return lax.all_to_all(parts, group, 0, 0, tiled=True)  47.2 us
    ppermute x50, starting transfers between devices, swap(): return lax.ppermute(block, axis, [(0, 1), (1, 0)])  37.9 us
    unnamed x92, local copies, waits for them, and re-layouts  29.7 us
    pallas_call x1, Pallas kernels, attend_back(): pl.pallas_call(attend_back_kernel, grid=(blocks, heads), in_specs=specs +...  28.2 us
    pallas_call x1, Pallas kernels, gate_up(): pl.pallas_call(kernel, grid=(rows // ROWS,), in_specs=[by_rows(ROWS, dept...  24.5 us
    dot_general x3, matrix products, matmul(): return jnp.dot(left, right, preferred_element_type=F32)  24.3 us
  transfers between devices with their start and end apart: 70, of which 50 were waited for; matrix products, arithmetic and copies ran while one was open for 23% of the time, Pallas kernels for 15%

profile of v3, /device:TPU:0, one launch (start us, length us, event | category | flops | bytes accessed | tf_op | source)
XLA Modules:
  0.0 859.5 jit_solution(16420001375633180499)
XLA Ops:
  22.2 16.3 %all_to_all.30 = bf16[8,64,768]{2,1,0:T(8,128)(2,1)} all-to-all(bf16[8,64,768]{2,1,0:T(8,128)(2,1)S(1)} %pad_maximum_fusion.15), channel_id=1, replica_groups=mesh['zh'=2,'zl'=2,'y'=2,'x'=2,'c'=2] {'y','x','c'}, dimensions={0} | all-to-all | bytes 1572864 | tf_op jit(solution)/shard_map/all_to_all | solution.py:494
  38.6 4.2 shard_map.246
  42.8 4.9 all-gather.5.cloned.1.call-done
  47.7 30.9 %all_to_all.31 = bf16[8,64,2048]{2,1,0:T(8,128)(2,1)} all-to-all(bf16[8,64,2048]{2,1,0:T(8,128)(2,1)} %shard_map.246), channel_id=1, replica_groups=mesh['zh'=2,'zl'=2,'y'=2,'x'=2,'c'=2] {'y','x','c'}, dimensions={0} | all-to-all | bytes 4194304 | tf_op jit(solution)/shard_map/all_to_all | solution.py:494
  96.3 18.5 %collective-permute-done.26 = bf16[256,2048]{1,0:T(8,128)(2,1)S(1)} collective-permute-done((bf16[256,2048]{1,0:T(8,128)(2,1)S(1)}, bf16[256,2048]{1,0:T(8,128)(2,1)S(1)}, u32[]{:S(2)}, u32[]{:S(2)}) %collective-permute-start.26) | collective-permute-done | bytes 1048608 | tf_op jit(solution)/shard_map/ppermute | solution.py:50
  117.7 5.5 fusion.19
  140.0 4.0 collective-permute-done.28
  158.4 10.0 %fusion.25.p_ref = f32[2048,768]{1,0:T(8,128)S(1)} fusion(bf16[2048,2048]{1,0:T(8,128)(2,1)} %constant_dynamic-update-slice_fusion.14, bf16[2048,768]{1,0:T(8,128)(2,1)} %all-gather.7.cloned.1.call-done), kind=kOutput, calls=%fused_computation.240 | convolution fusion | flops 6442450944 | bytes 17825792 | tf_op jit(solution)/shard_map/dot_general | solution.py:23
  178.4 4.6 all_to_all.32
  185.5 121.1 %conditional.3 = (bf16[2048,256]{1,0:T(8,128)(2,1)S(1)}, f32[256,2048]{1,0:T(8,128)S(1)}, f32[256,2048]{1,0:T(8,128)}, bf16[2048,2048]{1,0:T(8,128)(2,1)}, f32[256,1]{0,1:T(1,128)S(1)}) conditional(s32[]{:T(128)} %bitcast.34, () %tuple.50, (f32[2048,768]{1,0:T(8,128)}, f32[2048,4]{0,1:T(4,128)S(1)}, f32[2048,128]{1,0:T(8,128)}, ...), branch_computations={%region_4.5_spmd, %region_5.7_spmd} | conditional | flops 4327473664 | bytes 193024704 | solution.py:46
  187.4 16.9 %branch_1_fun.1 = bf16[2,2,512,256]{3,2,1,0:T(8,128)(2,1)S(1)} custom-call(f32[2,2,512,768]{3,2,1,0:T(8,128)} %bitcast.269, f32[2,2,512,768]{3,2,1,0:T(8,128)} %bitcast.270, f32[2,2,512,768]{3,2,1,0:T(8,128)} %bitcast.271, f32[2,2,512,4]{3,2,1,0:T(8,128)} %bitcast.291, f32[2,2,512,128]{3,2,1,0:T(8,128)} %bitcast.288, f32[2,2,512,128]{3,2,1,0:T(8,128)} %bitcast.287, ...), custom_call_target="tpu_custom_call" | custom-call | flops 2147483648 | bytes 8388608 | tf_op jit(solution)/shard_map/cond/branch_1_fun/pallas_call | solution.py:390
  207.2 7.0 collective-permute-done
  218.2 23.8 %collective-permute-done.1 = bf16[2,128,2048]{2,1,0:T(8,128)(2,1)S(1)} collective-permute-done((bf16[2,128,2048]{2,1,0:T(8,128)(2,1)S(1)}, bf16[2,128,2048]{2,1,0:T(8,128)(2,1)S(1)}, u32[]{:S(2)}, u32[]{:S(2)}) %collective-permute-start.1) | collective-permute-done | bytes 1048608 | tf_op jit(solution)/shard_map/cond/branch_1_fun/ppermute | solution.py:50
  245.3 11.0 %collective-permute-done.4 = bf16[128,2048]{1,0:T(8,128)(2,1)S(1)} collective-permute-done((bf16[128,2048]{1,0:T(8,128)(2,1)S(1)}, bf16[128,2048]{1,0:T(8,128)(2,1)S(1)}, u32[]{:S(2)}, u32[]{:S(2)}) %collective-permute-start.4) | collective-permute-done | bytes 524320 | tf_op jit(solution)/shard_map/cond/branch_1_fun/ppermute | solution.py:50
  261.6 21.8 %collective-permute-done.5 = bf16[256,2048]{1,0:T(8,128)(2,1)S(1)} collective-permute-done((bf16[256,2048]{1,0:T(8,128)(2,1)S(1)}, bf16[256,2048]{1,0:T(8,128)(2,1)S(1)}, u32[]{:S(2)}, u32[]{:S(2)}) %collective-permute-start.5) | collective-permute-done | bytes 1048608 | tf_op jit(solution)/shard_map/cond/branch_1_fun/ppermute | solution.py:50
  286.4 12.4 %collective-permute-done.7 = bf16[128,2048]{1,0:T(8,128)(2,1)S(1)} collective-permute-done((bf16[128,2048]{1,0:T(8,128)(2,1)S(1)}, bf16[128,2048]{1,0:T(8,128)(2,1)S(1)}, u32[]{:S(2)}, u32[]{:S(2)}) %collective-permute-start.7) | collective-permute-done | bytes 524320 | tf_op jit(solution)/shard_map/cond/branch_1_fun/ppermute | solution.py:50
  306.6 24.5 %shard_map.247 = (f32[2048,2048]{1,0:T(8,128)}, bf16[2048,1024]{1,0:T(8,128)(2,1)}) custom-call(bf16[2048,2048]{1,0:T(8,128)(2,1)} %get-tuple-element.139.v_ref, bf16[2048,2048]{1,0:T(8,128)(2,1)} %all-gather.9.cloned.1.call-done.w_ref), custom_call_target="tpu_custom_call" | custom-call | flops 17179869184 | bytes 29360128 | tf_op jit(solution)/shard_map/pallas_call | solution.py:304
  331.1 12.1 %all-gather.11.cloned.1.call-done.w_ref = bf16[1024,2048]{1,0:T(8,128)(2,1)} async-done(((bf16[256,2048]{1,0:T(8,128)(2,1)}), bf16[1024,2048]{1,0:T(8,128)(2,1)}) %all-gather.11.cloned.1.call-update) | async-done | bytes 4194320 | tf_op jit(solution)/shard_map/all_gather | solution.py:120
  343.2 11.9 %convolution_convert_fusion.3 = bf16[2048,2048]{1,0:T(8,128)(2,1)S(1)} fusion(bf16[2048,1024]{1,0:T(8,128)(2,1)} %get-tuple-element.140, bf16[1024,2048]{1,0:T(8,128)(2,1)} %all-gather.11.cloned.1.call-done.w_ref), kind=kOutput, calls=%fused_computation.79 | convolution fusion | flops 8594128896 | bytes 16777216 | tf_op jit(solution)/shard_map/dot_general | solution.py:23
  355.5 7.1 collective-permute-done.38
  368.3 22.0 %collective-permute-done.39 = bf16[2,128,2048]{2,1,0:T(8,128)(2,1)S(1)} collective-permute-done((bf16[2,128,2048]{2,1,0:T(8,128)(2,1)S(1)}, bf16[2,128,2048]{2,1,0:T(8,128)(2,1)S(1)}, u32[]{:S(2)}, u32[]{:S(2)}) %collective-permute-start.39) | collective-permute-done | bytes 1048608 | tf_op jit(solution)/shard_map/ppermute | solution.py:50
  396.5 10.2 %collective-permute-done.42 = bf16[128,2048]{1,0:T(8,128)(2,1)} collective-permute-done((bf16[128,2048]{1,0:T(8,128)(2,1)}, bf16[128,2048]{1,0:T(8,128)(2,1)}, u32[]{:S(2)}, u32[]{:S(2)}) %collective-permute-start.42) | collective-permute-done | bytes 524320 | tf_op jit(solution)/shard_map/ppermute | solution.py:50
  417.9 20.5 %collective-permute-done.43 = bf16[256,2048]{1,0:T(8,128)(2,1)S(1)} collective-permute-done((bf16[256,2048]{1,0:T(8,128)(2,1)S(1)}, bf16[256,2048]{1,0:T(8,128)(2,1)S(1)}, u32[]{:S(2)}, u32[]{:S(2)}) %collective-permute-start.43) | collective-permute-done | bytes 1048608 | tf_op jit(solution)/shard_map/ppermute | solution.py:50
  442.7 11.6 %collective-permute-done.45 = bf16[128,2048]{1,0:T(8,128)(2,1)S(1)} collective-permute-done((bf16[128,2048]{1,0:T(8,128)(2,1)S(1)}, bf16[128,2048]{1,0:T(8,128)(2,1)S(1)}, u32[]{:S(2)}, u32[]{:S(2)}) %collective-permute-start.45) | collective-permute-done | bytes 524320 | tf_op jit(solution)/shard_map/ppermute | solution.py:50
  461.8 11.0 %convolution_convert_fusion.4 = bf16[1024,2048]{1,0:T(8,128)(2,1)} fusion(bf16[2048,1024]{1,0:T(8,128)(2,1)S(1)} %copy-done.42, bf16[2048,2048]{1,0:T(8,128)(2,1)S(1)} %constant_dynamic-update-slice_fusion.26.g_ref), kind=kOutput, calls=%fused_computation.80 | convolution fusion | flops 8592031744 | bytes 16777216 | tf_op jit(solution)/shard_map/dot_general | solution.py:31
  472.8 19.6 %shard_map.248.v_ref = bf16[2048,2048]{1,0:T(8,128)(2,1)} custom-call(bf16[2048,2048]{1,0:T(8,128)(2,1)} %copy-done.9, bf16[1024,2048]{1,0:T(8,128)(2,1)} %all-gather.11.cloned.1.call-done.w_ref, f32[2048,2048]{1,0:T(8,128)} %get-tuple-element.143.both_ref), custom_call_target="tpu_custom_call" | custom-call | flops 8589934592 | bytes 33554432 | tf_op jit(solution)/shard_map/pallas_call | solution.py:329
  492.5 23.7 %shard_map.249 = bf16[2048,2048]{1,0:T(8,128)(2,1)} custom-call(bf16[2048,2048]{1,0:T(8,128)(2,1)} %shard_map.248.v_ref, bf16[2048,2048]{1,0:T(8,128)(2,1)} %all-gather.9.cloned.1.call-done.w_ref), custom_call_target="tpu_custom_call" | custom-call | flops 17179869184 | bytes 16777216 | tf_op jit(solution)/shard_map/pallas_call | solution.py:350
  516.2 23.9 %convolution_convert_fusion.2 = bf16[2048,2048]{1,0:T(8,128)(2,1)} fusion(bf16[2048,2048]{1,0:T(8,128)(2,1)} %get-tuple-element.139.v_ref, bf16[2048,2048]{1,0:T(8,128)(2,1)} %shard_map.248.v_ref), kind=kOutput, calls=%fused_computation.78 | convolution fusion | flops 17184063488 | bytes 25165824 | tf_op jit(solution)/shard_map/dot_general | solution.py:31
  542.9 7.1 collective-permute-done.49
  550.0 4.1 add_convert_fusion.2
  573.7 7.0 collective-permute-done.50
  583.3 77.5 %conditional.4 = (f32[256,2048]{1,0:T(8,128)}, bf16[2048,2048]{1,0:T(8,128)(2,1)}, f32[1,4,8,64]{3,2,1,0:T(8,128)S(1)}) conditional(s32[]{:T(128)} %bitcast.34, () %tuple.59, (bf16[2,2,2,128,2048]{4,3,2,1,0:T(8,128)(2,1)S(1)}, bf16[2,128,2048]{2,1,0:T(8,128)(2,1)}, bf16[2,128,2048]{2,1,0:T(8,128)(2,1)}, f32[256,2048]{1,0:T(8,128)}, ...), branch_computations={%region_9.10_spmd, %region_10.13_spmd} | conditional | flops 23067392 | bytes 97569144 | solution.py:46
  588.2 10.0 %collective-permute-done.17 = bf16[128,2048]{1,0:T(8,128)(2,1)S(1)} collective-permute-done((bf16[128,2048]{1,0:T(8,128)(2,1)S(1)}, bf16[128,2048]{1,0:T(8,128)(2,1)S(1)}, u32[]{:S(2)}, u32[]{:S(2)}) %collective-permute-start.17) | collective-permute-done | bytes 524320 | tf_op jit(solution)/shard_map/cond/branch_1_fun/ppermute | solution.py:50
  607.2 21.8 %collective-permute-done.18 = bf16[256,2048]{1,0:T(8,128)(2,1)S(1)} collective-permute-done((bf16[256,2048]{1,0:T(8,128)(2,1)S(1)}, bf16[256,2048]{1,0:T(8,128)(2,1)S(1)}, u32[]{:S(2)}, u32[]{:S(2)}) %collective-permute-start.18) | collective-permute-done | bytes 1048608 | tf_op jit(solution)/shard_map/cond/branch_1_fun/ppermute | solution.py:50
  634.7 12.4 %collective-permute-done.20 = bf16[128,2048]{1,0:T(8,128)(2,1)} collective-permute-done((bf16[128,2048]{1,0:T(8,128)(2,1)}, bf16[128,2048]{1,0:T(8,128)(2,1)}, u32[]{:S(2)}, u32[]{:S(2)}) %collective-permute-start.20) | collective-permute-done | bytes 524320 | tf_op jit(solution)/shard_map/cond/branch_1_fun/ppermute | solution.py:50
  660.8 6.7 convolution_convert_fusion.7
  667.6 28.2 %shard_map.250 = (f32[2,2,512,256]{3,2,1,0:T(8,128)}, f32[2,2,512,256]{3,2,1,0:T(8,128)}, bf16[2,2,512,256]{3,2,1,0:T(8,128)(2,1)}, f32[2,2,2,512,2]{4,3,2,1,0:T(8,128)}) custom-call(f32[2,2,512,768]{3,2,1,0:T(8,128)} %bitcast.266, f32[2,2,512,768]{3,2,1,0:T(8,128)} %bitcast.267, f32[2,2,512,768]{3,2,1,0:T(8,128)} %bitcast.268, ...), custom_call_target="tpu_custom_call" | custom-call | flops 5368709120 | bytes 12582912 | tf_op jit(solution)/shard_map/pallas_call | solution.py:410
  714.0 7.7 shard_map.251
  721.7 17.1 %all-to-all-done.3.p_ref = bf16[8,64,2048]{2,1,0:T(8,128)(2,1)S(1)} async-done(((bf16[8,64,2048]{2,1,0:T(8,128)(2,1)}), bf16[8,64,2048]{2,1,0:T(8,128)(2,1)S(1)}, u32[]{:S(2)}, u32[]{:S(2)}) %all-to-all-start.3) | async-done | bytes 2097184 | tf_op jit(solution)/shard_map/all_to_all | solution.py:494
  738.8 12.1 %convolution_convert_fusion.5 = bf16[2048,768]{1,0:T(8,128)(2,1)} fusion(bf16[2048,2048]{1,0:T(8,128)(2,1)} %constant_dynamic-update-slice_fusion.14, bf16[2048,768]{1,0:T(8,128)(2,1)} %get-tuple-element.160), kind=kOutput, calls=%fused_computation.81 | convolution fusion | flops 6444023808 | bytes 14680064 | tf_op jit(solution)/shard_map/dot_general | solution.py:31
  752.2 6.3 convolution_convert_fusion.6
  758.6 5.4 all_to_all.33
  769.7 62.4 %conditional.5 = (f32[256,2048]{1,0:T(8,128)S(1)}) conditional(s32[]{:T(128)} %bitcast.34, () %tuple.58, (bf16[2048,768]{1,0:T(8,128)(2,1)}, bf16[2048,768]{1,0:T(8,128)(2,1)}, f32[256,2048]{1,0:T(8,128)}) %tuple.70), branch_computations={%region_16.17_spmd, %region_17.18_spmd} | conditional | flops 6460276736 | bytes 91226320 | solution.py:46
  769.8 9.4 %convolution_convert_fusion.1 = bf16[2048,2048]{1,0:T(8,128)(2,1)S(1)} fusion(bf16[2048,768]{1,0:T(8,128)(2,1)} %get-tuple-element.81, bf16[2048,768]{1,0:T(8,128)(2,1)} %get-tuple-element.82), kind=kOutput, calls=%fused_computation.58 | convolution fusion | flops 6446645248 | bytes 14680064 | tf_op jit(solution)/shard_map/cond/branch_1_fun/dot_general | solution.py:27
  779.6 7.1 collective-permute-done.11
  791.2 23.2 %collective-permute-done.12 = bf16[2,128,2048]{2,1,0:T(8,128)(2,1)S(1)} collective-permute-done((bf16[2,128,2048]{2,1,0:T(8,128)(2,1)S(1)}, bf16[2,128,2048]{2,1,0:T(8,128)(2,1)S(1)}, u32[]{:S(2)}, u32[]{:S(2)}) %collective-permute-start.12) | collective-permute-done | bytes 1048608 | tf_op jit(solution)/shard_map/cond/branch_1_fun/ppermute | solution.py:50
  818.7 9.9 %collective-permute-done.15 = bf16[128,2048]{1,0:T(8,128)(2,1)S(1)} collective-permute-done((bf16[128,2048]{1,0:T(8,128)(2,1)S(1)}, bf16[128,2048]{1,0:T(8,128)(2,1)S(1)}, u32[]{:S(2)}, u32[]{:S(2)}) %collective-permute-start.15) | collective-permute-done | bytes 524320 | tf_op jit(solution)/shard_map/cond/branch_1_fun/ppermute | solution.py:50
  839.9 4.1 shard_map.253
  (438 shorter events, 251.8 us)
Async XLA Ops:
  7.2 40.5 %all-gather.5.cloned.1.call-start = ((), (), s32[]{:S(2)}) async-start(), calls=%async_computation.10 | async-start | bytes 1310720 | tf_op jit(solution)/shard_map/all_gather | solution.py:120
  18.2 140.1 %all-gather.7.cloned.1.call-start = ((), (), s32[]{:S(2)}) async-start(), calls=%async_computation.11 | async-start | bytes 3932160 | tf_op jit(solution)/shard_map/all_gather | solution.py:120
  38.6 268.0 %all-gather.9.cloned.1.call-start = ((), (), s32[]{:S(2)}) async-start(), calls=%async_computation.12 | async-start | bytes 10485760 | tf_op jit(solution)/shard_map/all_gather | solution.py:120
  78.7 264.5 %all-gather.11.cloned.1.call-start = ((), (), s32[]{:S(2)}) async-start(), calls=%async_computation.13 | async-start | bytes 5242880 | tf_op jit(solution)/shard_map/all_gather | solution.py:120
  90.5 24.3 %collective-permute-start.26 = (bf16[256,2048]{1,0:T(8,128)(2,1)S(1)}, bf16[256,2048]{1,0:T(8,128)(2,1)S(1)}, u32[]{:S(2)}, u32[]{:S(2)}) collective-permute-start(bf16[256,2048]{1,0:T(8,128)(2,1)S(1)} %copy-done.10), channel_id=1, source_target_pairs={{0,2},{2,0},{1,3},{3,1},{4,6},{6,4},{5,7},{7,5},{8,10},{10,8},{9,1... | collective-permute-start | bytes 3145736 | tf_op jit(solution)/shard_map/ppermute | solution.py:50
  91.1 24.7 %collective-permute-start.27 = (bf16[256,2048]{1,0:T(8,128)(2,1)S(1)}, bf16[256,2048]{1,0:T(8,128)(2,1)S(1)}, u32[]{:S(2)}, u32[]{:S(2)}) collective-permute-start(bf16[256,2048]{1,0:T(8,128)(2,1)S(1)} %copy-done.10), channel_id=1, source_target_pairs={{0,4},{4,0},{1,5},{5,1},{2,6},{6,2},{3,7},{7,3},{8,12},{12,8},{9,1... | collective-permute-start | bytes 3145736 | tf_op jit(solution)/shard_map/ppermute | solution.py:50
  117.7 35.6 %collective-permute-start.30 = (bf16[768,2048]{1,0:T(8,128)(2,1)}, bf16[768,2048]{1,0:T(8,128)(2,1)}, u32[]{:S(2)}, u32[]{:S(2)}) collective-permute-start(bf16[768,2048]{1,0:T(8,128)(2,1)} %pad_maximum_fusion.5), channel_id=1, source_target_pairs={{0,1},{1,0},{2,3},{3,2},{4,5},{5,4},{6,7},{7,6},{8,9},{9,8},{10,11... | collective-permute-start | bytes 9437192 | tf_op jit(solution)/shard_map/ppermute | solution.py:50
  130.4 13.6 %collective-permute-start.28 = (bf16[128,2048]{1,0:T(8,128)(2,1)}, bf16[128,2048]{1,0:T(8,128)(2,1)}, u32[]{:S(2)}, u32[]{:S(2)}) collective-permute-start(bf16[128,2048]{1,0:T(8,128)(2,1)} %slice.268), channel_id=1, source_target_pairs={{0,4},{4,0},{1,5},{5,1},{2,6},{6,2},{3,7},{7,3},{8,12},{12,8},{9,1... | collective-permute-start | bytes 1572872 | tf_op jit(solution)/shard_map/ppermute | solution.py:50
  132.6 13.4 %collective-permute-start.29 = (bf16[128,2048]{1,0:T(8,128)(2,1)}, bf16[128,2048]{1,0:T(8,128)(2,1)}, u32[]{:S(2)}, u32[]{:S(2)}) collective-permute-start(bf16[128,2048]{1,0:T(8,128)(2,1)} %slice.269), channel_id=1, source_target_pairs={{0,2},{2,0},{1,3},{3,1},{4,6},{6,4},{5,7},{7,5},{8,10},{10,8},{9,1... | collective-permute-start | bytes 1572872 | tf_op jit(solution)/shard_map/ppermute | solution.py:50
  138.7 522.1 %reduce-scatter.5.cloned.1.call-start = ((), (), s32[]{:S(2)}) async-start(), calls=%async_computation.14 | async-start | bytes 5242880 | tf_op jit(solution)/shard_map/reduce_scatter | solution.py:124
  216.6 25.3 %collective-permute-start.1 = (bf16[2,128,2048]{2,1,0:T(8,128)(2,1)S(1)}, bf16[2,128,2048]{2,1,0:T(8,128)(2,1)S(1)}, u32[]{:S(2)}, u32[]{:S(2)}) collective-permute-start(bf16[2,128,2048]{2,1,0:T(8,128)(2,1)S(1)} %slice_bitcast_fusion.4), channel_id=1, source_target_pairs={{0,2},{2,0},{1,3},{3,1},{4,6},{6,4},{5,7},{7,5},{8,10},{10,8},{9,1... | collective-permute-start | bytes 3145736 | tf_op jit(solution)/shard_map/cond/branch_1_fun/ppermute | solution.py:50
  217.5 25.0 %collective-permute-start.3 = (bf16[2,128,2048]{2,1,0:T(8,128)(2,1)S(1)}, bf16[2,128,2048]{2,1,0:T(8,128)(2,1)S(1)}, u32[]{:S(2)}, u32[]{:S(2)}) collective-permute-start(bf16[2,128,2048]{2,1,0:T(8,128)(2,1)S(1)} %slice_bitcast_fusion.1), channel_id=1, source_target_pairs={{0,4},{4,0},{1,5},{5,1},{2,6},{6,2},{3,7},{7,3},{8,12},{12,8},{9,1... | collective-permute-start | bytes 3145736 | tf_op jit(solution)/shard_map/cond/branch_1_fun/ppermute | solution.py:50
  243.3 13.0 %collective-permute-start.4 = (bf16[128,2048]{1,0:T(8,128)(2,1)S(1)}, bf16[128,2048]{1,0:T(8,128)(2,1)S(1)}, u32[]{:S(2)}, u32[]{:S(2)}) collective-permute-start(bf16[128,2048]{1,0:T(8,128)(2,1)S(1)} %fusion.3), channel_id=1, source_target_pairs={{0,2},{2,0},{1,3},{3,1},{4,6},{6,4},{5,7},{7,5},{8,10},{10,8},{9,1... | collective-permute-start | bytes 1572872 | tf_op jit(solution)/shard_map/cond/branch_1_fun/ppermute | solution.py:50
  244.8 12.7 %collective-permute-start.2 = (bf16[128,2048]{1,0:T(8,128)(2,1)S(1)}, bf16[128,2048]{1,0:T(8,128)(2,1)S(1)}, u32[]{:S(2)}, u32[]{:S(2)}) collective-permute-start(bf16[128,2048]{1,0:T(8,128)(2,1)S(1)} %fusion.2), channel_id=1, source_target_pairs={{0,4},{4,0},{1,5},{5,1},{2,6},{6,2},{3,7},{7,3},{8,12},{12,8},{9,1... | collective-permute-start | bytes 1572872 | tf_op jit(solution)/shard_map/cond/branch_1_fun/ppermute | solution.py:50
  260.3 23.1 %collective-permute-start.5 = (bf16[256,2048]{1,0:T(8,128)(2,1)S(1)}, bf16[256,2048]{1,0:T(8,128)(2,1)S(1)}, u32[]{:S(2)}, u32[]{:S(2)}) collective-permute-start(bf16[256,2048]{1,0:T(8,128)(2,1)S(1)} %get-tuple-element.233), channel_id=1, source_target_pairs={{0,2},{2,0},{1,3},{3,1},{4,6},{6,4},{5,7},{7,5},{8,10},{10,8},{9,1... | collective-permute-start | bytes 3145736 | tf_op jit(solution)/shard_map/cond/branch_1_fun/ppermute | solution.py:50
  261.0 22.8 %collective-permute-start.6 = (bf16[256,2048]{1,0:T(8,128)(2,1)S(1)}, bf16[256,2048]{1,0:T(8,128)(2,1)S(1)}, u32[]{:S(2)}, u32[]{:S(2)}) collective-permute-start(bf16[256,2048]{1,0:T(8,128)(2,1)S(1)} %get-tuple-element.233), channel_id=1, source_target_pairs={{0,4},{4,0},{1,5},{5,1},{2,6},{6,2},{3,7},{7,3},{8,12},{12,8},{9,1... | collective-permute-start | bytes 3145736 | tf_op jit(solution)/shard_map/cond/branch_1_fun/ppermute | solution.py:50
  284.3 18.9 %collective-permute-start.9 = (bf16[768,2048]{1,0:T(8,128)(2,1)S(1)}, bf16[768,2048]{1,0:T(8,128)(2,1)S(1)}, u32[]{:S(2)}, u32[]{:S(2)}) collective-permute-start(bf16[768,2048]{1,0:T(8,128)(2,1)S(1)} %pad_maximum_fusion), channel_id=1, source_target_pairs={{0,1},{1,0},{2,3},{3,2},{4,5},{5,4},{6,7},{7,6},{8,9},{9,8},{10,11... | collective-permute-start | bytes 9437192 | tf_op jit(solution)/shard_map/cond/branch_1_fun/ppermute | solution.py:50
  284.5 14.4 %collective-permute-start.7 = (bf16[128,2048]{1,0:T(8,128)(2,1)S(1)}, bf16[128,2048]{1,0:T(8,128)(2,1)S(1)}, u32[]{:S(2)}, u32[]{:S(2)}) collective-permute-start(bf16[128,2048]{1,0:T(8,128)(2,1)S(1)} %slice.248), channel_id=1, source_target_pairs={{0,4},{4,0},{1,5},{5,1},{2,6},{6,2},{3,7},{7,3},{8,12},{12,8},{9,1... | collective-permute-start | bytes 1572872 | tf_op jit(solution)/shard_map/cond/branch_1_fun/ppermute | solution.py:50
  285.1 14.1 %collective-permute-start.8 = (bf16[128,2048]{1,0:T(8,128)(2,1)S(1)}, bf16[128,2048]{1,0:T(8,128)(2,1)S(1)}, u32[]{:S(2)}, u32[]{:S(2)}) collective-permute-start(bf16[128,2048]{1,0:T(8,128)(2,1)S(1)} %slice.249), channel_id=1, source_target_pairs={{0,2},{2,0},{1,3},{3,1},{4,6},{6,4},{5,7},{7,5},{8,10},{10,8},{9,1... | collective-permute-start | bytes 1572872 | tf_op jit(solution)/shard_map/cond/branch_1_fun/ppermute | solution.py:50
  365.1 25.3 %collective-permute-start.39 = (bf16[2,128,2048]{2,1,0:T(8,128)(2,1)S(1)}, bf16[2,128,2048]{2,1,0:T(8,128)(2,1)S(1)}, u32[]{:S(2)}, u32[]{:S(2)}) collective-permute-start(bf16[2,128,2048]{2,1,0:T(8,128)(2,1)S(1)} %slice_bitcast_fusion.22), channel_id=1, source_target_pairs={{0,2},{2,0},{1,3},{3,1},{4,6},{6,4},{5,7},{7,5},{8,10},{10,8},{9,1... | collective-permute-start | bytes 3145736 | tf_op jit(solution)/shard_map/ppermute | solution.py:50
  366.8 25.0 %collective-permute-start.41 = (bf16[2,128,2048]{2,1,0:T(8,128)(2,1)S(1)}, bf16[2,128,2048]{2,1,0:T(8,128)(2,1)S(1)}, u32[]{:S(2)}, u32[]{:S(2)}) collective-permute-start(bf16[2,128,2048]{2,1,0:T(8,128)(2,1)S(1)} %slice_bitcast_fusion.19), channel_id=1, source_target_pairs={{0,4},{4,0},{1,5},{5,1},{2,6},{6,2},{3,7},{7,3},{8,12},{12,8},{9,1... | collective-permute-start | bytes 3145736 | tf_op jit(solution)/shard_map/ppermute | solution.py:50
  393.5 13.1 %collective-permute-start.42 = (bf16[128,2048]{1,0:T(8,128)(2,1)}, bf16[128,2048]{1,0:T(8,128)(2,1)}, u32[]{:S(2)}, u32[]{:S(2)}) collective-permute-start(bf16[128,2048]{1,0:T(8,128)(2,1)} %fusion.18), channel_id=1, source_target_pairs={{0,2},{2,0},{1,3},{3,1},{4,6},{6,4},{5,7},{7,5},{8,10},{10,8},{9,1... | collective-permute-start | bytes 1572872 | tf_op jit(solution)/shard_map/ppermute | solution.py:50
  394.9 13.2 %collective-permute-start.40 = (bf16[128,2048]{1,0:T(8,128)(2,1)}, bf16[128,2048]{1,0:T(8,128)(2,1)}, u32[]{:S(2)}, u32[]{:S(2)}) collective-permute-start(bf16[128,2048]{1,0:T(8,128)(2,1)} %fusion.17), channel_id=1, source_target_pairs={{0,4},{4,0},{1,5},{5,1},{2,6},{6,2},{3,7},{7,3},{8,12},{12,8},{9,1... | collective-permute-start | bytes 1572872 | tf_op jit(solution)/shard_map/ppermute | solution.py:50
  415.3 23.1 %collective-permute-start.43 = (bf16[256,2048]{1,0:T(8,128)(2,1)S(1)}, bf16[256,2048]{1,0:T(8,128)(2,1)S(1)}, u32[]{:S(2)}, u32[]{:S(2)}) collective-permute-start(bf16[256,2048]{1,0:T(8,128)(2,1)S(1)} %get-tuple-element.241), channel_id=1, source_target_pairs={{0,2},{2,0},{1,3},{3,1},{4,6},{6,4},{5,7},{7,5},{8,10},{10,8},{9,1... | collective-permute-start | bytes 3145736 | tf_op jit(solution)/shard_map/ppermute | solution.py:50
  416.4 22.6 %collective-permute-start.44 = (bf16[256,2048]{1,0:T(8,128)(2,1)S(1)}, bf16[256,2048]{1,0:T(8,128)(2,1)S(1)}, u32[]{:S(2)}, u32[]{:S(2)}) collective-permute-start(bf16[256,2048]{1,0:T(8,128)(2,1)S(1)} %get-tuple-element.241), channel_id=1, source_target_pairs={{0,4},{4,0},{1,5},{5,1},{2,6},{6,2},{3,7},{7,3},{8,12},{12,8},{9,1... | collective-permute-start | bytes 3145736 | tf_op jit(solution)/shard_map/ppermute | solution.py:50
  439.8 16.3 %collective-permute-start.47 = (bf16[768,2048]{1,0:T(8,128)(2,1)S(1)}, bf16[768,2048]{1,0:T(8,128)(2,1)S(1)}, u32[]{:S(2)}, u32[]{:S(2)}) collective-permute-start(bf16[768,2048]{1,0:T(8,128)(2,1)S(1)} %pad_maximum_fusion.6), channel_id=1, source_target_pairs={{0,1},{1,0},{2,3},{3,2},{4,5},{5,4},{6,7},{7,6},{8,9},{9,8},{10,11... | collective-permute-start | bytes 9437192 | tf_op jit(solution)/shard_map/ppermute | solution.py:50
  439.9 14.4 %collective-permute-start.45 = (bf16[128,2048]{1,0:T(8,128)(2,1)S(1)}, bf16[128,2048]{1,0:T(8,128)(2,1)S(1)}, u32[]{:S(2)}, u32[]{:S(2)}) collective-permute-start(bf16[128,2048]{1,0:T(8,128)(2,1)S(1)} %slice.286), channel_id=1, source_target_pairs={{0,4},{4,0},{1,5},{5,1},{2,6},{6,2},{3,7},{7,3},{8,12},{12,8},{9,1... | collective-permute-start | bytes 1572872 | tf_op jit(solution)/shard_map/ppermute | solution.py:50
  441.5 14.1 %collective-permute-start.46 = (bf16[128,2048]{1,0:T(8,128)(2,1)S(1)}, bf16[128,2048]{1,0:T(8,128)(2,1)S(1)}, u32[]{:S(2)}, u32[]{:S(2)}) collective-permute-start(bf16[128,2048]{1,0:T(8,128)(2,1)S(1)} %slice.287), channel_id=1, source_target_pairs={{0,2},{2,0},{1,3},{3,1},{4,6},{6,4},{5,7},{7,5},{8,10},{10,8},{9,1... | collective-permute-start | bytes 1572872 | tf_op jit(solution)/shard_map/ppermute | solution.py:50
  472.8 235.8 %reduce-scatter.7.cloned.1.call-start = ((), (), s32[]{:S(2)}) async-start(), calls=%async_computation.15 | async-start | bytes 10485760 | tf_op jit(solution)/shard_map/reduce_scatter | solution.py:124
  555.2 25.5 %collective-permute-start.50 = (bf16[2,128,2048]{2,1,0:T(8,128)(2,1)}, bf16[2,128,2048]{2,1,0:T(8,128)(2,1)}, u32[]{:S(2)}, u32[]{:S(2)}) collective-permute-start(bf16[2,128,2048]{2,1,0:T(8,128)(2,1)} %slice_bitcast_fusion.17), channel_id=1, source_target_pairs={{0,2},{2,0},{1,3},{3,1},{4,6},{6,4},{5,7},{7,5},{8,10},{10,8},{9,1... | collective-permute-start | bytes 3145736 | tf_op jit(solution)/shard_map/ppermute | solution.py:50
  557.7 25.5 %collective-permute-start.51 = (bf16[2,128,2048]{2,1,0:T(8,128)(2,1)}, bf16[2,128,2048]{2,1,0:T(8,128)(2,1)}, u32[]{:S(2)}, u32[]{:S(2)}) collective-permute-start(bf16[2,128,2048]{2,1,0:T(8,128)(2,1)} %slice_bitcast_fusion.16), channel_id=1, source_target_pairs={{0,4},{4,0},{1,5},{5,1},{2,6},{6,2},{3,7},{7,3},{8,12},{12,8},{9,1... | collective-permute-start | bytes 3145736 | tf_op jit(solution)/shard_map/ppermute | solution.py:50
  585.0 13.2 %collective-permute-start.17 = (bf16[128,2048]{1,0:T(8,128)(2,1)S(1)}, bf16[128,2048]{1,0:T(8,128)(2,1)S(1)}, u32[]{:S(2)}, u32[]{:S(2)}) collective-permute-start(bf16[128,2048]{1,0:T(8,128)(2,1)S(1)} %fusion.7), channel_id=1, source_target_pairs={{0,2},{2,0},{1,3},{3,1},{4,6},{6,4},{5,7},{7,5},{8,10},{10,8},{9,1... | collective-permute-start | bytes 1572872 | tf_op jit(solution)/shard_map/cond/branch_1_fun/ppermute | solution.py:50
  587.6 13.0 %collective-permute-start.16 = (bf16[128,2048]{1,0:T(8,128)(2,1)S(1)}, bf16[128,2048]{1,0:T(8,128)(2,1)S(1)}, u32[]{:S(2)}, u32[]{:S(2)}) collective-permute-start(bf16[128,2048]{1,0:T(8,128)(2,1)S(1)} %fusion.6), channel_id=1, source_target_pairs={{0,4},{4,0},{1,5},{5,1},{2,6},{6,2},{3,7},{7,3},{8,12},{12,8},{9,1... | collective-permute-start | bytes 1572872 | tf_op jit(solution)/shard_map/cond/branch_1_fun/ppermute | solution.py:50
  605.7 23.4 %collective-permute-start.18 = (bf16[256,2048]{1,0:T(8,128)(2,1)S(1)}, bf16[256,2048]{1,0:T(8,128)(2,1)S(1)}, u32[]{:S(2)}, u32[]{:S(2)}) collective-permute-start(bf16[256,2048]{1,0:T(8,128)(2,1)S(1)} %get-tuple-element.238), channel_id=1, source_target_pairs={{0,2},{2,0},{1,3},{3,1},{4,6},{6,4},{5,7},{7,5},{8,10},{10,8},{9,1... | collective-permute-start | bytes 3145736 | tf_op jit(solution)/shard_map/cond/branch_1_fun/ppermute | solution.py:50
  606.8 23.0 %collective-permute-start.19 = (bf16[256,2048]{1,0:T(8,128)(2,1)S(1)}, bf16[256,2048]{1,0:T(8,128)(2,1)S(1)}, u32[]{:S(2)}, u32[]{:S(2)}) collective-permute-start(bf16[256,2048]{1,0:T(8,128)(2,1)S(1)} %get-tuple-element.238), channel_id=1, source_target_pairs={{0,4},{4,0},{1,5},{5,1},{2,6},{6,2},{3,7},{7,3},{8,12},{12,8},{9,1... | collective-permute-start | bytes 3145736 | tf_op jit(solution)/shard_map/cond/branch_1_fun/ppermute | solution.py:50
  631.7 23.9 %collective-permute-start.22 = (bf16[768,2048]{1,0:T(8,128)(2,1)}, bf16[768,2048]{1,0:T(8,128)(2,1)}, u32[]{:S(2)}, u32[]{:S(2)}) collective-permute-start(bf16[768,2048]{1,0:T(8,128)(2,1)} %pad_maximum_fusion.3), channel_id=1, source_target_pairs={{0,1},{1,0},{2,3},{3,2},{4,5},{5,4},{6,7},{7,6},{8,9},{9,8},{10,11... | collective-permute-start | bytes 9437192 | tf_op jit(solution)/shard_map/cond/branch_1_fun/ppermute | solution.py:50
  632.5 14.7 %collective-permute-start.20 = (bf16[128,2048]{1,0:T(8,128)(2,1)}, bf16[128,2048]{1,0:T(8,128)(2,1)}, u32[]{:S(2)}, u32[]{:S(2)}) collective-permute-start(bf16[128,2048]{1,0:T(8,128)(2,1)} %slice.256), channel_id=1, source_target_pairs={{0,4},{4,0},{1,5},{5,1},{2,6},{6,2},{3,7},{7,3},{8,12},{12,8},{9,1... | collective-permute-start | bytes 1572872 | tf_op jit(solution)/shard_map/cond/branch_1_fun/ppermute | solution.py:50
  633.8 14.4 %collective-permute-start.21 = (bf16[128,2048]{1,0:T(8,128)(2,1)}, bf16[128,2048]{1,0:T(8,128)(2,1)}, u32[]{:S(2)}, u32[]{:S(2)}) collective-permute-start(bf16[128,2048]{1,0:T(8,128)(2,1)} %slice.257), channel_id=1, source_target_pairs={{0,2},{2,0},{1,3},{3,1},{4,6},{6,4},{5,7},{7,5},{8,10},{10,8},{9,1... | collective-permute-start | bytes 1572872 | tf_op jit(solution)/shard_map/cond/branch_1_fun/ppermute | solution.py:50
  708.6 30.2 %all-to-all-start.3 = ((bf16[8,64,2048]{2,1,0:T(8,128)(2,1)}), bf16[8,64,2048]{2,1,0:T(8,128)(2,1)S(1)}, u32[]{:S(2)}, u32[]{:S(2)}) async-start(bf16[8,64,2048]{2,1,0:T(8,128)(2,1)} %bitcast.298), calls=%async_computation.5 | async-start | bytes 4194304 | tf_op jit(solution)/shard_map/all_to_all | solution.py:494
  712.2 119.8 %reduce-scatter.9.cloned.1.call-start = ((), (), s32[]{:S(2)}) async-start(), calls=%async_computation.16 | async-start | bytes 3932160 | tf_op jit(solution)/shard_map/reduce_scatter | solution.py:124
  751.0 93.1 %reduce-scatter.11.cloned.1.call-start = ((), (), s32[]{:S(2)}) async-start(), calls=%async_computation.17 | async-start | bytes 1310720 | tf_op jit(solution)/shard_map/reduce_scatter | solution.py:124
  751.3 12.7 %collective-permute-start.55 = (f32[16,4,64]{2,1,0:T(4,128)S(1)}, f32[16,4,64]{2,1,0:T(4,128)S(1)}, u32[]{:S(2)}, u32[]{:S(2)}) collective-permute-start(f32[16,4,64]{2,1,0:T(4,128)S(1)} %bitcast.323), channel_id=1, source_target_pairs={{0,4},{4,0},{1,5},{5,1},{2,6},{6,2},{3,7},{7,3},{8,12},{12,8},{9,1... | collective-permute-start | bytes 49160 | tf_op jit(solution)/shard_map/ppermute | solution.py:111
  769.1 66.5 %collective-permute-start.58 = (f32[2,4,64]{2,1,0:T(4,128)S(1)}, f32[2,4,64]{2,1,0:T(4,128)S(1)}, u32[]{:S(2)}, u32[]{:S(2)}) collective-permute-start(f32[2,4,64]{2,1,0:T(4,128)S(1)} %slice_select_fusion.4), channel_id=1, source_target_pairs={{0,16},{16,0},{1,17},{17,1},{2,18},{18,2},{3,19},{19,3},{4,20},{20... | collective-permute-start | bytes 6152 | tf_op jit(solution)/shard_map/ppermute | solution.py:111
  789.2 25.3 %collective-permute-start.12 = (bf16[2,128,2048]{2,1,0:T(8,128)(2,1)S(1)}, bf16[2,128,2048]{2,1,0:T(8,128)(2,1)S(1)}, u32[]{:S(2)}, u32[]{:S(2)}) collective-permute-start(bf16[2,128,2048]{2,1,0:T(8,128)(2,1)S(1)} %slice_bitcast_fusion.14), channel_id=1, source_target_pairs={{0,2},{2,0},{1,3},{3,1},{4,6},{6,4},{5,7},{7,5},{8,10},{10,8},{9,1... | collective-permute-start | bytes 3145736 | tf_op jit(solution)/shard_map/cond/branch_1_fun/ppermute | solution.py:50
  789.9 25.0 %collective-permute-start.14 = (bf16[2,128,2048]{2,1,0:T(8,128)(2,1)S(1)}, bf16[2,128,2048]{2,1,0:T(8,128)(2,1)S(1)}, u32[]{:S(2)}, u32[]{:S(2)}) collective-permute-start(bf16[2,128,2048]{2,1,0:T(8,128)(2,1)S(1)} %slice_bitcast_fusion.11), channel_id=1, source_target_pairs={{0,4},{4,0},{1,5},{5,1},{2,6},{6,2},{3,7},{7,3},{8,12},{12,8},{9,1... | collective-permute-start | bytes 3145736 | tf_op jit(solution)/shard_map/cond/branch_1_fun/ppermute | solution.py:50
  815.7 12.9 %collective-permute-start.15 = (bf16[128,2048]{1,0:T(8,128)(2,1)S(1)}, bf16[128,2048]{1,0:T(8,128)(2,1)S(1)}, u32[]{:S(2)}, u32[]{:S(2)}) collective-permute-start(bf16[128,2048]{1,0:T(8,128)(2,1)S(1)} %fusion.12), channel_id=1, source_target_pairs={{0,2},{2,0},{1,3},{3,1},{4,6},{6,4},{5,7},{7,5},{8,10},{10,8},{9,1... | collective-permute-start | bytes 1572872 | tf_op jit(solution)/shard_map/cond/branch_1_fun/ppermute | solution.py:50
  817.3 12.6 %collective-permute-start.13 = (bf16[128,2048]{1,0:T(8,128)(2,1)S(1)}, bf16[128,2048]{1,0:T(8,128)(2,1)S(1)}, u32[]{:S(2)}, u32[]{:S(2)}) collective-permute-start(bf16[128,2048]{1,0:T(8,128)(2,1)S(1)} %fusion.11), channel_id=1, source_target_pairs={{0,4},{4,0},{1,5},{5,1},{2,6},{6,2},{3,7},{7,3},{8,12},{12,8},{9,1... | collective-permute-start | bytes 1572872 | tf_op jit(solution)/shard_map/cond/branch_1_fun/ppermute | solution.py:50
  832.1 16.1 %all-to-all-start.5 = ((bf16[8,64,768]{2,1,0:T(8,128)(2,1)}), bf16[8,64,768]{2,1,0:T(8,128)(2,1)S(1)}, u32[]{:S(2)}, u32[]{:S(2)}) async-start(bf16[8,64,768]{2,1,0:T(8,128)(2,1)} %bitcast.307), calls=%async_computation.8 | async-start | bytes 1572864 | tf_op jit(solution)/shard_map/all_to_all | solution.py:494
  (65 other events, 661.5 us)
Sparse Core Ops, SparseCore 0:
  18.4 29.2 all-gather.4
  49.3 62.9 all-gather.6
  113.9 148.2 all-gather.8
  264.2 78.9 all-gather.10
  472.9 74.0 reduce-scatter.4
  549.3 144.9 reduce-scatter.6
  751.1 57.3 reduce-scatter.8
  810.9 27.1 reduce-scatter.10

commit v4 on v3

--- a/solution.py
+++ b/solution.py
@@ -68,15 +68,19 @@
     return total.reshape(terms.shape)
 
 
-def scatter_start(parts, rows, *others):
-    width = parts.shape[1]
-    half = rows // 2
-    arrived = swap(parts[4 * rows :], "c")
-    mine = parts[: 4 * rows].astype(F32) + arrived.astype(F32)
-    mine = mine.astype(BF16).reshape(2, 2, 2, half, width)
-    got_x = after(swap(mine[:, 1, 0], "x"), *others)
-    got_y = after(swap(mine[1, :, 1], "y"), *others)
-    return mine[:, 0, 0].astype(F32) + got_x.astype(F32), mine[0, :, 1].astype(F32) + got_y.astype(F32)
+def core_sum(mine, arrived):
+    total = mine.astype(F32) + arrived.astype(F32)
+    return total.astype(BF16).reshape(2, 2, 2, mine.shape[0] // 8, mine.shape[1])
+
+
+def scatter_sends(sums):
+    return sums[:, 1, 0], sums[1, :, 1]
+
+
+def scatter_start(sums, sends, *others):
+    got_x = after(swap(sends[0], "x"), *others)
+    got_y = after(swap(sends[1], "y"), *others)
+    return sums[:, 0, 0].astype(F32) + got_x.astype(F32), sums[0, :, 1].astype(F32) + got_y.astype(F32)
 
 
 def scatter_end(top, bottom):
@@ -85,8 +89,15 @@
     return jnp.concatenate([top[0] + top_last.astype(F32), bottom[0] + bottom_last.astype(F32)], 0)
 
 
-def group_scatter(parts, rows):
-    return scatter_end(*scatter_start(parts, rows))
+def group_scatter(mine, other):
+    sums = core_sum(mine, swap(other, "c"))
+    return scatter_end(*scatter_start(sums, scatter_sends(sums)))
+
+
+def by_core(product, values, weight):
+    half = values.shape[0] // 2
+    other = product(values[half:], weight).astype(BF16)
+    return product(after(values[:half], other), weight).astype(BF16), other
 
 
 def doubled(own, axes):
@@ -239,22 +250,20 @@
 
 def from_units(parts, unit_rows):
     _, rows, units = parts.shape
-    units //= 2
-
-    def kernel(p_ref, *out_refs):
-        for i, out_ref in enumerate(out_refs):
-            for m in range(8):
-                for r in range(units // unit_rows):
-                    target, source = (r * 8 + m) * unit_rows, i * units + r * unit_rows
-                    out_ref[:, target : target + unit_rows] = p_ref[m, :, source : source + unit_rows].astype(F32)
+
+    def kernel(p_ref, out_ref):
+        for m in range(8):
+            for r in range(units // unit_rows):
+                target, source = (r * 8 + m) * unit_rows, r * unit_rows
+                out_ref[:, target : target + unit_rows] = p_ref[m, :, source : source + unit_rows].astype(F32)
 
     step = min(rows, 16)
     return pl.pallas_call(
         kernel,
         grid=(rows // step,),
-        in_specs=[pl.BlockSpec((8, step, 2 * units), lambda i: (0, i, 0))],
-        out_specs=[pl.BlockSpec((step, 8 * units), lambda i: (i, 0))] * 2,
-        out_shape=[jax.ShapeDtypeStruct((rows, 8 * units), F32)] * 2,
+        in_specs=[pl.BlockSpec((8, step, units), lambda i: (0, i, 0))],
+        out_specs=pl.BlockSpec((step, 8 * units), lambda i: (i, 0)),
+        out_shape=jax.ShapeDtypeStruct((rows, 8 * units), F32),
         compiler_params=PARAMS,
     )(parts)
 
@@ -339,9 +348,8 @@
     )(grad, weight, both)
 
 
-def times_transposed(values, weight):
-    rows, depth = values.shape
-    width = weight.shape[0]
+def times_transposed(values, weight, first, rows):
+    depth, width = values.shape[1], weight.shape[0]
 
     def kernel(v_ref, w_ref, out_ref):
         for c in range(0, width, 512):
@@ -350,7 +358,7 @@
     return pl.pallas_call(
         kernel,
         grid=(rows // ROWS,),
-        in_specs=[by_rows(ROWS, depth), whole(weight)],
+        in_specs=[pl.BlockSpec((ROWS, depth), lambda i: (first // ROWS + i, 0)), whole(weight)],
         out_specs=by_rows(ROWS, width),
         out_shape=jax.ShapeDtypeStruct((rows, width), BF16),
         compiler_params=PARAMS,
@@ -551,19 +559,19 @@
         squares = [jnp.sum(jnp.square(projected[:, i * columns : (i + 1) * columns]), -1) for i in (0, 1)]
         inverse = lax.rsqrt(group_sum(jnp.stack(squares)) / width + NORM_EPS)
         inverse = after(inverse, weight_out)
-        info = jnp.stack([first_seen, end_seen, inverse[0], inverse[1]], 1)
+        info = lax.optimization_barrier(jnp.stack([first_seen, end_seen, inverse[0], inverse[1]], 1))
         attention = (projected, info, cosine, sine, gain_q, gain_k, place)
 
         def mix(attention, weight_out):
             mixed_low = attend(*attention)
-            branch = group_scatter(matmul(mixed_low, weight_out).astype(BF16), rows)
+            branch = group_scatter(*by_core(matmul, mixed_low, weight_out))
             hidden_in = tokens.astype(F32) + branch * inverse_rms(branch) * gain_a
             return mixed_low, branch, hidden_in, group_gather(hidden_in.astype(BF16))
 
         mixed_low, branch, hidden_in, group_hidden_in = region(mix, segment_ids, attention, weight_out)
         r_a = inverse_rms(branch)
         both, hidden = gate_up(group_hidden_in, weight_feed)
-        result = group_scatter(matmul(hidden, weight_down).astype(BF16), rows)
+        result = group_scatter(*by_core(matmul, hidden, weight_down))
         r_m = inverse_rms(result)
         out_tokens = (hidden_in + result * r_m * gain_f).astype(BF16)
 
@@ -577,12 +585,26 @@
         group_result_grad = group_gather(result_grad.astype(BF16))
 
         down_term = inner_t(hidden, group_result_grad).astype(BF16)
-        feed_grad = gate_up_back(after(group_result_grad, down_term), weight_down, both)
-        hidden_in_parts = times_transposed(feed_grad, weight_feed)
-        feed_term = inner_t(group_hidden_in, after(feed_grad, hidden_in_parts)).astype(BF16)
         down_share = scatter_planes(down_term)
-        top, bottom = scatter_start(hidden_in_parts, rows, feed_term)
-        feed_share = scatter_planes(feed_term)
+
+        def feed_mix(group_result_grad, weight_down, weight_feed, both, group_hidden_in):
+            feed_grad = gate_up_back(group_result_grad, weight_down, both)
+            half = group_rows // 2
+            for_other = times_transposed(feed_grad, weight_feed, half, half)
+            arrived = swap(for_other, "c")
+            for_mine = times_transposed(after(feed_grad, for_other), weight_feed, 0, half)
+            sums = core_sum(for_mine, arrived)
+            sends = lax.optimization_barrier(scatter_sends(sums))
+            ready = after(feed_grad, *sends)
+            gate_term = inner_t(group_hidden_in, ready[:, :units]).astype(BF16)
+            up_term = inner_t(group_hidden_in, ready[:, units:]).astype(BF16)
+            return gate_term, up_term, *scatter_start(sums, sends, gate_term, up_term)
+
+        gate_term, up_term, top, bottom = region(
+            feed_mix, segment_ids, after(group_result_grad, down_term), weight_down, weight_feed, both, group_hidden_in
+        )
+        gate_share = scatter_planes(gate_term)
+        up_share = scatter_planes(up_term)
 
         def to_mixer(top, bottom, branch, r_a):
             hidden_in_grad = grad_out + scatter_end(top, bottom)
@@ -593,23 +615,39 @@
         group_branch_grad = after(group_branch_grad, down_share)
         mixed_grad = matmul_t(group_branch_grad, weight_out).astype(BF16)
         q_back, k_back, v_grad, means = attend_back(*attention, mixed_grad)
-        means = group_sum(means.T).T / width
+        gate_back = exchange(after(gate_share, group_branch_grad).reshape(8, weight_rows, units), GROUP)
+        means = group_sum(after(means, gate_back).T).T / width
         grads, head_terms = qkv_grads(projected, q_back, k_back, v_grad, info, means, gain_q, gain_k)
-        feed_back = exchange(after(feed_share, means).reshape(8, weight_rows, 2 * units), GROUP)
-        grads = after(grads, feed_back)
+        up_back = exchange(after(up_share, means).reshape(8, weight_rows, units), GROUP)
         qkv_term = inner_t(group_tokens, grads).astype(BF16)
         qkv_share = scatter_planes(qkv_term)
-        out_term = inner_t(mixed_low, after(group_branch_grad, qkv_term))
+        out_term = inner_t(mixed_low, after(group_branch_grad, qkv_term, up_share))
         out_parts = out_term.astype(BF16).reshape(own_heads, per_head, weight_rows, width)
         out_parts = lax.all_to_all(out_parts.transpose(1, 0, 2, 3), head_axes, 0, 0, tiled=True)
         out_share = scatter_planes(out_parts.reshape(replicas * weight_rows, width))
 
-        def to_tokens(grads, weight_qkv, hidden_in_grad):
-            return hidden_in_grad + group_scatter(matmul_t(grads, weight_qkv).astype(BF16), rows)
-
-        g_tokens = region(to_tokens, segment_ids, after(grads, out_parts), weight_qkv, hidden_in_grad)
-
-        qkv_back = exchange(after(qkv_share, g_tokens).reshape(8, weight_rows, 3 * columns), GROUP)
+        head_terms = head_terms.reshape(2, 1, columns)
+        spread = jnp.zeros((2, 8, columns), F32)
+        spread = lax.dynamic_update_slice(spread, head_terms, (0, member, 0))
+        spread = spread.reshape((2,) + head_shape_put + (HEAD,)).transpose(0, 2, 3, 1, 4)
+        gain_terms = jnp.concatenate([spread.reshape(2, width), jnp.stack([mixer_gain_term, feed_gain_term])], 0)
+        gain_terms = gain_terms.reshape(4, replicas, 8, weight_rows).transpose(2, 1, 0, 3)
+        gain_terms = gain_terms.reshape(count, 4, weight_rows)
+
+        def to_tokens(grads, weight_qkv, gain_terms, gate_back, down_share):
+            mine, other = by_core(matmul_t, grads, weight_qkv)
+            sums = core_sum(mine, swap(other, "c"))
+            sends = scatter_sends(sums)
+            done = halved(gain_terms, GROUP), from_units(gate_back, unit_rows), down_share.astype(F32)
+            return scatter_start(sums, sends), *done
+
+        token_sums, gain_terms, g_w_gate, g_w_down = region(
+            to_tokens, segment_ids, after(grads, out_parts), weight_qkv, gain_terms, gate_back, down_share
+        )
+        g_gains = halved(gain_terms, PLANES)[0]
+        qkv_back = exchange(after(qkv_share, *token_sums, up_back).reshape(8, weight_rows, 3 * columns), GROUP)
+        top, bottom = token_sums
+        g_tokens = hidden_in_grad + scatter_end(after(top, qkv_back), after(bottom, qkv_back))
         heads_of = [
             [(e * own_heads + j) * (8 // per_head) + t for j in range(own_heads)]
             for t in range(8 // per_head)
@@ -617,16 +655,8 @@
         ]
         g_qkv = from_heads(qkv_back, heads_of)
         g_w_out = out_share.astype(F32)
-        g_w_down = down_share.astype(F32)
-        g_w_gate, g_w_up = from_units(feed_back, unit_rows)
-
-        head_terms = head_terms.reshape(2, 1, columns)
-        spread = jnp.zeros((2, 8, columns), F32)
-        spread = lax.dynamic_update_slice(spread, head_terms, (0, member, 0))
-        spread = spread.reshape((2,) + head_shape_put + (HEAD,)).transpose(0, 2, 3, 1, 4)
-        gain_terms = jnp.concatenate([spread.reshape(2, width), jnp.stack([mixer_gain_term, feed_gain_term])], 0)
-        gain_terms = gain_terms.reshape(4, replicas, 8, weight_rows).transpose(2, 1, 0, 3)
-        g_gains = halved(gain_terms.reshape(count, 4, weight_rows), GROUP + PLANES)[0]
+        g_w_up = from_units(after(up_back, token_sums[0]), unit_rows)
+
         return (
             out_tokens,
             g_tokens,

time: 867 us -> 841 us (0.970)
  waiting for transfers between devices: 341 us -> 299 us
  starting transfers between devices: 56.4 us -> 66.6 us
    ppermute x50, waiting for transfers between devices: 297 us -> 238 us  [swap(): return lax.ppermute(block, axis, [(0, 1), (1, 0)])]
    ppermute x5, waiting for transfers between devices: 4.94 us -> 31.9 us  [halved(): lax.ppermute(jnp.where(low_side, second, first), axis, [(i, i ^ step) for...]
    all_to_all x2 -> x3, waiting for transfers between devices: 19.5 us -> 4 us  [exchange(): return lax.all_to_all(parts, group, 0, 0, tiled=True)]
    dot_general x2 -> x3, matrix products: 16.1 us -> 21 us  [matmul_t(): lax.dot_general(left, right, (((1,), (1,)), ((), ())), preferred_element_...]
    pallas_call x1 -> x2, Pallas kernels: 23.7 us -> 28.5 us  [times_transposed(): pl.pallas_call(kernel, grid=(rows // ROWS,), in_specs=[pl.BlockSpec((ROWS...]
    dot_general x4 -> x5, matrix products: 53.3 us -> 54.4 us  [inner_t(): lax.dot_general(left, right, (((0,), (0,)), ((), ())), preferred_element_...]
    unnamed x92 -> x82, local copies, waits for them, and re-layouts: 29.7 us -> 28.9 us
    dot_general x3 -> x5, matrix products: 24.3 us -> 24.7 us  [matmul(): return jnp.dot(left, right, preferred_element_type=F32)]
  transfers between devices with their start and end apart: 70 -> 72, of which waited for: 50 -> 46; matrix products, arithmetic and copies ran while one was open for 23% -> 25% of each run, Pallas kernels for 15% -> 17%
where the time goes in v4:
time: 841 us; the launch traced here: 833 us
  waiting for transfers between devices  299 us (36%)
  Pallas kernels  138 us (16%)
  matrix products  100 us (12%)
  local copies, waits for them, and re-layouts  78.7 us (9%)
  other arithmetic  76.2 us (9%)
  starting transfers between devices  66.6 us (8%)
  blocking collectives  57.2 us (7%)
  between operations  15.8 us (2%)
    ppermute x50, waiting for transfers between devices, swap(): return lax.ppermute(block, axis, [(0, 1), (1, 0)])  238 us
    dot_general x5, matrix products, inner_t(): lax.dot_general(left, right, (((0,), (0,)), ((), ())), preferred_element_...  54.4 us
    all_to_all x2, blocking collectives, exchange(): return lax.all_to_all(parts, group, 0, 0, tiled=True)  47.2 us
    ppermute x50, starting transfers between devices, swap(): return lax.ppermute(block, axis, [(0, 1), (1, 0)])  42.4 us
    ppermute x5, waiting for transfers between devices, halved(): lax.ppermute(jnp.where(low_side, second, first), axis, [(i, i ^ step) for...  31.9 us
    unnamed x82, local copies, waits for them, and re-layouts  28.9 us
    pallas_call x2, Pallas kernels, times_transposed(): pl.pallas_call(kernel, grid=(rows // ROWS,), in_specs=[pl.BlockSpec((ROWS...  28.5 us
    pallas_call x1, Pallas kernels, attend_back(): pl.pallas_call(attend_back_kernel, grid=(blocks, heads), in_specs=specs +...  28.4 us
  transfers between devices with their start and end apart: 72, of which 46 were waited for; matrix products, arithmetic and copies ran while one was open for 25% of the time, Pallas kernels for 17%

profile of v4, /device:TPU:0, one launch (start us, length us, event | category | flops | bytes accessed | tf_op | source)
XLA Modules:
  0.0 833.2 jit_solution(3168428088068774479)
XLA Ops:
  21.3 16.3 %all_to_all.35 = bf16[8,64,768]{2,1,0:T(8,128)(2,1)} all-to-all(bf16[8,64,768]{2,1,0:T(8,128)(2,1)S(1)} %pad_maximum_fusion.14), channel_id=1, replica_groups=mesh['zh'=2,'zl'=2,'y'=2,'x'=2,'c'=2] {'y','x','c'}, dimensions={0} | all-to-all | bytes 1572864 | tf_op jit(solution)/shard_map/all_to_all | solution.py:502
  37.6 4.2 shard_map.246
  41.8 5.9 all-gather.5.cloned.1.call-done
  47.7 30.9 %all_to_all.36 = bf16[8,64,2048]{2,1,0:T(8,128)(2,1)} all-to-all(bf16[8,64,2048]{2,1,0:T(8,128)(2,1)} %shard_map.246), channel_id=1, replica_groups=mesh['zh'=2,'zl'=2,'y'=2,'x'=2,'c'=2] {'y','x','c'}, dimensions={0} | all-to-all | bytes 4194304 | tf_op jit(solution)/shard_map/all_to_all | solution.py:502
  95.8 19.1 %collective-permute-done.30 = bf16[256,2048]{1,0:T(8,128)(2,1)S(1)} collective-permute-done((bf16[256,2048]{1,0:T(8,128)(2,1)S(1)}, bf16[256,2048]{1,0:T(8,128)(2,1)S(1)}, u32[]{:S(2)}, u32[]{:S(2)}) %collective-permute-start.30) | collective-permute-done | bytes 1048608 | tf_op jit(solution)/shard_map/ppermute | solution.py:50
  117.8 5.5 fusion.25
  158.4 10.0 %fusion.33.p_ref = f32[2048,768]{1,0:T(8,128)S(1)} fusion(bf16[2048,2048]{1,0:T(8,128)(2,1)} %constant_dynamic-update-slice_fusion.14, bf16[2048,768]{1,0:T(8,128)(2,1)} %all-gather.7.cloned.1.call-done), kind=kOutput, calls=%fused_computation.239 | convolution fusion | flops 6442450944 | bytes 17825792 | tf_op jit(solution)/shard_map/dot_general | solution.py:23
  178.4 4.6 all_to_all.37
  184.3 119.1 %conditional.4 = (bf16[2048,256]{1,0:T(8,128)(2,1)S(1)}, f32[256,2048]{1,0:T(8,128)S(1)}, f32[256,2048]{1,0:T(8,128)}, bf16[2048,2048]{1,0:T(8,128)(2,1)}, f32[256,1]{0,1:T(1,128)S(1)}) conditional(s32[]{:T(128)} %bitcast.39, () %tuple.71, (f32[2048,768]{1,0:T(8,128)}, f32[2048,4]{0,1:T(4,128)S(1)}, f32[2048,128]{1,0:T(8,128)}, ...), branch_computations={%region_4.5_spmd, %region_5.7_spmd} | conditional | flops 4327473664 | bytes 171004576 | solution.py:46
  185.8 16.9 %branch_1_fun.5 = bf16[2,2,512,256]{3,2,1,0:T(8,128)(2,1)S(1)} custom-call(f32[2,2,512,768]{3,2,1,0:T(8,128)} %bitcast.277, f32[2,2,512,768]{3,2,1,0:T(8,128)} %bitcast.278, f32[2,2,512,768]{3,2,1,0:T(8,128)} %bitcast.279, f32[2,2,512,4]{3,2,1,0:T(8,128)} %bitcast.295, f32[2,2,512,128]{3,2,1,0:T(8,128)} %bitcast.292, f32[2,2,512,128]{3,2,1,0:T(8,128)} %bitcast.291, ...), custom_call_target="tpu_custom_call" | custom-call | flops 2147483648 | bytes 8388608 | tf_op jit(solution)/shard_map/cond/branch_1_fun/pallas_call | solution.py:398
  204.3 7.0 collective-permute-done.8
  214.1 23.8 %collective-permute-done.9 = bf16[2,128,2048]{2,1,0:T(8,128)(2,1)S(1)} collective-permute-done((bf16[2,128,2048]{2,1,0:T(8,128)(2,1)S(1)}, bf16[2,128,2048]{2,1,0:T(8,128)(2,1)S(1)}, u32[]{:S(2)}, u32[]{:S(2)}) %collective-permute-start.9) | collective-permute-done | bytes 1048608 | tf_op jit(solution)/shard_map/cond/branch_1_fun/ppermute | solution.py:50
  241.3 11.0 %collective-permute-done.10 = bf16[128,2048]{1,0:T(8,128)(2,1)S(1)} collective-permute-done((bf16[128,2048]{1,0:T(8,128)(2,1)S(1)}, bf16[128,2048]{1,0:T(8,128)(2,1)S(1)}, u32[]{:S(2)}, u32[]{:S(2)}) %collective-permute-start.10) | collective-permute-done | bytes 524320 | tf_op jit(solution)/shard_map/cond/branch_1_fun/ppermute | solution.py:50
  258.3 20.3 %collective-permute-done.13 = bf16[256,2048]{1,0:T(8,128)(2,1)S(1)} collective-permute-done((bf16[256,2048]{1,0:T(8,128)(2,1)S(1)}, bf16[256,2048]{1,0:T(8,128)(2,1)S(1)}, u32[]{:S(2)}, u32[]{:S(2)}) %collective-permute-start.13) | collective-permute-done | bytes 1048608 | tf_op jit(solution)/shard_map/cond/branch_1_fun/ppermute | solution.py:50
  282.6 12.1 %collective-permute-done.15 = bf16[128,2048]{1,0:T(8,128)(2,1)S(1)} collective-permute-done((bf16[128,2048]{1,0:T(8,128)(2,1)S(1)}, bf16[128,2048]{1,0:T(8,128)(2,1)S(1)}, u32[]{:S(2)}, u32[]{:S(2)}) %collective-permute-start.15) | collective-permute-done | bytes 524320 | tf_op jit(solution)/shard_map/cond/branch_1_fun/ppermute | solution.py:50
  303.4 24.5 %shard_map.247 = (f32[2048,2048]{1,0:T(8,128)}, bf16[2048,1024]{1,0:T(8,128)(2,1)}) custom-call(bf16[2048,2048]{1,0:T(8,128)(2,1)} %get-tuple-element.164.v_ref, bf16[2048,2048]{1,0:T(8,128)(2,1)} %all-gather.9.cloned.1.call-done.w_ref), custom_call_target="tpu_custom_call" | custom-call | flops 17179869184 | bytes 29360128 | tf_op jit(solution)/shard_map/pallas_call | solution.py:313
  327.9 15.3 %all-gather.11.cloned.1.call-done = bf16[1024,2048]{1,0:T(8,128)(2,1)} async-done(((bf16[256,2048]{1,0:T(8,128)(2,1)}), bf16[1024,2048]{1,0:T(8,128)(2,1)}) %all-gather.11.cloned.1.call-update) | async-done | bytes 4194320 | tf_op jit(solution)/shard_map/all_gather | solution.py:131
  343.3 7.5 convolution_convert_fusion.3
  351.0 7.0 collective-permute-done.42
  358.0 4.7 add_convert_fusion.3
  366.0 22.0 %collective-permute-done.43 = bf16[2,128,2048]{2,1,0:T(8,128)(2,1)S(1)} collective-permute-done((bf16[2,128,2048]{2,1,0:T(8,128)(2,1)S(1)}, bf16[2,128,2048]{2,1,0:T(8,128)(2,1)S(1)}, u32[]{:S(2)}, u32[]{:S(2)}) %collective-permute-start.43) | collective-permute-done | bytes 1048608 | tf_op jit(solution)/shard_map/ppermute | solution.py:50
  394.2 10.1 %collective-permute-done.44 = bf16[128,2048]{1,0:T(8,128)(2,1)S(1)} collective-permute-done((bf16[128,2048]{1,0:T(8,128)(2,1)}, bf16[128,2048]{1,0:T(8,128)(2,1)S(1)}, u32[]{:S(2)}, u32[]{:S(2)}) %collective-permute-start.44) | collective-permute-done | bytes 524320 | tf_op jit(solution)/shard_map/ppermute | solution.py:50
  413.5 21.5 %collective-permute-done.47 = bf16[256,2048]{1,0:T(8,128)(2,1)S(1)} collective-permute-done((bf16[256,2048]{1,0:T(8,128)(2,1)S(1)}, bf16[256,2048]{1,0:T(8,128)(2,1)S(1)}, u32[]{:S(2)}, u32[]{:S(2)}) %collective-permute-start.47) | collective-permute-done | bytes 1048608 | tf_op jit(solution)/shard_map/ppermute | solution.py:50
  438.5 11.7 %collective-permute-done.49 = bf16[128,2048]{1,0:T(8,128)(2,1)S(1)} collective-permute-done((bf16[128,2048]{1,0:T(8,128)(2,1)S(1)}, bf16[128,2048]{1,0:T(8,128)(2,1)S(1)}, u32[]{:S(2)}, u32[]{:S(2)}) %collective-permute-start.49) | collective-permute-done | bytes 524320 | tf_op jit(solution)/shard_map/ppermute | solution.py:50
  457.3 11.4 %convolution_convert_fusion.2 = bf16[1024,2048]{1,0:T(8,128)(2,1)} fusion(bf16[2048,1024]{1,0:T(8,128)(2,1)S(1)} %copy-done.23, bf16[2048,2048]{1,0:T(8,128)(2,1)S(1)} %constant_dynamic-update-slice_fusion.26), kind=kOutput, calls=%fused_computation.83 | convolution fusion | flops 8592031744 | bytes 16777216 | tf_op jit(solution)/shard_map/dot_general | solution.py:31
  468.7 84.9 %conditional.5 = (bf16[2048,1024]{0,1:T(8,128)(2,1)}, bf16[2048,1024]{0,1:T(8,128)(2,1)}, f32[2,128,2048]{2,1,0:T(8,128)}, f32[2,128,2048]{2,1,0:T(8,128)}) conditional(s32[]{:T(128)} %bitcast.39, () %tuple.81, (bf16[2048,2048]{1,0:T(8,128)(2,1)}, bf16[1024,2048]{1,0:T(8,128)(2,1)}, f32[2048,2048]{1,0:T(8,128)}, bf16[2048,2048]{1,0:T(8,128)(2,1)}, ...), branch_computations={%region_9.10_spmd, %region_10.11_spmd} | conditional | flops 42965401600 | bytes 167772320 | solution.py:46
  468.7 19.7 %branch_1_fun.6.v_ref = bf16[2048,2048]{1,0:T(8,128)(2,1)} custom-call(bf16[2048,2048]{1,0:T(8,128)(2,1)} %get-tuple-element.75.g_ref, bf16[1024,2048]{1,0:T(8,128)(2,1)} %get-tuple-element.76.w_ref, f32[2048,2048]{1,0:T(8,128)} %get-tuple-element.77.both_ref), custom_call_target="tpu_custom_call" | custom-call | flops 8589934592 | bytes 33554432 | tf_op jit(solution)/shard_map/cond/branch_1_fun/pallas_call | solution.py:338
  488.5 14.3 %branch_1_fun.7 = bf16[1024,2048]{1,0:T(8,128)(2,1)} custom-call(bf16[2048,2048]{1,0:T(8,128)(2,1)} %branch_1_fun.6.v_ref, bf16[2048,2048]{1,0:T(8,128)(2,1)} %get-tuple-element.78.w_ref), custom_call_target="tpu_custom_call" | custom-call | flops 8589934592 | bytes 8388608 | tf_op jit(solution)/shard_map/cond/branch_1_fun/pallas_call | solution.py:358
  502.9 14.2 %branch_1_fun.8 = bf16[1024,2048]{1,0:T(8,128)(2,1)} custom-call(bf16[2048,2048]{1,0:T(8,128)(2,1)} %branch_1_fun.6.v_ref, bf16[2048,2048]{1,0:T(8,128)(2,1)} %get-tuple-element.78.w_ref), custom_call_target="tpu_custom_call" | custom-call | flops 8589934592 | bytes 8388608 | tf_op jit(solution)/shard_map/cond/branch_1_fun/pallas_call | solution.py:358
  517.1 4.4 add_convert_fusion.1
  524.1 13.0 %convert_bitcast_fusion = bf16[2048,1024]{0,1:T(8,128)(2,1)} fusion(bf16[2048,2048]{1,0:T(8,128)(2,1)} %get-tuple-element.83, bf16[2048,2048]{1,0:T(8,128)(2,1)S(1)} %copy-done.12), kind=kOutput, calls=%fused_computation.30 | convolution fusion | flops 8592031744 | bytes 16777216 | tf_op jit(solution)/shard_map/cond/branch_1_fun/dot_general | solution.py:31
  537.2 13.3 %convert_bitcast_fusion.1 = bf16[2048,1024]{0,1:T(8,128)(2,1)} fusion(bf16[2048,2048]{1,0:T(8,128)(2,1)} %get-tuple-element.83, bf16[2048,2048]{1,0:T(8,128)(2,1)S(1)} %copy-done.12), kind=kOutput, calls=%fused_computation.33 | convolution fusion | flops 8592031744 | bytes 16777216 | tf_op jit(solution)/shard_map/cond/branch_1_fun/dot_general | solution.py:31
  562.2 76.2 %conditional.6 = (f32[256,2048]{1,0:T(8,128)}, bf16[2048,2048]{1,0:T(8,128)(2,1)}, f32[1,4,8,64]{3,2,1,0:T(8,128)S(1)}) conditional(s32[]{:T(128)} %bitcast.39, () %tuple.80, (f32[2,128,2048]{2,1,0:T(8,128)}, f32[2,128,2048]{2,1,0:T(8,128)}, f32[256,2048]{1,0:T(8,128)}, f32[256,1]{0,1:T(1,128)S(1)}, f32[1,2048]{1,0:T(1,128)S(1)}, ...), branch_computations={%region_11.12_spmd, %region_12.15_spmd} | conditional | flops 19921664 | bytes 89180528 | solution.py:46
  566.8 10.5 %collective-permute-done.1 = bf16[128,2048]{1,0:T(8,128)(2,1)S(1)} collective-permute-done((bf16[128,2048]{1,0:T(8,128)(2,1)S(1)}, bf16[128,2048]{1,0:T(8,128)(2,1)S(1)}, u32[]{:S(2)}, u32[]{:S(2)}) %collective-permute-start.1) | collective-permute-done | bytes 524320 | tf_op jit(solution)/shard_map/cond/branch_1_fun/ppermute | solution.py:50
  588.0 21.3 %collective-permute-done.2 = bf16[256,2048]{1,0:T(8,128)(2,1)S(1)} collective-permute-done((bf16[256,2048]{1,0:T(8,128)(2,1)S(1)}, bf16[256,2048]{1,0:T(8,128)(2,1)S(1)}, u32[]{:S(2)}, u32[]{:S(2)}) %collective-permute-start.2) | collective-permute-done | bytes 1048608 | tf_op jit(solution)/shard_map/cond/branch_1_fun/ppermute | solution.py:50
  615.7 12.0 %collective-permute-done.4 = bf16[128,2048]{1,0:T(8,128)(2,1)S(1)} collective-permute-done((bf16[128,2048]{1,0:T(8,128)(2,1)}, bf16[128,2048]{1,0:T(8,128)(2,1)S(1)}, u32[]{:S(2)}, u32[]{:S(2)}) %collective-permute-start.4) | collective-permute-done | bytes 524320 | tf_op jit(solution)/shard_map/cond/branch_1_fun/ppermute | solution.py:50
  633.3 4.0 constant_dynamic-update-slice_fusion.8
  644.4 6.9 convolution_convert_fusion.6
  651.3 28.4 %shard_map.248 = (f32[2,2,512,256]{3,2,1,0:T(8,128)}, f32[2,2,512,256]{3,2,1,0:T(8,128)}, bf16[2,2,512,256]{3,2,1,0:T(8,128)(2,1)}, f32[2,2,2,512,2]{4,3,2,1,0:T(8,128)}) custom-call(f32[2,2,512,768]{3,2,1,0:T(8,128)} %bitcast.274, f32[2,2,512,768]{3,2,1,0:T(8,128)} %bitcast.275, f32[2,2,512,768]{3,2,1,0:T(8,128)} %bitcast.276, f32[2,2,512,4]{3,2,1,0:T(8,128)} %bitcast.287, ...), custom_call_target="tpu_custom_call" | custom-call | flops 5368709120 | bytes 12582912 | tf_op jit(solution)/shard_map/pallas_call | solution.py:418
  692.4 7.0 shard_map.249
  701.0 10.6 %convolution_convert_fusion.4 = bf16[2048,768]{1,0:T(8,128)(2,1)} fusion(bf16[2048,2048]{1,0:T(8,128)(2,1)} %constant_dynamic-update-slice_fusion.14, bf16[2048,768]{1,0:T(8,128)(2,1)S(1)} %get-tuple-element.188), kind=kOutput, calls=%fused_computation.85 | convolution fusion | flops 6444023808 | bytes 14680064 | tf_op jit(solution)/shard_map/dot_general | solution.py:31
  714.1 6.2 convolution_convert_fusion.5
  720.4 5.4 all_to_all.38
  725.8 4.3 all-to-all-start.5
  730.3 58.7 %conditional.7 = (f32[2,128,2048]{2,1,0:T(8,128)S(1)}, f32[2,128,2048]{2,1,0:T(8,128)}, f32[4,4,64]{2,1,0:T(4,128)}, f32[64,8192]{1,0:T(8,128)}, f32[256,2048]{1...) conditional(s32[]{:T(128)} %bitcast.39, () %tuple.85, (bf16[2048,768]{1,0:T(8,128)(2,1)}, ...), branch_computations={%region_20.21_spmd, %region_21.22_spmd} | conditional | flops 6458725376 | bytes 104198672 | solution.py:46
  730.4 7.8 convolution_convert_fusion.1
  745.7 6.3 add_convert_fusion.2
  758.4 22.1 %collective-permute-done.26 = f32[8,4,64]{2,1,0:T(4,128)S(1)} collective-permute-done((f32[8,4,64]{2,1,0:T(4,128)S(1)}, f32[8,4,64]{2,1,0:T(4,128)S(1)}, u32[]{:S(2)}, u32[]{:S(2)}) %collective-permute-start.26) | collective-permute-done | bytes 8224 | tf_op jit(solution)/shard_map/cond/branch_1_fun/ppermute | solution.py:122
  (436 shorter events, 261.3 us)
Async XLA Ops:
  7.2 40.5 %all-gather.5.cloned.1.call-start = ((), (), s32[]{:S(2)}) async-start(), calls=%async_computation.12 | async-start | bytes 1310720 | tf_op jit(solution)/shard_map/all_gather | solution.py:131
  18.3 140.1 %all-gather.7.cloned.1.call-start = ((), (), s32[]{:S(2)}) async-start(), calls=%async_computation.13 | async-start | bytes 3932160 | tf_op jit(solution)/shard_map/all_gather | solution.py:131
  37.6 265.8 %all-gather.9.cloned.1.call-start = ((), (), s32[]{:S(2)}) async-start(), calls=%async_computation.14 | async-start | bytes 10485760 | tf_op jit(solution)/shard_map/all_gather | solution.py:131
  78.7 264.6 %all-gather.11.cloned.1.call-start = ((), (), s32[]{:S(2)}) async-start(), calls=%async_computation.15 | async-start | bytes 5242880 | tf_op jit(solution)/shard_map/all_gather | solution.py:131
  90.5 24.3 %collective-permute-start.30 = (bf16[256,2048]{1,0:T(8,128)(2,1)S(1)}, bf16[256,2048]{1,0:T(8,128)(2,1)S(1)}, u32[]{:S(2)}, u32[]{:S(2)}) collective-permute-start(bf16[256,2048]{1,0:T(8,128)(2,1)S(1)} %copy-done.8), channel_id=1, source_target_pairs={{0,2},{2,0},{1,3},{3,1},{4,6},{6,4},{5,7},{7,5},{8,10},{10,8},{9,1... | collective-permute-start | bytes 3145736 | tf_op jit(solution)/shard_map/ppermute | solution.py:50
  91.2 24.7 %collective-permute-start.31 = (bf16[256,2048]{1,0:T(8,128)(2,1)S(1)}, bf16[256,2048]{1,0:T(8,128)(2,1)S(1)}, u32[]{:S(2)}, u32[]{:S(2)}) collective-permute-start(bf16[256,2048]{1,0:T(8,128)(2,1)S(1)} %copy-done.8), channel_id=1, source_target_pairs={{0,4},{4,0},{1,5},{5,1},{2,6},{6,2},{3,7},{7,3},{8,12},{12,8},{9,1... | collective-permute-start | bytes 3145736 | tf_op jit(solution)/shard_map/ppermute | solution.py:50
  117.8 35.5 %collective-permute-start.34 = (bf16[768,2048]{1,0:T(8,128)(2,1)}, bf16[768,2048]{1,0:T(8,128)(2,1)}, u32[]{:S(2)}, u32[]{:S(2)}) collective-permute-start(bf16[768,2048]{1,0:T(8,128)(2,1)} %pad_maximum_fusion.5), channel_id=1, source_target_pairs={{0,1},{1,0},{2,3},{3,2},{4,5},{5,4},{6,7},{7,6},{8,9},{9,8},{10,11... | collective-permute-start | bytes 9437192 | tf_op jit(solution)/shard_map/ppermute | solution.py:50
  130.5 13.6 %collective-permute-start.32 = (bf16[128,2048]{1,0:T(8,128)(2,1)}, bf16[128,2048]{1,0:T(8,128)(2,1)}, u32[]{:S(2)}, u32[]{:S(2)}) collective-permute-start(bf16[128,2048]{1,0:T(8,128)(2,1)} %slice.267), channel_id=1, source_target_pairs={{0,4},{4,0},{1,5},{5,1},{2,6},{6,2},{3,7},{7,3},{8,12},{12,8},{9,1... | collective-permute-start | bytes 1572872 | tf_op jit(solution)/shard_map/ppermute | solution.py:50
  132.7 13.4 %collective-permute-start.33 = (bf16[128,2048]{1,0:T(8,128)(2,1)}, bf16[128,2048]{1,0:T(8,128)(2,1)}, u32[]{:S(2)}, u32[]{:S(2)}) collective-permute-start(bf16[128,2048]{1,0:T(8,128)(2,1)} %slice.268), channel_id=1, source_target_pairs={{0,2},{2,0},{1,3},{3,1},{4,6},{6,4},{5,7},{7,5},{8,10},{10,8},{9,1... | collective-permute-start | bytes 1572872 | tf_op jit(solution)/shard_map/ppermute | solution.py:50
  138.7 499.7 %reduce-scatter.6.cloned.1.call-start = ((), (), s32[]{:S(2)}) async-start(), calls=%async_computation.16 | async-start | bytes 5242880 | tf_op jit(solution)/shard_map/reduce_scatter | solution.py:135
  212.6 25.3 %collective-permute-start.9 = (bf16[2,128,2048]{2,1,0:T(8,128)(2,1)S(1)}, bf16[2,128,2048]{2,1,0:T(8,128)(2,1)S(1)}, u32[]{:S(2)}, u32[]{:S(2)}) collective-permute-start(bf16[2,128,2048]{2,1,0:T(8,128)(2,1)S(1)} %slice_bitcast_fusion.4), channel_id=1, source_target_pairs={{0,2},{2,0},{1,3},{3,1},{4,6},{6,4},{5,7},{7,5},{8,10},{10,8},{9,1... | collective-permute-start | bytes 3145736 | tf_op jit(solution)/shard_map/cond/branch_1_fun/ppermute | solution.py:50
  213.5 25.0 %collective-permute-start.11 = (bf16[2,128,2048]{2,1,0:T(8,128)(2,1)S(1)}, bf16[2,128,2048]{2,1,0:T(8,128)(2,1)S(1)}, u32[]{:S(2)}, u32[]{:S(2)}) collective-permute-start(bf16[2,128,2048]{2,1,0:T(8,128)(2,1)S(1)} %slice_bitcast_fusion.1), channel_id=1, source_target_pairs={{0,4},{4,0},{1,5},{5,1},{2,6},{6,2},{3,7},{7,3},{8,12},{12,8},{9,1... | collective-permute-start | bytes 3145736 | tf_op jit(solution)/shard_map/cond/branch_1_fun/ppermute | solution.py:50
  239.3 13.0 %collective-permute-start.10 = (bf16[128,2048]{1,0:T(8,128)(2,1)S(1)}, bf16[128,2048]{1,0:T(8,128)(2,1)S(1)}, u32[]{:S(2)}, u32[]{:S(2)}) collective-permute-start(bf16[128,2048]{1,0:T(8,128)(2,1)S(1)} %fusion.2), channel_id=1, source_target_pairs={{0,4},{4,0},{1,5},{5,1},{2,6},{6,2},{3,7},{7,3},{8,12},{12,8},{9,1... | collective-permute-start | bytes 1572872 | tf_op jit(solution)/shard_map/cond/branch_1_fun/ppermute | solution.py:50
  255.5 23.1 %collective-permute-start.13 = (bf16[256,2048]{1,0:T(8,128)(2,1)S(1)}, bf16[256,2048]{1,0:T(8,128)(2,1)S(1)}, u32[]{:S(2)}, u32[]{:S(2)}) collective-permute-start(bf16[256,2048]{1,0:T(8,128)(2,1)S(1)} %get-tuple-element.288), channel_id=1, source_target_pairs={{0,2},{2,0},{1,3},{3,1},{4,6},{6,4},{5,7},{7,5},{8,10},{10,8},{9,1... | collective-permute-start | bytes 3145736 | tf_op jit(solution)/shard_map/cond/branch_1_fun/ppermute | solution.py:50
  256.7 22.9 %collective-permute-start.14 = (bf16[256,2048]{1,0:T(8,128)(2,1)S(1)}, bf16[256,2048]{1,0:T(8,128)(2,1)S(1)}, u32[]{:S(2)}, u32[]{:S(2)}) collective-permute-start(bf16[256,2048]{1,0:T(8,128)(2,1)S(1)} %get-tuple-element.288), channel_id=1, source_target_pairs={{0,4},{4,0},{1,5},{5,1},{2,6},{6,2},{3,7},{7,3},{8,12},{12,8},{9,1... | collective-permute-start | bytes 3145736 | tf_op jit(solution)/shard_map/cond/branch_1_fun/ppermute | solution.py:50
  280.1 19.8 %collective-permute-start.17 = (bf16[768,2048]{1,0:T(8,128)(2,1)S(1)}, bf16[768,2048]{1,0:T(8,128)(2,1)S(1)}, u32[]{:S(2)}, u32[]{:S(2)}) collective-permute-start(bf16[768,2048]{1,0:T(8,128)(2,1)S(1)} %pad_maximum_fusion), channel_id=1, source_target_pairs={{0,1},{1,0},{2,3},{3,2},{4,5},{5,4},{6,7},{7,6},{8,9},{9,8},{10,11... | collective-permute-start | bytes 9437192 | tf_op jit(solution)/shard_map/cond/branch_1_fun/ppermute | solution.py:50
  280.3 14.4 %collective-permute-start.15 = (bf16[128,2048]{1,0:T(8,128)(2,1)S(1)}, bf16[128,2048]{1,0:T(8,128)(2,1)S(1)}, u32[]{:S(2)}, u32[]{:S(2)}) collective-permute-start(bf16[128,2048]{1,0:T(8,128)(2,1)S(1)} %slice.253), channel_id=1, source_target_pairs={{0,4},{4,0},{1,5},{5,1},{2,6},{6,2},{3,7},{7,3},{8,12},{12,8},{9,1... | collective-permute-start | bytes 1572872 | tf_op jit(solution)/shard_map/cond/branch_1_fun/ppermute | solution.py:50
  281.9 14.1 %collective-permute-start.16 = (bf16[128,2048]{1,0:T(8,128)(2,1)S(1)}, bf16[128,2048]{1,0:T(8,128)(2,1)S(1)}, u32[]{:S(2)}, u32[]{:S(2)}) collective-permute-start(bf16[128,2048]{1,0:T(8,128)(2,1)S(1)} %slice.254), channel_id=1, source_target_pairs={{0,2},{2,0},{1,3},{3,1},{4,6},{6,4},{5,7},{7,5},{8,10},{10,8},{9,1... | collective-permute-start | bytes 1572872 | tf_op jit(solution)/shard_map/cond/branch_1_fun/ppermute | solution.py:50
  362.8 25.3 %collective-permute-start.43 = (bf16[2,128,2048]{2,1,0:T(8,128)(2,1)S(1)}, bf16[2,128,2048]{2,1,0:T(8,128)(2,1)S(1)}, u32[]{:S(2)}, u32[]{:S(2)}) collective-permute-start(bf16[2,128,2048]{2,1,0:T(8,128)(2,1)S(1)} %slice_bitcast_fusion.18), channel_id=1, source_target_pairs={{0,2},{2,0},{1,3},{3,1},{4,6},{6,4},{5,7},{7,5},{8,10},{10,8},{9,1... | collective-permute-start | bytes 3145736 | tf_op jit(solution)/shard_map/ppermute | solution.py:50
  364.5 25.0 %collective-permute-start.45 = (bf16[2,128,2048]{2,1,0:T(8,128)(2,1)S(1)}, bf16[2,128,2048]{2,1,0:T(8,128)(2,1)S(1)}, u32[]{:S(2)}, u32[]{:S(2)}) collective-permute-start(bf16[2,128,2048]{2,1,0:T(8,128)(2,1)S(1)} %slice_bitcast_fusion.15), channel_id=1, source_target_pairs={{0,4},{4,0},{1,5},{5,1},{2,6},{6,2},{3,7},{7,3},{8,12},{12,8},{9,1... | collective-permute-start | bytes 3145736 | tf_op jit(solution)/shard_map/ppermute | solution.py:50
  391.2 13.0 %collective-permute-start.44 = (bf16[128,2048]{1,0:T(8,128)(2,1)}, bf16[128,2048]{1,0:T(8,128)(2,1)S(1)}, u32[]{:S(2)}, u32[]{:S(2)}) collective-permute-start(bf16[128,2048]{1,0:T(8,128)(2,1)} %fusion.21), channel_id=1, source_target_pairs={{0,4},{4,0},{1,5},{5,1},{2,6},{6,2},{3,7},{7,3},{8,12},{12,8},{9,1... | collective-permute-start | bytes 1572872 | tf_op jit(solution)/shard_map/ppermute | solution.py:50
  393.5 12.8 %collective-permute-start.46 = (bf16[128,2048]{1,0:T(8,128)(2,1)}, bf16[128,2048]{1,0:T(8,128)(2,1)S(1)}, u32[]{:S(2)}, u32[]{:S(2)}) collective-permute-start(bf16[128,2048]{1,0:T(8,128)(2,1)} %fusion.22), channel_id=1, source_target_pairs={{0,2},{2,0},{1,3},{3,1},{4,6},{6,4},{5,7},{7,5},{8,10},{10,8},{9,1... | collective-permute-start | bytes 1572872 | tf_op jit(solution)/shard_map/ppermute | solution.py:50
  412.2 22.9 %collective-permute-start.47 = (bf16[256,2048]{1,0:T(8,128)(2,1)S(1)}, bf16[256,2048]{1,0:T(8,128)(2,1)S(1)}, u32[]{:S(2)}, u32[]{:S(2)}) collective-permute-start(bf16[256,2048]{1,0:T(8,128)(2,1)S(1)} %get-tuple-element.298), channel_id=1, source_target_pairs={{0,2},{2,0},{1,3},{3,1},{4,6},{6,4},{5,7},{7,5},{8,10},{10,8},{9,1... | collective-permute-start | bytes 3145736 | tf_op jit(solution)/shard_map/ppermute | solution.py:50
  412.7 22.6 %collective-permute-start.48 = (bf16[256,2048]{1,0:T(8,128)(2,1)S(1)}, bf16[256,2048]{1,0:T(8,128)(2,1)S(1)}, u32[]{:S(2)}, u32[]{:S(2)}) collective-permute-start(bf16[256,2048]{1,0:T(8,128)(2,1)S(1)} %get-tuple-element.298), channel_id=1, source_target_pairs={{0,4},{4,0},{1,5},{5,1},{2,6},{6,2},{3,7},{7,3},{8,12},{12,8},{9,1... | collective-permute-start | bytes 3145736 | tf_op jit(solution)/shard_map/ppermute | solution.py:50
  435.7 15.9 %collective-permute-start.51 = (bf16[768,2048]{1,0:T(8,128)(2,1)S(1)}, bf16[768,2048]{1,0:T(8,128)(2,1)S(1)}, u32[]{:S(2)}, u32[]{:S(2)}) collective-permute-start(bf16[768,2048]{1,0:T(8,128)(2,1)S(1)} %pad_maximum_fusion.6), channel_id=1, source_target_pairs={{0,1},{1,0},{2,3},{3,2},{4,5},{5,4},{6,7},{7,6},{8,9},{9,8},{10,11... | collective-permute-start | bytes 9437192 | tf_op jit(solution)/shard_map/ppermute | solution.py:50
  435.9 14.4 %collective-permute-start.49 = (bf16[128,2048]{1,0:T(8,128)(2,1)S(1)}, bf16[128,2048]{1,0:T(8,128)(2,1)S(1)}, u32[]{:S(2)}, u32[]{:S(2)}) collective-permute-start(bf16[128,2048]{1,0:T(8,128)(2,1)S(1)} %slice.283), channel_id=1, source_target_pairs={{0,4},{4,0},{1,5},{5,1},{2,6},{6,2},{3,7},{7,3},{8,12},{12,8},{9,1... | collective-permute-start | bytes 1572872 | tf_op jit(solution)/shard_map/ppermute | solution.py:50
  437.0 14.1 %collective-permute-start.50 = (bf16[128,2048]{1,0:T(8,128)(2,1)S(1)}, bf16[128,2048]{1,0:T(8,128)(2,1)S(1)}, u32[]{:S(2)}, u32[]{:S(2)}) collective-permute-start(bf16[128,2048]{1,0:T(8,128)(2,1)S(1)} %slice.284), channel_id=1, source_target_pairs={{0,2},{2,0},{1,3},{3,1},{4,6},{6,4},{5,7},{7,5},{8,10},{10,8},{9,1... | collective-permute-start | bytes 1572872 | tf_op jit(solution)/shard_map/ppermute | solution.py:50
  468.7 169.8 %reduce-scatter.8.cloned.1.call-start = ((), (), s32[]{:S(2)}) async-start(), calls=%async_computation.17 | async-start | bytes 5242880 | tf_op jit(solution)/shard_map/reduce_scatter | solution.py:135
  502.7 14.4 %collective-permute-start.19 = (bf16[1024,2048]{1,0:T(8,128)(2,1)}, bf16[1024,2048]{1,0:T(8,128)(2,1)S(1)}, u32[]{:S(2)}, u32[]{:S(2)}) collective-permute-start(bf16[1024,2048]{1,0:T(8,128)(2,1)} %branch_1_fun.7), channel_id=1, source_target_pairs={{0,1},{1,0},{2,3},{3,2},{4,5},{5,4},{6,7},{7,6},{8,9},{9,8},{10,11... | collective-permute-start | bytes 12582920 | tf_op jit(solution)/shard_map/cond/branch_1_fun/ppermute | solution.py:50
  521.7 28.8 %collective-permute-start.20 = (bf16[2,128,2048]{2,1,0:T(8,128)(2,1)S(1)}, bf16[2,128,2048]{2,1,0:T(8,128)(2,1)S(1)}, u32[]{:S(2)}, u32[]{:S(2)}) collective-permute-start(bf16[2,128,2048]{2,1,0:T(8,128)(2,1)S(1)} %slice_bitcast_fusion.9), channel_id=1, source_target_pairs={{0,2},{2,0},{1,3},{3,1},{4,6},{6,4},{5,7},{7,5},{8,10},{10,8},{9,1... | collective-permute-start | bytes 3145736 | tf_op jit(solution)/shard_map/cond/branch_1_fun/ppermute | solution.py:50
  523.2 27.3 %collective-permute-start.21 = (bf16[2,128,2048]{2,1,0:T(8,128)(2,1)S(1)}, bf16[2,128,2048]{2,1,0:T(8,128)(2,1)S(1)}, u32[]{:S(2)}, u32[]{:S(2)}) collective-permute-start(bf16[2,128,2048]{2,1,0:T(8,128)(2,1)S(1)} %slice_bitcast_fusion.8), channel_id=1, source_target_pairs={{0,4},{4,0},{1,5},{5,1},{2,6},{6,2},{3,7},{7,3},{8,12},{12,8},{9,1... | collective-permute-start | bytes 3145736 | tf_op jit(solution)/shard_map/cond/branch_1_fun/ppermute | solution.py:50
  553.7 157.9 %reduce-scatter.10.cloned.1.call-start = ((), (), s32[]{:S(2)}) async-start(), calls=%async_computation.18 | async-start | bytes 5242880 | tf_op jit(solution)/shard_map/reduce_scatter | solution.py:135
  563.5 13.7 %collective-permute-start.1 = (bf16[128,2048]{1,0:T(8,128)(2,1)S(1)}, bf16[128,2048]{1,0:T(8,128)(2,1)S(1)}, u32[]{:S(2)}, u32[]{:S(2)}) collective-permute-start(bf16[128,2048]{1,0:T(8,128)(2,1)S(1)} %fusion.13), channel_id=1, source_target_pairs={{0,2},{2,0},{1,3},{3,1},{4,6},{6,4},{5,7},{7,5},{8,10},{10,8},{9,1... | collective-permute-start | bytes 1572872 | tf_op jit(solution)/shard_map/cond/branch_1_fun/ppermute | solution.py:50
  565.6 13.5 %collective-permute-start = (bf16[128,2048]{1,0:T(8,128)(2,1)S(1)}, bf16[128,2048]{1,0:T(8,128)(2,1)S(1)}, u32[]{:S(2)}, u32[]{:S(2)}) collective-permute-start(bf16[128,2048]{1,0:T(8,128)(2,1)S(1)} %fusion.12), channel_id=1, source_target_pairs={{0,4},{4,0},{1,5},{5,1},{2,6},{6,2},{3,7},{7,3},{8,12},{12,8},{9,1... | collective-permute-start | bytes 1572872 | tf_op jit(solution)/shard_map/cond/branch_1_fun/ppermute | solution.py:50
  585.5 23.9 %collective-permute-start.2 = (bf16[256,2048]{1,0:T(8,128)(2,1)S(1)}, bf16[256,2048]{1,0:T(8,128)(2,1)S(1)}, u32[]{:S(2)}, u32[]{:S(2)}) collective-permute-start(bf16[256,2048]{1,0:T(8,128)(2,1)S(1)} %get-tuple-element.293), channel_id=1, source_target_pairs={{0,2},{2,0},{1,3},{3,1},{4,6},{6,4},{5,7},{7,5},{8,10},{10,8},{9,1... | collective-permute-start | bytes 3145736 | tf_op jit(solution)/shard_map/cond/branch_1_fun/ppermute | solution.py:50
  586.9 23.5 %collective-permute-start.3 = (bf16[256,2048]{1,0:T(8,128)(2,1)S(1)}, bf16[256,2048]{1,0:T(8,128)(2,1)S(1)}, u32[]{:S(2)}, u32[]{:S(2)}) collective-permute-start(bf16[256,2048]{1,0:T(8,128)(2,1)S(1)} %get-tuple-element.293), channel_id=1, source_target_pairs={{0,4},{4,0},{1,5},{5,1},{2,6},{6,2},{3,7},{7,3},{8,12},{12,8},{9,1... | collective-permute-start | bytes 3145736 | tf_op jit(solution)/shard_map/cond/branch_1_fun/ppermute | solution.py:50
  612.3 21.0 %collective-permute-start.6 = (bf16[768,2048]{1,0:T(8,128)(2,1)}, bf16[768,2048]{1,0:T(8,128)(2,1)}, u32[]{:S(2)}, u32[]{:S(2)}) collective-permute-start(bf16[768,2048]{1,0:T(8,128)(2,1)} %pad_maximum_fusion.3), channel_id=1, source_target_pairs={{0,1},{1,0},{2,3},{3,2},{4,5},{5,4},{6,7},{7,6},{8,9},{9,8},{10,11... | collective-permute-start | bytes 9437192 | tf_op jit(solution)/shard_map/cond/branch_1_fun/ppermute | solution.py:50
  613.1 14.5 %collective-permute-start.4 = (bf16[128,2048]{1,0:T(8,128)(2,1)}, bf16[128,2048]{1,0:T(8,128)(2,1)S(1)}, u32[]{:S(2)}, u32[]{:S(2)}) collective-permute-start(bf16[128,2048]{1,0:T(8,128)(2,1)} %slice.261), channel_id=1, source_target_pairs={{0,4},{4,0},{1,5},{5,1},{2,6},{6,2},{3,7},{7,3},{8,12},{12,8},{9,1... | collective-permute-start | bytes 1572872 | tf_op jit(solution)/shard_map/cond/branch_1_fun/ppermute | solution.py:50
  615.1 14.3 %collective-permute-start.5 = (bf16[128,2048]{1,0:T(8,128)(2,1)}, bf16[128,2048]{1,0:T(8,128)(2,1)S(1)}, u32[]{:S(2)}, u32[]{:S(2)}) collective-permute-start(bf16[128,2048]{1,0:T(8,128)(2,1)} %slice.262), channel_id=1, source_target_pairs={{0,2},{2,0},{1,3},{3,1},{4,6},{6,4},{5,7},{7,5},{8,10},{10,8},{9,1... | collective-permute-start | bytes 1572872 | tf_op jit(solution)/shard_map/cond/branch_1_fun/ppermute | solution.py:50
  640.8 40.9 %all-to-all-start.3 = ((bf16[8,64,1024]{2,1,0:T(8,128)(2,1)}), bf16[8,64,1024]{2,1,0:T(8,128)(2,1)S(1)}, u32[]{:S(2)}, u32[]{:S(2)}) async-start(bf16[8,64,1024]{2,1,0:T(8,128)(2,1)} %bitcast.91), calls=%async_computation.5 | async-start | bytes 2097152 | tf_op jit(solution)/shard_map/all_to_all | solution.py:502
  644.4 144.7 %reduce-scatter.12.cloned.1.call-start = ((), (), s32[]{:S(2)}) async-start(), calls=%async_computation.19 | async-start | bytes 3932160 | tf_op jit(solution)/shard_map/reduce_scatter | solution.py:135
  725.8 63.3 %all-to-all-start.5 = ((bf16[8,64,1024]{2,1,0:T(8,128)(2,1)}), bf16[8,64,1024]{2,1,0:T(8,128)(2,1)}, u32[]{:S(2)}, u32[]{:S(2)}) async-start(bf16[8,64,1024]{2,1,0:T(8,128)(2,1)} %bitcast.103), calls=%async_computation.9 | async-start | bytes 2097152 | tf_op jit(solution)/shard_map/all_to_all | solution.py:502
  730.0 85.2 %reduce-scatter.14.cloned.1.call-start = ((), (), s32[]{:S(2)}) async-start(), calls=%async_computation.20 | async-start | bytes 1310720 | tf_op jit(solution)/shard_map/reduce_scatter | solution.py:135
  754.4 31.0 %collective-permute-start.23 = (bf16[2,128,2048]{2,1,0:T(8,128)(2,1)}, bf16[2,128,2048]{2,1,0:T(8,128)(2,1)}, u32[]{:S(2)}, u32[]{:S(2)}) collective-permute-start(bf16[2,128,2048]{2,1,0:T(8,128)(2,1)} %slice_bitcast_fusion.12), channel_id=1, source_target_pairs={{0,2},{2,0},{1,3},{3,1},{4,6},{6,4},{5,7},{7,5},{8,10},{10,8},{9,1... | collective-permute-start | bytes 3145736 | tf_op jit(solution)/shard_map/cond/branch_1_fun/ppermute | solution.py:50
  756.3 29.0 %collective-permute-start.24 = (bf16[2,128,2048]{2,1,0:T(8,128)(2,1)S(1)}, bf16[2,128,2048]{2,1,0:T(8,128)(2,1)}, u32[]{:S(2)}, u32[]{:S(2)}) collective-permute-start(bf16[2,128,2048]{2,1,0:T(8,128)(2,1)S(1)} %slice_bitcast_fusion.10), channel_id=1, source_target_pairs={{0,4},{4,0},{1,5},{5,1},{2,6},{6,2},{3,7},{7,3},{8,12},{12,8},{9,1... | collective-permute-start | bytes 3145736 | tf_op jit(solution)/shard_map/cond/branch_1_fun/ppermute | solution.py:50
  757.8 22.7 %collective-permute-start.26 = (f32[8,4,64]{2,1,0:T(4,128)S(1)}, f32[8,4,64]{2,1,0:T(4,128)S(1)}, u32[]{:S(2)}, u32[]{:S(2)}) collective-permute-start(f32[8,4,64]{2,1,0:T(4,128)S(1)} %slice_select_fusion.2), channel_id=1, source_target_pairs={{0,2},{2,0},{1,3},{3,1},{4,6},{6,4},{5,7},{7,5},{8,10},{10,8},{9,1... | collective-permute-start | bytes 24584 | tf_op jit(solution)/shard_map/cond/branch_1_fun/ppermute | solution.py:122
  789.1 16.6 %all-to-all-start.6 = ((bf16[8,64,768]{2,1,0:T(8,128)(2,1)}), bf16[8,64,768]{2,1,0:T(8,128)(2,1)S(1)}, u32[]{:S(2)}, u32[]{:S(2)}) async-start(bf16[8,64,768]{2,1,0:T(8,128)(2,1)} %bitcast.316), calls=%async_computation.10 | async-start | bytes 1572864 | tf_op jit(solution)/shard_map/all_to_all | solution.py:502
  806.6 13.8 %collective-permute-start.56 = (bf16[128,2048]{1,0:T(8,128)(2,1)}, bf16[128,2048]{1,0:T(8,128)(2,1)}, u32[]{:S(2)}, u32[]{:S(2)}) collective-permute-start(bf16[128,2048]{1,0:T(8,128)(2,1)} %fusion.23), channel_id=1, source_target_pairs={{0,4},{4,0},{1,5},{5,1},{2,6},{6,2},{3,7},{7,3},{8,12},{12,8},{9,1... | collective-permute-start | bytes 1572872 | tf_op jit(solution)/shard_map/ppermute | solution.py:50
  (64 other events, 530.6 us)
Sparse Core Ops, SparseCore 0:
  18.4 29.2 all-gather.4
  49.3 62.9 all-gather.6
  113.9 148.2 all-gather.8
  264.2 78.9 all-gather.10
  468.8 74.7 reduce-scatter.5
  553.8 74.5 reduce-scatter.7
  630.7 77.2 reduce-scatter.9
  711.7 59.6 reduce-scatter.11
  789.2 26.0 reduce-scatter.13

commit v5 on v4

--- a/solution.py
+++ b/solution.py
@@ -57,8 +57,11 @@
     top = swap(near_x[:half], "y")
     low = swap(near_y[half:], "x")
     first = jnp.concatenate([own, near_x, near_y], 0)
-    last = jnp.concatenate([top, low], 0)
-    return jnp.concatenate([first, last, swap(first, "c"), swap(last, "c")], 0)
+    blocks = lax.optimization_barrier(jnp.concatenate([first, own, swap(first, "c"), own], 0))
+    last = jnp.concatenate([after(top, blocks), after(low, blocks)], 0)
+    last_other = swap(last, "c")
+    blocks = lax.dynamic_update_slice(blocks, last, (3 * 2 * half, 0))
+    return lax.dynamic_update_slice(blocks, last_other, (7 * 2 * half, 0))
 
 
 def group_sum(terms):
@@ -137,6 +140,7 @@
 
 SCALE = HEAD ** (-0.5)
 ROWS = 256
+FEED_ROWS = 512
 PARAMS = pltpu.CompilerParams(vmem_limit_bytes=56 * 2**20)
 
 
@@ -250,20 +254,22 @@
 
 def from_units(parts, unit_rows):
     _, rows, units = parts.shape
-
-    def kernel(p_ref, out_ref):
-        for m in range(8):
-            for r in range(units // unit_rows):
-                target, source = (r * 8 + m) * unit_rows, r * unit_rows
-                out_ref[:, target : target + unit_rows] = p_ref[m, :, source : source + unit_rows].astype(F32)
+    units //= 2
+
+    def kernel(p_ref, *out_refs):
+        for i, out_ref in enumerate(out_refs):
+            for m in range(8):
+                for r in range(units // unit_rows):
+                    target, source = (r * 8 + m) * unit_rows, i * units + r * unit_rows
+                    out_ref[:, target : target + unit_rows] = p_ref[m, :, source : source + unit_rows].astype(F32)
 
     step = min(rows, 16)
     return pl.pallas_call(
         kernel,
         grid=(rows // step,),
-        in_specs=[pl.BlockSpec((8, step, units), lambda i: (0, i, 0))],
-        out_specs=pl.BlockSpec((step, 8 * units), lambda i: (i, 0)),
-        out_shape=jax.ShapeDtypeStruct((rows, 8 * units), F32),
+        in_specs=[pl.BlockSpec((8, step, 2 * units), lambda i: (0, i, 0))],
+        out_specs=[pl.BlockSpec((step, 8 * units), lambda i: (i, 0))] * 2,
+        out_shape=[jax.ShapeDtypeStruct((rows, 8 * units), F32)] * 2,
         compiler_params=PARAMS,
     )(parts)
 
@@ -337,9 +343,9 @@
 
     return pl.pallas_call(
         kernel,
-        grid=(rows // ROWS,),
-        in_specs=[by_rows(ROWS, depth), whole(weight), by_rows(ROWS, 2 * units)],
-        out_specs=by_rows(ROWS, 2 * units),
+        grid=(rows // FEED_ROWS,),
+        in_specs=[by_rows(FEED_ROWS, depth), whole(weight), by_rows(FEED_ROWS, 2 * units)],
+        out_specs=by_rows(FEED_ROWS, 2 * units),
         out_shape=jax.ShapeDtypeStruct((rows, 2 * units), BF16),
         compiler_params=PARAMS,
         cost_estimate=pl.CostEstimate(
@@ -357,9 +363,9 @@
 
     return pl.pallas_call(
         kernel,
-        grid=(rows // ROWS,),
-        in_specs=[pl.BlockSpec((ROWS, depth), lambda i: (first // ROWS + i, 0)), whole(weight)],
-        out_specs=by_rows(ROWS, width),
+        grid=(rows // FEED_ROWS,),
+        in_specs=[pl.BlockSpec((FEED_ROWS, depth), lambda i: (first // FEED_ROWS + i, 0)), whole(weight)],
+        out_specs=by_rows(FEED_ROWS, width),
         out_shape=jax.ShapeDtypeStruct((rows, width), BF16),
         compiler_params=PARAMS,
         cost_estimate=pl.CostEstimate(
@@ -502,17 +508,16 @@
             return lax.all_to_all(parts, group, 0, 0, tiled=True)
 
         own_gains = jnp.stack([query_gain, key_gain, mixer_gain, feed_gain]).astype(BF16)
-        plane_gains = doubled(own_gains.reshape(1, 4, weight_rows), PLANES)
+        qkv_parts = jnp.concatenate([by_head(w_query), by_head(w_key), by_head(w_value)], 2)
+        qkv_piece = exchange(qkv_parts, GROUP).reshape(8 * weight_rows, 3 * columns)
+        out_halves = gather_planes(w_out.astype(BF16))
+        feed_parts = after(to_units(w_gate, w_up, unit_rows), qkv_piece, out_halves)
+        feed_piece = exchange(feed_parts, GROUP).reshape(8 * weight_rows, 2 * units)
+        plane_gains = doubled(after(own_gains, feed_piece).reshape(1, 4, weight_rows), PLANES)
         gains = doubled(plane_gains, GROUP).reshape(8, replicas, 4, weight_rows)
         gains = gains.transpose(2, 1, 0, 3).reshape(4, width).astype(F32)
-
-        qkv_parts = jnp.concatenate([by_head(w_query), by_head(w_key), by_head(w_value)], 2)
-        qkv_piece = exchange(qkv_parts, GROUP).reshape(8 * weight_rows, 3 * columns)
-        out_halves = gather_planes(after(w_out.astype(BF16), plane_gains))
-        feed_parts = after(to_units(w_gate, w_up, unit_rows), qkv_piece, out_halves)
-        feed_piece = exchange(feed_parts, GROUP).reshape(8 * weight_rows, 2 * units)
         group_tokens = group_gather(after(tokens, feed_piece))
-        weight_qkv = gather_planes(after(qkv_piece, plane_gains))
+        weight_qkv = gather_planes(qkv_piece)
         weight_feed = gather_planes(feed_piece)
         weight_down = gather_planes(after(w_down.astype(BF16), feed_piece))
         out_halves = out_halves.reshape(per_head, own_heads, weight_rows, width)
@@ -595,16 +600,13 @@
             for_mine = times_transposed(after(feed_grad, for_other), weight_feed, 0, half)
             sums = core_sum(for_mine, arrived)
             sends = lax.optimization_barrier(scatter_sends(sums))
-            ready = after(feed_grad, *sends)
-            gate_term = inner_t(group_hidden_in, ready[:, :units]).astype(BF16)
-            up_term = inner_t(group_hidden_in, ready[:, units:]).astype(BF16)
-            return gate_term, up_term, *scatter_start(sums, sends, gate_term, up_term)
-
-        gate_term, up_term, top, bottom = region(
+            feed_term = inner_t(group_hidden_in, after(feed_grad, *sends)).astype(BF16)
+            return feed_term, *scatter_start(sums, sends, feed_term)
+
+        feed_term, top, bottom = region(
             feed_mix, segment_ids, after(group_result_grad, down_term), weight_down, weight_feed, both, group_hidden_in
         )
-        gate_share = scatter_planes(gate_term)
-        up_share = scatter_planes(up_term)
+        feed_share = scatter_planes(feed_term)
 
         def to_mixer(top, bottom, branch, r_a):
             hidden_in_grad = grad_out + scatter_end(top, bottom)
@@ -615,13 +617,12 @@
         group_branch_grad = after(group_branch_grad, down_share)
         mixed_grad = matmul_t(group_branch_grad, weight_out).astype(BF16)
         q_back, k_back, v_grad, means = attend_back(*attention, mixed_grad)
-        gate_back = exchange(after(gate_share, group_branch_grad).reshape(8, weight_rows, units), GROUP)
-        means = group_sum(after(means, gate_back).T).T / width
+        means = group_sum(means.T).T / width
         grads, head_terms = qkv_grads(projected, q_back, k_back, v_grad, info, means, gain_q, gain_k)
-        up_back = exchange(after(up_share, means).reshape(8, weight_rows, units), GROUP)
+        feed_back = exchange(after(feed_share, means).reshape(8, weight_rows, 2 * units), GROUP)
         qkv_term = inner_t(group_tokens, grads).astype(BF16)
         qkv_share = scatter_planes(qkv_term)
-        out_term = inner_t(mixed_low, after(group_branch_grad, qkv_term, up_share))
+        out_term = inner_t(mixed_low, after(group_branch_grad, qkv_term, feed_share))
         out_parts = out_term.astype(BF16).reshape(own_heads, per_head, weight_rows, width)
         out_parts = lax.all_to_all(out_parts.transpose(1, 0, 2, 3), head_axes, 0, 0, tiled=True)
         out_share = scatter_planes(out_parts.reshape(replicas * weight_rows, width))
@@ -634,20 +635,18 @@
         gain_terms = gain_terms.reshape(4, replicas, 8, weight_rows).transpose(2, 1, 0, 3)
         gain_terms = gain_terms.reshape(count, 4, weight_rows)
 
-        def to_tokens(grads, weight_qkv, gain_terms, gate_back, down_share):
+        def to_tokens(grads, weight_qkv, gain_terms, down_share, hidden_in_grad):
             mine, other = by_core(matmul_t, grads, weight_qkv)
             sums = core_sum(mine, swap(other, "c"))
             sends = scatter_sends(sums)
-            done = halved(gain_terms, GROUP), from_units(gate_back, unit_rows), down_share.astype(F32)
-            return scatter_start(sums, sends), *done
-
-        token_sums, gain_terms, g_w_gate, g_w_down = region(
-            to_tokens, segment_ids, after(grads, out_parts), weight_qkv, gain_terms, gate_back, down_share
+            done = halved(gain_terms, GROUP), down_share.astype(F32)
+            return hidden_in_grad + scatter_end(*scatter_start(sums, sends, *done)), *done
+
+        g_tokens, gain_terms, g_w_down = region(
+            to_tokens, segment_ids, after(grads, out_parts), weight_qkv, gain_terms, down_share, hidden_in_grad
         )
         g_gains = halved(gain_terms, PLANES)[0]
-        qkv_back = exchange(after(qkv_share, *token_sums, up_back).reshape(8, weight_rows, 3 * columns), GROUP)
-        top, bottom = token_sums
-        g_tokens = hidden_in_grad + scatter_end(after(top, qkv_back), after(bottom, qkv_back))
+        qkv_back = exchange(after(qkv_share, g_tokens, feed_back).reshape(8, weight_rows, 3 * columns), GROUP)
         heads_of = [
             [(e * own_heads + j) * (8 // per_head) + t for j in range(own_heads)]
             for t in range(8 // per_head)
@@ -655,7 +654,7 @@
         ]
         g_qkv = from_heads(qkv_back, heads_of)
         g_w_out = out_share.astype(F32)
-        g_w_up = from_units(after(up_back, token_sums[0]), unit_rows)
+        g_w_gate, g_w_up = from_units(after(feed_back, g_tokens), unit_rows)
 
         return (
             out_tokens,

time: 841 us -> 824 us (0.980)
    ppermute x50, waiting for transfers between devices: 238 us -> 250 us  [swap(): return lax.ppermute(block, axis, [(0, 1), (1, 0)])]
    unnamed x82 -> x96, local copies, waits for them, and re-layouts: 28.9 us -> 22.5 us
    dot_general x5 -> x4, matrix products: 54.4 us -> 49.9 us  [inner_t(): lax.dot_general(left, right, (((0,), (0,)), ((), ())), preferred_element_...]
  transfers between devices with their start and end apart: 72 -> 70, of which waited for: 46 -> 51; matrix products, arithmetic and copies ran while one was open for 25% -> 24% of each run, Pallas kernels for 17% -> 16%
where the time goes in v5:
time: 824 us; the launch traced here: 815 us
  waiting for transfers between devices  303 us (37%)
  Pallas kernels  137 us (17%)
  matrix products  96.4 us (12%)
  local copies, waits for them, and re-layouts  70.9 us (9%)
  other arithmetic  70.7 us (9%)
  starting transfers between devices  61.6 us (7%)
  blocking collectives  58.6 us (7%)
  between operations  16.2 us (2%)
    ppermute x50, waiting for transfers between devices, swap(): return lax.ppermute(block, axis, [(0, 1), (1, 0)])  250 us
    dot_general x4, matrix products, inner_t(): lax.dot_general(left, right, (((0,), (0,)), ((), ())), preferred_element_...  49.9 us
    all_to_all x2, blocking collectives, exchange(): return lax.all_to_all(parts, group, 0, 0, tiled=True)  48.6 us
    ppermute x50, starting transfers between devices, swap(): return lax.ppermute(block, axis, [(0, 1), (1, 0)])  41.7 us
    pallas_call x2, Pallas kernels, times_transposed(): pl.pallas_call(kernel, grid=(rows // FEED_ROWS,), in_specs=[pl.BlockSpec(...  28.9 us
    pallas_call x1, Pallas kernels, attend_back(): pl.pallas_call(attend_back_kernel, grid=(blocks, heads), in_specs=specs +...  28.4 us
    ppermute x5, waiting for transfers between devices, halved(): lax.ppermute(jnp.where(low_side, second, first), axis, [(i, i ^ step) for...  26.6 us
    dot_general x5, matrix products, matmul(): return jnp.dot(left, right, preferred_element_type=F32)  24.7 us
  transfers between devices with their start and end apart: 70, of which 51 were waited for; matrix products, arithmetic and copies ran while one was open for 24% of the time, Pallas kernels for 16%

profile of v5, /device:TPU:0, one launch (start us, length us, event | category | flops | bytes accessed | tf_op | source)
XLA Modules:
  0.0 815.4 jit_solution(16955927344824055439)
XLA Ops:
  13.1 17.6 %all_to_all.30 = bf16[8,64,768]{2,1,0:T(8,128)(2,1)} all-to-all(bf16[8,64,768]{2,1,0:T(8,128)(2,1)S(1)} %pad_maximum_fusion.10), channel_id=1, replica_groups=mesh['zh'=2,'zl'=2,'y'=2,'x'=2,'c'=2] {'y','x','c'}, dimensions={0} | all-to-all | bytes 1572864 | tf_op jit(solution)/shard_map/all_to_all | solution.py:508
  30.8 4.2 shard_map.246
  35.0 5.9 all-gather.5.cloned.1.call-done
  40.8 30.9 %all_to_all.31 = bf16[8,64,2048]{2,1,0:T(8,128)(2,1)} all-to-all(bf16[8,64,2048]{2,1,0:T(8,128)(2,1)} %shard_map.246), channel_id=1, replica_groups=mesh['zh'=2,'zl'=2,'y'=2,'x'=2,'c'=2] {'y','x','c'}, dimensions={0} | all-to-all | bytes 4194304 | tf_op jit(solution)/shard_map/all_to_all | solution.py:508
  88.9 20.2 %collective-permute-done.30 = bf16[256,2048]{1,0:T(8,128)(2,1)S(1)} collective-permute-done((bf16[256,2048]{1,0:T(8,128)(2,1)S(1)}, bf16[256,2048]{1,0:T(8,128)(2,1)S(1)}, u32[]{:S(2)}, u32[]{:S(2)}) %collective-permute-start.30) | collective-permute-done | bytes 1048608 | tf_op jit(solution)/shard_map/ppermute | solution.py:50
  113.6 5.7 fusion.19
  133.2 8.8 %collective-permute-done.34 = bf16[128,2048]{1,0:T(8,128)(2,1)S(1)} collective-permute-done((bf16[128,2048]{1,0:T(8,128)(2,1)S(1)}, bf16[128,2048]{1,0:T(8,128)(2,1)S(1)}, u32[]{:S(2)}, u32[]{:S(2)}) %collective-permute-start.34) | collective-permute-done | bytes 524320 | tf_op jit(solution)/shard_map/ppermute | solution.py:50
  150.2 4.6 all_to_all.32
  159.5 10.0 %fusion.29.p_ref = f32[2048,768]{1,0:T(8,128)S(1)} fusion(bf16[2048,2048]{1,0:T(8,128)(2,1)} %constant_dynamic-update-slice_fusion.64, bf16[2048,768]{1,0:T(8,128)(2,1)} %all-gather.7.cloned.1.call-done), kind=kOutput, calls=%fused_computation.246 | convolution fusion | flops 6442450944 | bytes 17825792 | tf_op jit(solution)/shard_map/dot_general | solution.py:23
  181.9 115.6 %conditional.4 = (bf16[2048,256]{1,0:T(8,128)(2,1)S(1)}, f32[256,2048]{1,0:T(8,128)S(1)}, f32[256,2048]{1,0:T(8,128)}, bf16[2048,2048]{1,0:T(8,128)(2,1)}, f32[256,1]{0,1:T(1,128)S(1)}) conditional(s32[]{:T(128)} %bitcast.42, () %tuple.76, (f32[2048,768]{1,0:T(8,128)}, f32[2048,4]{0,1:T(4,128)S(1)}, f32[2048,128]{1,0:T(8,128)}, ...), branch_computations={%region_4.5_spmd, %region_5.7_spmd} | conditional | flops 4325376512 | bytes 175198848 | solution.py:46
  183.3 16.9 %branch_1_fun.4 = bf16[2,2,512,256]{3,2,1,0:T(8,128)(2,1)S(1)} custom-call(f32[2,2,512,768]{3,2,1,0:T(8,128)} %bitcast.282, f32[2,2,512,768]{3,2,1,0:T(8,128)} %bitcast.283, f32[2,2,512,768]{3,2,1,0:T(8,128)} %bitcast.284, f32[2,2,512,4]{3,2,1,0:T(8,128)} %bitcast.301, f32[2,2,512,128]{3,2,1,0:T(8,128)} %bitcast.298, f32[2,2,512,128]{3,2,1,0:T(8,128)} %bitcast.297, ...), custom_call_target="tpu_custom_call" | custom-call | flops 2147483648 | bytes 8388608 | tf_op jit(solution)/shard_map/cond/branch_1_fun/pallas_call | solution.py:404
  201.6 7.1 collective-permute-done.8
  212.4 23.0 %collective-permute-done.9 = bf16[2,128,2048]{2,1,0:T(8,128)(2,1)S(1)} collective-permute-done((bf16[2,128,2048]{2,1,0:T(8,128)(2,1)S(1)}, bf16[2,128,2048]{2,1,0:T(8,128)(2,1)S(1)}, u32[]{:S(2)}, u32[]{:S(2)}) %collective-permute-start.9) | collective-permute-done | bytes 1048608 | tf_op jit(solution)/shard_map/cond/branch_1_fun/ppermute | solution.py:50
  238.9 11.6 %collective-permute-done.10 = bf16[128,2048]{1,0:T(8,128)(2,1)S(1)} collective-permute-done((bf16[128,2048]{1,0:T(8,128)(2,1)S(1)}, bf16[128,2048]{1,0:T(8,128)(2,1)S(1)}, u32[]{:S(2)}, u32[]{:S(2)}) %collective-permute-start.10) | collective-permute-done | bytes 524320 | tf_op jit(solution)/shard_map/cond/branch_1_fun/ppermute | solution.py:50
  255.8 21.1 %collective-permute-done.13 = bf16[256,2048]{1,0:T(8,128)(2,1)S(1)} collective-permute-done((bf16[256,2048]{1,0:T(8,128)(2,1)S(1)}, bf16[256,2048]{1,0:T(8,128)(2,1)S(1)}, u32[]{:S(2)}, u32[]{:S(2)}) %collective-permute-start.13) | collective-permute-done | bytes 1048608 | tf_op jit(solution)/shard_map/cond/branch_1_fun/ppermute | solution.py:50
  287.3 4.9 collective-permute-done.17
  297.6 24.5 %shard_map.247 = (f32[2048,2048]{1,0:T(8,128)}, bf16[2048,1024]{1,0:T(8,128)(2,1)}) custom-call(bf16[2048,2048]{1,0:T(8,128)(2,1)} %get-tuple-element.169.v_ref, bf16[2048,2048]{1,0:T(8,128)(2,1)} %all-gather.9.cloned.1.call-done.w_ref), custom_call_target="tpu_custom_call" | custom-call | flops 17179869184 | bytes 29360128 | tf_op jit(solution)/shard_map/pallas_call | solution.py:319
  322.1 14.3 %all-gather.11.cloned.1.call-done = bf16[1024,2048]{1,0:T(8,128)(2,1)} async-done(((bf16[256,2048]{1,0:T(8,128)(2,1)}), bf16[1024,2048]{1,0:T(8,128)(2,1)}) %all-gather.11.cloned.1.call-update) | async-done | bytes 4194320 | tf_op jit(solution)/shard_map/all_gather | solution.py:134
  336.4 7.5 convolution_convert_fusion.3
  344.1 7.0 collective-permute-done.44
  351.1 4.7 add_convert_fusion.3
  359.2 22.0 %collective-permute-done.45 = bf16[2,128,2048]{2,1,0:T(8,128)(2,1)S(1)} collective-permute-done((bf16[2,128,2048]{2,1,0:T(8,128)(2,1)S(1)}, bf16[2,128,2048]{2,1,0:T(8,128)(2,1)S(1)}, u32[]{:S(2)}, u32[]{:S(2)}) %collective-permute-start.45) | collective-permute-done | bytes 1048608 | tf_op jit(solution)/shard_map/ppermute | solution.py:50
  387.3 10.2 %collective-permute-done.46 = bf16[128,2048]{1,0:T(8,128)(2,1)} collective-permute-done((bf16[128,2048]{1,0:T(8,128)(2,1)}, bf16[128,2048]{1,0:T(8,128)(2,1)}, u32[]{:S(2)}, u32[]{:S(2)}) %collective-permute-start.46) | collective-permute-done | bytes 524320 | tf_op jit(solution)/shard_map/ppermute | solution.py:50
  408.2 21.4 %collective-permute-done.49 = bf16[256,2048]{1,0:T(8,128)(2,1)S(1)} collective-permute-done((bf16[256,2048]{1,0:T(8,128)(2,1)S(1)}, bf16[256,2048]{1,0:T(8,128)(2,1)S(1)}, u32[]{:S(2)}, u32[]{:S(2)}) %collective-permute-start.49) | collective-permute-done | bytes 1048608 | tf_op jit(solution)/shard_map/ppermute | solution.py:50
  436.4 8.3 %collective-permute-done.53 = bf16[128,2048]{1,0:T(8,128)(2,1)S(1)} collective-permute-done((bf16[128,2048]{1,0:T(8,128)(2,1)S(1)}, bf16[128,2048]{1,0:T(8,128)(2,1)S(1)}, u32[]{:S(2)}, u32[]{:S(2)}) %collective-permute-start.53) | collective-permute-done | bytes 524320 | tf_op jit(solution)/shard_map/ppermute | solution.py:50
  452.1 11.4 %convolution_convert_fusion.2 = bf16[1024,2048]{1,0:T(8,128)(2,1)} fusion(bf16[2048,1024]{1,0:T(8,128)(2,1)S(1)} %copy-done.24, bf16[2048,2048]{1,0:T(8,128)(2,1)S(1)} %constant_dynamic-update-slice_fusion.62), kind=kOutput, calls=%fused_computation.91 | convolution fusion | flops 8592031744 | bytes 16777216 | tf_op jit(solution)/shard_map/dot_general | solution.py:31
  463.6 82.0 %conditional.5 = (bf16[2048,2048]{0,1:T(8,128)(2,1)}, f32[2,128,2048]{2,1,0:T(8,128)}, f32[2,128,2048]{2,1,0:T(8,128)}) conditional(s32[]{:T(128)} %bitcast.42, () %tuple.88, (bf16[2048,2048]{1,0:T(8,128)(2,1)}, bf16[1024,2048]{1,0:T(8,128)(2,1)}, f32[2048,2048]{1,0:T(8,128)}, bf16[2048,2048]{1,0:T(8,128)(2,1)}, ...), branch_computations={%region_9.10_spmd, %region_10.11_spmd} | conditional | flops 42965401600 | bytes 159383712 | solution.py:46
  463.6 19.6 %branch_1_fun.5.v_ref = bf16[2048,2048]{1,0:T(8,128)(2,1)} custom-call(bf16[2048,2048]{1,0:T(8,128)(2,1)} %get-tuple-element.77.g_ref, bf16[1024,2048]{1,0:T(8,128)(2,1)} %get-tuple-element.78.w_ref, f32[2048,2048]{1,0:T(8,128)} %get-tuple-element.79.both_ref), custom_call_target="tpu_custom_call" | custom-call | flops 8589934592 | bytes 33554432 | tf_op jit(solution)/shard_map/cond/branch_1_fun/pallas_call | solution.py:344
  483.2 14.5 %branch_1_fun.6 = bf16[1024,2048]{1,0:T(8,128)(2,1)} custom-call(bf16[2048,2048]{1,0:T(8,128)(2,1)} %branch_1_fun.5.v_ref, bf16[2048,2048]{1,0:T(8,128)(2,1)} %get-tuple-element.80.w_ref), custom_call_target="tpu_custom_call" | custom-call | flops 8589934592 | bytes 8388608 | tf_op jit(solution)/shard_map/cond/branch_1_fun/pallas_call | solution.py:364
  497.8 14.4 %branch_1_fun.7 = bf16[1024,2048]{1,0:T(8,128)(2,1)} custom-call(bf16[2048,2048]{1,0:T(8,128)(2,1)} %branch_1_fun.5.v_ref, bf16[2048,2048]{1,0:T(8,128)(2,1)} %get-tuple-element.80.w_ref), custom_call_target="tpu_custom_call" | custom-call | flops 8589934592 | bytes 8388608 | tf_op jit(solution)/shard_map/cond/branch_1_fun/pallas_call | solution.py:364
  512.2 4.4 add_convert_fusion.1
  518.0 22.4 %convert_bitcast_fusion = bf16[2048,2048]{0,1:T(8,128)(2,1)} fusion(bf16[2048,2048]{1,0:T(8,128)(2,1)S(1)} %copy-done.13, bf16[2048,2048]{1,0:T(8,128)(2,1)} %get-tuple-element.85), kind=kOutput, calls=%fused_computation.31 | convolution fusion | flops 17184063488 | bytes 25165824 | tf_op jit(solution)/shard_map/cond/branch_1_fun/dot_general | solution.py:31
  554.0 67.3 %conditional.6 = (f32[256,2048]{1,0:T(8,128)}, bf16[2048,2048]{1,0:T(8,128)(2,1)}, f32[1,4,8,64]{3,2,1,0:T(8,128)S(1)}) conditional(s32[]{:T(128)} %bitcast.42, () %tuple.87, (f32[2,128,2048]{2,1,0:T(8,128)}, f32[2,128,2048]{2,1,0:T(8,128)}, f32[256,2048]{1,0:T(8,128)}, f32[256,1]{0,1:T(1,128)S(1)}, f32[1,2048]{1,0:T(1,128)S(1)}, ...), branch_computations={%region_11.12_spmd, %region_12.15_spmd} | conditional | flops 17824512 | bytes 93374832 | solution.py:46
  559.7 9.2 %collective-permute-done.1 = bf16[128,2048]{1,0:T(8,128)(2,1)S(1)} collective-permute-done((bf16[128,2048]{1,0:T(8,128)(2,1)S(1)}, bf16[128,2048]{1,0:T(8,128)(2,1)S(1)}, u32[]{:S(2)}, u32[]{:S(2)}) %collective-permute-start.1) | collective-permute-done | bytes 524320 | tf_op jit(solution)/shard_map/cond/branch_1_fun/ppermute | solution.py:50
  579.7 21.3 %collective-permute-done.2 = bf16[256,2048]{1,0:T(8,128)(2,1)S(1)} collective-permute-done((bf16[256,2048]{1,0:T(8,128)(2,1)S(1)}, bf16[256,2048]{1,0:T(8,128)(2,1)S(1)}, u32[]{:S(2)}, u32[]{:S(2)}) %collective-permute-start.2) | collective-permute-done | bytes 1048608 | tf_op jit(solution)/shard_map/cond/branch_1_fun/ppermute | solution.py:50
  611.2 5.4 collective-permute-done.6
  621.3 6.8 convolution_convert_fusion.6
  628.1 28.4 %shard_map.248 = (f32[2,2,512,256]{3,2,1,0:T(8,128)}, f32[2,2,512,256]{3,2,1,0:T(8,128)}, bf16[2,2,512,256]{3,2,1,0:T(8,128)(2,1)}, f32[2,2,2,512,2]{4,3,2,1,0:T(8,128)}) custom-call(f32[2,2,512,768]{3,2,1,0:T(8,128)} %bitcast.279, f32[2,2,512,768]{3,2,1,0:T(8,128)} %bitcast.280, f32[2,2,512,768]{3,2,1,0:T(8,128)} %bitcast.281, f32[2,2,512,4]{3,2,1,0:T(8,128)} %bitcast.292, ...), custom_call_target="tpu_custom_call" | custom-call | flops 5368709120 | bytes 12582912 | tf_op jit(solution)/shard_map/pallas_call | solution.py:424
  669.0 6.9 shard_map.249
  677.7 10.4 %convolution_convert_fusion.4 = bf16[2048,768]{1,0:T(8,128)(2,1)} fusion(bf16[2048,2048]{1,0:T(8,128)(2,1)} %constant_dynamic-update-slice_fusion.64, bf16[2048,768]{1,0:T(8,128)(2,1)S(1)} %get-tuple-element.191), kind=kOutput, calls=%fused_computation.93 | convolution fusion | flops 6444023808 | bytes 14680064 | tf_op jit(solution)/shard_map/dot_general | solution.py:31
  688.3 4.2 copy.245
  692.4 5.7 convolution_convert_fusion.5
  698.3 5.5 all_to_all.33
  708.4 76.0 %conditional.7 = (f32[256,2048]{1,0:T(8,128)}, f32[4,4,64]{2,1,0:T(4,128)}, f32[256,2048]{1,0:T(8,128)}, f32[2,4,64]{2,1,0:T(4,128)S(1)}, f32[2,4,64]{2,1,0:T(4,128)S(1)}) conditional(s32[]{:T(128)} %bitcast.42, () %tuple.86, (bf16[2048,768]{1,0:T(8,128)(2,1)}, bf16[2048,768]{1,0:T(8,128)(2,1)}, f32[8,4,4,64]{3,0,1,2:T(8,128)S(1)}, ...), branch_computations={%region_19.20_spmd, %region_20.21_spmd} | conditional | flops 6460822528 | bytes 101069360 | solution.py:46
  708.4 7.9 convolution_convert_fusion.1
  723.8 7.1 add_convert_fusion.2
  738.3 23.4 %collective-permute-done.25 = f32[8,4,64]{2,1,0:T(4,128)S(1)} collective-permute-done((f32[8,4,64]{2,1,0:T(4,128)S(1)}, f32[8,4,64]{2,1,0:T(4,128)S(1)}, u32[]{:S(2)}, u32[]{:S(2)}) %collective-permute-start.25) | collective-permute-done | bytes 8224 | tf_op jit(solution)/shard_map/cond/branch_1_fun/ppermute | solution.py:125
  768.7 12.2 %collective-permute-done.27 = bf16[128,2048]{1,0:T(8,128)(2,1)S(1)} collective-permute-done((bf16[128,2048]{1,0:T(8,128)(2,1)S(1)}, bf16[128,2048]{1,0:T(8,128)(2,1)S(1)}, u32[]{:S(2)}, u32[]{:S(2)}) %collective-permute-start.27) | collective-permute-done | bytes 524320 | tf_op jit(solution)/shard_map/cond/branch_1_fun/ppermute | solution.py:50
  (448 shorter events, 244.7 us)
Async XLA Ops:
  7.2 33.6 %all-gather.5.cloned.1.call-start = ((), (), s32[]{:S(2)}) async-start(), calls=%async_computation.10 | async-start | bytes 1310720 | tf_op jit(solution)/shard_map/all_gather | solution.py:134
  9.1 150.4 %all-gather.7.cloned.1.call-start = ((), (), s32[]{:S(2)}) async-start(), calls=%async_computation.11 | async-start | bytes 3932160 | tf_op jit(solution)/shard_map/all_gather | solution.py:134
  30.7 266.9 %all-gather.9.cloned.1.call-start = ((), (), s32[]{:S(2)}) async-start(), calls=%async_computation.12 | async-start | bytes 10485760 | tf_op jit(solution)/shard_map/all_gather | solution.py:134
  71.8 264.6 %all-gather.11.cloned.1.call-start = ((), (), s32[]{:S(2)}) async-start(), calls=%async_computation.13 | async-start | bytes 5242880 | tf_op jit(solution)/shard_map/all_gather | solution.py:134
  84.8 24.3 %collective-permute-start.30 = (bf16[256,2048]{1,0:T(8,128)(2,1)S(1)}, bf16[256,2048]{1,0:T(8,128)(2,1)S(1)}, u32[]{:S(2)}, u32[]{:S(2)}) collective-permute-start(bf16[256,2048]{1,0:T(8,128)(2,1)S(1)} %copy-done.3), channel_id=1, source_target_pairs={{0,2},{2,0},{1,3},{3,1},{4,6},{6,4},{5,7},{7,5},{8,10},{10,8},{9,1... | collective-permute-start | bytes 3145736 | tf_op jit(solution)/shard_map/ppermute | solution.py:50
  85.4 24.7 %collective-permute-start.31 = (bf16[256,2048]{1,0:T(8,128)(2,1)S(1)}, bf16[256,2048]{1,0:T(8,128)(2,1)S(1)}, u32[]{:S(2)}, u32[]{:S(2)}) collective-permute-start(bf16[256,2048]{1,0:T(8,128)(2,1)S(1)} %copy-done.3), channel_id=1, source_target_pairs={{0,4},{4,0},{1,5},{5,1},{2,6},{6,2},{3,7},{7,3},{8,12},{12,8},{9,1... | collective-permute-start | bytes 3145736 | tf_op jit(solution)/shard_map/ppermute | solution.py:50
  112.0 18.7 %collective-permute-start.32 = (bf16[768,2048]{1,0:T(8,128)(2,1)}, bf16[768,2048]{1,0:T(8,128)(2,1)}, u32[]{:S(2)}, u32[]{:S(2)}) collective-permute-start(bf16[768,2048]{1,0:T(8,128)(2,1)} %pad_maximum_fusion.3), channel_id=1, source_target_pairs={{0,1},{1,0},{2,3},{3,2},{4,5},{5,4},{6,7},{7,6},{8,9},{9,8},{10,11... | collective-permute-start | bytes 9437192 | tf_op jit(solution)/shard_map/ppermute | solution.py:50
  126.7 17.3 %collective-permute-start.42 = (bf16[8,4,64]{2,1,0:T(4,128)(2,1)S(1)}, bf16[8,4,64]{2,1,0:T(4,128)(2,1)S(1)}, u32[]{:S(2)}, u32[]{:S(2)}) collective-permute-start(bf16[8,4,64]{2,1,0:T(4,128)(2,1)S(1)} %pad_maximum_fusion.14), channel_id=1, source_target_pairs={{0,2},{2,0},{1,3},{3,1},{4,6},{6,4},{5,7},{7,5},{8,10},{10,8},{9,1... | collective-permute-start | bytes 12296 | tf_op jit(solution)/shard_map/ppermute | solution.py:111
  128.2 13.8 %collective-permute-start.34 = (bf16[128,2048]{1,0:T(8,128)(2,1)S(1)}, bf16[128,2048]{1,0:T(8,128)(2,1)S(1)}, u32[]{:S(2)}, u32[]{:S(2)}) collective-permute-start(bf16[128,2048]{1,0:T(8,128)(2,1)S(1)} %slice.262), channel_id=1, source_target_pairs={{0,2},{2,0},{1,3},{3,1},{4,6},{6,4},{5,7},{7,5},{8,10},{10,8},{9,1... | collective-permute-start | bytes 1572872 | tf_op jit(solution)/shard_map/ppermute | solution.py:50
  128.9 13.6 %collective-permute-start.33 = (bf16[128,2048]{1,0:T(8,128)(2,1)S(1)}, bf16[128,2048]{1,0:T(8,128)(2,1)S(1)}, u32[]{:S(2)}, u32[]{:S(2)}) collective-permute-start(bf16[128,2048]{1,0:T(8,128)(2,1)S(1)} %slice.261), channel_id=1, source_target_pairs={{0,4},{4,0},{1,5},{5,1},{2,6},{6,2},{3,7},{7,3},{8,12},{12,8},{9,1... | collective-permute-start | bytes 1572872 | tf_op jit(solution)/shard_map/ppermute | solution.py:50
  142.5 14.6 %collective-permute-start.35 = (bf16[256,2048]{1,0:T(8,128)(2,1)S(1)}, bf16[256,2048]{1,0:T(8,128)(2,1)}, u32[]{:S(2)}, u32[]{:S(2)}) collective-permute-start(bf16[256,2048]{1,0:T(8,128)(2,1)S(1)} %constant_dynamic-update-slice_fusion.26), channel_id=1, source_target_pairs={{0,1},{1,0},{2,3},{3,2},{4,5},{5,4},{6,7},{7,6},{8,9},{9,8},{10,11... | collective-permute-start | bytes 3145736 | tf_op jit(solution)/shard_map/ppermute | solution.py:50
  155.8 465.5 %reduce-scatter.5.cloned.1.call-start = ((), (), s32[]{:S(2)}) async-start(), calls=%async_computation.14 | async-start | bytes 5242880 | tf_op jit(solution)/shard_map/reduce_scatter | solution.py:138
  210.1 25.3 %collective-permute-start.9 = (bf16[2,128,2048]{2,1,0:T(8,128)(2,1)S(1)}, bf16[2,128,2048]{2,1,0:T(8,128)(2,1)S(1)}, u32[]{:S(2)}, u32[]{:S(2)}) collective-permute-start(bf16[2,128,2048]{2,1,0:T(8,128)(2,1)S(1)} %slice_bitcast_fusion.4), channel_id=1, source_target_pairs={{0,2},{2,0},{1,3},{3,1},{4,6},{6,4},{5,7},{7,5},{8,10},{10,8},{9,1... | collective-permute-start | bytes 3145736 | tf_op jit(solution)/shard_map/cond/branch_1_fun/ppermute | solution.py:50
  211.7 25.0 %collective-permute-start.11 = (bf16[2,128,2048]{2,1,0:T(8,128)(2,1)S(1)}, bf16[2,128,2048]{2,1,0:T(8,128)(2,1)S(1)}, u32[]{:S(2)}, u32[]{:S(2)}) collective-permute-start(bf16[2,128,2048]{2,1,0:T(8,128)(2,1)S(1)} %slice_bitcast_fusion.1), channel_id=1, source_target_pairs={{0,4},{4,0},{1,5},{5,1},{2,6},{6,2},{3,7},{7,3},{8,12},{12,8},{9,1... | collective-permute-start | bytes 3145736 | tf_op jit(solution)/shard_map/cond/branch_1_fun/ppermute | solution.py:50
  237.6 13.0 %collective-permute-start.10 = (bf16[128,2048]{1,0:T(8,128)(2,1)S(1)}, bf16[128,2048]{1,0:T(8,128)(2,1)S(1)}, u32[]{:S(2)}, u32[]{:S(2)}) collective-permute-start(bf16[128,2048]{1,0:T(8,128)(2,1)S(1)} %fusion.2), channel_id=1, source_target_pairs={{0,4},{4,0},{1,5},{5,1},{2,6},{6,2},{3,7},{7,3},{8,12},{12,8},{9,1... | collective-permute-start | bytes 1572872 | tf_op jit(solution)/shard_map/cond/branch_1_fun/ppermute | solution.py:50
  238.3 12.7 %collective-permute-start.12 = (bf16[128,2048]{1,0:T(8,128)(2,1)S(1)}, bf16[128,2048]{1,0:T(8,128)(2,1)S(1)}, u32[]{:S(2)}, u32[]{:S(2)}) collective-permute-start(bf16[128,2048]{1,0:T(8,128)(2,1)S(1)} %fusion.3), channel_id=1, source_target_pairs={{0,2},{2,0},{1,3},{3,1},{4,6},{6,4},{5,7},{7,5},{8,10},{10,8},{9,1... | collective-permute-start | bytes 1572872 | tf_op jit(solution)/shard_map/cond/branch_1_fun/ppermute | solution.py:50
  253.8 23.1 %collective-permute-start.13 = (bf16[256,2048]{1,0:T(8,128)(2,1)S(1)}, bf16[256,2048]{1,0:T(8,128)(2,1)S(1)}, u32[]{:S(2)}, u32[]{:S(2)}) collective-permute-start(bf16[256,2048]{1,0:T(8,128)(2,1)S(1)} %get-tuple-element.290), channel_id=1, source_target_pairs={{0,2},{2,0},{1,3},{3,1},{4,6},{6,4},{5,7},{7,5},{8,10},{10,8},{9,1... | collective-permute-start | bytes 3145736 | tf_op jit(solution)/shard_map/cond/branch_1_fun/ppermute | solution.py:50
  254.4 22.8 %collective-permute-start.14 = (bf16[256,2048]{1,0:T(8,128)(2,1)S(1)}, bf16[256,2048]{1,0:T(8,128)(2,1)S(1)}, u32[]{:S(2)}, u32[]{:S(2)}) collective-permute-start(bf16[256,2048]{1,0:T(8,128)(2,1)S(1)} %get-tuple-element.290), channel_id=1, source_target_pairs={{0,4},{4,0},{1,5},{5,1},{2,6},{6,2},{3,7},{7,3},{8,12},{12,8},{9,1... | collective-permute-start | bytes 3145736 | tf_op jit(solution)/shard_map/cond/branch_1_fun/ppermute | solution.py:50
  277.8 14.4 %collective-permute-start.17 = (bf16[128,2048]{1,0:T(8,128)(2,1)S(1)}, bf16[128,2048]{1,0:T(8,128)(2,1)S(1)}, u32[]{:S(2)}, u32[]{:S(2)}) collective-permute-start(bf16[128,2048]{1,0:T(8,128)(2,1)S(1)} %slice.244), channel_id=1, source_target_pairs={{0,2},{2,0},{1,3},{3,1},{4,6},{6,4},{5,7},{7,5},{8,10},{10,8},{9,1... | collective-permute-start | bytes 1572872 | tf_op jit(solution)/shard_map/cond/branch_1_fun/ppermute | solution.py:50
  279.3 14.1 %collective-permute-start.16 = (bf16[128,2048]{1,0:T(8,128)(2,1)S(1)}, bf16[128,2048]{1,0:T(8,128)(2,1)S(1)}, u32[]{:S(2)}, u32[]{:S(2)}) collective-permute-start(bf16[128,2048]{1,0:T(8,128)(2,1)S(1)} %slice.243), channel_id=1, source_target_pairs={{0,4},{4,0},{1,5},{5,1},{2,6},{6,2},{3,7},{7,3},{8,12},{12,8},{9,1... | collective-permute-start | bytes 1572872 | tf_op jit(solution)/shard_map/cond/branch_1_fun/ppermute | solution.py:50
  355.9 25.3 %collective-permute-start.45 = (bf16[2,128,2048]{2,1,0:T(8,128)(2,1)S(1)}, bf16[2,128,2048]{2,1,0:T(8,128)(2,1)S(1)}, u32[]{:S(2)}, u32[]{:S(2)}) collective-permute-start(bf16[2,128,2048]{2,1,0:T(8,128)(2,1)S(1)} %slice_bitcast_fusion.20), channel_id=1, source_target_pairs={{0,2},{2,0},{1,3},{3,1},{4,6},{6,4},{5,7},{7,5},{8,10},{10,8},{9,1... | collective-permute-start | bytes 3145736 | tf_op jit(solution)/shard_map/ppermute | solution.py:50
  357.6 25.0 %collective-permute-start.47 = (bf16[2,128,2048]{2,1,0:T(8,128)(2,1)S(1)}, bf16[2,128,2048]{2,1,0:T(8,128)(2,1)S(1)}, u32[]{:S(2)}, u32[]{:S(2)}) collective-permute-start(bf16[2,128,2048]{2,1,0:T(8,128)(2,1)S(1)} %slice_bitcast_fusion.17), channel_id=1, source_target_pairs={{0,4},{4,0},{1,5},{5,1},{2,6},{6,2},{3,7},{7,3},{8,12},{12,8},{9,1... | collective-permute-start | bytes 3145736 | tf_op jit(solution)/shard_map/ppermute | solution.py:50
  384.3 13.1 %collective-permute-start.46 = (bf16[128,2048]{1,0:T(8,128)(2,1)}, bf16[128,2048]{1,0:T(8,128)(2,1)}, u32[]{:S(2)}, u32[]{:S(2)}) collective-permute-start(bf16[128,2048]{1,0:T(8,128)(2,1)} %fusion.17), channel_id=1, source_target_pairs={{0,4},{4,0},{1,5},{5,1},{2,6},{6,2},{3,7},{7,3},{8,12},{12,8},{9,1... | collective-permute-start | bytes 1572872 | tf_op jit(solution)/shard_map/ppermute | solution.py:50
  386.7 12.9 %collective-permute-start.48 = (bf16[128,2048]{1,0:T(8,128)(2,1)}, bf16[128,2048]{1,0:T(8,128)(2,1)}, u32[]{:S(2)}, u32[]{:S(2)}) collective-permute-start(bf16[128,2048]{1,0:T(8,128)(2,1)} %fusion.18), channel_id=1, source_target_pairs={{0,2},{2,0},{1,3},{3,1},{4,6},{6,4},{5,7},{7,5},{8,10},{10,8},{9,1... | collective-permute-start | bytes 1572872 | tf_op jit(solution)/shard_map/ppermute | solution.py:50
  406.8 22.9 %collective-permute-start.49 = (bf16[256,2048]{1,0:T(8,128)(2,1)S(1)}, bf16[256,2048]{1,0:T(8,128)(2,1)S(1)}, u32[]{:S(2)}, u32[]{:S(2)}) collective-permute-start(bf16[256,2048]{1,0:T(8,128)(2,1)S(1)} %get-tuple-element.298), channel_id=1, source_target_pairs={{0,2},{2,0},{1,3},{3,1},{4,6},{6,4},{5,7},{7,5},{8,10},{10,8},{9,1... | collective-permute-start | bytes 3145736 | tf_op jit(solution)/shard_map/ppermute | solution.py:50
  407.3 22.6 %collective-permute-start.50 = (bf16[256,2048]{1,0:T(8,128)(2,1)S(1)}, bf16[256,2048]{1,0:T(8,128)(2,1)S(1)}, u32[]{:S(2)}, u32[]{:S(2)}) collective-permute-start(bf16[256,2048]{1,0:T(8,128)(2,1)S(1)} %get-tuple-element.298), channel_id=1, source_target_pairs={{0,4},{4,0},{1,5},{5,1},{2,6},{6,2},{3,7},{7,3},{8,12},{12,8},{9,1... | collective-permute-start | bytes 3145736 | tf_op jit(solution)/shard_map/ppermute | solution.py:50
  430.3 14.4 %collective-permute-start.53 = (bf16[128,2048]{1,0:T(8,128)(2,1)S(1)}, bf16[128,2048]{1,0:T(8,128)(2,1)S(1)}, u32[]{:S(2)}, u32[]{:S(2)}) collective-permute-start(bf16[128,2048]{1,0:T(8,128)(2,1)S(1)} %slice.278), channel_id=1, source_target_pairs={{0,2},{2,0},{1,3},{3,1},{4,6},{6,4},{5,7},{7,5},{8,10},{10,8},{9,1... | collective-permute-start | bytes 1572872 | tf_op jit(solution)/shard_map/ppermute | solution.py:50
  431.9 14.1 %collective-permute-start.52 = (bf16[128,2048]{1,0:T(8,128)(2,1)S(1)}, bf16[128,2048]{1,0:T(8,128)(2,1)S(1)}, u32[]{:S(2)}, u32[]{:S(2)}) collective-permute-start(bf16[128,2048]{1,0:T(8,128)(2,1)S(1)} %slice.277), channel_id=1, source_target_pairs={{0,4},{4,0},{1,5},{5,1},{2,6},{6,2},{3,7},{7,3},{8,12},{12,8},{9,1... | collective-permute-start | bytes 1572872 | tf_op jit(solution)/shard_map/ppermute | solution.py:50
  463.5 224.7 %reduce-scatter.7.cloned.1.call-start = ((), (), s32[]{:S(2)}) async-start(), calls=%async_computation.15 | async-start | bytes 10485760 | tf_op jit(solution)/shard_map/reduce_scatter | solution.py:138
  497.6 14.5 %collective-permute-start.19 = (bf16[1024,2048]{1,0:T(8,128)(2,1)}, bf16[1024,2048]{1,0:T(8,128)(2,1)S(1)}, u32[]{:S(2)}, u32[]{:S(2)}) collective-permute-start(bf16[1024,2048]{1,0:T(8,128)(2,1)} %branch_1_fun.6), channel_id=1, source_target_pairs={{0,1},{1,0},{2,3},{3,2},{4,5},{5,4},{6,7},{7,6},{8,9},{9,8},{10,11... | collective-permute-start | bytes 12582920 | tf_op jit(solution)/shard_map/cond/branch_1_fun/ppermute | solution.py:50
  516.8 25.5 %collective-permute-start.20 = (bf16[2,128,2048]{2,1,0:T(8,128)(2,1)S(1)}, bf16[2,128,2048]{2,1,0:T(8,128)(2,1)S(1)}, u32[]{:S(2)}, u32[]{:S(2)}) collective-permute-start(bf16[2,128,2048]{2,1,0:T(8,128)(2,1)S(1)} %slice_bitcast_fusion.9), channel_id=1, source_target_pairs={{0,2},{2,0},{1,3},{3,1},{4,6},{6,4},{5,7},{7,5},{8,10},{10,8},{9,1... | collective-permute-start | bytes 3145736 | tf_op jit(solution)/shard_map/cond/branch_1_fun/ppermute | solution.py:50
  516.8 25.5 %collective-permute-start.21 = (bf16[2,128,2048]{2,1,0:T(8,128)(2,1)S(1)}, bf16[2,128,2048]{2,1,0:T(8,128)(2,1)S(1)}, u32[]{:S(2)}, u32[]{:S(2)}) collective-permute-start(bf16[2,128,2048]{2,1,0:T(8,128)(2,1)S(1)} %slice_bitcast_fusion.8), channel_id=1, source_target_pairs={{0,4},{4,0},{1,5},{5,1},{2,6},{6,2},{3,7},{7,3},{8,12},{12,8},{9,1... | collective-permute-start | bytes 3145736 | tf_op jit(solution)/shard_map/cond/branch_1_fun/ppermute | solution.py:50
  545.6 242.0 %reduce-scatter.9.cloned.1.call-start = ((), (), s32[]{:S(2)}) async-start(), calls=%async_computation.16 | async-start | bytes 3932160 | tf_op jit(solution)/shard_map/reduce_scatter | solution.py:138
  555.4 13.4 %collective-permute-start.1 = (bf16[128,2048]{1,0:T(8,128)(2,1)S(1)}, bf16[128,2048]{1,0:T(8,128)(2,1)S(1)}, u32[]{:S(2)}, u32[]{:S(2)}) collective-permute-start(bf16[128,2048]{1,0:T(8,128)(2,1)S(1)} %fusion.5), channel_id=1, source_target_pairs={{0,2},{2,0},{1,3},{3,1},{4,6},{6,4},{5,7},{7,5},{8,10},{10,8},{9,1... | collective-permute-start | bytes 1572872 | tf_op jit(solution)/shard_map/cond/branch_1_fun/ppermute | solution.py:50
  558.5 12.8 %collective-permute-start = (bf16[128,2048]{1,0:T(8,128)(2,1)S(1)}, bf16[128,2048]{1,0:T(8,128)(2,1)S(1)}, u32[]{:S(2)}, u32[]{:S(2)}) collective-permute-start(bf16[128,2048]{1,0:T(8,128)(2,1)S(1)} %fusion.4), channel_id=1, source_target_pairs={{0,4},{4,0},{1,5},{5,1},{2,6},{6,2},{3,7},{7,3},{8,12},{12,8},{9,1... | collective-permute-start | bytes 1572872 | tf_op jit(solution)/shard_map/cond/branch_1_fun/ppermute | solution.py:50
  577.7 23.2 %collective-permute-start.2 = (bf16[256,2048]{1,0:T(8,128)(2,1)S(1)}, bf16[256,2048]{1,0:T(8,128)(2,1)S(1)}, u32[]{:S(2)}, u32[]{:S(2)}) collective-permute-start(bf16[256,2048]{1,0:T(8,128)(2,1)S(1)} %get-tuple-element.295), channel_id=1, source_target_pairs={{0,2},{2,0},{1,3},{3,1},{4,6},{6,4},{5,7},{7,5},{8,10},{10,8},{9,1... | collective-permute-start | bytes 3145736 | tf_op jit(solution)/shard_map/cond/branch_1_fun/ppermute | solution.py:50
  578.4 23.3 %collective-permute-start.3 = (bf16[256,2048]{1,0:T(8,128)(2,1)S(1)}, bf16[256,2048]{1,0:T(8,128)(2,1)S(1)}, u32[]{:S(2)}, u32[]{:S(2)}) collective-permute-start(bf16[256,2048]{1,0:T(8,128)(2,1)S(1)} %get-tuple-element.295), channel_id=1, source_target_pairs={{0,4},{4,0},{1,5},{5,1},{2,6},{6,2},{3,7},{7,3},{8,12},{12,8},{9,1... | collective-permute-start | bytes 3145736 | tf_op jit(solution)/shard_map/cond/branch_1_fun/ppermute | solution.py:50
  602.2 14.4 %collective-permute-start.6 = (bf16[128,2048]{1,0:T(8,128)(2,1)S(1)}, bf16[128,2048]{1,0:T(8,128)(2,1)S(1)}, u32[]{:S(2)}, u32[]{:S(2)}) collective-permute-start(bf16[128,2048]{1,0:T(8,128)(2,1)S(1)} %slice.252), channel_id=1, source_target_pairs={{0,2},{2,0},{1,3},{3,1},{4,6},{6,4},{5,7},{7,5},{8,10},{10,8},{9,1... | collective-permute-start | bytes 1572872 | tf_op jit(solution)/shard_map/cond/branch_1_fun/ppermute | solution.py:50
  603.4 14.1 %collective-permute-start.5 = (bf16[128,2048]{1,0:T(8,128)(2,1)S(1)}, bf16[128,2048]{1,0:T(8,128)(2,1)S(1)}, u32[]{:S(2)}, u32[]{:S(2)}) collective-permute-start(bf16[128,2048]{1,0:T(8,128)(2,1)S(1)} %slice.251), channel_id=1, source_target_pairs={{0,4},{4,0},{1,5},{5,1},{2,6},{6,2},{3,7},{7,3},{8,12},{12,8},{9,1... | collective-permute-start | bytes 1572872 | tf_op jit(solution)/shard_map/cond/branch_1_fun/ppermute | solution.py:50
  703.7 83.9 %all-to-all-start.4 = ((bf16[8,64,2048]{2,1,0:T(8,128)(2,1)}), bf16[8,64,2048]{2,1,0:T(8,128)(2,1)S(1)}, u32[]{:S(2)}, u32[]{:S(2)}) async-start(bf16[8,64,2048]{2,1,0:T(8,128)(2,1)} %bitcast.296), calls=%async_computation.7 | async-start | bytes 4194304 | tf_op jit(solution)/shard_map/all_to_all | solution.py:508
  707.4 92.5 %reduce-scatter.11.cloned.1.call-start = ((), (), s32[]{:S(2)}) async-start(), calls=%async_computation.17 | async-start | bytes 1310720 | tf_op jit(solution)/shard_map/reduce_scatter | solution.py:138
  716.8 20.9 %collective-permute-start.24 = (f32[16,4,64]{2,1,0:T(4,128)S(1)}, f32[16,4,64]{2,1,0:T(4,128)S(1)}, u32[]{:S(2)}, u32[]{:S(2)}) collective-permute-start(f32[16,4,64]{2,1,0:T(4,128)S(1)} %bitcast.344), channel_id=1, source_target_pairs={{0,4},{4,0},{1,5},{5,1},{2,6},{6,2},{3,7},{7,3},{8,12},{12,8},{9,1... | collective-permute-start | bytes 49160 | tf_op jit(solution)/shard_map/cond/branch_1_fun/ppermute | solution.py:125
  734.3 29.1 %collective-permute-start.28 = (bf16[2,128,2048]{2,1,0:T(8,128)(2,1)}, bf16[2,128,2048]{2,1,0:T(8,128)(2,1)}, u32[]{:S(2)}, u32[]{:S(2)}) collective-permute-start(bf16[2,128,2048]{2,1,0:T(8,128)(2,1)} %slice_bitcast_fusion.11), channel_id=1, source_target_pairs={{0,4},{4,0},{1,5},{5,1},{2,6},{6,2},{3,7},{7,3},{8,12},{12,8},{9,1... | collective-permute-start | bytes 3145736 | tf_op jit(solution)/shard_map/cond/branch_1_fun/ppermute | solution.py:50
  736.2 27.2 %collective-permute-start.23 = (bf16[2,128,2048]{2,1,0:T(8,128)(2,1)}, bf16[2,128,2048]{2,1,0:T(8,128)(2,1)}, u32[]{:S(2)}, u32[]{:S(2)}) collective-permute-start(bf16[2,128,2048]{2,1,0:T(8,128)(2,1)} %slice_bitcast_fusion.14), channel_id=1, source_target_pairs={{0,2},{2,0},{1,3},{3,1},{4,6},{6,4},{5,7},{7,5},{8,10},{10,8},{9,1... | collective-permute-start | bytes 3145736 | tf_op jit(solution)/shard_map/cond/branch_1_fun/ppermute | solution.py:50
  737.7 24.0 %collective-permute-start.25 = (f32[8,4,64]{2,1,0:T(4,128)S(1)}, f32[8,4,64]{2,1,0:T(4,128)S(1)}, u32[]{:S(2)}, u32[]{:S(2)}) collective-permute-start(f32[8,4,64]{2,1,0:T(4,128)S(1)} %slice_select_fusion.2), channel_id=1, source_target_pairs={{0,2},{2,0},{1,3},{3,1},{4,6},{6,4},{5,7},{7,5},{8,10},{10,8},{9,1... | collective-permute-start | bytes 24584 | tf_op jit(solution)/shard_map/cond/branch_1_fun/ppermute | solution.py:125
  766.5 14.4 %collective-permute-start.27 = (bf16[128,2048]{1,0:T(8,128)(2,1)S(1)}, bf16[128,2048]{1,0:T(8,128)(2,1)S(1)}, u32[]{:S(2)}, u32[]{:S(2)}) collective-permute-start(bf16[128,2048]{1,0:T(8,128)(2,1)S(1)} %fusion.10), channel_id=1, source_target_pairs={{0,4},{4,0},{1,5},{5,1},{2,6},{6,2},{3,7},{7,3},{8,12},{12,8},{9,1... | collective-permute-start | bytes 1572872 | tf_op jit(solution)/shard_map/cond/branch_1_fun/ppermute | solution.py:50
  766.9 14.1 %collective-permute-start.29 = (bf16[128,2048]{1,0:T(8,128)(2,1)S(1)}, bf16[128,2048]{1,0:T(8,128)(2,1)S(1)}, u32[]{:S(2)}, u32[]{:S(2)}) collective-permute-start(bf16[128,2048]{1,0:T(8,128)(2,1)S(1)} %fusion.11), channel_id=1, source_target_pairs={{0,2},{2,0},{1,3},{3,1},{4,6},{6,4},{5,7},{7,5},{8,10},{10,8},{9,1... | collective-permute-start | bytes 1572872 | tf_op jit(solution)/shard_map/cond/branch_1_fun/ppermute | solution.py:50
  787.6 16.4 %all-to-all-start.5 = ((bf16[8,64,768]{2,1,0:T(8,128)(2,1)}), bf16[8,64,768]{2,1,0:T(8,128)(2,1)S(1)}, u32[]{:S(2)}, u32[]{:S(2)}) async-start(bf16[8,64,768]{2,1,0:T(8,128)(2,1)} %bitcast.322), calls=%async_computation.8 | async-start | bytes 1572864 | tf_op jit(solution)/shard_map/all_to_all | solution.py:508
  (68 other events, 781.4 us)
Sparse Core Ops, SparseCore 0:
  10.2 30.6 all-gather.4
  42.4 62.9 all-gather.6
  107.0 148.3 all-gather.8
  257.4 78.9 all-gather.10
  463.6 74.0 reduce-scatter.4
  545.7 142.4 reduce-scatter.6
  690.7 60.9 reduce-scatter.8
  754.1 27.1 reduce-scatter.10

commit v6 on v5

--- a/solution.py
+++ b/solution.py
@@ -100,7 +100,8 @@
 def by_core(product, values, weight):
     half = values.shape[0] // 2
     other = product(values[half:], weight).astype(BF16)
-    return product(after(values[:half], other), weight).astype(BF16), other
+    mine = product(after(values[:half], other), weight).astype(BF16)
+    return lax.optimization_barrier(mine), other
 
 
 def doubled(own, axes):

time: 824 us -> 821 us (level)
  waiting for transfers between devices: 303 us -> 289 us
  other arithmetic: 70.7 us -> 81.5 us
    convert_element_type x1 -> x4, other arithmetic: 4.38 us -> 14.9 us  [core_sum(): total.astype(BF16).reshape(2, 2, 2, mine.shape[0] // 8, mine.shape[1])]
    ppermute x50, waiting for transfers between devices: 250 us -> 240 us  [swap(): return lax.ppermute(block, axis, [(0, 1), (1, 0)])]
  transfers between devices with their start and end apart: 70 -> 70, of which waited for: 51 -> 49; matrix products, arithmetic and copies ran while one was open for 24% -> 25% of each run, Pallas kernels for 16% -> 16%
where the time goes in v6:
time: 821 us; the launch traced here: 812 us
  waiting for transfers between devices  289 us (35%)
  Pallas kernels  137 us (17%)
  matrix products  94.7 us (12%)
  other arithmetic  81.5 us (10%)
  local copies, waits for them, and re-layouts  72.9 us (9%)
  starting transfers between devices  60.5 us (7%)
  blocking collectives  58.6 us (7%)
  between operations  16.4 us (2%)
    ppermute x50, waiting for transfers between devices, swap(): return lax.ppermute(block, axis, [(0, 1), (1, 0)])  240 us
    dot_general x4, matrix products, inner_t(): lax.dot_general(left, right, (((0,), (0,)), ((), ())), preferred_element_...  49.4 us
    all_to_all x2, blocking collectives, exchange(): return lax.all_to_all(parts, group, 0, 0, tiled=True)  48.6 us
    ppermute x50, starting transfers between devices, swap(): return lax.ppermute(block, axis, [(0, 1), (1, 0)])  41 us
    pallas_call x2, Pallas kernels, times_transposed(): pl.pallas_call(kernel, grid=(rows // FEED_ROWS,), in_specs=[pl.BlockSpec(...  28.9 us
    pallas_call x1, Pallas kernels, attend_back(): pl.pallas_call(attend_back_kernel, grid=(blocks, heads), in_specs=specs +...  28.5 us
    ppermute x5, waiting for transfers between devices, halved(): lax.ppermute(jnp.where(low_side, second, first), axis, [(i, i ^ step) for...  26.6 us
    dot_general x5, matrix products, matmul(): return jnp.dot(left, right, preferred_element_type=F32)  24.9 us
  transfers between devices with their start and end apart: 70, of which 49 were waited for; matrix products, arithmetic and copies ran while one was open for 25% of the time, Pallas kernels for 16%

profile of v6, /device:TPU:0, one launch (start us, length us, event | category | flops | bytes accessed | tf_op | source)
XLA Modules:
  0.0 812.4 jit_solution(10691216953380961967)
XLA Ops:
  13.1 17.6 %all_to_all.30 = bf16[8,64,768]{2,1,0:T(8,128)(2,1)} all-to-all(bf16[8,64,768]{2,1,0:T(8,128)(2,1)S(1)} %pad_maximum_fusion.10), channel_id=1, replica_groups=mesh['zh'=2,'zl'=2,'y'=2,'x'=2,'c'=2] {'y','x','c'}, dimensions={0} | all-to-all | bytes 1572864 | tf_op jit(solution)/shard_map/all_to_all | solution.py:509
  30.8 4.2 shard_map.246
  35.0 5.9 all-gather.5.cloned.1.call-done
  40.8 31.0 %all_to_all.31 = bf16[8,64,2048]{2,1,0:T(8,128)(2,1)} all-to-all(bf16[8,64,2048]{2,1,0:T(8,128)(2,1)} %shard_map.246), channel_id=1, replica_groups=mesh['zh'=2,'zl'=2,'y'=2,'x'=2,'c'=2] {'y','x','c'}, dimensions={0} | all-to-all | bytes 4194304 | tf_op jit(solution)/shard_map/all_to_all | solution.py:509
  88.9 20.2 %collective-permute-done.30 = bf16[256,2048]{1,0:T(8,128)(2,1)S(1)} collective-permute-done((bf16[256,2048]{1,0:T(8,128)(2,1)S(1)}, bf16[256,2048]{1,0:T(8,128)(2,1)S(1)}, u32[]{:S(2)}, u32[]{:S(2)}) %collective-permute-start.30) | collective-permute-done | bytes 1048608 | tf_op jit(solution)/shard_map/ppermute | solution.py:50
  113.6 5.7 fusion.19
  133.2 8.8 %collective-permute-done.34 = bf16[128,2048]{1,0:T(8,128)(2,1)S(1)} collective-permute-done((bf16[128,2048]{1,0:T(8,128)(2,1)S(1)}, bf16[128,2048]{1,0:T(8,128)(2,1)S(1)}, u32[]{:S(2)}, u32[]{:S(2)}) %collective-permute-start.34) | collective-permute-done | bytes 524320 | tf_op jit(solution)/shard_map/ppermute | solution.py:50
  150.2 4.6 all_to_all.32
  159.5 10.0 %fusion.29.p_ref = f32[2048,768]{1,0:T(8,128)S(1)} fusion(bf16[2048,2048]{1,0:T(8,128)(2,1)} %constant_dynamic-update-slice_fusion.64, bf16[2048,768]{1,0:T(8,128)(2,1)} %all-gather.7.cloned.1.call-done), kind=kOutput, calls=%fused_computation.249 | convolution fusion | flops 6442450944 | bytes 17825792 | tf_op jit(solution)/shard_map/dot_general | solution.py:23
  182.0 118.9 %conditional.4 = (bf16[2048,256]{1,0:T(8,128)(2,1)S(1)}, f32[256,2048]{1,0:T(8,128)S(1)}, f32[256,2048]{1,0:T(8,128)}, bf16[2048,2048]{1,0:T(8,128)(2,1)}, f32[256,1]{0,1:T(1,128)S(1)}) conditional(s32[]{:T(128)} %bitcast.42, () %tuple.76, (f32[2048,768]{1,0:T(8,128)}, f32[2048,4]{0,1:T(4,128)S(1)}, f32[2048,128]{1,0:T(8,128)}, ...), branch_computations={%region_4.5_spmd, %region_5.7_spmd} | conditional | flops 4325376512 | bytes 183587456 | solution.py:46
  183.3 16.9 %branch_1_fun.4 = bf16[2,2,512,256]{3,2,1,0:T(8,128)(2,1)S(1)} custom-call(f32[2,2,512,768]{3,2,1,0:T(8,128)} %bitcast.282, f32[2,2,512,768]{3,2,1,0:T(8,128)} %bitcast.283, f32[2,2,512,768]{3,2,1,0:T(8,128)} %bitcast.284, f32[2,2,512,4]{3,2,1,0:T(8,128)} %bitcast.307, f32[2,2,512,128]{3,2,1,0:T(8,128)} %bitcast.304, f32[2,2,512,128]{3,2,1,0:T(8,128)} %bitcast.303, ...), custom_call_target="tpu_custom_call" | custom-call | flops 2147483648 | bytes 8388608 | tf_op jit(solution)/shard_map/cond/branch_1_fun/pallas_call | solution.py:405
  203.0 6.0 collective-permute-done.8
  215.5 23.0 %collective-permute-done.9 = bf16[2,128,2048]{2,1,0:T(8,128)(2,1)S(1)} collective-permute-done((bf16[2,128,2048]{2,1,0:T(8,128)(2,1)S(1)}, bf16[2,128,2048]{2,1,0:T(8,128)(2,1)S(1)}, u32[]{:S(2)}, u32[]{:S(2)}) %collective-permute-start.9) | collective-permute-done | bytes 1048608 | tf_op jit(solution)/shard_map/cond/branch_1_fun/ppermute | solution.py:50
  242.0 11.6 %collective-permute-done.10 = bf16[128,2048]{1,0:T(8,128)(2,1)S(1)} collective-permute-done((bf16[128,2048]{1,0:T(8,128)(2,1)S(1)}, bf16[128,2048]{1,0:T(8,128)(2,1)S(1)}, u32[]{:S(2)}, u32[]{:S(2)}) %collective-permute-start.10) | collective-permute-done | bytes 524320 | tf_op jit(solution)/shard_map/cond/branch_1_fun/ppermute | solution.py:50
  258.9 21.1 %collective-permute-done.13 = bf16[256,2048]{1,0:T(8,128)(2,1)S(1)} collective-permute-done((bf16[256,2048]{1,0:T(8,128)(2,1)S(1)}, bf16[256,2048]{1,0:T(8,128)(2,1)S(1)}, u32[]{:S(2)}, u32[]{:S(2)}) %collective-permute-start.13) | collective-permute-done | bytes 1048608 | tf_op jit(solution)/shard_map/cond/branch_1_fun/ppermute | solution.py:50
  290.4 4.9 collective-permute-done.17
  300.9 24.5 %shard_map.247 = (f32[2048,2048]{1,0:T(8,128)}, bf16[2048,1024]{1,0:T(8,128)(2,1)}) custom-call(bf16[2048,2048]{1,0:T(8,128)(2,1)} %get-tuple-element.169.v_ref, bf16[2048,2048]{1,0:T(8,128)(2,1)} %all-gather.9.cloned.1.call-done.w_ref), custom_call_target="tpu_custom_call" | custom-call | flops 17179869184 | bytes 29360128 | tf_op jit(solution)/shard_map/pallas_call | solution.py:320
  325.4 11.0 %all-gather.11.cloned.1.call-done = bf16[1024,2048]{1,0:T(8,128)(2,1)} async-done(((bf16[256,2048]{1,0:T(8,128)(2,1)}), bf16[1024,2048]{1,0:T(8,128)(2,1)}) %all-gather.11.cloned.1.call-update) | async-done | bytes 4194320 | tf_op jit(solution)/shard_map/all_gather | solution.py:135
  336.4 7.5 convolution_convert_fusion.6
  346.0 4.9 convolution_convert_fusion.5
  356.7 22.0 %collective-permute-done.45 = bf16[2,128,2048]{2,1,0:T(8,128)(2,1)S(1)} collective-permute-done((bf16[2,128,2048]{2,1,0:T(8,128)(2,1)S(1)}, bf16[2,128,2048]{2,1,0:T(8,128)(2,1)S(1)}, u32[]{:S(2)}, u32[]{:S(2)}) %collective-permute-start.45) | collective-permute-done | bytes 1048608 | tf_op jit(solution)/shard_map/ppermute | solution.py:50
  384.9 10.2 %collective-permute-done.46 = bf16[128,2048]{1,0:T(8,128)(2,1)} collective-permute-done((bf16[128,2048]{1,0:T(8,128)(2,1)}, bf16[128,2048]{1,0:T(8,128)(2,1)}, u32[]{:S(2)}, u32[]{:S(2)}) %collective-permute-start.46) | collective-permute-done | bytes 524320 | tf_op jit(solution)/shard_map/ppermute | solution.py:50
  405.9 21.4 %collective-permute-done.49 = bf16[256,2048]{1,0:T(8,128)(2,1)S(1)} collective-permute-done((bf16[256,2048]{1,0:T(8,128)(2,1)S(1)}, bf16[256,2048]{1,0:T(8,128)(2,1)S(1)}, u32[]{:S(2)}, u32[]{:S(2)}) %collective-permute-start.49) | collective-permute-done | bytes 1048608 | tf_op jit(solution)/shard_map/ppermute | solution.py:50
  434.0 8.3 %collective-permute-done.53 = bf16[128,2048]{1,0:T(8,128)(2,1)S(1)} collective-permute-done((bf16[128,2048]{1,0:T(8,128)(2,1)S(1)}, bf16[128,2048]{1,0:T(8,128)(2,1)S(1)}, u32[]{:S(2)}, u32[]{:S(2)}) %collective-permute-start.53) | collective-permute-done | bytes 524320 | tf_op jit(solution)/shard_map/ppermute | solution.py:50
  449.7 11.0 %convolution_convert_fusion.4 = bf16[1024,2048]{1,0:T(8,128)(2,1)} fusion(bf16[2048,1024]{1,0:T(8,128)(2,1)S(1)} %copy-done.24, bf16[2048,2048]{1,0:T(8,128)(2,1)S(1)} %constant_dynamic-update-slice_fusion.62), kind=kOutput, calls=%fused_computation.93 | convolution fusion | flops 8592031744 | bytes 16777216 | tf_op jit(solution)/shard_map/dot_general | solution.py:31
  460.8 82.0 %conditional.5 = (bf16[2048,2048]{0,1:T(8,128)(2,1)}, f32[2,128,2048]{2,1,0:T(8,128)}, f32[2,128,2048]{2,1,0:T(8,128)}) conditional(s32[]{:T(128)} %bitcast.42, () %tuple.88, (bf16[2048,2048]{1,0:T(8,128)(2,1)}, bf16[1024,2048]{1,0:T(8,128)(2,1)}, f32[2048,2048]{1,0:T(8,128)}, bf16[2048,2048]{1,0:T(8,128)(2,1)}, ...), branch_computations={%region_9.10_spmd, %region_10.11_spmd} | conditional | flops 42965401600 | bytes 159383712 | solution.py:46
  460.8 19.8 %branch_1_fun.5.v_ref = bf16[2048,2048]{1,0:T(8,128)(2,1)} custom-call(bf16[2048,2048]{1,0:T(8,128)(2,1)} %get-tuple-element.77.g_ref, bf16[1024,2048]{1,0:T(8,128)(2,1)} %get-tuple-element.78.w_ref, f32[2048,2048]{1,0:T(8,128)} %get-tuple-element.79.both_ref), custom_call_target="tpu_custom_call" | custom-call | flops 8589934592 | bytes 33554432 | tf_op jit(solution)/shard_map/cond/branch_1_fun/pallas_call | solution.py:345
  480.6 14.5 %branch_1_fun.6 = bf16[1024,2048]{1,0:T(8,128)(2,1)} custom-call(bf16[2048,2048]{1,0:T(8,128)(2,1)} %branch_1_fun.5.v_ref, bf16[2048,2048]{1,0:T(8,128)(2,1)} %get-tuple-element.80.w_ref), custom_call_target="tpu_custom_call" | custom-call | flops 8589934592 | bytes 8388608 | tf_op jit(solution)/shard_map/cond/branch_1_fun/pallas_call | solution.py:365
  495.2 14.4 %branch_1_fun.7 = bf16[1024,2048]{1,0:T(8,128)(2,1)} custom-call(bf16[2048,2048]{1,0:T(8,128)(2,1)} %branch_1_fun.5.v_ref, bf16[2048,2048]{1,0:T(8,128)(2,1)} %get-tuple-element.80.w_ref), custom_call_target="tpu_custom_call" | custom-call | flops 8589934592 | bytes 8388608 | tf_op jit(solution)/shard_map/cond/branch_1_fun/pallas_call | solution.py:365
  509.7 4.4 add_convert_fusion.1
  515.5 22.3 %convert_bitcast_fusion = bf16[2048,2048]{0,1:T(8,128)(2,1)} fusion(bf16[2048,2048]{1,0:T(8,128)(2,1)S(1)} %copy-done.14, bf16[2048,2048]{1,0:T(8,128)(2,1)} %get-tuple-element.85), kind=kOutput, calls=%fused_computation.32 | convolution fusion | flops 17184063488 | bytes 25165824 | tf_op jit(solution)/shard_map/cond/branch_1_fun/dot_general | solution.py:31
  551.2 67.3 %conditional.6 = (f32[256,2048]{1,0:T(8,128)}, bf16[2048,2048]{1,0:T(8,128)(2,1)}, f32[1,4,8,64]{3,2,1,0:T(8,128)S(1)}) conditional(s32[]{:T(128)} %bitcast.42, () %tuple.87, (f32[2,128,2048]{2,1,0:T(8,128)}, f32[2,128,2048]{2,1,0:T(8,128)}, f32[256,2048]{1,0:T(8,128)}, f32[256,1]{0,1:T(1,128)S(1)}, f32[1,2048]{1,0:T(1,128)S(1)}, ...), branch_computations={%region_11.12_spmd, %region_12.15_spmd} | conditional | flops 17824512 | bytes 93374832 | solution.py:46
  556.9 9.2 %collective-permute-done.1 = bf16[128,2048]{1,0:T(8,128)(2,1)S(1)} collective-permute-done((bf16[128,2048]{1,0:T(8,128)(2,1)S(1)}, bf16[128,2048]{1,0:T(8,128)(2,1)S(1)}, u32[]{:S(2)}, u32[]{:S(2)}) %collective-permute-start.1) | collective-permute-done | bytes 524320 | tf_op jit(solution)/shard_map/cond/branch_1_fun/ppermute | solution.py:50
  576.8 21.3 %collective-permute-done.2 = bf16[256,2048]{1,0:T(8,128)(2,1)S(1)} collective-permute-done((bf16[256,2048]{1,0:T(8,128)(2,1)S(1)}, bf16[256,2048]{1,0:T(8,128)(2,1)S(1)}, u32[]{:S(2)}, u32[]{:S(2)}) %collective-permute-start.2) | collective-permute-done | bytes 1048608 | tf_op jit(solution)/shard_map/cond/branch_1_fun/ppermute | solution.py:50
  608.2 5.6 collective-permute-done.6
  618.5 6.8 convolution_convert_fusion.9
  625.3 28.5 %shard_map.248 = (f32[2,2,512,256]{3,2,1,0:T(8,128)}, f32[2,2,512,256]{3,2,1,0:T(8,128)}, bf16[2,2,512,256]{3,2,1,0:T(8,128)(2,1)}, f32[2,2,2,512,2]{4,3,2,1,0:T(8,128)}) custom-call(f32[2,2,512,768]{3,2,1,0:T(8,128)} %bitcast.279, f32[2,2,512,768]{3,2,1,0:T(8,128)} %bitcast.280, f32[2,2,512,768]{3,2,1,0:T(8,128)} %bitcast.281, f32[2,2,512,4]{3,2,1,0:T(8,128)} %bitcast.298, ...), custom_call_target="tpu_custom_call" | custom-call | flops 5368709120 | bytes 12582912 | tf_op jit(solution)/shard_map/pallas_call | solution.py:425
  666.3 7.0 shard_map.249
  675.0 10.4 %convolution_convert_fusion.7 = bf16[2048,768]{1,0:T(8,128)(2,1)} fusion(bf16[2048,2048]{1,0:T(8,128)(2,1)} %constant_dynamic-update-slice_fusion.64, bf16[2048,768]{1,0:T(8,128)(2,1)S(1)} %get-tuple-element.191), kind=kOutput, calls=%fused_computation.96 | convolution fusion | flops 6444023808 | bytes 14680064 | tf_op jit(solution)/shard_map/dot_general | solution.py:31
  685.5 4.2 copy.245
  689.7 5.7 convolution_convert_fusion.8
  695.5 5.5 all_to_all.33
  705.7 76.0 %conditional.7 = (f32[256,2048]{1,0:T(8,128)}, f32[4,4,64]{2,1,0:T(4,128)}, f32[256,2048]{1,0:T(8,128)}, f32[2,4,64]{2,1,0:T(4,128)S(1)}, f32[2,4,64]{2,1,0:T(4,128)S(1)}) conditional(s32[]{:T(128)} %bitcast.42, () %tuple.86, (bf16[2048,768]{1,0:T(8,128)(2,1)}, bf16[2048,768]{1,0:T(8,128)(2,1)}, f32[8,4,4,64]{3,0,1,2:T(8,128)S(1)}, ...), branch_computations={%region_19.20_spmd, %region_20.21_spmd} | conditional | flops 6460822528 | bytes 109457968 | solution.py:46
  705.7 7.9 convolution_convert_fusion.3
  718.5 5.8 convolution_convert_fusion.2
  724.3 4.2 add_convert_fusion.2
  734.2 23.4 %collective-permute-done.25 = f32[8,4,64]{2,1,0:T(4,128)S(1)} collective-permute-done((f32[8,4,64]{2,1,0:T(4,128)S(1)}, f32[8,4,64]{2,1,0:T(4,128)S(1)}, u32[]{:S(2)}, u32[]{:S(2)}) %collective-permute-start.25) | collective-permute-done | bytes 8224 | tf_op jit(solution)/shard_map/cond/branch_1_fun/ppermute | solution.py:126
  765.8 11.0 %collective-permute-done.27 = bf16[128,2048]{1,0:T(8,128)(2,1)S(1)} collective-permute-done((bf16[128,2048]{1,0:T(8,128)(2,1)S(1)}, bf16[128,2048]{1,0:T(8,128)(2,1)S(1)}, u32[]{:S(2)}, u32[]{:S(2)}) %collective-permute-start.27) | collective-permute-done | bytes 524320 | tf_op jit(solution)/shard_map/cond/branch_1_fun/ppermute | solution.py:50
  (451 shorter events, 251.0 us)
Async XLA Ops:
  7.2 33.6 %all-gather.5.cloned.1.call-start = ((), (), s32[]{:S(2)}) async-start(), calls=%async_computation.10 | async-start | bytes 1310720 | tf_op jit(solution)/shard_map/all_gather | solution.py:135
  9.1 150.4 %all-gather.7.cloned.1.call-start = ((), (), s32[]{:S(2)}) async-start(), calls=%async_computation.11 | async-start | bytes 3932160 | tf_op jit(solution)/shard_map/all_gather | solution.py:135
  30.7 270.2 %all-gather.9.cloned.1.call-start = ((), (), s32[]{:S(2)}) async-start(), calls=%async_computation.12 | async-start | bytes 10485760 | tf_op jit(solution)/shard_map/all_gather | solution.py:135
  71.8 264.6 %all-gather.11.cloned.1.call-start = ((), (), s32[]{:S(2)}) async-start(), calls=%async_computation.13 | async-start | bytes 5242880 | tf_op jit(solution)/shard_map/all_gather | solution.py:135
  84.8 24.3 %collective-permute-start.30 = (bf16[256,2048]{1,0:T(8,128)(2,1)S(1)}, bf16[256,2048]{1,0:T(8,128)(2,1)S(1)}, u32[]{:S(2)}, u32[]{:S(2)}) collective-permute-start(bf16[256,2048]{1,0:T(8,128)(2,1)S(1)} %copy-done.3), channel_id=1, source_target_pairs={{0,2},{2,0},{1,3},{3,1},{4,6},{6,4},{5,7},{7,5},{8,10},{10,8},{9,1... | collective-permute-start | bytes 3145736 | tf_op jit(solution)/shard_map/ppermute | solution.py:50
  85.4 24.7 %collective-permute-start.31 = (bf16[256,2048]{1,0:T(8,128)(2,1)S(1)}, bf16[256,2048]{1,0:T(8,128)(2,1)S(1)}, u32[]{:S(2)}, u32[]{:S(2)}) collective-permute-start(bf16[256,2048]{1,0:T(8,128)(2,1)S(1)} %copy-done.3), channel_id=1, source_target_pairs={{0,4},{4,0},{1,5},{5,1},{2,6},{6,2},{3,7},{7,3},{8,12},{12,8},{9,1... | collective-permute-start | bytes 3145736 | tf_op jit(solution)/shard_map/ppermute | solution.py:50
  112.0 18.7 %collective-permute-start.32 = (bf16[768,2048]{1,0:T(8,128)(2,1)}, bf16[768,2048]{1,0:T(8,128)(2,1)}, u32[]{:S(2)}, u32[]{:S(2)}) collective-permute-start(bf16[768,2048]{1,0:T(8,128)(2,1)} %pad_maximum_fusion.3), channel_id=1, source_target_pairs={{0,1},{1,0},{2,3},{3,2},{4,5},{5,4},{6,7},{7,6},{8,9},{9,8},{10,11... | collective-permute-start | bytes 9437192 | tf_op jit(solution)/shard_map/ppermute | solution.py:50
  126.7 17.3 %collective-permute-start.42 = (bf16[8,4,64]{2,1,0:T(4,128)(2,1)S(1)}, bf16[8,4,64]{2,1,0:T(4,128)(2,1)S(1)}, u32[]{:S(2)}, u32[]{:S(2)}) collective-permute-start(bf16[8,4,64]{2,1,0:T(4,128)(2,1)S(1)} %pad_maximum_fusion.14), channel_id=1, source_target_pairs={{0,2},{2,0},{1,3},{3,1},{4,6},{6,4},{5,7},{7,5},{8,10},{10,8},{9,1... | collective-permute-start | bytes 12296 | tf_op jit(solution)/shard_map/ppermute | solution.py:112
  128.2 13.8 %collective-permute-start.34 = (bf16[128,2048]{1,0:T(8,128)(2,1)S(1)}, bf16[128,2048]{1,0:T(8,128)(2,1)S(1)}, u32[]{:S(2)}, u32[]{:S(2)}) collective-permute-start(bf16[128,2048]{1,0:T(8,128)(2,1)S(1)} %slice.262), channel_id=1, source_target_pairs={{0,2},{2,0},{1,3},{3,1},{4,6},{6,4},{5,7},{7,5},{8,10},{10,8},{9,1... | collective-permute-start | bytes 1572872 | tf_op jit(solution)/shard_map/ppermute | solution.py:50
  128.9 13.6 %collective-permute-start.33 = (bf16[128,2048]{1,0:T(8,128)(2,1)S(1)}, bf16[128,2048]{1,0:T(8,128)(2,1)S(1)}, u32[]{:S(2)}, u32[]{:S(2)}) collective-permute-start(bf16[128,2048]{1,0:T(8,128)(2,1)S(1)} %slice.261), channel_id=1, source_target_pairs={{0,4},{4,0},{1,5},{5,1},{2,6},{6,2},{3,7},{7,3},{8,12},{12,8},{9,1... | collective-permute-start | bytes 1572872 | tf_op jit(solution)/shard_map/ppermute | solution.py:50
  142.5 14.6 %collective-permute-start.35 = (bf16[256,2048]{1,0:T(8,128)(2,1)S(1)}, bf16[256,2048]{1,0:T(8,128)(2,1)}, u32[]{:S(2)}, u32[]{:S(2)}) collective-permute-start(bf16[256,2048]{1,0:T(8,128)(2,1)S(1)} %constant_dynamic-update-slice_fusion.26), channel_id=1, source_target_pairs={{0,1},{1,0},{2,3},{3,2},{4,5},{5,4},{6,7},{7,6},{8,9},{9,8},{10,11... | collective-permute-start | bytes 3145736 | tf_op jit(solution)/shard_map/ppermute | solution.py:50
  155.8 462.7 %reduce-scatter.5.cloned.1.call-start = ((), (), s32[]{:S(2)}) async-start(), calls=%async_computation.14 | async-start | bytes 5242880 | tf_op jit(solution)/shard_map/reduce_scatter | solution.py:139
  213.2 25.3 %collective-permute-start.9 = (bf16[2,128,2048]{2,1,0:T(8,128)(2,1)S(1)}, bf16[2,128,2048]{2,1,0:T(8,128)(2,1)S(1)}, u32[]{:S(2)}, u32[]{:S(2)}) collective-permute-start(bf16[2,128,2048]{2,1,0:T(8,128)(2,1)S(1)} %slice_bitcast_fusion.4), channel_id=1, source_target_pairs={{0,2},{2,0},{1,3},{3,1},{4,6},{6,4},{5,7},{7,5},{8,10},{10,8},{9,1... | collective-permute-start | bytes 3145736 | tf_op jit(solution)/shard_map/cond/branch_1_fun/ppermute | solution.py:50
  214.8 25.0 %collective-permute-start.11 = (bf16[2,128,2048]{2,1,0:T(8,128)(2,1)S(1)}, bf16[2,128,2048]{2,1,0:T(8,128)(2,1)S(1)}, u32[]{:S(2)}, u32[]{:S(2)}) collective-permute-start(bf16[2,128,2048]{2,1,0:T(8,128)(2,1)S(1)} %slice_bitcast_fusion.1), channel_id=1, source_target_pairs={{0,4},{4,0},{1,5},{5,1},{2,6},{6,2},{3,7},{7,3},{8,12},{12,8},{9,1... | collective-permute-start | bytes 3145736 | tf_op jit(solution)/shard_map/cond/branch_1_fun/ppermute | solution.py:50
  240.7 13.0 %collective-permute-start.10 = (bf16[128,2048]{1,0:T(8,128)(2,1)S(1)}, bf16[128,2048]{1,0:T(8,128)(2,1)S(1)}, u32[]{:S(2)}, u32[]{:S(2)}) collective-permute-start(bf16[128,2048]{1,0:T(8,128)(2,1)S(1)} %fusion.2), channel_id=1, source_target_pairs={{0,4},{4,0},{1,5},{5,1},{2,6},{6,2},{3,7},{7,3},{8,12},{12,8},{9,1... | collective-permute-start | bytes 1572872 | tf_op jit(solution)/shard_map/cond/branch_1_fun/ppermute | solution.py:50
  241.4 12.7 %collective-permute-start.12 = (bf16[128,2048]{1,0:T(8,128)(2,1)S(1)}, bf16[128,2048]{1,0:T(8,128)(2,1)S(1)}, u32[]{:S(2)}, u32[]{:S(2)}) collective-permute-start(bf16[128,2048]{1,0:T(8,128)(2,1)S(1)} %fusion.3), channel_id=1, source_target_pairs={{0,2},{2,0},{1,3},{3,1},{4,6},{6,4},{5,7},{7,5},{8,10},{10,8},{9,1... | collective-permute-start | bytes 1572872 | tf_op jit(solution)/shard_map/cond/branch_1_fun/ppermute | solution.py:50
  256.9 23.1 %collective-permute-start.13 = (bf16[256,2048]{1,0:T(8,128)(2,1)S(1)}, bf16[256,2048]{1,0:T(8,128)(2,1)S(1)}, u32[]{:S(2)}, u32[]{:S(2)}) collective-permute-start(bf16[256,2048]{1,0:T(8,128)(2,1)S(1)} %get-tuple-element.290), channel_id=1, source_target_pairs={{0,2},{2,0},{1,3},{3,1},{4,6},{6,4},{5,7},{7,5},{8,10},{10,8},{9,1... | collective-permute-start | bytes 3145736 | tf_op jit(solution)/shard_map/cond/branch_1_fun/ppermute | solution.py:50
  257.5 22.8 %collective-permute-start.14 = (bf16[256,2048]{1,0:T(8,128)(2,1)S(1)}, bf16[256,2048]{1,0:T(8,128)(2,1)S(1)}, u32[]{:S(2)}, u32[]{:S(2)}) collective-permute-start(bf16[256,2048]{1,0:T(8,128)(2,1)S(1)} %get-tuple-element.290), channel_id=1, source_target_pairs={{0,4},{4,0},{1,5},{5,1},{2,6},{6,2},{3,7},{7,3},{8,12},{12,8},{9,1... | collective-permute-start | bytes 3145736 | tf_op jit(solution)/shard_map/cond/branch_1_fun/ppermute | solution.py:50
  280.9 14.4 %collective-permute-start.17 = (bf16[128,2048]{1,0:T(8,128)(2,1)S(1)}, bf16[128,2048]{1,0:T(8,128)(2,1)S(1)}, u32[]{:S(2)}, u32[]{:S(2)}) collective-permute-start(bf16[128,2048]{1,0:T(8,128)(2,1)S(1)} %slice.244), channel_id=1, source_target_pairs={{0,2},{2,0},{1,3},{3,1},{4,6},{6,4},{5,7},{7,5},{8,10},{10,8},{9,1... | collective-permute-start | bytes 1572872 | tf_op jit(solution)/shard_map/cond/branch_1_fun/ppermute | solution.py:50
  282.5 14.1 %collective-permute-start.16 = (bf16[128,2048]{1,0:T(8,128)(2,1)S(1)}, bf16[128,2048]{1,0:T(8,128)(2,1)S(1)}, u32[]{:S(2)}, u32[]{:S(2)}) collective-permute-start(bf16[128,2048]{1,0:T(8,128)(2,1)S(1)} %slice.243), channel_id=1, source_target_pairs={{0,4},{4,0},{1,5},{5,1},{2,6},{6,2},{3,7},{7,3},{8,12},{12,8},{9,1... | collective-permute-start | bytes 1572872 | tf_op jit(solution)/shard_map/cond/branch_1_fun/ppermute | solution.py:50
  353.5 25.3 %collective-permute-start.45 = (bf16[2,128,2048]{2,1,0:T(8,128)(2,1)S(1)}, bf16[2,128,2048]{2,1,0:T(8,128)(2,1)S(1)}, u32[]{:S(2)}, u32[]{:S(2)}) collective-permute-start(bf16[2,128,2048]{2,1,0:T(8,128)(2,1)S(1)} %slice_bitcast_fusion.20), channel_id=1, source_target_pairs={{0,2},{2,0},{1,3},{3,1},{4,6},{6,4},{5,7},{7,5},{8,10},{10,8},{9,1... | collective-permute-start | bytes 3145736 | tf_op jit(solution)/shard_map/ppermute | solution.py:50
  355.2 25.0 %collective-permute-start.47 = (bf16[2,128,2048]{2,1,0:T(8,128)(2,1)S(1)}, bf16[2,128,2048]{2,1,0:T(8,128)(2,1)S(1)}, u32[]{:S(2)}, u32[]{:S(2)}) collective-permute-start(bf16[2,128,2048]{2,1,0:T(8,128)(2,1)S(1)} %slice_bitcast_fusion.17), channel_id=1, source_target_pairs={{0,4},{4,0},{1,5},{5,1},{2,6},{6,2},{3,7},{7,3},{8,12},{12,8},{9,1... | collective-permute-start | bytes 3145736 | tf_op jit(solution)/shard_map/ppermute | solution.py:50
  382.0 13.1 %collective-permute-start.46 = (bf16[128,2048]{1,0:T(8,128)(2,1)}, bf16[128,2048]{1,0:T(8,128)(2,1)}, u32[]{:S(2)}, u32[]{:S(2)}) collective-permute-start(bf16[128,2048]{1,0:T(8,128)(2,1)} %fusion.17), channel_id=1, source_target_pairs={{0,4},{4,0},{1,5},{5,1},{2,6},{6,2},{3,7},{7,3},{8,12},{12,8},{9,1... | collective-permute-start | bytes 1572872 | tf_op jit(solution)/shard_map/ppermute | solution.py:50
  384.3 12.8 %collective-permute-start.48 = (bf16[128,2048]{1,0:T(8,128)(2,1)}, bf16[128,2048]{1,0:T(8,128)(2,1)}, u32[]{:S(2)}, u32[]{:S(2)}) collective-permute-start(bf16[128,2048]{1,0:T(8,128)(2,1)} %fusion.18), channel_id=1, source_target_pairs={{0,2},{2,0},{1,3},{3,1},{4,6},{6,4},{5,7},{7,5},{8,10},{10,8},{9,1... | collective-permute-start | bytes 1572872 | tf_op jit(solution)/shard_map/ppermute | solution.py:50
  404.4 22.8 %collective-permute-start.49 = (bf16[256,2048]{1,0:T(8,128)(2,1)S(1)}, bf16[256,2048]{1,0:T(8,128)(2,1)S(1)}, u32[]{:S(2)}, u32[]{:S(2)}) collective-permute-start(bf16[256,2048]{1,0:T(8,128)(2,1)S(1)} %get-tuple-element.298), channel_id=1, source_target_pairs={{0,2},{2,0},{1,3},{3,1},{4,6},{6,4},{5,7},{7,5},{8,10},{10,8},{9,1... | collective-permute-start | bytes 3145736 | tf_op jit(solution)/shard_map/ppermute | solution.py:50
  405.0 22.6 %collective-permute-start.50 = (bf16[256,2048]{1,0:T(8,128)(2,1)S(1)}, bf16[256,2048]{1,0:T(8,128)(2,1)S(1)}, u32[]{:S(2)}, u32[]{:S(2)}) collective-permute-start(bf16[256,2048]{1,0:T(8,128)(2,1)S(1)} %get-tuple-element.298), channel_id=1, source_target_pairs={{0,4},{4,0},{1,5},{5,1},{2,6},{6,2},{3,7},{7,3},{8,12},{12,8},{9,1... | collective-permute-start | bytes 3145736 | tf_op jit(solution)/shard_map/ppermute | solution.py:50
  427.9 14.4 %collective-permute-start.53 = (bf16[128,2048]{1,0:T(8,128)(2,1)S(1)}, bf16[128,2048]{1,0:T(8,128)(2,1)S(1)}, u32[]{:S(2)}, u32[]{:S(2)}) collective-permute-start(bf16[128,2048]{1,0:T(8,128)(2,1)S(1)} %slice.278), channel_id=1, source_target_pairs={{0,2},{2,0},{1,3},{3,1},{4,6},{6,4},{5,7},{7,5},{8,10},{10,8},{9,1... | collective-permute-start | bytes 1572872 | tf_op jit(solution)/shard_map/ppermute | solution.py:50
  429.5 14.1 %collective-permute-start.52 = (bf16[128,2048]{1,0:T(8,128)(2,1)S(1)}, bf16[128,2048]{1,0:T(8,128)(2,1)S(1)}, u32[]{:S(2)}, u32[]{:S(2)}) collective-permute-start(bf16[128,2048]{1,0:T(8,128)(2,1)S(1)} %slice.277), channel_id=1, source_target_pairs={{0,4},{4,0},{1,5},{5,1},{2,6},{6,2},{3,7},{7,3},{8,12},{12,8},{9,1... | collective-permute-start | bytes 1572872 | tf_op jit(solution)/shard_map/ppermute | solution.py:50
  460.7 224.7 %reduce-scatter.7.cloned.1.call-start = ((), (), s32[]{:S(2)}) async-start(), calls=%async_computation.15 | async-start | bytes 10485760 | tf_op jit(solution)/shard_map/reduce_scatter | solution.py:139
  495.1 14.6 %collective-permute-start.19 = (bf16[1024,2048]{1,0:T(8,128)(2,1)}, bf16[1024,2048]{1,0:T(8,128)(2,1)S(1)}, u32[]{:S(2)}, u32[]{:S(2)}) collective-permute-start(bf16[1024,2048]{1,0:T(8,128)(2,1)} %branch_1_fun.6), channel_id=1, source_target_pairs={{0,1},{1,0},{2,3},{3,2},{4,5},{5,4},{6,7},{7,6},{8,9},{9,8},{10,11... | collective-permute-start | bytes 12582920 | tf_op jit(solution)/shard_map/cond/branch_1_fun/ppermute | solution.py:50
  514.3 25.5 %collective-permute-start.20 = (bf16[2,128,2048]{2,1,0:T(8,128)(2,1)S(1)}, bf16[2,128,2048]{2,1,0:T(8,128)(2,1)S(1)}, u32[]{:S(2)}, u32[]{:S(2)}) collective-permute-start(bf16[2,128,2048]{2,1,0:T(8,128)(2,1)S(1)} %slice_bitcast_fusion.9), channel_id=1, source_target_pairs={{0,2},{2,0},{1,3},{3,1},{4,6},{6,4},{5,7},{7,5},{8,10},{10,8},{9,1... | collective-permute-start | bytes 3145736 | tf_op jit(solution)/shard_map/cond/branch_1_fun/ppermute | solution.py:50
  514.4 25.4 %collective-permute-start.21 = (bf16[2,128,2048]{2,1,0:T(8,128)(2,1)S(1)}, bf16[2,128,2048]{2,1,0:T(8,128)(2,1)S(1)}, u32[]{:S(2)}, u32[]{:S(2)}) collective-permute-start(bf16[2,128,2048]{2,1,0:T(8,128)(2,1)S(1)} %slice_bitcast_fusion.8), channel_id=1, source_target_pairs={{0,4},{4,0},{1,5},{5,1},{2,6},{6,2},{3,7},{7,3},{8,12},{12,8},{9,1... | collective-permute-start | bytes 3145736 | tf_op jit(solution)/shard_map/cond/branch_1_fun/ppermute | solution.py:50
  542.8 242.0 %reduce-scatter.9.cloned.1.call-start = ((), (), s32[]{:S(2)}) async-start(), calls=%async_computation.16 | async-start | bytes 3932160 | tf_op jit(solution)/shard_map/reduce_scatter | solution.py:139
  552.7 13.4 %collective-permute-start.1 = (bf16[128,2048]{1,0:T(8,128)(2,1)S(1)}, bf16[128,2048]{1,0:T(8,128)(2,1)S(1)}, u32[]{:S(2)}, u32[]{:S(2)}) collective-permute-start(bf16[128,2048]{1,0:T(8,128)(2,1)S(1)} %fusion.5), channel_id=1, source_target_pairs={{0,2},{2,0},{1,3},{3,1},{4,6},{6,4},{5,7},{7,5},{8,10},{10,8},{9,1... | collective-permute-start | bytes 1572872 | tf_op jit(solution)/shard_map/cond/branch_1_fun/ppermute | solution.py:50
  555.7 12.8 %collective-permute-start = (bf16[128,2048]{1,0:T(8,128)(2,1)S(1)}, bf16[128,2048]{1,0:T(8,128)(2,1)S(1)}, u32[]{:S(2)}, u32[]{:S(2)}) collective-permute-start(bf16[128,2048]{1,0:T(8,128)(2,1)S(1)} %fusion.4), channel_id=1, source_target_pairs={{0,4},{4,0},{1,5},{5,1},{2,6},{6,2},{3,7},{7,3},{8,12},{12,8},{9,1... | collective-permute-start | bytes 1572872 | tf_op jit(solution)/shard_map/cond/branch_1_fun/ppermute | solution.py:50
  574.9 23.2 %collective-permute-start.2 = (bf16[256,2048]{1,0:T(8,128)(2,1)S(1)}, bf16[256,2048]{1,0:T(8,128)(2,1)S(1)}, u32[]{:S(2)}, u32[]{:S(2)}) collective-permute-start(bf16[256,2048]{1,0:T(8,128)(2,1)S(1)} %get-tuple-element.295), channel_id=1, source_target_pairs={{0,2},{2,0},{1,3},{3,1},{4,6},{6,4},{5,7},{7,5},{8,10},{10,8},{9,1... | collective-permute-start | bytes 3145736 | tf_op jit(solution)/shard_map/cond/branch_1_fun/ppermute | solution.py:50
  575.6 23.3 %collective-permute-start.3 = (bf16[256,2048]{1,0:T(8,128)(2,1)S(1)}, bf16[256,2048]{1,0:T(8,128)(2,1)S(1)}, u32[]{:S(2)}, u32[]{:S(2)}) collective-permute-start(bf16[256,2048]{1,0:T(8,128)(2,1)S(1)} %get-tuple-element.295), channel_id=1, source_target_pairs={{0,4},{4,0},{1,5},{5,1},{2,6},{6,2},{3,7},{7,3},{8,12},{12,8},{9,1... | collective-permute-start | bytes 3145736 | tf_op jit(solution)/shard_map/cond/branch_1_fun/ppermute | solution.py:50
  599.4 14.4 %collective-permute-start.6 = (bf16[128,2048]{1,0:T(8,128)(2,1)S(1)}, bf16[128,2048]{1,0:T(8,128)(2,1)S(1)}, u32[]{:S(2)}, u32[]{:S(2)}) collective-permute-start(bf16[128,2048]{1,0:T(8,128)(2,1)S(1)} %slice.252), channel_id=1, source_target_pairs={{0,2},{2,0},{1,3},{3,1},{4,6},{6,4},{5,7},{7,5},{8,10},{10,8},{9,1... | collective-permute-start | bytes 1572872 | tf_op jit(solution)/shard_map/cond/branch_1_fun/ppermute | solution.py:50
  600.5 14.1 %collective-permute-start.5 = (bf16[128,2048]{1,0:T(8,128)(2,1)S(1)}, bf16[128,2048]{1,0:T(8,128)(2,1)S(1)}, u32[]{:S(2)}, u32[]{:S(2)}) collective-permute-start(bf16[128,2048]{1,0:T(8,128)(2,1)S(1)} %slice.251), channel_id=1, source_target_pairs={{0,4},{4,0},{1,5},{5,1},{2,6},{6,2},{3,7},{7,3},{8,12},{12,8},{9,1... | collective-permute-start | bytes 1572872 | tf_op jit(solution)/shard_map/cond/branch_1_fun/ppermute | solution.py:50
  701.0 83.8 %all-to-all-start.4 = ((bf16[8,64,2048]{2,1,0:T(8,128)(2,1)}), bf16[8,64,2048]{2,1,0:T(8,128)(2,1)S(1)}, u32[]{:S(2)}, u32[]{:S(2)}) async-start(bf16[8,64,2048]{2,1,0:T(8,128)(2,1)} %bitcast.302), calls=%async_computation.7 | async-start | bytes 4194304 | tf_op jit(solution)/shard_map/all_to_all | solution.py:509
  704.6 92.1 %reduce-scatter.11.cloned.1.call-start = ((), (), s32[]{:S(2)}) async-start(), calls=%async_computation.17 | async-start | bytes 1310720 | tf_op jit(solution)/shard_map/reduce_scatter | solution.py:139
  714.1 19.7 %collective-permute-start.24 = (f32[16,4,64]{2,1,0:T(4,128)S(1)}, f32[16,4,64]{2,1,0:T(4,128)S(1)}, u32[]{:S(2)}, u32[]{:S(2)}) collective-permute-start(f32[16,4,64]{2,1,0:T(4,128)S(1)} %bitcast.344), channel_id=1, source_target_pairs={{0,4},{4,0},{1,5},{5,1},{2,6},{6,2},{3,7},{7,3},{8,12},{12,8},{9,1... | collective-permute-start | bytes 49160 | tf_op jit(solution)/shard_map/cond/branch_1_fun/ppermute | solution.py:126
  731.9 27.5 %collective-permute-start.28 = (bf16[2,128,2048]{2,1,0:T(8,128)(2,1)}, bf16[2,128,2048]{2,1,0:T(8,128)(2,1)}, u32[]{:S(2)}, u32[]{:S(2)}) collective-permute-start(bf16[2,128,2048]{2,1,0:T(8,128)(2,1)} %slice_bitcast_fusion.11), channel_id=1, source_target_pairs={{0,4},{4,0},{1,5},{5,1},{2,6},{6,2},{3,7},{7,3},{8,12},{12,8},{9,1... | collective-permute-start | bytes 3145736 | tf_op jit(solution)/shard_map/cond/branch_1_fun/ppermute | solution.py:50
  732.1 27.2 %collective-permute-start.23 = (bf16[2,128,2048]{2,1,0:T(8,128)(2,1)}, bf16[2,128,2048]{2,1,0:T(8,128)(2,1)}, u32[]{:S(2)}, u32[]{:S(2)}) collective-permute-start(bf16[2,128,2048]{2,1,0:T(8,128)(2,1)} %slice_bitcast_fusion.14), channel_id=1, source_target_pairs={{0,2},{2,0},{1,3},{3,1},{4,6},{6,4},{5,7},{7,5},{8,10},{10,8},{9,1... | collective-permute-start | bytes 3145736 | tf_op jit(solution)/shard_map/cond/branch_1_fun/ppermute | solution.py:50
  733.8 23.8 %collective-permute-start.25 = (f32[8,4,64]{2,1,0:T(4,128)S(1)}, f32[8,4,64]{2,1,0:T(4,128)S(1)}, u32[]{:S(2)}, u32[]{:S(2)}) collective-permute-start(f32[8,4,64]{2,1,0:T(4,128)S(1)} %slice_select_fusion.2), channel_id=1, source_target_pairs={{0,2},{2,0},{1,3},{3,1},{4,6},{6,4},{5,7},{7,5},{8,10},{10,8},{9,1... | collective-permute-start | bytes 24584 | tf_op jit(solution)/shard_map/cond/branch_1_fun/ppermute | solution.py:126
  762.4 14.4 %collective-permute-start.27 = (bf16[128,2048]{1,0:T(8,128)(2,1)S(1)}, bf16[128,2048]{1,0:T(8,128)(2,1)S(1)}, u32[]{:S(2)}, u32[]{:S(2)}) collective-permute-start(bf16[128,2048]{1,0:T(8,128)(2,1)S(1)} %fusion.10), channel_id=1, source_target_pairs={{0,4},{4,0},{1,5},{5,1},{2,6},{6,2},{3,7},{7,3},{8,12},{12,8},{9,1... | collective-permute-start | bytes 1572872 | tf_op jit(solution)/shard_map/cond/branch_1_fun/ppermute | solution.py:50
  764.3 14.1 %collective-permute-start.29 = (bf16[128,2048]{1,0:T(8,128)(2,1)S(1)}, bf16[128,2048]{1,0:T(8,128)(2,1)S(1)}, u32[]{:S(2)}, u32[]{:S(2)}) collective-permute-start(bf16[128,2048]{1,0:T(8,128)(2,1)S(1)} %fusion.11), channel_id=1, source_target_pairs={{0,2},{2,0},{1,3},{3,1},{4,6},{6,4},{5,7},{7,5},{8,10},{10,8},{9,1... | collective-permute-start | bytes 1572872 | tf_op jit(solution)/shard_map/cond/branch_1_fun/ppermute | solution.py:50
  784.8 16.1 %all-to-all-start.5 = ((bf16[8,64,768]{2,1,0:T(8,128)(2,1)}), bf16[8,64,768]{2,1,0:T(8,128)(2,1)S(1)}, u32[]{:S(2)}, u32[]{:S(2)}) async-start(bf16[8,64,768]{2,1,0:T(8,128)(2,1)} %bitcast.322), calls=%async_computation.8 | async-start | bytes 1572864 | tf_op jit(solution)/shard_map/all_to_all | solution.py:509
  (68 other events, 780.3 us)
Sparse Core Ops, SparseCore 0:
  10.2 30.6 all-gather.4
  42.4 62.9 all-gather.6
  107.0 148.3 all-gather.8
  257.4 78.9 all-gather.10
  460.9 74.0 reduce-scatter.4
  542.9 142.4 reduce-scatter.6
  687.9 60.9 reduce-scatter.8
  751.3 27.1 reduce-scatter.10
